TPU v7x, 32 devices: a whole 2x2x4 slice. The times are simulated.
32 devices in a mesh: rows: 32 (over z, y, x, core).
Axes of the slice: x: 2, y: 2, z: 4, core: 2. Of those that a mesh axis runs over, the one named last changes fastest.
Arguments:
- residual: float32 [16384, 128], P('rows'), may hold values from -6 to 6
- inv_diag: float32 [16384, 512], P('rows'), may hold values from -0.25 to 0.25
- coupling_tiles: float32 [16384, 6, 512], P('rows'), may hold values from -0.0546875 to 0.0546875
- colour: int32 [32], P('rows'), may hold values from 0 to 3, as said below
- tile_cols: int32 [32, 6], P('rows'), may hold values from 0 to 31, as said below
Outputs:
- precond: float32 [16384, 128], P('rows')
Inputs may be any that keep to these rules, and one draw needn't show every extreme that they name: Every aligned group of 4 blocks (blocks 4 g to 4 g + 3) holds each colour exactly once. `tile_cols`: row b lists 6 distinct blocks, each within 4 places of b along the cycle of blocks (indices modulo 32), none equal to b and none of b's colour.
All inputs are finite; a program needn't handle non-finite values.
Results may differ from a plain program's by a relative error of at most 0.0001.
Values sent between devices are 32-bit elements; how exact they have to be, the bound alone decides.
No kernel may reach another device: no remote copies, remote signals or barrier semaphores. Data moves between devices by JAX's collectives and lax.ppermute only.
A program may use at most 128 MiB of HBM per device.

v0:
```python
import functools

import jax
import jax.numpy as jnp
from jax import lax
from jax.experimental import pallas as pl
from jax.experimental.pallas import tpu as pltpu
from jax.sharding import PartitionSpec as P

COLOURS = 4
SIDES = 3
OWN_COLOUR = 0
SIB_COLOUR = 1
TILE_START = 2
VMEM_LIMIT = 56 * 1024 * 1024


def dot(a, b):
    return jnp.dot(a, b, preferred_element_type=jnp.float32)


def split(value):
    high = value.astype(jnp.bfloat16).astype(jnp.float32)
    return high, value - high


def left_lanes(shape):
    return lax.broadcasted_iota(jnp.int32, shape, 1) < shape[1] // 2


def swap_halves(value):
    return pltpu.roll(value, value.shape[1] // 2, 1)


def both_parts(packed):
    high, low = split(packed)
    left = left_lanes(packed.shape)
    upper = jnp.where(left, high, swap_halves(low))
    lower = jnp.where(left, swap_halves(high), low)
    return jnp.concatenate([upper, lower], axis=0).astype(jnp.bfloat16)


def vmem():
    return pl.BlockSpec(memory_space=pltpu.VMEM)


def smem():
    return pl.BlockSpec(memory_space=pltpu.SMEM)


def anywhere():
    return pl.BlockSpec(memory_space=pl.ANY)


def params():
    return pltpu.CompilerParams(vmem_limit_bytes=VMEM_LIMIT)


def first_kernel(core_ref, inverse_ref, residual_ref, keep_ref, send_ref):
    d_high, d_low = split(inverse_ref[...])
    r_high, r_low = split(residual_ref[...])
    d_high, d_low, r_high, r_low = (v.astype(jnp.bfloat16) for v in (d_high, d_low, r_high, r_low))
    value = dot(d_high, r_high) + (dot(d_high, r_low) + dot(d_low, r_high))
    half = value.shape[0] // 2
    upper, lower = value[:half], value[half:]
    left = left_lanes(upper.shape)
    first = jnp.where(left, upper, swap_halves(lower))
    second = jnp.where(left, swap_halves(upper), lower)
    is_first = core_ref[0] == 0
    keep_ref[...] = jnp.where(is_first, first, second)
    send_ref[...] = jnp.where(is_first, second, first)


def last_kernel(core_ref, mine_ref, other_ref, out_ref):
    is_first = core_ref[0] == 0
    mine, other = mine_ref[...], other_ref[...]
    first = jnp.where(is_first, mine, other)
    second = jnp.where(is_first, other, mine)
    half = mine.shape[0]
    left = left_lanes(mine.shape)
    out_ref[:half] = jnp.where(left, first, swap_halves(second))
    out_ref[half:] = jnp.where(left, swap_halves(first), second)


def tile_of(meta_ref, own, tiles, colour, side):
    wanted = meta_ref[TILE_START + 2 * tiles + side * COLOURS + colour]
    start = jnp.where(own, TILE_START, TILE_START + tiles)
    found = jnp.int32(-1)
    for k in range(tiles):
        found = jnp.where(meta_ref[start + k] == wanted, k, found)
    return found


def gather_kernel(now, newest, older, meta_ref, own_tiles, sib_tiles, own_inverse, sib_inverse, *refs):
    known = refs[: SIDES * len(older)]
    w_high, w_low, d_high, d_low, partial = refs[SIDES * len(older) : SIDES * len(older) + 5]
    buffer, total, sems = refs[SIDES * len(older) + 5 :]
    tiles, block = own_tiles.shape[0], own_tiles.shape[1]
    own = meta_ref[OWN_COLOUR] == now
    active = own | (meta_ref[SIB_COLOUR] == now)
    slots = [(newest, side) for side in range(SIDES)] + [(c, side) for c in older for side in range(SIDES)]

    @pl.when(active)
    def _():
        def fetch(own_src, sib_src, slot, start):
            @pl.when(own)
            def _():
                copy = pltpu.make_async_copy(own_src, buffer.at[slot], sems.at[slot])
                copy.start() if start else copy.wait()

            @pl.when(jnp.logical_not(own))
            def _():
                copy = pltpu.make_async_copy(sib_src, buffer.at[slot], sems.at[slot])
                copy.start() if start else copy.wait()

        which = [tile_of(meta_ref, own, tiles, c, side) for c, side in slots]
        fetch(own_inverse, sib_inverse, len(slots), True)
        for slot, k in enumerate(which):
            @pl.when(k >= 0)
            def _():
                fetch(own_tiles.at[k], sib_tiles.at[k], slot, True)

        fetch(own_inverse, sib_inverse, len(slots), False)
        high, low = split(buffer[len(slots)])
        d_high[...] = high.astype(jnp.bfloat16)
        d_low[...] = low.astype(jnp.bfloat16)
        total[...] = jnp.zeros_like(total)
        for slot, k in enumerate(which):
            span = pl.ds(slot * block, block)

            @pl.when(k >= 0)
            def _():
                fetch(own_tiles.at[k], sib_tiles.at[k], slot, False)
                high, low = split(buffer[slot])
                high, low = high.astype(jnp.bfloat16), low.astype(jnp.bfloat16)
                if slot < SIDES:
                    w_high[:, span] = high
                    w_low[:, span] = low
                else:
                    value = both_parts(known[slot - SIDES][...])
                    total[...] += dot(high, value) + dot(low, value)

            if slot < SIDES:
                @pl.when(k < 0)
                def _():
                    w_high[:, span] = jnp.zeros((block, block), jnp.bfloat16)
                    w_low[:, span] = jnp.zeros((block, block), jnp.bfloat16)

        partial[...] = total[...] + swap_halves(total[...])


def relax_kernel(now, meta_ref, w_high, w_low, d_high, d_low, partial, behind, here, ahead, own_start, sib_start, out_ref, stacked):
    own = meta_ref[OWN_COLOUR] == now
    active = own | (meta_ref[SIB_COLOUR] == now)
    block = d_high.shape[0]

    @pl.when(active)
    def _():
        for side, ref in enumerate((behind, here, ahead)):
            stacked[pl.ds(side * block, block), :] = both_parts(ref[...])
        value = stacked[...]
        coupled = dot(w_high[...], value) + dot(w_low[...], value)
        coupled = partial[...] + (coupled + swap_halves(coupled))
        high, low = split(coupled)
        operand = jnp.where(left_lanes(high.shape), high, low).astype(jnp.bfloat16)
        change = dot(d_high[...], operand) + dot(d_low[...], operand)
        change = change + swap_halves(change)
        upper, lower = change[: block // 2], change[block // 2 :]
        start = jnp.where(own, own_start[...], sib_start[...])
        out_ref[...] = start - jnp.where(left_lanes(upper.shape), upper, lower)


def gather(now, newest, older, meta, own_tiles, sib_tiles, own_inverse, sib_inverse, known):
    block, cols = own_tiles.shape[1], known[newest][0].shape[1]
    slots = SIDES * (1 + len(older)) + 1
    operands = [value for c in older for value in known[c]]
    return pl.pallas_call(
        functools.partial(gather_kernel, now, newest, older),
        out_shape=[
            pltpu.VMEM((block, SIDES * block), jnp.bfloat16),
            pltpu.VMEM((block, SIDES * block), jnp.bfloat16),
            pltpu.VMEM((block, block), jnp.bfloat16),
            pltpu.VMEM((block, block), jnp.bfloat16),
            pltpu.VMEM((block, cols), jnp.float32),
        ],
        in_specs=[smem()] + [anywhere()] * 4 + [vmem()] * len(operands),
        out_specs=[vmem()] * 5,
        scratch_shapes=[
            pltpu.VMEM((slots, block, block), jnp.float32),
            pltpu.VMEM((block, cols), jnp.float32),
            pltpu.SemaphoreType.DMA((slots,)),
        ],
        compiler_params=params(),
        cost_estimate=pl.CostEstimate(
            flops=4 * block * block * cols * slots, bytes_accessed=4 * block * block * slots, transcendentals=0
        ),
        name=f"gather_{now}_{newest}",
    )(meta, own_tiles, sib_tiles, own_inverse, sib_inverse, *operands)


def relax(now, meta, gathered, latest, own_start, sib_start):
    block, cols = gathered[2].shape[0], own_start.shape[1]
    gathered = [pltpu.with_memory_space_constraint(g, pltpu.VMEM) for g in gathered]
    return pl.pallas_call(
        functools.partial(relax_kernel, now),
        out_shape=jax.ShapeDtypeStruct(own_start.shape, jnp.float32),
        in_specs=[smem()] + [vmem()] * 10,
        out_specs=vmem(),
        scratch_shapes=[pltpu.VMEM((SIDES * block, cols), jnp.bfloat16)],
        compiler_params=params(),
        cost_estimate=pl.CostEstimate(
            flops=16 * block * block * cols, bytes_accessed=16 * block * block, transcendentals=0
        ),
        name=f"relax_{now}",
    )(meta, *gathered, *latest, own_start, sib_start)


def per_device(residual, inv_diag, coupling_tiles, colour, tile_cols):
    axis = "rows"
    count = lax.axis_size(axis)
    groups = count // COLOURS
    me = lax.axis_index(axis)
    core = (me % 2).reshape(1)
    place = me % COLOURS
    group = me // COLOURS
    block, cols = residual.shape
    tiles = jnp.transpose(coupling_tiles, (1, 0, 2))
    number = tiles.shape[0]

    def flip(value, bit):
        return lax.ppermute(value, axis, [(i, i ^ bit) for i in range(count)])

    def shift(value, by):
        return lax.ppermute(value, axis, [(i, (i + by) % count) for i in range(count)])

    own_facts = jnp.concatenate([colour, tile_cols[0]])
    sib_facts = flip(own_facts, 1)
    own_colour, sib_colour = own_facts[0], sib_facts[0]
    wheel = jnp.arange(COLOURS, dtype=jnp.int32)
    pair_places = jnp.where(wheel == own_colour, place, 0) + jnp.where(wheel == sib_colour, place ^ 1, 0)
    group_places = pair_places + flip(pair_places, 2)
    places = [shift(group_places, COLOURS), group_places, shift(group_places, -COLOURS)]
    blocks = [(((group + side - 1) % groups) * COLOURS + places[side]).astype(jnp.int32) for side in range(SIDES)]
    meta = jnp.concatenate([own_facts[:1], sib_facts[:1], own_facts[1:], sib_facts[1:]] + blocks)

    keep, send = pl.pallas_call(
        first_kernel,
        out_shape=[jax.ShapeDtypeStruct((block // 2, cols), jnp.float32)] * 2,
        in_specs=[smem(), vmem(), vmem()],
        out_specs=[vmem()] * 2,
        compiler_params=params(),
        name="first",
    )(core, inv_diag, residual)
    own_start, sib_start = keep, flip(send, 1)
    sib_inverse = flip(inv_diag, 1)
    sib_tiles = flip(tiles, 1)

    def spread(candidate, now):
        here_now = (own_colour == now) | (sib_colour == now)
        here = jnp.where(here_now, candidate, flip(candidate, 2))
        return [shift(here, COLOURS), here, shift(here, -COLOURS)]

    candidate = jnp.where(own_colour == 0, own_start, sib_start)
    own_final, sib_final = own_start, sib_start
    known = {0: spread(candidate, 0)}
    order = list(range(1, COLOURS)) + list(range(COLOURS - 2, -1, -1))
    newest = 0
    for step, now in enumerate(order):
        older = tuple(c for c in sorted(known) if c not in (now, newest))
        gathered = gather(now, newest, older, meta, tiles, sib_tiles, inv_diag, sib_inverse, known)
        candidate = relax(now, meta, gathered, known[newest], own_start, sib_start)
        if step >= COLOURS - 2:
            own_final = jnp.where(own_colour == now, candidate, own_final)
            sib_final = jnp.where(sib_colour == now, candidate, sib_final)
        if step < len(order) - 1:
            known[now] = spread(candidate, now)
        newest = now

    return pl.pallas_call(
        last_kernel,
        out_shape=jax.ShapeDtypeStruct((block, cols), jnp.float32),
        in_specs=[smem(), vmem(), vmem()],
        out_specs=vmem(),
        compiler_params=params(),
        name="last",
    )(core, own_final, flip(sib_final, 1))


def solution(mesh):
    in_specs = (P("rows", None), P("rows", None), P("rows", None, None), P("rows"), P("rows", None))
    out_specs = P("rows", None)
    return jax.shard_map(
        per_device, mesh=mesh, in_specs=in_specs, out_specs=out_specs, check_vma=False
    )
```

profile of v0, /device:TPU:0, one launch (start us, length us, event | category | flops | bytes accessed | tf_op | source)
XLA Modules:
  0.0 146.3 jit_solution(5032740379522529137)
XLA Ops:
  1.1 0.7 pad_add_fusion
  2.4 2.6 %first.1 = (f32[256,128]{1,0:T(8,128)}, f32[256,128]{1,0:T(8,128)}) custom-call(s32[1]{0:T(128)} %bitcast.core_ref, f32[512,512]{1,0:T(8,128)} %own_inverse.11, f32[512,128]{1,0:T(8,128)} %residual_ref.1), custom_call_target="tpu_custom_call" | custom-call | tf_op jit(solution)/shard_map/first/pallas_call | solution.py:246
  5.0 5.2 %collective-permute-done = s32[7]{0:T(128)S(1)} collective-permute-done((s32[7]{0:T(128)S(1)}, s32[7]{0:T(128)S(1)}, u32[]{:S(2)}, u32[]{:S(2)}) %collective-permute-start) | collective-permute-done | bytes 60 | tf_op jit(solution)/shard_map/ppermute | solution.py:231
  10.3 2.9 %collective-permute-start.1 = (s32[4]{0:T(128)S(1)}, s32[4]{0:T(128)S(1)}, u32[]{:S(2)}, u32[]{:S(2)}) collective-permute-start(s32[4]{0:T(128)S(1)} %fusion), channel_id=1, source_target_pairs={{0,2},{1,3},{2,0},{3,1},{4,6},{5,7},{6,4},{7,5},{8,10},{9,11},{10,... | collective-permute-start | bytes 56 | tf_op jit(solution)/shard_map/ppermute | solution.py:231
  13.3 1.4 collective-permute-done.1
  14.8 5.1 %collective-permute-start.3 = (s32[4]{0:T(128)S(1)}, s32[4]{0:T(128)S(1)}, u32[]{:S(2)}, u32[]{:S(2)}) collective-permute-start(s32[4]{0:T(128)S(1)} %get-tuple-element.70), channel_id=1, source_target_pairs={{0,28},{1,29},{2,30},{3,31},{4,0},{5,1},{6,2},{7,3},{8,4},{9,5},{1... | collective-permute-start | bytes 56 | tf_op jit(solution)/shard_map/ppermute | solution.py:234
  19.9 1.0 broadcast_select_fusion.6
  21.5 4.4 %collective-permute-done.7 = f32[256,128]{1,0:T(8,128)S(1)} collective-permute-done((f32[256,128]{1,0:T(8,128)S(1)}, f32[256,128]{1,0:T(8,128)S(1)}, u32[]{:S(2)}, u32[]{:S(2)}) %collective-permute-start.7) | collective-permute-done | bytes 131104 | tf_op jit(solution)/shard_map/ppermute | solution.py:231
  26.0 4.8 %collective-permute-start.9 = (f32[256,128]{1,0:T(8,128)S(1)}, f32[256,128]{1,0:T(8,128)S(1)}, u32[]{:S(2)}, u32[]{:S(2)}) collective-permute-start(f32[256,128]{1,0:T(8,128)S(1)} %broadcast_select_fusion.3.here.refs_1_), channel_id=1, source_target_pairs={{0,28},{1,29},{2,30},{3,31},{4,0},{5,1},{6,2},{7,3},{8,4},{9,5},{1... | collective-permute-start | bytes 393224 | tf_op jit(solution)/shard_map/ppermute | solution.py:234
  31.4 1.0 copy-done
  33.3 5.1 %collective-permute-done.8.behind.refs_0_ = f32[256,128]{1,0:T(8,128)S(1)} collective-permute-done((f32[256,128]{1,0:T(8,128)S(1)}, f32[256,128]{1,0:T(8,128)S(1)}, u32[]{:S(2)}, u32[]{:S(2)}) %collective-permute-start.8) | collective-permute-done | bytes 131104 | tf_op jit(solution)/shard_map/ppermute | solution.py:234
  39.1 1.8 %relax_1.2 = f32[256,128]{1,0:T(8,128)} custom-call(s32[26]{0:T(128)} %concatenate.7.meta_ref, bf16[512,1536]{1,0:T(8,128)(2,1)S(1)} %get-tuple-element.39.w_high, bf16[512,1536]{1,0:T(8,128)(2,1)S(1)} %get-tuple-element.40.w_low, bf16[512,512]{1,0:T(8,128)(2,1)S(1)} %get-tuple-element.41.d_high, bf16[512,512]{1,0:T(8,128)(2,1)S(1)} %get-tuple-element.42.d_low, ...), custom_call_target="tpu_custom_call" | custom-call | flops 536870912 | bytes 4194304 | tf_op jit(solution)/shard_map/relax_1/pallas_call | solution.py:204
  40.9 2.6 %collective-permute-start.10 = (f32[256,128]{1,0:T(8,128)}, f32[256,128]{1,0:T(8,128)S(1)}, u32[]{:S(2)}, u32[]{:S(2)}) collective-permute-start(f32[256,128]{1,0:T(8,128)} %relax_1.2), channel_id=1, source_target_pairs={{0,2},{1,3},{2,0},{3,1},{4,6},{5,7},{6,4},{7,5},{8,10},{9,11},{10,... | collective-permute-start | bytes 393224 | tf_op jit(solution)/shard_map/ppermute | solution.py:231
  43.6 3.1 %collective-permute-done.10 = f32[256,128]{1,0:T(8,128)S(1)} collective-permute-done((f32[256,128]{1,0:T(8,128)}, f32[256,128]{1,0:T(8,128)S(1)}, u32[]{:S(2)}, u32[]{:S(2)}) %collective-permute-start.10) | collective-permute-done | bytes 131104 | tf_op jit(solution)/shard_map/ppermute | solution.py:231
  46.7 1.7 %collective-permute-start.12 = (f32[256,128]{1,0:T(8,128)S(1)}, f32[256,128]{1,0:T(8,128)S(1)}, u32[]{:S(2)}, u32[]{:S(2)}) collective-permute-start(f32[256,128]{1,0:T(8,128)S(1)} %broadcast_select_fusion.2.refs_4_.here), channel_id=1, source_target_pairs={{0,28},{1,29},{2,30},{3,31},{4,0},{5,1},{6,2},{7,3},{8,4},{9,5},{1... | collective-permute-start | bytes 393224 | tf_op jit(solution)/shard_map/ppermute | solution.py:234
  48.8 1.1 gather_2_1.1
  49.9 2.2 %collective-permute-done.12.refs_5_.ahead = f32[256,128]{1,0:T(8,128)S(1)} collective-permute-done((f32[256,128]{1,0:T(8,128)S(1)}, f32[256,128]{1,0:T(8,128)S(1)}, u32[]{:S(2)}, u32[]{:S(2)}) %collective-permute-start.12) | collective-permute-done | bytes 131104 | tf_op jit(solution)/shard_map/ppermute | solution.py:234
  52.1 4.0 %collective-permute-done.11.refs_3_.behind = f32[256,128]{1,0:T(8,128)S(1)} collective-permute-done((f32[256,128]{1,0:T(8,128)S(1)}, f32[256,128]{1,0:T(8,128)S(1)}, u32[]{:S(2)}, u32[]{:S(2)}) %collective-permute-start.11) | collective-permute-done | bytes 131104 | tf_op jit(solution)/shard_map/ppermute | solution.py:234
  56.7 1.8 %relax_2.2 = f32[256,128]{1,0:T(8,128)} custom-call(s32[26]{0:T(128)} %concatenate.7.meta_ref, bf16[512,1536]{1,0:T(8,128)(2,1)S(1)} %get-tuple-element.54.w_high, bf16[512,1536]{1,0:T(8,128)(2,1)S(1)} %get-tuple-element.55.w_low, bf16[512,512]{1,0:T(8,128)(2,1)S(1)} %get-tuple-element.56.d_high, bf16[512,512]{1,0:T(8,128)(2,1)S(1)} %get-tuple-element.57.d_low, ...), custom_call_target="tpu_custom_call" | custom-call | flops 536870912 | bytes 4194304 | tf_op jit(solution)/shard_map/relax_2/pallas_call | solution.py:204
  58.5 5.0 %collective-permute-start.13 = (f32[256,128]{1,0:T(8,128)}, f32[256,128]{1,0:T(8,128)S(1)}, u32[]{:S(2)}, u32[]{:S(2)}) collective-permute-start(f32[256,128]{1,0:T(8,128)} %relax_2.2), channel_id=1, source_target_pairs={{0,2},{1,3},{2,0},{3,1},{4,6},{5,7},{6,4},{7,5},{8,10},{9,11},{10,... | collective-permute-start | bytes 393224 | tf_op jit(solution)/shard_map/ppermute | solution.py:231
  63.6 3.1 %collective-permute-done.13 = f32[256,128]{1,0:T(8,128)S(1)} collective-permute-done((f32[256,128]{1,0:T(8,128)}, f32[256,128]{1,0:T(8,128)S(1)}, u32[]{:S(2)}, u32[]{:S(2)}) %collective-permute-start.13) | collective-permute-done | bytes 131104 | tf_op jit(solution)/shard_map/ppermute | solution.py:231
  66.7 1.7 %collective-permute-start.15 = (f32[256,128]{1,0:T(8,128)S(1)}, f32[256,128]{1,0:T(8,128)S(1)}, u32[]{:S(2)}, u32[]{:S(2)}) collective-permute-start(f32[256,128]{1,0:T(8,128)S(1)} %broadcast_select_fusion.5.here), channel_id=1, source_target_pairs={{0,28},{1,29},{2,30},{3,31},{4,0},{5,1},{6,2},{7,3},{8,4},{9,5},{1... | collective-permute-start | bytes 393224 | tf_op jit(solution)/shard_map/ppermute | solution.py:234
  68.8 5.9 %gather_3_2.1 = (bf16[512,1536]{1,0:T(8,128)(2,1)S(1)}, bf16[512,1536]{1,0:T(8,128)(2,1)S(1)}, bf16[512,512]{1,0:T(8,128)(2,1)S(1)}, bf16[512,512]{1,0:T(8,128)(2,1)S(1)}, f32[512,128]{1,0:T(8,128)S(1)}) custom-call(s32[26]{0:T(128)} %concatenate.7.meta_ref, f32[6,512,512]{2,1,0:T(8,128)} %bitcast.15, f32[6,512,512]{2,1,0:T(8,128)} %collective-permute-done.4.sib_tiles, ...), custom_call_target="tpu_custom_call" | custom-call | flops 1342177280 | bytes 10485760 | tf_op jit(solution)/shard_map/gather_3_2/pallas_call | solution.py:177
  74.7 1.3 collective-permute-done.14.behind
  76.7 3.9 %relax_3.1 = f32[256,128]{1,0:T(8,128)} custom-call(s32[26]{0:T(128)} %concatenate.7.meta_ref, bf16[512,1536]{1,0:T(8,128)(2,1)S(1)} %get-tuple-element.49.w_high, bf16[512,1536]{1,0:T(8,128)(2,1)S(1)} %get-tuple-element.50.w_low, bf16[512,512]{1,0:T(8,128)(2,1)S(1)} %get-tuple-element.51.d_high, bf16[512,512]{1,0:T(8,128)(2,1)S(1)} %get-tuple-element.52.d_low, ...), custom_call_target="tpu_custom_call" | custom-call | flops 536870912 | bytes 4194304 | tf_op jit(solution)/shard_map/relax_3/pallas_call | solution.py:204
  80.7 5.1 %collective-permute-done.16 = f32[256,128]{1,0:T(8,128)S(1)} collective-permute-done((f32[256,128]{1,0:T(8,128)}, f32[256,128]{1,0:T(8,128)S(1)}, u32[]{:S(2)}, u32[]{:S(2)}) %collective-permute-start.16) | collective-permute-done | bytes 131104 | tf_op jit(solution)/shard_map/ppermute | solution.py:231
  85.8 0.9 broadcast_select_fusion.here.refs_4_
  86.7 1.8 %collective-permute-start.18 = (f32[256,128]{1,0:T(8,128)S(1)}, f32[256,128]{1,0:T(8,128)S(1)}, u32[]{:S(2)}, u32[]{:S(2)}) collective-permute-start(f32[256,128]{1,0:T(8,128)S(1)} %broadcast_select_fusion.here.refs_4_), channel_id=1, source_target_pairs={{0,28},{1,29},{2,30},{3,31},{4,0},{5,1},{6,2},{7,3},{8,4},{9,5},{1... | collective-permute-start | bytes 393224 | tf_op jit(solution)/shard_map/ppermute | solution.py:234
  88.8 1.3 gather_2_3.1
  90.1 1.6 %collective-permute-done.18.ahead.refs_5_ = f32[256,128]{1,0:T(8,128)S(1)} collective-permute-done((f32[256,128]{1,0:T(8,128)S(1)}, f32[256,128]{1,0:T(8,128)S(1)}, u32[]{:S(2)}, u32[]{:S(2)}) %collective-permute-start.18) | collective-permute-done | bytes 131104 | tf_op jit(solution)/shard_map/ppermute | solution.py:234
  91.8 4.4 %collective-permute-done.17.behind.refs_3_ = f32[256,128]{1,0:T(8,128)S(1)} collective-permute-done((f32[256,128]{1,0:T(8,128)S(1)}, f32[256,128]{1,0:T(8,128)S(1)}, u32[]{:S(2)}, u32[]{:S(2)}) %collective-permute-start.17) | collective-permute-done | bytes 131104 | tf_op jit(solution)/shard_map/ppermute | solution.py:234
  96.8 1.8 %relax_2.3 = f32[256,128]{1,0:T(8,128)} custom-call(s32[26]{0:T(128)} %concatenate.7.meta_ref, bf16[512,1536]{1,0:T(8,128)(2,1)S(1)} %get-tuple-element.44.w_high, bf16[512,1536]{1,0:T(8,128)(2,1)S(1)} %get-tuple-element.45.w_low, bf16[512,512]{1,0:T(8,128)(2,1)S(1)} %get-tuple-element.46.d_high, bf16[512,512]{1,0:T(8,128)(2,1)S(1)} %get-tuple-element.47.d_low, ...), custom_call_target="tpu_custom_call" | custom-call | flops 536870912 | bytes 4194304 | tf_op jit(solution)/shard_map/relax_2/pallas_call | solution.py:204
  98.7 5.0 %collective-permute-start.19 = (f32[256,128]{1,0:T(8,128)}, f32[256,128]{1,0:T(8,128)S(1)}, u32[]{:S(2)}, u32[]{:S(2)}) collective-permute-start(f32[256,128]{1,0:T(8,128)} %relax_2.3), channel_id=1, source_target_pairs={{0,2},{1,3},{2,0},{3,1},{4,6},{5,7},{6,4},{7,5},{8,10},{9,11},{10,... | collective-permute-start | bytes 393224 | tf_op jit(solution)/shard_map/ppermute | solution.py:231
  103.7 3.2 %collective-permute-done.19 = f32[256,128]{1,0:T(8,128)S(1)} collective-permute-done((f32[256,128]{1,0:T(8,128)}, f32[256,128]{1,0:T(8,128)S(1)}, u32[]{:S(2)}, u32[]{:S(2)}) %collective-permute-start.19) | collective-permute-done | bytes 131104 | tf_op jit(solution)/shard_map/ppermute | solution.py:231
  106.9 3.0 %collective-permute-start.21 = (f32[256,128]{1,0:T(8,128)S(1)}, f32[256,128]{1,0:T(8,128)S(1)}, u32[]{:S(2)}, u32[]{:S(2)}) collective-permute-start(f32[256,128]{1,0:T(8,128)S(1)} %broadcast_select_fusion.4.refs_1_.here), channel_id=1, source_target_pairs={{0,28},{1,29},{2,30},{3,31},{4,0},{5,1},{6,2},{7,3},{8,4},{9,5},{1... | collective-permute-start | bytes 393224 | tf_op jit(solution)/shard_map/ppermute | solution.py:234
  109.8 1.3 gather_1_2.1
  111.2 1.2 collective-permute-done.21.refs_2_.ahead
  112.3 5.2 %collective-permute-done.20.refs_0_.behind = f32[256,128]{1,0:T(8,128)S(1)} collective-permute-done((f32[256,128]{1,0:T(8,128)S(1)}, f32[256,128]{1,0:T(8,128)S(1)}, u32[]{:S(2)}, u32[]{:S(2)}) %collective-permute-start.20) | collective-permute-done | bytes 131104 | tf_op jit(solution)/shard_map/ppermute | solution.py:234
  118.2 2.1 %relax_1.3 = f32[256,128]{1,0:T(8,128)} custom-call(s32[26]{0:T(128)} %concatenate.7.meta_ref, bf16[512,1536]{1,0:T(8,128)(2,1)S(1)} %get-tuple-element.64.w_high, bf16[512,1536]{1,0:T(8,128)(2,1)S(1)} %get-tuple-element.65.w_low, bf16[512,512]{1,0:T(8,128)(2,1)S(1)} %get-tuple-element.66.d_high, bf16[512,512]{1,0:T(8,128)(2,1)S(1)} %get-tuple-element.67.d_low, ...), custom_call_target="tpu_custom_call" | custom-call | flops 536870912 | bytes 4194304 | tf_op jit(solution)/shard_map/relax_1/pallas_call | solution.py:204
  120.3 2.2 %collective-permute-start.22 = (f32[256,128]{1,0:T(8,128)}, f32[256,128]{1,0:T(8,128)S(1)}, u32[]{:S(2)}, u32[]{:S(2)}) collective-permute-start(f32[256,128]{1,0:T(8,128)} %relax_1.3), channel_id=1, source_target_pairs={{0,2},{1,3},{2,0},{3,1},{4,6},{5,7},{6,4},{7,5},{8,10},{9,11},{10,... | collective-permute-start | bytes 393224 | tf_op jit(solution)/shard_map/ppermute | solution.py:231
  122.5 3.2 %collective-permute-done.22 = f32[256,128]{1,0:T(8,128)S(1)} collective-permute-done((f32[256,128]{1,0:T(8,128)}, f32[256,128]{1,0:T(8,128)S(1)}, u32[]{:S(2)}, u32[]{:S(2)}) %collective-permute-start.22) | collective-permute-done | bytes 131104 | tf_op jit(solution)/shard_map/ppermute | solution.py:231
  125.7 2.8 %collective-permute-start.24 = (f32[256,128]{1,0:T(8,128)S(1)}, f32[256,128]{1,0:T(8,128)S(1)}, u32[]{:S(2)}, u32[]{:S(2)}) collective-permute-start(f32[256,128]{1,0:T(8,128)S(1)} %broadcast_select_fusion.1.here), channel_id=1, source_target_pairs={{0,28},{1,29},{2,30},{3,31},{4,0},{5,1},{6,2},{7,3},{8,4},{9,5},{1... | collective-permute-start | bytes 393224 | tf_op jit(solution)/shard_map/ppermute | solution.py:234
  128.5 6.0 %gather_0_1.1 = (bf16[512,1536]{1,0:T(8,128)(2,1)S(1)}, bf16[512,1536]{1,0:T(8,128)(2,1)S(1)}, bf16[512,512]{1,0:T(8,128)(2,1)S(1)}, bf16[512,512]{1,0:T(8,128)(2,1)S(1)}, f32[512,128]{1,0:T(8,128)S(1)}) custom-call(s32[26]{0:T(128)} %concatenate.7.meta_ref, f32[6,512,512]{2,1,0:T(8,128)} %bitcast.18, f32[6,512,512]{2,1,0:T(8,128)} %collective-permute-done.4.sib_tiles, ...), custom_call_target="tpu_custom_call" | custom-call | flops 1342177280 | bytes 10485760 | tf_op jit(solution)/shard_map/gather_0_1/pallas_call | solution.py:177
  134.5 1.7 %collective-permute-done.23.behind = f32[256,128]{1,0:T(8,128)S(1)} collective-permute-done((f32[256,128]{1,0:T(8,128)S(1)}, f32[256,128]{1,0:T(8,128)S(1)}, u32[]{:S(2)}, u32[]{:S(2)}) %collective-permute-start.23) | collective-permute-done | bytes 131104 | tf_op jit(solution)/shard_map/ppermute | solution.py:234
  136.9 4.0 %relax_0.1 = f32[256,128]{1,0:T(8,128)} custom-call(s32[26]{0:T(128)} %concatenate.7.meta_ref, bf16[512,1536]{1,0:T(8,128)(2,1)S(1)} %get-tuple-element.59.w_high, bf16[512,1536]{1,0:T(8,128)(2,1)S(1)} %get-tuple-element.60.w_low, bf16[512,512]{1,0:T(8,128)(2,1)S(1)} %get-tuple-element.61.d_high, bf16[512,512]{1,0:T(8,128)(2,1)S(1)} %get-tuple-element.62.d_low, ...), custom_call_target="tpu_custom_call" | custom-call | flops 536870912 | bytes 4194304 | tf_op jit(solution)/shard_map/relax_0/pallas_call | solution.py:204
  140.9 1.6 %select_select_fusion = (f32[256,128]{1,0:T(8,128)S(1)}, f32[256,128]{1,0:T(8,128)}) fusion(f32[256,128]{1,0:T(8,128)} %relax_0.1, f32[256,128]{1,0:T(8,128)S(1)} %copy-done.16, f32[256,128]{1,0:T(8,128)S(1)} %copy-done.15, f32[256,128]{1,0:T(8,128)S(1)} %copy-done.14, f32[256,128]{1,0:T(8,128)S(1)} %copy-done.3, pred[]{:T(512)S(6)} %eq.66, pred[]{:T(512)S(6)} %eq.61, ...), kind=kLoop, calls=%fused_computation | loop fusion | flops 262144 | bytes 1048584 | tf_op jit(solution)/shard_map/jit(_where)/select_n | solution.py:274
  142.5 1.3 collective-permute-done.25.other_ref
  144.5 1.8 %last.1 = f32[512,128]{1,0:T(8,128)} custom-call(s32[1]{0:T(128)} %bitcast.core_ref, f32[256,128]{1,0:T(8,128)} %get-tuple-element.72.mine_ref, f32[256,128]{1,0:T(8,128)} %copy-done.25), custom_call_target="tpu_custom_call" | custom-call | tf_op jit(solution)/shard_map/last/pallas_call | solution.py:279
  (87 shorter events, 9.2 us)
Async XLA Ops:
  0.0 30.8 %copy-start.26 = (s32[1,6]{1,0:T(1,128)S(1)}, s32[1,6]{1,0:T(1,128)}, u32[]{:S(2)}) copy-start(s32[1,6]{1,0:T(1,128)} %param.9) | copy-start | bytes 76
  0.0 31.4 %collective-permute-start.4 = (f32[6,512,512]{2,1,0:T(8,128)}, f32[6,512,512]{2,1,0:T(8,128)}, u32[]{:S(2)}, u32[]{:S(2)}) collective-permute-start(f32[6,512,512]{2,1,0:T(8,128)} %bitcast.12), channel_id=1, source_target_pairs={{0,1},{1,0},{2,3},{3,2},{4,5},{5,4},{6,7},{7,6},{8,9},{9,8},{10,11... | collective-permute-start | bytes 18874376 | tf_op jit(solution)/shard_map/ppermute | solution.py:231
  1.8 8.4 %collective-permute-start = (s32[7]{0:T(128)S(1)}, s32[7]{0:T(128)S(1)}, u32[]{:S(2)}, u32[]{:S(2)}) collective-permute-start(s32[7]{0:T(128)S(1)} %pad_add_fusion), channel_id=1, source_target_pairs={{0,1},{1,0},{2,3},{3,2},{4,5},{5,4},{6,7},{7,6},{8,9},{9,8},{10,11... | collective-permute-start | bytes 92 | tf_op jit(solution)/shard_map/ppermute | solution.py:231
  1.9 29.5 %collective-permute-start.5 = (f32[512,512]{1,0:T(8,128)}, f32[512,512]{1,0:T(8,128)S(1)}, u32[]{:S(2)}, u32[]{:S(2)}) collective-permute-start(f32[512,512]{1,0:T(8,128)} %own_inverse.11), channel_id=1, source_target_pairs={{0,1},{1,0},{2,3},{3,2},{4,5},{5,4},{6,7},{7,6},{8,9},{9,8},{10,11... | collective-permute-start | bytes 3145736 | tf_op jit(solution)/shard_map/ppermute | solution.py:231
  5.0 15.0 %collective-permute-start.6 = (f32[256,128]{1,0:T(8,128)}, f32[256,128]{1,0:T(8,128)S(1)}, u32[]{:S(2)}, u32[]{:S(2)}) collective-permute-start(f32[256,128]{1,0:T(8,128)} %get-tuple-element.38), channel_id=1, source_target_pairs={{0,1},{1,0},{2,3},{3,2},{4,5},{5,4},{6,7},{7,6},{8,9},{9,8},{10,11... | collective-permute-start | bytes 393224 | tf_op jit(solution)/shard_map/ppermute | solution.py:231
  10.3 4.4 %collective-permute-start.1 = (s32[4]{0:T(128)S(1)}, s32[4]{0:T(128)S(1)}, u32[]{:S(2)}, u32[]{:S(2)}) collective-permute-start(s32[4]{0:T(128)S(1)} %fusion), channel_id=1, source_target_pairs={{0,2},{1,3},{2,0},{3,1},{4,6},{5,7},{6,4},{7,5},{8,10},{9,11},{10,... | collective-permute-start | bytes 56 | tf_op jit(solution)/shard_map/ppermute | solution.py:231
  14.8 6.7 %collective-permute-start.3 = (s32[4]{0:T(128)S(1)}, s32[4]{0:T(128)S(1)}, u32[]{:S(2)}, u32[]{:S(2)}) collective-permute-start(s32[4]{0:T(128)S(1)} %get-tuple-element.70), channel_id=1, source_target_pairs={{0,28},{1,29},{2,30},{3,31},{4,0},{5,1},{6,2},{7,3},{8,4},{9,5},{1... | collective-permute-start | bytes 56 | tf_op jit(solution)/shard_map/ppermute | solution.py:234
  19.9 10.8 %collective-permute-start.2 = (s32[4]{0:T(128)S(1)}, s32[4]{0:T(128)S(1)}, u32[]{:S(2)}, u32[]{:S(2)}) collective-permute-start(s32[4]{0:T(128)S(1)} %get-tuple-element.70), channel_id=1, source_target_pairs={{0,4},{1,5},{2,6},{3,7},{4,8},{5,9},{6,10},{7,11},{8,12},{9,13},{1... | collective-permute-start | bytes 56 | tf_op jit(solution)/shard_map/ppermute | solution.py:234
  19.9 13.2 %copy-start.2 = (f32[256,128]{1,0:T(8,128)}, f32[256,128]{1,0:T(8,128)S(1)}, u32[]{:S(2)}) copy-start(f32[256,128]{1,0:T(8,128)S(1)} %collective-permute-done.6.sib_start) | copy-start | bytes 393220
  20.9 5.0 %collective-permute-start.7 = (f32[256,128]{1,0:T(8,128)S(1)}, f32[256,128]{1,0:T(8,128)S(1)}, u32[]{:S(2)}, u32[]{:S(2)}) collective-permute-start(f32[256,128]{1,0:T(8,128)S(1)} %broadcast_select_fusion.6), channel_id=1, source_target_pairs={{0,2},{1,3},{2,0},{3,1},{4,6},{5,7},{6,4},{7,5},{8,10},{9,11},{10,... | collective-permute-start | bytes 393224 | tf_op jit(solution)/shard_map/ppermute | solution.py:231
  26.0 7.1 %copy-start.4 = (f32[256,128]{1,0:T(8,128)}, f32[256,128]{1,0:T(8,128)S(1)}, u32[]{:S(2)}) copy-start(f32[256,128]{1,0:T(8,128)S(1)} %broadcast_select_fusion.3.here.refs_1_) | copy-start | bytes 393220
  26.0 7.3 %collective-permute-start.9 = (f32[256,128]{1,0:T(8,128)S(1)}, f32[256,128]{1,0:T(8,128)S(1)}, u32[]{:S(2)}, u32[]{:S(2)}) collective-permute-start(f32[256,128]{1,0:T(8,128)S(1)} %broadcast_select_fusion.3.here.refs_1_), channel_id=1, source_target_pairs={{0,28},{1,29},{2,30},{3,31},{4,0},{5,1},{6,2},{7,3},{8,4},{9,5},{1... | collective-permute-start | bytes 393224 | tf_op jit(solution)/shard_map/ppermute | solution.py:234
  30.7 7.7 %collective-permute-start.8 = (f32[256,128]{1,0:T(8,128)S(1)}, f32[256,128]{1,0:T(8,128)S(1)}, u32[]{:S(2)}, u32[]{:S(2)}) collective-permute-start(f32[256,128]{1,0:T(8,128)S(1)} %broadcast_select_fusion.3.here.refs_1_), channel_id=1, source_target_pairs={{0,4},{1,5},{2,6},{3,7},{4,8},{5,9},{6,10},{7,11},{8,12},{9,13},{1... | collective-permute-start | bytes 393224 | tf_op jit(solution)/shard_map/ppermute | solution.py:234
  31.4 1.0 copy-start
  33.3 5.1 %copy-start.5 = (f32[256,128]{1,0:T(8,128)}, f32[256,128]{1,0:T(8,128)S(1)}, u32[]{:S(2)}) copy-start(f32[256,128]{1,0:T(8,128)S(1)} %collective-permute-done.9.ahead.refs_2_) | copy-start | bytes 393220
  40.9 5.8 %collective-permute-start.10 = (f32[256,128]{1,0:T(8,128)}, f32[256,128]{1,0:T(8,128)S(1)}, u32[]{:S(2)}, u32[]{:S(2)}) collective-permute-start(f32[256,128]{1,0:T(8,128)} %relax_1.2), channel_id=1, source_target_pairs={{0,2},{1,3},{2,0},{3,1},{4,6},{5,7},{6,4},{7,5},{8,10},{9,11},{10,... | collective-permute-start | bytes 393224 | tf_op jit(solution)/shard_map/ppermute | solution.py:231
  46.7 3.2 %copy-start.7 = (f32[256,128]{1,0:T(8,128)}, f32[256,128]{1,0:T(8,128)S(1)}, u32[]{:S(2)}) copy-start(f32[256,128]{1,0:T(8,128)S(1)} %broadcast_select_fusion.2.refs_4_.here) | copy-start | bytes 393220
  46.7 5.4 %collective-permute-start.12 = (f32[256,128]{1,0:T(8,128)S(1)}, f32[256,128]{1,0:T(8,128)S(1)}, u32[]{:S(2)}, u32[]{:S(2)}) collective-permute-start(f32[256,128]{1,0:T(8,128)S(1)} %broadcast_select_fusion.2.refs_4_.here), channel_id=1, source_target_pairs={{0,28},{1,29},{2,30},{3,31},{4,0},{5,1},{6,2},{7,3},{8,4},{9,5},{1... | collective-permute-start | bytes 393224 | tf_op jit(solution)/shard_map/ppermute | solution.py:234
  48.4 7.7 %collective-permute-start.11 = (f32[256,128]{1,0:T(8,128)S(1)}, f32[256,128]{1,0:T(8,128)S(1)}, u32[]{:S(2)}, u32[]{:S(2)}) collective-permute-start(f32[256,128]{1,0:T(8,128)S(1)} %broadcast_select_fusion.2.refs_4_.here), channel_id=1, source_target_pairs={{0,4},{1,5},{2,6},{3,7},{4,8},{5,9},{6,10},{7,11},{8,12},{9,13},{1... | collective-permute-start | bytes 393224 | tf_op jit(solution)/shard_map/ppermute | solution.py:234
  52.1 4.0 %copy-start.9 = (f32[256,128]{1,0:T(8,128)}, f32[256,128]{1,0:T(8,128)S(1)}, u32[]{:S(2)}) copy-start(f32[256,128]{1,0:T(8,128)S(1)} %collective-permute-done.12.refs_5_.ahead) | copy-start | bytes 393220
  58.5 8.2 %collective-permute-start.13 = (f32[256,128]{1,0:T(8,128)}, f32[256,128]{1,0:T(8,128)S(1)}, u32[]{:S(2)}, u32[]{:S(2)}) collective-permute-start(f32[256,128]{1,0:T(8,128)} %relax_2.2), channel_id=1, source_target_pairs={{0,2},{1,3},{2,0},{3,1},{4,6},{5,7},{6,4},{7,5},{8,10},{9,11},{10,... | collective-permute-start | bytes 393224 | tf_op jit(solution)/shard_map/ppermute | solution.py:231
  66.7 8.0 %copy-start.20 = (f32[256,128]{1,0:T(8,128)}, f32[256,128]{1,0:T(8,128)S(1)}, u32[]{:S(2)}) copy-start(f32[256,128]{1,0:T(8,128)S(1)} %broadcast_select_fusion.5.here) | copy-start | bytes 393220
  66.7 8.0 %collective-permute-start.15 = (f32[256,128]{1,0:T(8,128)S(1)}, f32[256,128]{1,0:T(8,128)S(1)}, u32[]{:S(2)}, u32[]{:S(2)}) collective-permute-start(f32[256,128]{1,0:T(8,128)S(1)} %broadcast_select_fusion.5.here), channel_id=1, source_target_pairs={{0,28},{1,29},{2,30},{3,31},{4,0},{5,1},{6,2},{7,3},{8,4},{9,5},{1... | collective-permute-start | bytes 393224 | tf_op jit(solution)/shard_map/ppermute | solution.py:234
  68.4 7.7 %collective-permute-start.14 = (f32[256,128]{1,0:T(8,128)S(1)}, f32[256,128]{1,0:T(8,128)S(1)}, u32[]{:S(2)}, u32[]{:S(2)}) collective-permute-start(f32[256,128]{1,0:T(8,128)S(1)} %broadcast_select_fusion.5.here), channel_id=1, source_target_pairs={{0,4},{1,5},{2,6},{3,7},{4,8},{5,9},{6,10},{7,11},{8,12},{9,13},{1... | collective-permute-start | bytes 393224 | tf_op jit(solution)/shard_map/ppermute | solution.py:234
  74.7 1.3 copy-start.23
  80.6 5.2 %collective-permute-start.16 = (f32[256,128]{1,0:T(8,128)}, f32[256,128]{1,0:T(8,128)S(1)}, u32[]{:S(2)}, u32[]{:S(2)}) collective-permute-start(f32[256,128]{1,0:T(8,128)} %relax_3.1), channel_id=1, source_target_pairs={{0,2},{1,3},{2,0},{3,1},{4,6},{5,7},{6,4},{7,5},{8,10},{9,11},{10,... | collective-permute-start | bytes 393224 | tf_op jit(solution)/shard_map/ppermute | solution.py:231
  86.7 3.4 %copy-start.8 = (f32[256,128]{1,0:T(8,128)}, f32[256,128]{1,0:T(8,128)S(1)}, u32[]{:S(2)}) copy-start(f32[256,128]{1,0:T(8,128)S(1)} %broadcast_select_fusion.here.refs_4_) | copy-start | bytes 393220
  86.7 5.0 %collective-permute-start.18 = (f32[256,128]{1,0:T(8,128)S(1)}, f32[256,128]{1,0:T(8,128)S(1)}, u32[]{:S(2)}, u32[]{:S(2)}) collective-permute-start(f32[256,128]{1,0:T(8,128)S(1)} %broadcast_select_fusion.here.refs_4_), channel_id=1, source_target_pairs={{0,28},{1,29},{2,30},{3,31},{4,0},{5,1},{6,2},{7,3},{8,4},{9,5},{1... | collective-permute-start | bytes 393224 | tf_op jit(solution)/shard_map/ppermute | solution.py:234
  88.5 7.7 %collective-permute-start.17 = (f32[256,128]{1,0:T(8,128)S(1)}, f32[256,128]{1,0:T(8,128)S(1)}, u32[]{:S(2)}, u32[]{:S(2)}) collective-permute-start(f32[256,128]{1,0:T(8,128)S(1)} %broadcast_select_fusion.here.refs_4_), channel_id=1, source_target_pairs={{0,4},{1,5},{2,6},{3,7},{4,8},{5,9},{6,10},{7,11},{8,12},{9,13},{1... | collective-permute-start | bytes 393224 | tf_op jit(solution)/shard_map/ppermute | solution.py:234
  91.8 4.4 %copy-start.11 = (f32[256,128]{1,0:T(8,128)}, f32[256,128]{1,0:T(8,128)S(1)}, u32[]{:S(2)}) copy-start(f32[256,128]{1,0:T(8,128)S(1)} %collective-permute-done.18.ahead.refs_5_) | copy-start | bytes 393220
  98.7 8.2 %collective-permute-start.19 = (f32[256,128]{1,0:T(8,128)}, f32[256,128]{1,0:T(8,128)S(1)}, u32[]{:S(2)}, u32[]{:S(2)}) collective-permute-start(f32[256,128]{1,0:T(8,128)} %relax_2.3), channel_id=1, source_target_pairs={{0,2},{1,3},{2,0},{3,1},{4,6},{5,7},{6,4},{7,5},{8,10},{9,11},{10,... | collective-permute-start | bytes 393224 | tf_op jit(solution)/shard_map/ppermute | solution.py:231
  106.9 4.3 %copy-start.13 = (f32[256,128]{1,0:T(8,128)}, f32[256,128]{1,0:T(8,128)S(1)}, u32[]{:S(2)}) copy-start(f32[256,128]{1,0:T(8,128)S(1)} %broadcast_select_fusion.4.refs_1_.here) | copy-start | bytes 393220
  106.9 5.5 %collective-permute-start.21 = (f32[256,128]{1,0:T(8,128)S(1)}, f32[256,128]{1,0:T(8,128)S(1)}, u32[]{:S(2)}, u32[]{:S(2)}) collective-permute-start(f32[256,128]{1,0:T(8,128)S(1)} %broadcast_select_fusion.4.refs_1_.here), channel_id=1, source_target_pairs={{0,28},{1,29},{2,30},{3,31},{4,0},{5,1},{6,2},{7,3},{8,4},{9,5},{1... | collective-permute-start | bytes 393224 | tf_op jit(solution)/shard_map/ppermute | solution.py:234
  109.8 7.8 %collective-permute-start.20 = (f32[256,128]{1,0:T(8,128)S(1)}, f32[256,128]{1,0:T(8,128)S(1)}, u32[]{:S(2)}, u32[]{:S(2)}) collective-permute-start(f32[256,128]{1,0:T(8,128)S(1)} %broadcast_select_fusion.4.refs_1_.here), channel_id=1, source_target_pairs={{0,4},{1,5},{2,6},{3,7},{4,8},{5,9},{6,10},{7,11},{8,12},{9,13},{1... | collective-permute-start | bytes 393224 | tf_op jit(solution)/shard_map/ppermute | solution.py:234
  112.3 5.3 %copy-start.17 = (f32[256,128]{1,0:T(8,128)}, f32[256,128]{1,0:T(8,128)S(1)}, u32[]{:S(2)}) copy-start(f32[256,128]{1,0:T(8,128)S(1)} %collective-permute-done.21.refs_2_.ahead) | copy-start | bytes 393220
  120.3 5.4 %collective-permute-start.22 = (f32[256,128]{1,0:T(8,128)}, f32[256,128]{1,0:T(8,128)S(1)}, u32[]{:S(2)}, u32[]{:S(2)}) collective-permute-start(f32[256,128]{1,0:T(8,128)} %relax_1.3), channel_id=1, source_target_pairs={{0,2},{1,3},{2,0},{3,1},{4,6},{5,7},{6,4},{7,5},{8,10},{9,11},{10,... | collective-permute-start | bytes 393224 | tf_op jit(solution)/shard_map/ppermute | solution.py:231
  125.7 8.8 %copy-start.19 = (f32[256,128]{1,0:T(8,128)}, f32[256,128]{1,0:T(8,128)S(1)}, u32[]{:S(2)}) copy-start(f32[256,128]{1,0:T(8,128)S(1)} %broadcast_select_fusion.1.here) | copy-start | bytes 393220
  125.7 8.8 %collective-permute-start.24 = (f32[256,128]{1,0:T(8,128)S(1)}, f32[256,128]{1,0:T(8,128)S(1)}, u32[]{:S(2)}, u32[]{:S(2)}) collective-permute-start(f32[256,128]{1,0:T(8,128)S(1)} %broadcast_select_fusion.1.here), channel_id=1, source_target_pairs={{0,28},{1,29},{2,30},{3,31},{4,0},{5,1},{6,2},{7,3},{8,4},{9,5},{1... | collective-permute-start | bytes 393224 | tf_op jit(solution)/shard_map/ppermute | solution.py:234
  128.5 7.7 %collective-permute-start.23 = (f32[256,128]{1,0:T(8,128)S(1)}, f32[256,128]{1,0:T(8,128)S(1)}, u32[]{:S(2)}, u32[]{:S(2)}) collective-permute-start(f32[256,128]{1,0:T(8,128)S(1)} %broadcast_select_fusion.1.here), channel_id=1, source_target_pairs={{0,4},{1,5},{2,6},{3,7},{4,8},{5,9},{6,10},{7,11},{8,12},{9,13},{1... | collective-permute-start | bytes 393224 | tf_op jit(solution)/shard_map/ppermute | solution.py:234
  134.5 1.7 %copy-start.21 = (f32[256,128]{1,0:T(8,128)}, f32[256,128]{1,0:T(8,128)S(1)}, u32[]{:S(2)}) copy-start(f32[256,128]{1,0:T(8,128)S(1)} %collective-permute-done.24.ahead) | copy-start | bytes 393220
  136.2 0.7 copy-start.22
  136.8 4.0 %copy-start.1 = (f32[256,128]{1,0:T(8,128)S(1)}, f32[256,128]{1,0:T(8,128)}, u32[]{:S(2)}) copy-start(f32[256,128]{1,0:T(8,128)} %get-tuple-element.37.own_start) | copy-start | bytes 393220
  136.8 4.0 %copy-start.3 = (f32[256,128]{1,0:T(8,128)S(1)}, f32[256,128]{1,0:T(8,128)}, u32[]{:S(2)}) copy-start(f32[256,128]{1,0:T(8,128)} %copy-done.2) | copy-start | bytes 393220
  136.8 4.0 %copy-start.14 = (f32[256,128]{1,0:T(8,128)S(1)}, f32[256,128]{1,0:T(8,128)}, u32[]{:S(2)}) copy-start(f32[256,128]{1,0:T(8,128)} %relax_3.1) | copy-start | bytes 393220
  136.8 4.0 %copy-start.15 = (f32[256,128]{1,0:T(8,128)S(1)}, f32[256,128]{1,0:T(8,128)}, u32[]{:S(2)}) copy-start(f32[256,128]{1,0:T(8,128)} %relax_2.3) | copy-start | bytes 393220
  136.9 4.0 %copy-start.16 = (f32[256,128]{1,0:T(8,128)S(1)}, f32[256,128]{1,0:T(8,128)}, u32[]{:S(2)}) copy-start(f32[256,128]{1,0:T(8,128)} %relax_1.3) | copy-start | bytes 393220
  142.5 1.3 collective-permute-start.25
  143.8 0.7 copy-start.25
  (5 other events, 3.3 us)
where the time goes:
time: 145 us; the launch traced here: 146 us
  waiting for transfers between devices  57 us (39%)
  starting transfers between devices  41.3 us (28%)
  Pallas kernels  36.1 us (25%)
  local copies, waits for them, and re-layouts  6.31 us (4%)
  other arithmetic  4.41 us (3%)
    ppermute x12, waiting for transfers between devices, flip(): return lax.ppermute(value, axis, [(i, i ^ bit) for i in range(count)])  30.1 us
    ppermute x14, waiting for transfers between devices, shift(): lax.ppermute(value, axis, [(i, (i + by) % count) for i in range(count)])  26.9 us
    ppermute x14, starting transfers between devices, shift(): lax.ppermute(value, axis, [(i, (i + by) % count) for i in range(count)])  21.9 us
    ppermute x12, starting transfers between devices, flip(): return lax.ppermute(value, axis, [(i, i ^ bit) for i in range(count)])  19.4 us
    pallas_call x6, Pallas kernels, gather(): pl.pallas_call(functools.partial(gather_kernel, now, newest, older), out_...  16.3 us
    pallas_call x6, Pallas kernels, relax(): pl.pallas_call(functools.partial(relax_kernel, now), out_shape=jax.ShapeD...  15.4 us
    unnamed x54, local copies, waits for them, and re-layouts  5.6 us
  transfers between devices with their start and end apart: 26, of which 19 were waited for; matrix products, arithmetic and copies ran while one was open for 2% of the time, Pallas kernels for 13%

commit v1 on v0

v1 whole, which is shorter than its diff:
```python
import functools

import jax
import jax.numpy as jnp
from jax import lax
from jax.experimental import pallas as pl
from jax.experimental.pallas import tpu as pltpu
from jax.sharding import PartitionSpec as P

COLOURS = 4
SIDES = 3
CHAINS = 2
OWN_COLOUR = 0
SIB_COLOUR = 1
TILE_START = 2
VMEM_LIMIT = 48 * 1024 * 1024


def dot_t(a, b):
    return lax.dot_general(a, b, (((1,), (1,)), ((), ())), preferred_element_type=jnp.float32)


def split(value):
    high = value.astype(jnp.bfloat16)
    return high, (value - high.astype(jnp.float32)).astype(jnp.bfloat16)


def times(value, high, low):
    rows = value.shape[0]
    parts = jnp.concatenate(split(value), axis=0)
    product = dot_t(parts, high) + dot_t(parts, low)
    return product[:rows] + product[rows:]


def vmem():
    return pl.BlockSpec(memory_space=pltpu.VMEM)


def smem():
    return pl.BlockSpec(memory_space=pltpu.SMEM)


def anywhere():
    return pl.BlockSpec(memory_space=pl.ANY)


def params():
    return pltpu.CompilerParams(vmem_limit_bytes=VMEM_LIMIT)


def near(values):
    return [pltpu.with_memory_space_constraint(v, pltpu.VMEM) for v in values]


def first_kernel(core_ref, inverse_ref, residual_ref, keep_ref, send_ref):
    value = times(jnp.transpose(residual_ref[...]), *split(inverse_ref[...]))
    half = value.shape[0] // 2
    is_first = core_ref[0] == 0
    keep_ref[...] = jnp.where(is_first, value[:half], value[half:])
    send_ref[...] = jnp.where(is_first, value[half:], value[:half])


def last_kernel(core_ref, mine_ref, other_ref, out_ref):
    is_first = core_ref[0] == 0
    mine, other = mine_ref[...], other_ref[...]
    first = jnp.where(is_first, mine, other)
    second = jnp.where(is_first, other, mine)
    out_ref[...] = jnp.transpose(jnp.concatenate([first, second], axis=0))


def tile_of(meta_ref, own, tiles, colour, side):
    wanted = meta_ref[TILE_START + 2 * tiles + side * COLOURS + colour]
    start = jnp.where(own, TILE_START, TILE_START + tiles)
    found = jnp.int32(-1)
    for k in range(tiles):
        found = jnp.where(meta_ref[start + k] == wanted, k, found)
    return found


def gather_kernel(now, newest, older, has_base, n_after, meta_ref, own_tiles, sib_tiles, own_inverse, sib_inverse, *refs):
    count = SIDES * len(older) * CHAINS
    known, refs = refs[:count], refs[count:]
    base, refs = refs[: CHAINS * has_base], refs[CHAINS * has_base :]
    w_high, w_low, d_high, d_low, partial, buffer, sems = refs[n_after:]
    tiles, block = own_tiles.shape[0], own_tiles.shape[1]
    own = meta_ref[OWN_COLOUR] == now
    active = own | (meta_ref[SIB_COLOUR] == now)
    slots = [(newest, side) for side in range(SIDES)] + [(c, side) for c in older for side in range(SIDES)]

    @pl.when(active)
    def _():
        def fetch(own_src, sib_src, slot, start):
            @pl.when(own)
            def _():
                copy = pltpu.make_async_copy(own_src, buffer.at[slot], sems.at[slot])
                copy.start() if start else copy.wait()

            @pl.when(jnp.logical_not(own))
            def _():
                copy = pltpu.make_async_copy(sib_src, buffer.at[slot], sems.at[slot])
                copy.start() if start else copy.wait()

        which = [tile_of(meta_ref, own, tiles, c, side) for c, side in slots]
        fetch(own_inverse, sib_inverse, len(slots), True)
        for slot, k in enumerate(which):
            @pl.when(k >= 0)
            def _():
                fetch(own_tiles.at[k], sib_tiles.at[k], slot, True)

        if has_base:
            partial[...] = jnp.concatenate([b[...] for b in base], axis=0)
        else:
            partial[...] = jnp.zeros_like(partial)
        fetch(own_inverse, sib_inverse, len(slots), False)
        d_high[...], d_low[...] = split(buffer[len(slots)])
        for slot, k in enumerate(which):
            span = pl.ds(slot * block, block)

            @pl.when(k >= 0)
            def _():
                fetch(own_tiles.at[k], sib_tiles.at[k], slot, False)
                high, low = split(buffer[slot])
                if slot < SIDES:
                    w_high[:, span] = high
                    w_low[:, span] = low
                else:
                    at = (slot - SIDES) * CHAINS
                    value = jnp.concatenate([r[...] for r in known[at : at + CHAINS]], axis=0)
                    partial[...] += times(value, high, low)

            if slot < SIDES:
                @pl.when(k < 0)
                def _():
                    w_high[:, span] = jnp.zeros((block, block), jnp.bfloat16)
                    w_low[:, span] = jnp.zeros((block, block), jnp.bfloat16)


def relax_kernel(now, chain, meta_ref, w_high, w_low, d_high, d_low, partial, behind, here, ahead, own_start, sib_start, *refs):
    out_ref, sum_ref = refs[-2:]
    own = meta_ref[OWN_COLOUR] == now
    active = own | (meta_ref[SIB_COLOUR] == now)
    width = out_ref.shape[0]
    rows = pl.ds(chain * width, width)

    @pl.when(active)
    def _():
        value = jnp.concatenate([behind[...], here[...], ahead[...]], axis=1)
        coupled = partial[rows, :] + times(value, w_high[...], w_low[...])
        sum_ref[...] = coupled
        start = jnp.where(own, own_start[rows, :], sib_start[rows, :])
        out_ref[...] = start - times(coupled, d_high[...], d_low[...])


def gather(now, newest, older, meta, matrices, known, base, after):
    tiles, block, _ = matrices[0].shape
    width = known[newest][0][0].shape[0]
    slots = SIDES * (1 + len(older)) + 1
    operands = [known[c][chain][side] for c in older for side in range(SIDES) for chain in range(CHAINS)]
    operands = near(operands + (base or []))
    bf16 = jnp.bfloat16
    return pl.pallas_call(
        functools.partial(gather_kernel, now, newest, older, int(base is not None), len(after)),
        out_shape=[
            pltpu.VMEM((block, SIDES * block), bf16),
            pltpu.VMEM((block, SIDES * block), bf16),
            pltpu.VMEM((block, block), bf16),
            pltpu.VMEM((block, block), bf16),
            pltpu.VMEM((CHAINS * width, block), jnp.float32),
        ],
        in_specs=[smem()] + [anywhere()] * 4 + [vmem()] * len(operands) + [anywhere()] * len(after),
        out_specs=[vmem()] * 5,
        scratch_shapes=[
            pltpu.VMEM((slots, block, block), jnp.float32),
            pltpu.SemaphoreType.DMA((slots,)),
        ],
        compiler_params=params(),
        cost_estimate=pl.CostEstimate(
            flops=4 * block * block * 128 * slots, bytes_accessed=4 * block * block * slots, transcendentals=0
        ),
        name=f"gather_{now}_{newest}",
    )(meta, *matrices, *operands, *after)


def relax(now, chain, meta, gathered, latest, own_start, sib_start, after):
    block = gathered[2].shape[0]
    width = own_start.shape[0] // CHAINS
    operands = near([*gathered, *latest, own_start, sib_start])
    return pl.pallas_call(
        functools.partial(relax_kernel, now, chain),
        out_shape=[pltpu.VMEM((width, block), jnp.float32)] * 2,
        in_specs=[smem()] + [vmem()] * len(operands) + [anywhere()] * len(after),
        out_specs=[vmem()] * 2,
        compiler_params=params(),
        cost_estimate=pl.CostEstimate(
            flops=16 * block * block * 128, bytes_accessed=16 * block * block, transcendentals=0
        ),
        name=f"relax_{now}_{chain}",
    )(meta, *operands, *after)


def per_device(residual, inv_diag, coupling_tiles, colour, tile_cols):
    axis = "rows"
    count = lax.axis_size(axis)
    groups = count // COLOURS
    me = lax.axis_index(axis)
    core = (me % 2).reshape(1)
    place = me % COLOURS
    group = me // COLOURS
    block, cols = residual.shape
    half = cols // 2
    width = half // CHAINS
    tiles = jnp.transpose(coupling_tiles, (1, 0, 2))

    def flip(value, bit):
        return lax.ppermute(value, axis, [(i, i ^ bit) for i in range(count)])

    def shift(value, by):
        return lax.ppermute(value, axis, [(i, (i + by) % count) for i in range(count)])

    own_facts = jnp.concatenate([colour, tile_cols[0]])
    sib_facts = flip(own_facts, 1)
    own_colour, sib_colour = own_facts[0], sib_facts[0]

    late_residual, _ = lax.optimization_barrier((residual, own_facts))
    keep, send = pl.pallas_call(
        first_kernel,
        out_shape=[pltpu.VMEM((half, block), jnp.float32)] * 2,
        in_specs=[smem(), vmem(), vmem()],
        out_specs=[vmem()] * 2,
        compiler_params=params(),
        name="first",
    )(core, inv_diag, late_residual)
    own_start, sib_start = keep, flip(send, 1)

    candidate = jnp.where(own_colour == 0, own_start, sib_start)
    candidates = [candidate[c * width : (c + 1) * width] for c in range(CHAINS)]

    late_tiles, late_inverse, _, _ = lax.optimization_barrier((tiles, inv_diag, sib_start, sib_facts))
    matrices = [tiles, flip(late_tiles, 1), inv_diag, flip(late_inverse, 1)]

    def across(candidate, now):
        here_now = (own_colour == now) | (sib_colour == now)
        return jnp.where(here_now, candidate, flip(candidate, 2))

    def around(here):
        return [shift(here, COLOURS), here, shift(here, -COLOURS)]

    here = [across(c, 0) for c in candidates]

    wheel = jnp.arange(COLOURS, dtype=jnp.int32)
    pair_places = jnp.where(wheel == own_colour, place, 0) + jnp.where(wheel == sib_colour, place ^ 1, 0)
    pair_places, _ = lax.optimization_barrier((pair_places, candidates[0]))
    group_places = pair_places + flip(pair_places, 2)
    group_places, _ = lax.optimization_barrier((group_places, here[0]))
    places = [shift(group_places, COLOURS), group_places, shift(group_places, -COLOURS)]
    blocks = [(((group + side - 1) % groups) * COLOURS + places[side]).astype(jnp.int32) for side in range(SIDES)]
    meta = jnp.concatenate([own_facts[:1], sib_facts[:1], own_facts[1:], sib_facts[1:]] + blocks)

    known = {0: [around(h) for h in here]}
    order = list(range(1, COLOURS)) + list(range(COLOURS - 2, -1, -1))
    newest, done = 0, {0}
    sums, used, finals = {}, {}, {}
    previous = candidates
    for step, now in enumerate(order):
        fresh = used.get(now, set())
        older = tuple(c for c in sorted(known) if c not in (now, newest) and (c, done_at(order, c, step)) not in fresh)
        gathered = gather(now, newest, older, meta, matrices, known, sums.get(now), [previous[-1]] if step else [])
        used[now] = {(c, done_at(order, c, step)) for c in known if c != now}
        candidates, sums[now], here = [], [], []
        for chain in range(CHAINS):
            after = [here[-1] if here else candidates[-1]] if chain else []
            candidate, total = relax(now, chain, meta, gathered, known[newest][chain], own_start, sib_start, after)
            candidates.append(candidate)
            sums[now].append(total)
            if step < len(order) - 1:
                here.append(across(candidate, now))
        finals[now] = candidates
        if here:
            known[now] = [around(h) for h in here]
        newest, previous = now, candidates

    own_final, sib_final = finals[0], finals[0]
    for c in range(1, COLOURS):
        own_final = [jnp.where(own_colour == c, a, b) for a, b in zip(finals[c], own_final)]
        sib_final = [jnp.where(sib_colour == c, a, b) for a, b in zip(finals[c], sib_final)]
    mine, other = jnp.concatenate(own_final), flip(jnp.concatenate(sib_final), 1)
    return pl.pallas_call(
        last_kernel,
        out_shape=jax.ShapeDtypeStruct((block, cols), jnp.float32),
        in_specs=[smem(), vmem(), vmem()],
        out_specs=vmem(),
        compiler_params=params(),
        name="last",
    )(core, *near([mine, other]))


def done_at(order, colour, step):
    return max([i for i in range(step) if order[i] == colour], default=-1)


def solution(mesh):
    in_specs = (P("rows", None), P("rows", None), P("rows", None, None), P("rows"), P("rows", None))
    out_specs = P("rows", None)
    return jax.shard_map(
        per_device, mesh=mesh, in_specs=in_specs, out_specs=out_specs, check_vma=False
    )
```

time: 145 us -> 147 us (1.014); the launches traced: 146 us -> 144 us
  waiting for transfers between devices: 57 us -> 16.6 us
  starting transfers between devices: 41.3 us -> 80.8 us
  other arithmetic: 4.41 us -> 1.83 us
    ppermute x14 -> x26, starting transfers between devices: 21.9 us -> 61.8 us  [shift(): lax.ppermute(value, axis, [(i, (i + by) % count) for i in range(count)])]
    ppermute x14 -> x26, waiting for transfers between devices: 26.9 us -> 6.41 us  [shift(): lax.ppermute(value, axis, [(i, (i + by) % count) for i in range(count)])]
    ppermute x12 -> x18, waiting for transfers between devices: 30.1 us -> 10.2 us  [flip(): return lax.ppermute(value, axis, [(i, i ^ bit) for i in range(count)])]
    select_n x7 -> x14, other arithmetic: 2.62 us -> 1.01 us  [the longest x12 0.97 us: across(): return jnp.where(here_now, candidate, flip(candidate, 2))]
    unnamed x54 -> x28, local copies, waits for them, and re-layouts: 5.6 us -> 7.14 us
    pallas_call x13 -> x19, Pallas kernels: 34.3 us -> 35.5 us  [the longest x12 21.3 us: relax(): pl.pallas_call(functools.partial(relax_kernel, now, chain), out_shape=[pl...]
    ppermute x12 -> x18, starting transfers between devices: 19.4 us -> 19 us  [flip(): return lax.ppermute(value, axis, [(i, i ^ bit) for i in range(count)])]
  transfers between devices with their start and end apart: 26 -> 44, of which waited for: 19 -> 8; matrix products, arithmetic and copies ran while one was open for 2% -> 1% of each run, Pallas kernels for 13% -> 22%
where the time goes in v1:
time: 147 us; the launch traced here: 144 us
  starting transfers between devices  80.8 us (55%)
  Pallas kernels  36.3 us (25%)
  waiting for transfers between devices  16.6 us (11%)
  local copies, waits for them, and re-layouts  7.33 us (5%)
  other arithmetic  1.83 us (1%)
    ppermute x26, starting transfers between devices, shift(): lax.ppermute(value, axis, [(i, (i + by) % count) for i in range(count)])  61.8 us
    pallas_call x12, Pallas kernels, relax(): pl.pallas_call(functools.partial(relax_kernel, now, chain), out_shape=[pl...  21.3 us
    ppermute x18, starting transfers between devices, flip(): return lax.ppermute(value, axis, [(i, i ^ bit) for i in range(count)])  19 us
    pallas_call x6, Pallas kernels, gather(): pl.pallas_call(functools.partial(gather_kernel, now, newest, older, int(b...  13.7 us
    ppermute x18, waiting for transfers between devices, flip(): return lax.ppermute(value, axis, [(i, i ^ bit) for i in range(count)])  10.2 us
    unnamed x28, local copies, waits for them, and re-layouts  7.14 us
    ppermute x26, waiting for transfers between devices, shift(): lax.ppermute(value, axis, [(i, (i + by) % count) for i in range(count)])  6.41 us
  transfers between devices with their start and end apart: 44, of which 8 were waited for; matrix products, arithmetic and copies ran while one was open for 1% of the time, Pallas kernels for 22%

profile of v1, /device:TPU:0, one launch (start us, length us, event | category | flops | bytes accessed | tf_op | source)
XLA Modules:
  0.0 144.1 jit_solution(1233974086942038916)
XLA Ops:
  1.4 1.2 copy-done
  2.6 0.9 copy-done.9
  4.7 1.0 collective-permute-done
  6.0 2.8 %collective-permute-start.9 = (f32[32,512]{1,0:T(8,128)S(1)}, f32[32,512]{1,0:T(8,128)S(1)}, u32[]{:S(2)}, u32[]{:S(2)}) collective-permute-start(f32[32,512]{1,0:T(8,128)S(1)} %slice.18), channel_id=1, source_target_pairs={{0,2},{1,3},{2,0},{3,1},{4,6},{5,7},{6,4},{7,5},{8,10},{9,11},{10,... | collective-permute-start | bytes 196616 | tf_op jit(solution)/shard_map/ppermute | solution.py:215
  9.0 2.3 %collective-permute-done.9 = f32[32,512]{1,0:T(8,128)S(1)} collective-permute-done((f32[32,512]{1,0:T(8,128)S(1)}, f32[32,512]{1,0:T(8,128)S(1)}, u32[]{:S(2)}, u32[]{:S(2)}) %collective-permute-start.9) | collective-permute-done | bytes 65568 | tf_op jit(solution)/shard_map/ppermute | solution.py:215
  11.3 1.8 %collective-permute-start.3 = (f32[32,512]{1,0:T(8,128)S(1)}, f32[32,512]{1,0:T(8,128)S(1)}, u32[]{:S(2)}, u32[]{:S(2)}) collective-permute-start(f32[32,512]{1,0:T(8,128)S(1)} %get-tuple-element.116), channel_id=1, source_target_pairs={{0,2},{1,3},{2,0},{3,1},{4,6},{5,7},{6,4},{7,5},{8,10},{9,11},{10,... | collective-permute-start | bytes 196616 | tf_op jit(solution)/shard_map/ppermute | solution.py:215
  13.5 3.3 %collective-permute-done.2 = s32[4]{0:T(128)S(1)} collective-permute-done((s32[4]{0:T(128)S(1)}, s32[4]{0:T(128)S(1)}, u32[]{:S(2)}, u32[]{:S(2)}) %collective-permute-start.2) | collective-permute-done | bytes 48 | tf_op jit(solution)/shard_map/ppermute | solution.py:215
  16.8 4.6 %collective-permute-start.5 = (s32[4]{0:T(128)S(1)}, s32[4]{0:T(128)S(1)}, u32[]{:S(2)}, u32[]{:S(2)}) collective-permute-start(s32[4]{0:T(128)S(1)} %add.55), channel_id=1, source_target_pairs={{0,28},{1,29},{2,30},{3,31},{4,0},{5,1},{6,2},{7,3},{8,4},{9,5},{1... | collective-permute-start | bytes 56 | tf_op jit(solution)/shard_map/ppermute | solution.py:218
  21.4 4.7 %collective-permute-start.11 = (f32[32,512]{1,0:T(8,128)S(1)}, f32[32,512]{1,0:T(8,128)}, u32[]{:S(2)}, u32[]{:S(2)}) collective-permute-start(f32[32,512]{1,0:T(8,128)S(1)} %broadcast_select_fusion.12.here.refs_2_), channel_id=1, source_target_pairs={{0,28},{1,29},{2,30},{3,31},{4,0},{5,1},{6,2},{7,3},{8,4},{9,5},{1... | collective-permute-start | bytes 196616 | tf_op jit(solution)/shard_map/ppermute | solution.py:218
  26.2 1.5 %collective-permute-done.4 = s32[4]{0:T(128)S(1)} collective-permute-done((s32[4]{0:T(128)S(1)}, s32[4]{0:T(128)S(1)}, u32[]{:S(2)}, u32[]{:S(2)}) %collective-permute-start.4) | collective-permute-done | bytes 48 | tf_op jit(solution)/shard_map/ppermute | solution.py:218
  27.8 1.0 copy-done.12
  29.4 3.8 %collective-permute-done.8.behind.refs_0_ = f32[32,512]{1,0:T(8,128)} collective-permute-done((f32[32,512]{1,0:T(8,128)S(1)}, f32[32,512]{1,0:T(8,128)}, u32[]{:S(2)}, u32[]{:S(2)}) %collective-permute-start.8) | collective-permute-done | bytes 65568 | tf_op jit(solution)/shard_map/ppermute | solution.py:218
  33.2 1.5 %relax_1_0.2 = (f32[32,512]{1,0:T(8,128)}, f32[32,512]{1,0:T(8,128)S(1)}) custom-call(s32[26]{0:T(128)S(1)} %concatenate.13.meta_ref, bf16[512,1536]{1,0:T(8,128)(2,1)S(1)} %get-tuple-element.65.w_high, bf16[512,1536]{1,0:T(8,128)(2,1)S(1)} %get-tuple-element.66.w_low, bf16[512,512]{1,0:T(8,128)(2,1)S(1)} %get-tuple-element.67.d_high, ...), custom_call_target="tpu_custom_call" | custom-call | flops 536870912 | bytes 4194304 | tf_op jit(solution)/shard_map/relax_1_0/pallas_call | solution.py:188
  35.4 2.1 %collective-permute-start.13 = (f32[32,512]{1,0:T(8,128)}, f32[32,512]{1,0:T(8,128)}, u32[]{:S(2)}, u32[]{:S(2)}) collective-permute-start(f32[32,512]{1,0:T(8,128)} %get-tuple-element.70), channel_id=1, source_target_pairs={{0,2},{1,3},{2,0},{3,1},{4,6},{5,7},{6,4},{7,5},{8,10},{9,11},{10,... | collective-permute-start | bytes 196616 | tf_op jit(solution)/shard_map/ppermute | solution.py:215
  37.7 4.7 %collective-permute-start.12 = (f32[32,512]{1,0:T(8,128)S(1)}, f32[32,512]{1,0:T(8,128)S(1)}, u32[]{:S(2)}, u32[]{:S(2)}) collective-permute-start(f32[32,512]{1,0:T(8,128)S(1)} %get-tuple-element.115.here.refs_3_), channel_id=1, source_target_pairs={{0,28},{1,29},{2,30},{3,31},{4,0},{5,1},{6,2},{7,3},{8,4},{9,5},{1... | collective-permute-start | bytes 196616 | tf_op jit(solution)/shard_map/ppermute | solution.py:218
  42.4 0.9 broadcast_select_fusion.10.refs_0_.here.refs_8_
  43.3 4.7 %collective-permute-start.17 = (f32[32,512]{1,0:T(8,128)S(1)}, f32[32,512]{1,0:T(8,128)S(1)}, u32[]{:S(2)}, u32[]{:S(2)}) collective-permute-start(f32[32,512]{1,0:T(8,128)S(1)} %broadcast_select_fusion.10.refs_0_.here.refs_8_), channel_id=1, source_target_pairs={{0,28},{1,29},{2,30},{3,31},{4,0},{5,1},{6,2},{7,3},{8,4},{9,5},{1... | collective-permute-start | bytes 196616 | tf_op jit(solution)/shard_map/ppermute | solution.py:218
  48.0 1.4 copy-done.4
  49.4 1.0 copy-done.6
  50.5 0.9 copy-done.8
  51.9 1.5 %collective-permute-start.15 = (f32[32,512]{1,0:T(8,128)S(1)}, f32[32,512]{1,0:T(8,128)S(1)}, u32[]{:S(2)}, u32[]{:S(2)}) collective-permute-start(f32[32,512]{1,0:T(8,128)S(1)} %get-tuple-element.71.refs_6_), channel_id=1, source_target_pairs={{0,2},{1,3},{2,0},{3,1},{4,6},{5,7},{6,4},{7,5},{8,10},{9,11},{10,... | collective-permute-start | bytes 196616 | tf_op jit(solution)/shard_map/ppermute | solution.py:215
  53.4 4.1 %gather_2_1.1 = (bf16[512,1536]{1,0:T(8,128)(2,1)S(1)}, bf16[512,1536]{1,0:T(8,128)(2,1)S(1)}, bf16[512,512]{1,0:T(8,128)(2,1)S(1)}, bf16[512,512]{1,0:T(8,128)(2,1)S(1)}, f32[64,512]{1,0:T(8,128)S(1)}) custom-call(s32[26]{0:T(128)S(1)} %concatenate.13.meta_ref, f32[6,512,512]{2,1,0:T(8,128)} %bitcast.13, f32[6,512,512]{2,1,0:T(8,128)} %collective-permute-done.6.sib_tiles, ...), custom_call_target="tpu_custom_call" | custom-call | flops 939524096 | bytes 7340032 | tf_op jit(solution)/shard_map/gather_2_1/pallas_call | solution.py:161
  57.6 2.0 %relax_2_0.2 = (f32[32,512]{1,0:T(8,128)S(1)}, f32[32,512]{1,0:T(8,128)S(1)}) custom-call(s32[26]{0:T(128)S(1)} %concatenate.13.meta_ref, bf16[512,1536]{1,0:T(8,128)(2,1)S(1)} %get-tuple-element.72.w_high, bf16[512,1536]{1,0:T(8,128)(2,1)S(1)} %get-tuple-element.73.w_low, bf16[512,512]{1,0:T(8,128)(2,1)S(1)} %get-tuple-element.74.d_high, ...), custom_call_target="tpu_custom_call" | custom-call | flops 536870912 | bytes 4194304 | tf_op jit(solution)/shard_map/relax_2_0/pallas_call | solution.py:188
  59.7 4.7 %collective-permute-start.18 = (f32[32,512]{1,0:T(8,128)S(1)}, f32[32,512]{1,0:T(8,128)S(1)}, u32[]{:S(2)}, u32[]{:S(2)}) collective-permute-start(f32[32,512]{1,0:T(8,128)S(1)} %broadcast_select_fusion.9.here.refs_9_), channel_id=1, source_target_pairs={{0,28},{1,29},{2,30},{3,31},{4,0},{5,1},{6,2},{7,3},{8,4},{9,5},{1... | collective-permute-start | bytes 196616 | tf_op jit(solution)/shard_map/ppermute | solution.py:218
  64.5 4.7 %collective-permute-start.21 = (f32[32,512]{1,0:T(8,128)S(1)}, f32[32,512]{1,0:T(8,128)S(1)}, u32[]{:S(2)}, u32[]{:S(2)}) collective-permute-start(f32[32,512]{1,0:T(8,128)S(1)} %broadcast_select_fusion.6.refs_0_.here), channel_id=1, source_target_pairs={{0,28},{1,29},{2,30},{3,31},{4,0},{5,1},{6,2},{7,3},{8,4},{9,5},{1... | collective-permute-start | bytes 196616 | tf_op jit(solution)/shard_map/ppermute | solution.py:218
  69.2 2.0 %relax_2_1.2 = (f32[32,512]{1,0:T(8,128)S(1)}, f32[32,512]{1,0:T(8,128)S(1)}) custom-call(s32[26]{0:T(128)S(1)} %concatenate.13.meta_ref, bf16[512,1536]{1,0:T(8,128)(2,1)S(1)} %get-tuple-element.72.w_high, bf16[512,1536]{1,0:T(8,128)(2,1)S(1)} %get-tuple-element.73.w_low, bf16[512,512]{1,0:T(8,128)(2,1)S(1)} %get-tuple-element.74.d_high, ...), custom_call_target="tpu_custom_call" | custom-call | flops 536870912 | bytes 4194304 | tf_op jit(solution)/shard_map/relax_2_1/pallas_call | solution.py:188
  71.9 5.1 %gather_3_2.1 = (bf16[512,1536]{1,0:T(8,128)(2,1)S(1)}, bf16[512,1536]{1,0:T(8,128)(2,1)S(1)}, bf16[512,512]{1,0:T(8,128)(2,1)S(1)}, bf16[512,512]{1,0:T(8,128)(2,1)S(1)}, f32[64,512]{1,0:T(8,128)S(1)}) custom-call(s32[26]{0:T(128)S(1)} %concatenate.13.meta_ref, f32[6,512,512]{2,1,0:T(8,128)} %bitcast.14, f32[6,512,512]{2,1,0:T(8,128)} %collective-permute-done.6.sib_tiles, ...), custom_call_target="tpu_custom_call" | custom-call | flops 1342177280 | bytes 10485760 | tf_op jit(solution)/shard_map/gather_3_2/pallas_call | solution.py:161
  77.0 2.6 %relax_3_0.1 = (f32[32,512]{1,0:T(8,128)S(1)}, f32[32,512]{1,0:T(8,128)}) custom-call(s32[26]{0:T(128)S(1)} %concatenate.13.meta_ref, bf16[512,1536]{1,0:T(8,128)(2,1)S(1)} %get-tuple-element.79.w_high, bf16[512,1536]{1,0:T(8,128)(2,1)S(1)} %get-tuple-element.80.w_low, bf16[512,512]{1,0:T(8,128)(2,1)S(1)} %get-tuple-element.81.d_high, ...), custom_call_target="tpu_custom_call" | custom-call | flops 536870912 | bytes 4194304 | tf_op jit(solution)/shard_map/relax_3_0/pallas_call | solution.py:188
  79.7 4.7 %collective-permute-start.24 = (f32[32,512]{1,0:T(8,128)S(1)}, f32[32,512]{1,0:T(8,128)S(1)}, u32[]{:S(2)}, u32[]{:S(2)}) collective-permute-start(f32[32,512]{1,0:T(8,128)S(1)} %broadcast_select_fusion.5.here), channel_id=1, source_target_pairs={{0,28},{1,29},{2,30},{3,31},{4,0},{5,1},{6,2},{7,3},{8,4},{9,5},{1... | collective-permute-start | bytes 196616 | tf_op jit(solution)/shard_map/ppermute | solution.py:218
  84.5 4.7 %collective-permute-start.27 = (f32[32,512]{1,0:T(8,128)S(1)}, f32[32,512]{1,0:T(8,128)S(1)}, u32[]{:S(2)}, u32[]{:S(2)}) collective-permute-start(f32[32,512]{1,0:T(8,128)S(1)} %broadcast_select_fusion.2.refs_0_.here.refs_2_.refs_8_), channel_id=1, source_target_pairs={{0,28},{1,29},{2,30},{3,31},{4,0},{5,1},{6,2},{7,3},{8,4},{9,5},{1... | collective-permute-start | bytes 196616 | tf_op jit(solution)/shard_map/ppermute | solution.py:218
  89.2 2.8 %relax_3_1.1 = (f32[32,512]{1,0:T(8,128)S(1)}, f32[32,512]{1,0:T(8,128)}) custom-call(s32[26]{0:T(128)S(1)} %concatenate.13.meta_ref, bf16[512,1536]{1,0:T(8,128)(2,1)S(1)} %get-tuple-element.79.w_high, bf16[512,1536]{1,0:T(8,128)(2,1)S(1)} %get-tuple-element.80.w_low, bf16[512,512]{1,0:T(8,128)(2,1)S(1)} %get-tuple-element.81.d_high, ...), custom_call_target="tpu_custom_call" | custom-call | flops 536870912 | bytes 4194304 | tf_op jit(solution)/shard_map/relax_3_1/pallas_call | solution.py:188
  92.6 2.6 %gather_2_3.1 = (bf16[512,1536]{1,0:T(8,128)(2,1)S(1)}, bf16[512,1536]{1,0:T(8,128)(2,1)S(1)}, bf16[512,512]{1,0:T(8,128)(2,1)S(1)}, bf16[512,512]{1,0:T(8,128)(2,1)S(1)}, f32[64,512]{1,0:T(8,128)S(1)}) custom-call(s32[26]{0:T(128)S(1)} %concatenate.13.meta_ref, f32[6,512,512]{2,1,0:T(8,128)} %bitcast.15, f32[6,512,512]{2,1,0:T(8,128)} %collective-permute-done.6.sib_tiles, ...), custom_call_target="tpu_custom_call" | custom-call | flops 536870912 | bytes 4194304 | tf_op jit(solution)/shard_map/gather_2_3/pallas_call | solution.py:161
  95.2 2.6 %relax_2_0.3 = (f32[32,512]{1,0:T(8,128)S(1)}, f32[32,512]{1,0:T(8,128)}) custom-call(s32[26]{0:T(128)S(1)} %concatenate.13.meta_ref, bf16[512,1536]{1,0:T(8,128)(2,1)S(1)} %get-tuple-element.88.w_high, bf16[512,1536]{1,0:T(8,128)(2,1)S(1)} %get-tuple-element.89.w_low, bf16[512,512]{1,0:T(8,128)(2,1)S(1)} %get-tuple-element.90.d_high, ...), custom_call_target="tpu_custom_call" | custom-call | flops 536870912 | bytes 4194304 | tf_op jit(solution)/shard_map/relax_2_0/pallas_call | solution.py:188
  97.9 4.7 %collective-permute-start.30 = (f32[32,512]{1,0:T(8,128)S(1)}, f32[32,512]{1,0:T(8,128)S(1)}, u32[]{:S(2)}, u32[]{:S(2)}) collective-permute-start(f32[32,512]{1,0:T(8,128)S(1)} %broadcast_select_fusion.1.here.refs_3_.refs_9_), channel_id=1, source_target_pairs={{0,28},{1,29},{2,30},{3,31},{4,0},{5,1},{6,2},{7,3},{8,4},{9,5},{1... | collective-permute-start | bytes 196616 | tf_op jit(solution)/shard_map/ppermute | solution.py:218
  102.7 4.7 %collective-permute-start.33 = (f32[32,512]{1,0:T(8,128)S(1)}, f32[32,512]{1,0:T(8,128)S(1)}, u32[]{:S(2)}, u32[]{:S(2)}) collective-permute-start(f32[32,512]{1,0:T(8,128)S(1)} %broadcast_select_fusion.4.refs_0_.here.refs_2_), channel_id=1, source_target_pairs={{0,28},{1,29},{2,30},{3,31},{4,0},{5,1},{6,2},{7,3},{8,4},{9,5},{1... | collective-permute-start | bytes 196616 | tf_op jit(solution)/shard_map/ppermute | solution.py:218
  107.4 2.6 %relax_2_1.3 = (f32[32,512]{1,0:T(8,128)S(1)}, f32[32,512]{1,0:T(8,128)}) custom-call(s32[26]{0:T(128)S(1)} %concatenate.13.meta_ref, bf16[512,1536]{1,0:T(8,128)(2,1)S(1)} %get-tuple-element.88.w_high, bf16[512,1536]{1,0:T(8,128)(2,1)S(1)} %get-tuple-element.89.w_low, bf16[512,512]{1,0:T(8,128)(2,1)S(1)} %get-tuple-element.90.d_high, ...), custom_call_target="tpu_custom_call" | custom-call | flops 536870912 | bytes 4194304 | tf_op jit(solution)/shard_map/relax_2_1/pallas_call | solution.py:188
  111.3 1.2 relax_1_0.3
  112.5 6.1 %collective-permute-start.37 = (f32[32,512]{1,0:T(8,128)S(1)}, f32[32,512]{1,0:T(8,128)S(1)}, u32[]{:S(2)}, u32[]{:S(2)}) collective-permute-start(f32[32,512]{1,0:T(8,128)S(1)} %get-tuple-element.102), channel_id=1, source_target_pairs={{0,2},{1,3},{2,0},{3,1},{4,6},{5,7},{6,4},{7,5},{8,10},{9,11},{10,... | collective-permute-start | bytes 196616 | tf_op jit(solution)/shard_map/ppermute | solution.py:215
  118.7 4.7 %collective-permute-start.36 = (f32[32,512]{1,0:T(8,128)S(1)}, f32[32,512]{1,0:T(8,128)S(1)}, u32[]{:S(2)}, u32[]{:S(2)}) collective-permute-start(f32[32,512]{1,0:T(8,128)S(1)} %broadcast_select_fusion.3.here.refs_3_), channel_id=1, source_target_pairs={{0,28},{1,29},{2,30},{3,31},{4,0},{5,1},{6,2},{7,3},{8,4},{9,5},{1... | collective-permute-start | bytes 196616 | tf_op jit(solution)/shard_map/ppermute | solution.py:218
  123.5 4.7 %collective-permute-start.39 = (f32[32,512]{1,0:T(8,128)S(1)}, f32[32,512]{1,0:T(8,128)S(1)}, u32[]{:S(2)}, u32[]{:S(2)}) collective-permute-start(f32[32,512]{1,0:T(8,128)S(1)} %broadcast_select_fusion.8.refs_0_.here), channel_id=1, source_target_pairs={{0,28},{1,29},{2,30},{3,31},{4,0},{5,1},{6,2},{7,3},{8,4},{9,5},{1... | collective-permute-start | bytes 196616 | tf_op jit(solution)/shard_map/ppermute | solution.py:218
  128.2 1.2 relax_1_1.3
  129.4 1.5 %collective-permute-start.40 = (f32[32,512]{1,0:T(8,128)S(1)}, f32[32,512]{1,0:T(8,128)S(1)}, u32[]{:S(2)}, u32[]{:S(2)}) collective-permute-start(f32[32,512]{1,0:T(8,128)S(1)} %get-tuple-element.103.refs_12_), channel_id=1, source_target_pairs={{0,2},{1,3},{2,0},{3,1},{4,6},{5,7},{6,4},{7,5},{8,10},{9,11},{10,... | collective-permute-start | bytes 196616 | tf_op jit(solution)/shard_map/ppermute | solution.py:215
  131.5 2.2 %collective-permute-done.40 = f32[32,512]{1,0:T(8,128)S(1)} collective-permute-done((f32[32,512]{1,0:T(8,128)S(1)}, f32[32,512]{1,0:T(8,128)S(1)}, u32[]{:S(2)}, u32[]{:S(2)}) %collective-permute-start.40) | collective-permute-done | bytes 65568 | tf_op jit(solution)/shard_map/ppermute | solution.py:215
  133.7 4.7 %collective-permute-start.42 = (f32[32,512]{1,0:T(8,128)S(1)}, f32[32,512]{1,0:T(8,128)S(1)}, u32[]{:S(2)}, u32[]{:S(2)}) collective-permute-start(f32[32,512]{1,0:T(8,128)S(1)} %broadcast_select_fusion.7.here), channel_id=1, source_target_pairs={{0,28},{1,29},{2,30},{3,31},{4,0},{5,1},{6,2},{7,3},{8,4},{9,5},{1... | collective-permute-start | bytes 196616 | tf_op jit(solution)/shard_map/ppermute | solution.py:218
  138.4 1.2 relax_0_0.1
  139.6 1.0 collective-permute-done.41.behind
  140.7 1.2 relax_0_1.1
  142.0 1.3 collective-permute-done.43.other_ref
  (114 shorter events, 9.4 us)
Async XLA Ops:
  0.0 27.7 %copy-start.13 = (s32[1,6]{1,0:T(1,128)S(1)}, s32[1,6]{1,0:T(1,128)}, u32[]{:S(2)}) copy-start(s32[1,6]{1,0:T(1,128)} %param.9) | copy-start | bytes 76
  4.1 1.6 %collective-permute-start.1 = (f32[64,512]{1,0:T(8,128)S(1)}, f32[64,512]{1,0:T(8,128)S(1)}, u32[]{:S(2)}, u32[]{:S(2)}) collective-permute-start(f32[64,512]{1,0:T(8,128)S(1)} %get-tuple-element.60), channel_id=1, source_target_pairs={{0,1},{1,0},{2,3},{3,2},{4,5},{5,4},{6,7},{7,6},{8,9},{9,8},{10,11... | collective-permute-start | bytes 393224 | tf_op jit(solution)/shard_map/ppermute | solution.py:215
  4.6 1.1 collective-permute-start
  5.7 23.1 %collective-permute-start.6 = (f32[6,512,512]{2,1,0:T(8,128)}, f32[6,512,512]{2,1,0:T(8,128)}, u32[]{:S(2)}, u32[]{:S(2)}) collective-permute-start(f32[6,512,512]{2,1,0:T(8,128)} %bitcast.11), channel_id=1, source_target_pairs={{0,1},{1,0},{2,3},{3,2},{4,5},{5,4},{6,7},{7,6},{8,9},{9,8},{10,11... | collective-permute-start | bytes 18874376 | tf_op jit(solution)/shard_map/ppermute | solution.py:215
  6.0 5.3 %collective-permute-start.9 = (f32[32,512]{1,0:T(8,128)S(1)}, f32[32,512]{1,0:T(8,128)S(1)}, u32[]{:S(2)}, u32[]{:S(2)}) collective-permute-start(f32[32,512]{1,0:T(8,128)S(1)} %slice.18), channel_id=1, source_target_pairs={{0,2},{1,3},{2,0},{3,1},{4,6},{5,7},{6,4},{7,5},{8,10},{9,11},{10,... | collective-permute-start | bytes 196616 | tf_op jit(solution)/shard_map/ppermute | solution.py:215
  8.9 18.9 %collective-permute-start.7 = (f32[512,512]{1,0:T(8,128)S(1)}, f32[512,512]{1,0:T(8,128)S(1)}, u32[]{:S(2)}, u32[]{:S(2)}) collective-permute-start(f32[512,512]{1,0:T(8,128)S(1)} %copy-done.1), channel_id=1, source_target_pairs={{0,1},{1,0},{2,3},{3,2},{4,5},{5,4},{6,7},{7,6},{8,9},{9,8},{10,11... | collective-permute-start | bytes 3145736 | tf_op jit(solution)/shard_map/ppermute | solution.py:215
  11.3 5.5 %collective-permute-start.3 = (f32[32,512]{1,0:T(8,128)S(1)}, f32[32,512]{1,0:T(8,128)S(1)}, u32[]{:S(2)}, u32[]{:S(2)}) collective-permute-start(f32[32,512]{1,0:T(8,128)S(1)} %get-tuple-element.116), channel_id=1, source_target_pairs={{0,2},{1,3},{2,0},{3,1},{4,6},{5,7},{6,4},{7,5},{8,10},{9,11},{10,... | collective-permute-start | bytes 196616 | tf_op jit(solution)/shard_map/ppermute | solution.py:215
  13.2 3.6 %collective-permute-start.2 = (s32[4]{0:T(128)S(1)}, s32[4]{0:T(128)S(1)}, u32[]{:S(2)}, u32[]{:S(2)}) collective-permute-start(s32[4]{0:T(128)S(1)} %fusion), channel_id=1, source_target_pairs={{0,2},{1,3},{2,0},{3,1},{4,6},{5,7},{6,4},{7,5},{8,10},{9,11},{10,... | collective-permute-start | bytes 56 | tf_op jit(solution)/shard_map/ppermute | solution.py:215
  16.8 9.3 %collective-permute-start.5 = (s32[4]{0:T(128)S(1)}, s32[4]{0:T(128)S(1)}, u32[]{:S(2)}, u32[]{:S(2)}) collective-permute-start(s32[4]{0:T(128)S(1)} %add.55), channel_id=1, source_target_pairs={{0,28},{1,29},{2,30},{3,31},{4,0},{5,1},{6,2},{7,3},{8,4},{9,5},{1... | collective-permute-start | bytes 56 | tf_op jit(solution)/shard_map/ppermute | solution.py:218
  21.4 6.2 %collective-permute-start.4 = (s32[4]{0:T(128)S(1)}, s32[4]{0:T(128)S(1)}, u32[]{:S(2)}, u32[]{:S(2)}) collective-permute-start(s32[4]{0:T(128)S(1)} %add.55), channel_id=1, source_target_pairs={{0,4},{1,5},{2,6},{3,7},{4,8},{5,9},{6,10},{7,11},{8,12},{9,13},{1... | collective-permute-start | bytes 56 | tf_op jit(solution)/shard_map/ppermute | solution.py:218
  21.4 8.0 %collective-permute-start.11 = (f32[32,512]{1,0:T(8,128)S(1)}, f32[32,512]{1,0:T(8,128)}, u32[]{:S(2)}, u32[]{:S(2)}) collective-permute-start(f32[32,512]{1,0:T(8,128)S(1)} %broadcast_select_fusion.12.here.refs_2_), channel_id=1, source_target_pairs={{0,28},{1,29},{2,30},{3,31},{4,0},{5,1},{6,2},{7,3},{8,4},{9,5},{1... | collective-permute-start | bytes 196616 | tf_op jit(solution)/shard_map/ppermute | solution.py:218
  26.2 7.1 %collective-permute-start.8 = (f32[32,512]{1,0:T(8,128)S(1)}, f32[32,512]{1,0:T(8,128)}, u32[]{:S(2)}, u32[]{:S(2)}) collective-permute-start(f32[32,512]{1,0:T(8,128)S(1)} %broadcast_select_fusion.12.here.refs_2_), channel_id=1, source_target_pairs={{0,4},{1,5},{2,6},{3,7},{4,8},{5,9},{6,10},{7,11},{8,12},{9,13},{1... | collective-permute-start | bytes 196616 | tf_op jit(solution)/shard_map/ppermute | solution.py:218
  29.4 5.4 %copy-start.3 = (bf16[512,1536]{1,0:T(8,128)(2,1)}, bf16[512,1536]{1,0:T(8,128)(2,1)S(1)}, u32[]{:S(2)}) copy-start(bf16[512,1536]{1,0:T(8,128)(2,1)S(1)} %get-tuple-element.66.w_low) | copy-start | bytes 4718596
  35.4 7.0 %collective-permute-start.13 = (f32[32,512]{1,0:T(8,128)}, f32[32,512]{1,0:T(8,128)}, u32[]{:S(2)}, u32[]{:S(2)}) collective-permute-start(f32[32,512]{1,0:T(8,128)} %get-tuple-element.70), channel_id=1, source_target_pairs={{0,2},{1,3},{2,0},{3,1},{4,6},{5,7},{6,4},{7,5},{8,10},{9,11},{10,... | collective-permute-start | bytes 196616 | tf_op jit(solution)/shard_map/ppermute | solution.py:215
  37.6 10.4 %collective-permute-start.10 = (f32[32,512]{1,0:T(8,128)S(1)}, f32[32,512]{1,0:T(8,128)S(1)}, u32[]{:S(2)}, u32[]{:S(2)}) collective-permute-start(f32[32,512]{1,0:T(8,128)S(1)} %get-tuple-element.115.here.refs_3_), channel_id=1, source_target_pairs={{0,4},{1,5},{2,6},{3,7},{4,8},{5,9},{6,10},{7,11},{8,12},{9,13},{1... | collective-permute-start | bytes 196616 | tf_op jit(solution)/shard_map/ppermute | solution.py:218
  37.7 10.4 %collective-permute-start.12 = (f32[32,512]{1,0:T(8,128)S(1)}, f32[32,512]{1,0:T(8,128)S(1)}, u32[]{:S(2)}, u32[]{:S(2)}) collective-permute-start(f32[32,512]{1,0:T(8,128)S(1)} %get-tuple-element.115.here.refs_3_), channel_id=1, source_target_pairs={{0,28},{1,29},{2,30},{3,31},{4,0},{5,1},{6,2},{7,3},{8,4},{9,5},{1... | collective-permute-start | bytes 196616 | tf_op jit(solution)/shard_map/ppermute | solution.py:218
  43.2 14.3 %collective-permute-start.14 = (f32[32,512]{1,0:T(8,128)S(1)}, f32[32,512]{1,0:T(8,128)S(1)}, u32[]{:S(2)}, u32[]{:S(2)}) collective-permute-start(f32[32,512]{1,0:T(8,128)S(1)} %broadcast_select_fusion.10.refs_0_.here.refs_8_), channel_id=1, source_target_pairs={{0,4},{1,5},{2,6},{3,7},{4,8},{5,9},{6,10},{7,11},{8,12},{9,13},{1... | collective-permute-start | bytes 196616 | tf_op jit(solution)/shard_map/ppermute | solution.py:218
  43.3 14.2 %collective-permute-start.17 = (f32[32,512]{1,0:T(8,128)S(1)}, f32[32,512]{1,0:T(8,128)S(1)}, u32[]{:S(2)}, u32[]{:S(2)}) collective-permute-start(f32[32,512]{1,0:T(8,128)S(1)} %broadcast_select_fusion.10.refs_0_.here.refs_8_), channel_id=1, source_target_pairs={{0,28},{1,29},{2,30},{3,31},{4,0},{5,1},{6,2},{7,3},{8,4},{9,5},{1... | collective-permute-start | bytes 196616 | tf_op jit(solution)/shard_map/ppermute | solution.py:218
  51.9 7.7 %collective-permute-start.15 = (f32[32,512]{1,0:T(8,128)S(1)}, f32[32,512]{1,0:T(8,128)S(1)}, u32[]{:S(2)}, u32[]{:S(2)}) collective-permute-start(f32[32,512]{1,0:T(8,128)S(1)} %get-tuple-element.71.refs_6_), channel_id=1, source_target_pairs={{0,2},{1,3},{2,0},{3,1},{4,6},{5,7},{6,4},{7,5},{8,10},{9,11},{10,... | collective-permute-start | bytes 196616 | tf_op jit(solution)/shard_map/ppermute | solution.py:215
  59.5 4.9 %collective-permute-start.19 = (f32[32,512]{1,0:T(8,128)S(1)}, f32[32,512]{1,0:T(8,128)S(1)}, u32[]{:S(2)}, u32[]{:S(2)}) collective-permute-start(f32[32,512]{1,0:T(8,128)S(1)} %get-tuple-element.77), channel_id=1, source_target_pairs={{0,2},{1,3},{2,0},{3,1},{4,6},{5,7},{6,4},{7,5},{8,10},{9,11},{10,... | collective-permute-start | bytes 196616 | tf_op jit(solution)/shard_map/ppermute | solution.py:215
  59.7 9.6 %collective-permute-start.16 = (f32[32,512]{1,0:T(8,128)S(1)}, f32[32,512]{1,0:T(8,128)S(1)}, u32[]{:S(2)}, u32[]{:S(2)}) collective-permute-start(f32[32,512]{1,0:T(8,128)S(1)} %broadcast_select_fusion.9.here.refs_9_), channel_id=1, source_target_pairs={{0,4},{1,5},{2,6},{3,7},{4,8},{5,9},{6,10},{7,11},{8,12},{9,13},{1... | collective-permute-start | bytes 196616 | tf_op jit(solution)/shard_map/ppermute | solution.py:218
  59.7 9.5 %collective-permute-start.18 = (f32[32,512]{1,0:T(8,128)S(1)}, f32[32,512]{1,0:T(8,128)S(1)}, u32[]{:S(2)}, u32[]{:S(2)}) collective-permute-start(f32[32,512]{1,0:T(8,128)S(1)} %broadcast_select_fusion.9.here.refs_9_), channel_id=1, source_target_pairs={{0,28},{1,29},{2,30},{3,31},{4,0},{5,1},{6,2},{7,3},{8,4},{9,5},{1... | collective-permute-start | bytes 196616 | tf_op jit(solution)/shard_map/ppermute | solution.py:218
  64.4 12.5 %collective-permute-start.20 = (f32[32,512]{1,0:T(8,128)S(1)}, f32[32,512]{1,0:T(8,128)S(1)}, u32[]{:S(2)}, u32[]{:S(2)}) collective-permute-start(f32[32,512]{1,0:T(8,128)S(1)} %broadcast_select_fusion.6.refs_0_.here), channel_id=1, source_target_pairs={{0,4},{1,5},{2,6},{3,7},{4,8},{5,9},{6,10},{7,11},{8,12},{9,13},{1... | collective-permute-start | bytes 196616 | tf_op jit(solution)/shard_map/ppermute | solution.py:218
  64.5 12.5 %collective-permute-start.21 = (f32[32,512]{1,0:T(8,128)S(1)}, f32[32,512]{1,0:T(8,128)S(1)}, u32[]{:S(2)}, u32[]{:S(2)}) collective-permute-start(f32[32,512]{1,0:T(8,128)S(1)} %broadcast_select_fusion.6.refs_0_.here), channel_id=1, source_target_pairs={{0,28},{1,29},{2,30},{3,31},{4,0},{5,1},{6,2},{7,3},{8,4},{9,5},{1... | collective-permute-start | bytes 196616 | tf_op jit(solution)/shard_map/ppermute | solution.py:218
  71.2 8.4 %collective-permute-start.22 = (f32[32,512]{1,0:T(8,128)S(1)}, f32[32,512]{1,0:T(8,128)S(1)}, u32[]{:S(2)}, u32[]{:S(2)}) collective-permute-start(f32[32,512]{1,0:T(8,128)S(1)} %get-tuple-element.78.refs_12_), channel_id=1, source_target_pairs={{0,2},{1,3},{2,0},{3,1},{4,6},{5,7},{6,4},{7,5},{8,10},{9,11},{10,... | collective-permute-start | bytes 196616 | tf_op jit(solution)/shard_map/ppermute | solution.py:215
  79.6 4.8 %collective-permute-start.25 = (f32[32,512]{1,0:T(8,128)S(1)}, f32[32,512]{1,0:T(8,128)S(1)}, u32[]{:S(2)}, u32[]{:S(2)}) collective-permute-start(f32[32,512]{1,0:T(8,128)S(1)} %get-tuple-element.84), channel_id=1, source_target_pairs={{0,2},{1,3},{2,0},{3,1},{4,6},{5,7},{6,4},{7,5},{8,10},{9,11},{10,... | collective-permute-start | bytes 196616 | tf_op jit(solution)/shard_map/ppermute | solution.py:215
  79.6 9.6 %collective-permute-start.23 = (f32[32,512]{1,0:T(8,128)S(1)}, f32[32,512]{1,0:T(8,128)S(1)}, u32[]{:S(2)}, u32[]{:S(2)}) collective-permute-start(f32[32,512]{1,0:T(8,128)S(1)} %broadcast_select_fusion.5.here), channel_id=1, source_target_pairs={{0,4},{1,5},{2,6},{3,7},{4,8},{5,9},{6,10},{7,11},{8,12},{9,13},{1... | collective-permute-start | bytes 196616 | tf_op jit(solution)/shard_map/ppermute | solution.py:218
  79.7 9.5 %collective-permute-start.24 = (f32[32,512]{1,0:T(8,128)S(1)}, f32[32,512]{1,0:T(8,128)S(1)}, u32[]{:S(2)}, u32[]{:S(2)}) collective-permute-start(f32[32,512]{1,0:T(8,128)S(1)} %broadcast_select_fusion.5.here), channel_id=1, source_target_pairs={{0,28},{1,29},{2,30},{3,31},{4,0},{5,1},{6,2},{7,3},{8,4},{9,5},{1... | collective-permute-start | bytes 196616 | tf_op jit(solution)/shard_map/ppermute | solution.py:218
  84.4 8.2 %copy-start.2 = (f32[512,512]{1,0:T(8,128)S(1)}, f32[512,512]{1,0:T(8,128)}, u32[]{:S(2)}) copy-start(f32[512,512]{1,0:T(8,128)} %own_inverse.11) | copy-start | bytes 3145732
  84.4 10.8 %collective-permute-start.26 = (f32[32,512]{1,0:T(8,128)S(1)}, f32[32,512]{1,0:T(8,128)S(1)}, u32[]{:S(2)}, u32[]{:S(2)}) collective-permute-start(f32[32,512]{1,0:T(8,128)S(1)} %broadcast_select_fusion.2.refs_0_.here.refs_2_.refs_8_), channel_id=1, source_target_pairs={{0,4},{1,5},{2,6},{3,7},{4,8},{5,9},{6,10},{7,11},{8,12},{9,13},{1... | collective-permute-start | bytes 196616 | tf_op jit(solution)/shard_map/ppermute | solution.py:218
  84.5 10.7 %collective-permute-start.27 = (f32[32,512]{1,0:T(8,128)S(1)}, f32[32,512]{1,0:T(8,128)S(1)}, u32[]{:S(2)}, u32[]{:S(2)}) collective-permute-start(f32[32,512]{1,0:T(8,128)S(1)} %broadcast_select_fusion.2.refs_0_.here.refs_2_.refs_8_), channel_id=1, source_target_pairs={{0,28},{1,29},{2,30},{3,31},{4,0},{5,1},{6,2},{7,3},{8,4},{9,5},{1... | collective-permute-start | bytes 196616 | tf_op jit(solution)/shard_map/ppermute | solution.py:218
  92.0 5.8 %collective-permute-start.28 = (f32[32,512]{1,0:T(8,128)S(1)}, f32[32,512]{1,0:T(8,128)S(1)}, u32[]{:S(2)}, u32[]{:S(2)}) collective-permute-start(f32[32,512]{1,0:T(8,128)S(1)} %get-tuple-element.87.refs_2_), channel_id=1, source_target_pairs={{0,2},{1,3},{2,0},{3,1},{4,6},{5,7},{6,4},{7,5},{8,10},{9,11},{10,... | collective-permute-start | bytes 196616 | tf_op jit(solution)/shard_map/ppermute | solution.py:215
  97.8 4.8 %collective-permute-start.31 = (f32[32,512]{1,0:T(8,128)S(1)}, f32[32,512]{1,0:T(8,128)S(1)}, u32[]{:S(2)}, u32[]{:S(2)}) collective-permute-start(f32[32,512]{1,0:T(8,128)S(1)} %get-tuple-element.93), channel_id=1, source_target_pairs={{0,2},{1,3},{2,0},{3,1},{4,6},{5,7},{6,4},{7,5},{8,10},{9,11},{10,... | collective-permute-start | bytes 196616 | tf_op jit(solution)/shard_map/ppermute | solution.py:215
  97.9 9.6 %collective-permute-start.29 = (f32[32,512]{1,0:T(8,128)S(1)}, f32[32,512]{1,0:T(8,128)S(1)}, u32[]{:S(2)}, u32[]{:S(2)}) collective-permute-start(f32[32,512]{1,0:T(8,128)S(1)} %broadcast_select_fusion.1.here.refs_3_.refs_9_), channel_id=1, source_target_pairs={{0,4},{1,5},{2,6},{3,7},{4,8},{5,9},{6,10},{7,11},{8,12},{9,13},{1... | collective-permute-start | bytes 196616 | tf_op jit(solution)/shard_map/ppermute | solution.py:218
  97.9 9.5 %collective-permute-start.30 = (f32[32,512]{1,0:T(8,128)S(1)}, f32[32,512]{1,0:T(8,128)S(1)}, u32[]{:S(2)}, u32[]{:S(2)}) collective-permute-start(f32[32,512]{1,0:T(8,128)S(1)} %broadcast_select_fusion.1.here.refs_3_.refs_9_), channel_id=1, source_target_pairs={{0,28},{1,29},{2,30},{3,31},{4,0},{5,1},{6,2},{7,3},{8,4},{9,5},{1... | collective-permute-start | bytes 196616 | tf_op jit(solution)/shard_map/ppermute | solution.py:218
  102.7 8.0 %copy-start.11 = (f32[32,512]{1,0:T(8,128)S(1)}, f32[32,512]{1,0:T(8,128)}, u32[]{:S(2)}) copy-start(f32[32,512]{1,0:T(8,128)} %copy-done.10) | copy-start | bytes 196612
  102.7 8.6 %collective-permute-start.32 = (f32[32,512]{1,0:T(8,128)S(1)}, f32[32,512]{1,0:T(8,128)S(1)}, u32[]{:S(2)}, u32[]{:S(2)}) collective-permute-start(f32[32,512]{1,0:T(8,128)S(1)} %broadcast_select_fusion.4.refs_0_.here.refs_2_), channel_id=1, source_target_pairs={{0,4},{1,5},{2,6},{3,7},{4,8},{5,9},{6,10},{7,11},{8,12},{9,13},{1... | collective-permute-start | bytes 196616 | tf_op jit(solution)/shard_map/ppermute | solution.py:218
  102.7 8.6 %collective-permute-start.33 = (f32[32,512]{1,0:T(8,128)S(1)}, f32[32,512]{1,0:T(8,128)S(1)}, u32[]{:S(2)}, u32[]{:S(2)}) collective-permute-start(f32[32,512]{1,0:T(8,128)S(1)} %broadcast_select_fusion.4.refs_0_.here.refs_2_), channel_id=1, source_target_pairs={{0,28},{1,29},{2,30},{3,31},{4,0},{5,1},{6,2},{7,3},{8,4},{9,5},{1... | collective-permute-start | bytes 196616 | tf_op jit(solution)/shard_map/ppermute | solution.py:218
  110.1 8.5 %collective-permute-start.34 = (f32[32,512]{1,0:T(8,128)S(1)}, f32[32,512]{1,0:T(8,128)S(1)}, u32[]{:S(2)}, u32[]{:S(2)}) collective-permute-start(f32[32,512]{1,0:T(8,128)S(1)} %get-tuple-element.96.refs_8_), channel_id=1, source_target_pairs={{0,2},{1,3},{2,0},{3,1},{4,6},{5,7},{6,4},{7,5},{8,10},{9,11},{10,... | collective-permute-start | bytes 196616 | tf_op jit(solution)/shard_map/ppermute | solution.py:215
  112.5 10.9 %collective-permute-start.37 = (f32[32,512]{1,0:T(8,128)S(1)}, f32[32,512]{1,0:T(8,128)S(1)}, u32[]{:S(2)}, u32[]{:S(2)}) collective-permute-start(f32[32,512]{1,0:T(8,128)S(1)} %get-tuple-element.102), channel_id=1, source_target_pairs={{0,2},{1,3},{2,0},{3,1},{4,6},{5,7},{6,4},{7,5},{8,10},{9,11},{10,... | collective-permute-start | bytes 196616 | tf_op jit(solution)/shard_map/ppermute | solution.py:215
  118.6 9.6 %collective-permute-start.35 = (f32[32,512]{1,0:T(8,128)S(1)}, f32[32,512]{1,0:T(8,128)S(1)}, u32[]{:S(2)}, u32[]{:S(2)}) collective-permute-start(f32[32,512]{1,0:T(8,128)S(1)} %broadcast_select_fusion.3.here.refs_3_), channel_id=1, source_target_pairs={{0,4},{1,5},{2,6},{3,7},{4,8},{5,9},{6,10},{7,11},{8,12},{9,13},{1... | collective-permute-start | bytes 196616 | tf_op jit(solution)/shard_map/ppermute | solution.py:218
  118.7 9.5 %collective-permute-start.36 = (f32[32,512]{1,0:T(8,128)S(1)}, f32[32,512]{1,0:T(8,128)S(1)}, u32[]{:S(2)}, u32[]{:S(2)}) collective-permute-start(f32[32,512]{1,0:T(8,128)S(1)} %broadcast_select_fusion.3.here.refs_3_), channel_id=1, source_target_pairs={{0,28},{1,29},{2,30},{3,31},{4,0},{5,1},{6,2},{7,3},{8,4},{9,5},{1... | collective-permute-start | bytes 196616 | tf_op jit(solution)/shard_map/ppermute | solution.py:218
  123.4 15.0 %collective-permute-start.38 = (f32[32,512]{1,0:T(8,128)S(1)}, f32[32,512]{1,0:T(8,128)S(1)}, u32[]{:S(2)}, u32[]{:S(2)}) collective-permute-start(f32[32,512]{1,0:T(8,128)S(1)} %broadcast_select_fusion.8.refs_0_.here), channel_id=1, source_target_pairs={{0,4},{1,5},{2,6},{3,7},{4,8},{5,9},{6,10},{7,11},{8,12},{9,13},{1... | collective-permute-start | bytes 196616 | tf_op jit(solution)/shard_map/ppermute | solution.py:218
  123.5 15.0 %collective-permute-start.39 = (f32[32,512]{1,0:T(8,128)S(1)}, f32[32,512]{1,0:T(8,128)S(1)}, u32[]{:S(2)}, u32[]{:S(2)}) collective-permute-start(f32[32,512]{1,0:T(8,128)S(1)} %broadcast_select_fusion.8.refs_0_.here), channel_id=1, source_target_pairs={{0,28},{1,29},{2,30},{3,31},{4,0},{5,1},{6,2},{7,3},{8,4},{9,5},{1... | collective-permute-start | bytes 196616 | tf_op jit(solution)/shard_map/ppermute | solution.py:218
  129.4 4.3 %collective-permute-start.40 = (f32[32,512]{1,0:T(8,128)S(1)}, f32[32,512]{1,0:T(8,128)S(1)}, u32[]{:S(2)}, u32[]{:S(2)}) collective-permute-start(f32[32,512]{1,0:T(8,128)S(1)} %get-tuple-element.103.refs_12_), channel_id=1, source_target_pairs={{0,2},{1,3},{2,0},{3,1},{4,6},{5,7},{6,4},{7,5},{8,10},{9,11},{10,... | collective-permute-start | bytes 196616 | tf_op jit(solution)/shard_map/ppermute | solution.py:215
  133.7 7.0 %collective-permute-start.41 = (f32[32,512]{1,0:T(8,128)S(1)}, f32[32,512]{1,0:T(8,128)S(1)}, u32[]{:S(2)}, u32[]{:S(2)}) collective-permute-start(f32[32,512]{1,0:T(8,128)S(1)} %broadcast_select_fusion.7.here), channel_id=1, source_target_pairs={{0,4},{1,5},{2,6},{3,7},{4,8},{5,9},{6,10},{7,11},{8,12},{9,13},{1... | collective-permute-start | bytes 196616 | tf_op jit(solution)/shard_map/ppermute | solution.py:218
  133.7 7.0 %collective-permute-start.42 = (f32[32,512]{1,0:T(8,128)S(1)}, f32[32,512]{1,0:T(8,128)S(1)}, u32[]{:S(2)}, u32[]{:S(2)}) collective-permute-start(f32[32,512]{1,0:T(8,128)S(1)} %broadcast_select_fusion.7.here), channel_id=1, source_target_pairs={{0,28},{1,29},{2,30},{3,31},{4,0},{5,1},{6,2},{7,3},{8,4},{9,5},{1... | collective-permute-start | bytes 196616 | tf_op jit(solution)/shard_map/ppermute | solution.py:218
  141.9 1.4 collective-permute-start.43
  (10 other events, 23.2 us)

commit v2 on v1

v2 whole, which is shorter than its diff:
```python
import functools

import jax
import jax.numpy as jnp
from jax import lax
from jax.experimental import pallas as pl
from jax.experimental.pallas import tpu as pltpu
from jax.sharding import PartitionSpec as P

COLOURS = 4
SIDES = 3
PIECES = 2
EXTRA = 8
OWN_COLOUR = 0
SIB_COLOUR = 1
TILE_START = 2


def dot_t(a, b):
    return lax.dot_general(a, b, (((1,), (1,)), ((), ())), preferred_element_type=jnp.float32)


def split(value):
    high = value.astype(jnp.bfloat16)
    return high, (value - high.astype(jnp.float32)).astype(jnp.bfloat16)


def times(value, high, low):
    rows = value.shape[0]
    parts = jnp.concatenate(split(value), axis=0)
    product = dot_t(parts, high) + dot_t(parts, low)
    return product[:rows] + product[rows:]


def vmem():
    return pl.BlockSpec(memory_space=pltpu.VMEM)


def smem():
    return pl.BlockSpec(memory_space=pltpu.SMEM)


def anywhere():
    return pl.BlockSpec(memory_space=pl.ANY)


def hbm():
    return pl.BlockSpec(memory_space=pltpu.HBM)


def params(mebibytes):
    return pltpu.CompilerParams(vmem_limit_bytes=mebibytes * 1024 * 1024)


def far(values):
    return [pltpu.with_memory_space_constraint(v, pltpu.HBM) for v in values]


def near(values):
    return [pltpu.with_memory_space_constraint(v, pltpu.VMEM) for v in values]


def whole(pieces, half):
    return jnp.concatenate([piece[: half // len(pieces), :] for piece in pieces], axis=0)


def first_kernel(facts_ref, inverse_hbm, residual_hbm, keep_ref, send_ref, inverse_ref, residual_ref, sems):
    copies = [
        pltpu.make_async_copy(residual_hbm, residual_ref, sems.at[0]),
        pltpu.make_async_copy(inverse_hbm, inverse_ref, sems.at[1]),
    ]
    for copy in copies:
        copy.start()
    for copy in copies:
        copy.wait()
    value = times(jnp.transpose(residual_ref[...]), *split(inverse_ref[...]))
    half, block = keep_ref.shape
    is_first = facts_ref[0] == 0
    keep_ref[...] = jnp.where(is_first, value[:half], value[half:])
    send_ref[:half, :] = jnp.where(is_first, value[half:], value[:half])
    row = lax.broadcasted_iota(jnp.int32, (EXTRA, block), 0)
    rows = jnp.zeros((EXTRA, block), jnp.int32)
    for i in range(1, facts_ref.shape[0]):
        rows = jnp.where(row == i - 1, facts_ref[i], rows)
    send_ref[half:, :] = rows.astype(jnp.float32)


def last_kernel(core_ref, mine_ref, other_ref, out_ref):
    is_first = core_ref[0] == 0
    mine, other = mine_ref[...], other_ref[...]
    first = jnp.where(is_first, mine, other)
    second = jnp.where(is_first, other, mine)
    out_ref[...] = jnp.transpose(jnp.concatenate([first, second], axis=0))


def tile_of(meta_ref, own, tiles, colour, side):
    wanted = meta_ref[TILE_START + 2 * tiles + side * COLOURS + colour]
    start = jnp.where(own, TILE_START, TILE_START + tiles)
    found = jnp.int32(-1)
    for k in range(tiles):
        found = jnp.where(meta_ref[start + k] == wanted, k, found)
    return found


def gather_kernel(now, newest, older, counts, has_base, n_after, meta_ref, own_tiles, sib_tiles, own_inverse, sib_inverse, own_start, sib_start, *refs):
    known = []
    for count in counts:
        known += [refs[side * count : (side + 1) * count] for side in range(SIDES)]
        refs = refs[SIDES * count :]
    base, refs = refs[:has_base], refs[has_base:]
    w_high, w_low, d_high, d_low, partial, begin, flag, buffer, sems = refs[n_after:]
    tiles, block = own_tiles.shape[0], own_tiles.shape[1]
    half = begin.shape[0]
    own = meta_ref[OWN_COLOUR] == now
    active = own | (meta_ref[SIB_COLOUR] == now)
    slots = [(newest, side) for side in range(SIDES)] + [(c, side) for c in older for side in range(SIDES)]
    flag[...] = jnp.broadcast_to(active.astype(jnp.int32), flag.shape)

    @pl.when(active)
    def _():
        def fetch(own_src, sib_src, slot, start):
            @pl.when(own)
            def _():
                copy = pltpu.make_async_copy(own_src, buffer.at[slot], sems.at[slot])
                copy.start() if start else copy.wait()

            @pl.when(jnp.logical_not(own))
            def _():
                copy = pltpu.make_async_copy(sib_src, buffer.at[slot], sems.at[slot])
                copy.start() if start else copy.wait()

        which = [tile_of(meta_ref, own, tiles, c, side) for c, side in slots]
        fetch(own_inverse, sib_inverse, len(slots), True)
        for slot, k in enumerate(which):
            @pl.when(k >= 0)
            def _():
                fetch(own_tiles.at[k], sib_tiles.at[k], slot, True)

        begin[...] = jnp.where(own, own_start[...], sib_start[:half, :])
        partial[...] = base[0][...] if has_base else jnp.zeros_like(partial)
        fetch(own_inverse, sib_inverse, len(slots), False)
        d_high[...], d_low[...] = split(buffer[len(slots)])
        for slot, k in enumerate(which):
            span = pl.ds(slot * block, block)

            @pl.when(k >= 0)
            def _():
                fetch(own_tiles.at[k], sib_tiles.at[k], slot, False)
                high, low = split(buffer[slot])
                if slot < SIDES:
                    w_high[:, span] = high
                    w_low[:, span] = low
                else:
                    partial[...] += times(whole(known[slot - SIDES], half), high, low)

            if slot < SIDES:
                @pl.when(k < 0)
                def _():
                    w_high[:, span] = jnp.zeros((block, block), jnp.bfloat16)
                    w_low[:, span] = jnp.zeros((block, block), jnp.bfloat16)


def relax_kernel(count, flag, w_high, w_low, d_high, d_low, partial, begin, *refs):
    latest, outs = refs[: SIDES * count], refs[SIDES * count :]
    half = begin.shape[0]
    width = outs[0].shape[0]

    @pl.when(flag[0, 0] != 0)
    def _():
        sides = [whole(latest[side * count : (side + 1) * count], half) for side in range(SIDES)]
        value = jnp.concatenate(sides, axis=1)
        coupled = partial[...] + times(value, w_high[...], w_low[...])
        for ref in outs[PIECES:]:
            ref[...] = coupled
        result = begin[...] - times(coupled, d_high[...], d_low[...])
        for piece in range(PIECES):
            outs[piece][...] = result[piece * width : (piece + 1) * width]


def gather(now, newest, older, meta, matrices, starts, known, base, after):
    tiles, block, _ = matrices[0].shape
    half = starts[0].shape[0]
    slots = SIDES * (1 + len(older)) + 1
    operands = [piece[side] for c in older for side in range(SIDES) for piece in known[c]]
    operands = near([*starts, *operands, *base])
    counts = [len(known[c]) for c in older]
    bf16 = jnp.bfloat16
    return pl.pallas_call(
        functools.partial(gather_kernel, now, newest, older, counts, len(base), len(after)),
        out_shape=[
            pltpu.VMEM((block, SIDES * block), bf16),
            pltpu.VMEM((block, SIDES * block), bf16),
            pltpu.VMEM((block, block), bf16),
            pltpu.VMEM((block, block), bf16),
            pltpu.VMEM((half, block), jnp.float32),
            pltpu.VMEM((half, block), jnp.float32),
            pltpu.VMEM((8, 128), jnp.int32),
        ],
        in_specs=[smem()] + [hbm(), anywhere()] * 2 + [vmem()] * len(operands) + [anywhere()] * len(after),
        out_specs=[vmem()] * 7,
        scratch_shapes=[
            pltpu.VMEM((slots, block, block), jnp.float32),
            pltpu.SemaphoreType.DMA((slots,)),
        ],
        compiler_params=params(28),
        cost_estimate=pl.CostEstimate(
            flops=4 * block * block * 128 * slots, bytes_accessed=4 * block * block * slots, transcendentals=0
        ),
        name=f"gather_{now}_{newest}",
    )(meta, *matrices, *operands, *after)


def relax(now, gathered, latest, keep_sum):
    *weights, partial, begin, flag = gathered
    half, block = begin.shape
    operands = [piece[side] for side in range(SIDES) for piece in latest]
    operands = near([flag, *weights, partial, begin, *operands])
    out_shape = [pltpu.VMEM((half // PIECES, block), jnp.float32)] * PIECES
    out_shape += [pltpu.VMEM((half, block), jnp.float32)] * keep_sum
    return pl.pallas_call(
        functools.partial(relax_kernel, len(latest)),
        out_shape=out_shape,
        in_specs=[vmem()] * len(operands),
        out_specs=[vmem()] * len(out_shape),
        compiler_params=params(16),
        cost_estimate=pl.CostEstimate(
            flops=16 * block * block * 128, bytes_accessed=16 * block * block, transcendentals=0
        ),
        name=f"relax_{now}",
    )(*operands)


def per_device(residual, inv_diag, coupling_tiles, colour, tile_cols):
    axis = "rows"
    count = lax.axis_size(axis)
    groups = count // COLOURS
    me = lax.axis_index(axis)
    core = (me % 2).reshape(1)
    place = me % COLOURS
    group = me // COLOURS
    block, cols = residual.shape
    half = cols // 2
    tiles = jnp.transpose(coupling_tiles, (1, 0, 2))
    number = tiles.shape[0]

    def flip(value, bit):
        return lax.ppermute(value, axis, [(i, i ^ bit) for i in range(count)])

    def shift(value, by):
        return lax.ppermute(value, axis, [(i, (i + by) % count) for i in range(count)])

    def across(candidates, here_now):
        swapped = [flip(c, 2) for c in candidates]
        return [jnp.where(here_now, c, s) for c, s in zip(candidates, swapped)], swapped

    def around(here):
        return [[shift(h, COLOURS), h, shift(h, -COLOURS)] for h in here]

    facts = jnp.concatenate([core, colour, tile_cols[0]])
    keep, send = pl.pallas_call(
        first_kernel,
        out_shape=[pltpu.VMEM((half, block), jnp.float32), pltpu.VMEM((half + EXTRA, block), jnp.float32)],
        in_specs=[smem(), hbm(), hbm()],
        out_specs=[vmem()] * 2,
        scratch_shapes=[
            pltpu.VMEM((block, block), jnp.float32),
            pltpu.VMEM((block, cols), jnp.float32),
            pltpu.SemaphoreType.DMA((2,)),
        ],
        compiler_params=params(16),
        name="first",
    )(facts, *far([inv_diag, residual]))
    arrived = flip(send, 1)
    starts = [keep, arrived]
    own_colour = colour[0]
    sib_facts = arrived[half : half + 1 + number, 0].astype(jnp.int32)
    sib_colour = sib_facts[0]

    late_tiles, late_inverse, _ = lax.optimization_barrier((tiles, inv_diag, arrived))
    own_tiles, own_inverse = far([tiles, inv_diag])
    matrices = [own_tiles, flip(late_tiles, 1), own_inverse, flip(late_inverse, 1)]

    candidate = jnp.where(own_colour == 0, keep, arrived[:half])
    wheel = lax.broadcasted_iota(jnp.int32, (EXTRA, block), 0)
    sib_wide = arrived[half : half + 1]
    places = jnp.where(wheel == own_colour, place, 0) + jnp.where(wheel.astype(jnp.float32) == sib_wide, place ^ 1, 0)
    places = places.astype(jnp.float32)
    here, swapped = across([jnp.concatenate([candidate, places])], (own_colour == 0) | (sib_colour == 0))
    known = {0: around([jnp.concatenate([here[0][:half], places + swapped[0][half:]])])}
    blocks = []
    for side in range(SIDES):
        found = known[0][0][side][half : half + COLOURS, 0].astype(jnp.int32)
        blocks.append((((group + side - 1) % groups) * COLOURS + found).astype(jnp.int32))
    meta = jnp.concatenate([colour, sib_facts[:1], tile_cols[0], sib_facts[1:]] + blocks)

    order = list(range(1, COLOURS)) + list(range(COLOURS - 2, -1, -1))
    newest = 0
    sums, used, finals = {}, {}, {}
    after = []
    for step, now in enumerate(order):
        fresh = used.get(now, set())
        older = tuple(c for c in sorted(known) if c not in (now, newest) and (c, done_at(order, c, step)) not in fresh)
        gathered = gather(now, newest, older, meta, matrices, starts, known, sums.get(now, []), after)
        used[now] = {(c, done_at(order, c, step)) for c in known if c != now}
        outs = relax(now, gathered, known[newest], int(now in order[step + 1 :]))
        candidates, sums[now] = outs[:PIECES], outs[PIECES:]
        finals[now], after, newest = candidates, candidates[:1], now
        if step < len(order) - 1:
            here, _ = across(candidates, (own_colour == now) | (sib_colour == now))
            known[now] = around(here)

    own_final, sib_final = finals[0], finals[0]
    for c in range(1, COLOURS):
        own_final = [jnp.where(own_colour == c, a, b) for a, b in zip(finals[c], own_final)]
        sib_final = [jnp.where(sib_colour == c, a, b) for a, b in zip(finals[c], sib_final)]
    mine, other = jnp.concatenate(own_final), flip(jnp.concatenate(sib_final), 1)
    return pl.pallas_call(
        last_kernel,
        out_shape=jax.ShapeDtypeStruct((block, cols), jnp.float32),
        in_specs=[smem(), vmem(), vmem()],
        out_specs=vmem(),
        compiler_params=params(16),
        name="last",
    )(core, *near([mine, other]))


def done_at(order, colour, step):
    return max([i for i in range(step) if order[i] == colour], default=-1)


def solution(mesh):
    in_specs = (P("rows", None), P("rows", None), P("rows", None, None), P("rows"), P("rows", None))
    out_specs = P("rows", None)
    return jax.shard_map(
        per_device, mesh=mesh, in_specs=in_specs, out_specs=out_specs, check_vma=False
    )
```

time: 147 us -> 123 us (0.84)
  the two profiles are of different devices: /device:TPU:0 before, /device:TPU:3 now
where the time goes in v2:
time: 123 us
  starting transfers between devices  74.3 us (60%)
  waiting for transfers between devices  21.3 us (17%)
  Pallas kernels  21 us (17%)
  between operations  3.75 us (3%)
  other arithmetic  1.47 us (1%)
  local copies, waits for them, and re-layouts  1.37 us (1%)
    ppermute x22, starting transfers between devices, shift(): lax.ppermute(value, axis, [(i, (i + by) % count) for i in range(count)])  43.1 us
    ppermute x15, starting transfers between devices, flip(): return lax.ppermute(value, axis, [(i, i ^ bit) for i in range(count)])  31.2 us
    ppermute x15, waiting for transfers between devices, flip(): return lax.ppermute(value, axis, [(i, i ^ bit) for i in range(count)])  14.3 us
    pallas_call x6, Pallas kernels, gather(): pl.pallas_call(functools.partial(gather_kernel, now, newest, older, count...  12.8 us
    ppermute x22, waiting for transfers between devices, shift(): lax.ppermute(value, axis, [(i, (i + by) % count) for i in range(count)])  6.99 us
    pallas_call x6, Pallas kernels, relax(): pl.pallas_call(functools.partial(relax_kernel, len(latest)), out_shape=ou...  5.06 us
  transfers between devices with their start and end apart: 37, of which 14 were waited for; matrix products, arithmetic and copies ran while one was open for 2% of the time, Pallas kernels for 10%

profile of v2, /device:TPU:3, one launch (start us, length us, event | category | flops | bytes accessed | tf_op | source)
XLA Modules:
  0.0 123.2 jit_solution(2706163341695015166)
XLA Ops:
  0.8 0.7 pad_add_fusion.facts_ref
  1.5 2.4 %first.1 = (f32[64,512]{1,0:T(8,128)S(1)}, f32[72,512]{1,0:T(8,128)S(1)}) custom-call(s32[8]{0:T(128)S(1)} %pad_add_fusion.facts_ref, f32[512,512]{1,0:T(8,128)} %own_inverse.11, f32[512,128]{1,0:T(8,128)} %residual_hbm.1), custom_call_target="tpu_custom_call" | custom-call | tf_op jit(solution)/shard_map/first/pallas_call | solution.py:260
  3.9 0.7 collective-permute-start
  4.6 1.0 collective-permute-done.sib_start
  5.6 0.4 collective-permute-start.4
  6.4 0.5 slice.38
  7.6 3.9 %collective-permute-done.1 = f32[72,512]{1,0:T(8,128)S(1)} collective-permute-done((f32[72,512]{1,0:T(8,128)S(1)}, f32[72,512]{1,0:T(8,128)S(1)}, u32[]{:S(2)}, u32[]{:S(2)}) %collective-permute-start.1) | collective-permute-done | bytes 147488 | tf_op jit(solution)/shard_map/ppermute | solution.py:247
  11.6 1.3 %collective-permute-start.2 = (f32[72,512]{1,0:T(8,128)S(1)}, f32[72,512]{1,0:T(8,128)S(1)}, u32[]{:S(2)}, u32[]{:S(2)}) collective-permute-start(f32[72,512]{1,0:T(8,128)S(1)} %pad_maximum_fusion.1.refs_1_), channel_id=1, source_target_pairs={{0,4},{1,5},{2,6},{3,7},{4,8},{5,9},{6,10},{7,11},{8,12},{9,13},{1... | collective-permute-start | bytes 442376 | tf_op jit(solution)/shard_map/ppermute | solution.py:250
  13.0 3.1 %collective-permute-start.3 = (f32[72,512]{1,0:T(8,128)S(1)}, f32[72,512]{1,0:T(8,128)S(1)}, u32[]{:S(2)}, u32[]{:S(2)}) collective-permute-start(f32[72,512]{1,0:T(8,128)S(1)} %pad_maximum_fusion.1.refs_1_), channel_id=1, source_target_pairs={{0,28},{1,29},{2,30},{3,31},{4,0},{5,1},{6,2},{7,3},{8,4},{9,5},{1... | collective-permute-start | bytes 442376 | tf_op jit(solution)/shard_map/ppermute | solution.py:250
  16.2 2.8 %collective-permute-done.2.refs_0_ = f32[72,512]{1,0:T(8,128)S(1)} collective-permute-done((f32[72,512]{1,0:T(8,128)S(1)}, f32[72,512]{1,0:T(8,128)S(1)}, u32[]{:S(2)}, u32[]{:S(2)}) %collective-permute-start.2) | collective-permute-done | bytes 147488 | tf_op jit(solution)/shard_map/ppermute | solution.py:250
  19.1 1.2 collective-permute-done.3.refs_2_
  20.4 0.7 concatenate.21.meta_ref
  21.2 0.6 gather_1_0.1
  21.8 3.7 %collective-permute-start.6 = (f32[32,512]{1,0:T(8,128)S(1)}, f32[32,512]{1,0:T(8,128)S(1)}, u32[]{:S(2)}, u32[]{:S(2)}) collective-permute-start(f32[32,512]{1,0:T(8,128)S(1)} %get-tuple-element.76.refs_3_), channel_id=1, source_target_pairs={{0,2},{1,3},{2,0},{3,1},{4,6},{5,7},{6,4},{7,5},{8,10},{9,11},{10,... | collective-permute-start | bytes 196616 | tf_op jit(solution)/shard_map/ppermute | solution.py:247
  26.2 0.9 collective-permute-done.6
  27.2 4.9 %collective-permute-start.10 = (f32[32,512]{1,0:T(8,128)S(1)}, f32[32,512]{1,0:T(8,128)S(1)}, u32[]{:S(2)}, u32[]{:S(2)}) collective-permute-start(f32[32,512]{1,0:T(8,128)S(1)} %broadcast_select_fusion.9.refs_2_.refs_5_), channel_id=1, source_target_pairs={{0,28},{1,29},{2,30},{3,31},{4,0},{5,1},{6,2},{7,3},{8,4},{9,5},{1... | collective-permute-start | bytes 196616 | tf_op jit(solution)/shard_map/ppermute | solution.py:250
  32.2 4.1 %collective-permute-start.11 = (f32[32,512]{1,0:T(8,128)S(1)}, f32[32,512]{1,0:T(8,128)S(1)}, u32[]{:S(2)}, u32[]{:S(2)}) collective-permute-start(f32[32,512]{1,0:T(8,128)S(1)} %broadcast_select_fusion.8.refs_3_.refs_6_), channel_id=1, source_target_pairs={{0,28},{1,29},{2,30},{3,31},{4,0},{5,1},{6,2},{7,3},{8,4},{9,5},{1... | collective-permute-start | bytes 196616 | tf_op jit(solution)/shard_map/ppermute | solution.py:250
  36.4 4.0 %gather_2_1.1 = (bf16[512,1536]{1,0:T(8,128)(2,1)S(1)}, bf16[512,1536]{1,0:T(8,128)(2,1)S(1)}, bf16[512,512]{1,0:T(8,128)(2,1)S(1)}, bf16[512,512]{1,0:T(8,128)(...) custom-call(s32[26]{0:T(128)S(1)} %concatenate.21.meta_ref, ...), custom_call_target="tpu_custom_call" | custom-call | flops 939524096 | bytes 7340032 | tf_op jit(solution)/shard_map/gather_2_1/pallas_call | solution.py:188
  40.4 1.6 %relax_2.2 = (f32[32,512]{1,0:T(8,128)S(1)}, f32[32,512]{1,0:T(8,128)S(1)}, f32[64,512]{1,0:T(8,128)S(1)}) custom-call(s32[8,128]{1,0:T(8,128)S(1)} %get-tuple-element.78.flag, bf16[512,1536]{1,0:T(8,128)(2,1)S(1)} %get-tuple-element.79.w_high, bf16[512,1536]{1,0:T(8,128)(2,1)S(1)} %get-tuple-element.80.w_low, ...), custom_call_target="tpu_custom_call" | custom-call | flops 536870912 | bytes 4194304 | tf_op jit(solution)/shard_map/relax_2/pallas_call | solution.py:220
  42.7 1.5 %collective-permute-start.14 = (f32[32,512]{1,0:T(8,128)S(1)}, f32[32,512]{1,0:T(8,128)S(1)}, u32[]{:S(2)}, u32[]{:S(2)}) collective-permute-start(f32[32,512]{1,0:T(8,128)S(1)} %get-tuple-element.93), channel_id=1, source_target_pairs={{0,2},{1,3},{2,0},{3,1},{4,6},{5,7},{6,4},{7,5},{8,10},{9,11},{10,... | collective-permute-start | bytes 196616 | tf_op jit(solution)/shard_map/ppermute | solution.py:247
  44.3 0.9 collective-permute-done.12
  45.3 4.1 %collective-permute-start.16 = (f32[32,512]{1,0:T(8,128)S(1)}, f32[32,512]{1,0:T(8,128)S(1)}, u32[]{:S(2)}, u32[]{:S(2)}) collective-permute-start(f32[32,512]{1,0:T(8,128)S(1)} %broadcast_select_fusion.5.refs_2_), channel_id=1, source_target_pairs={{0,28},{1,29},{2,30},{3,31},{4,0},{5,1},{6,2},{7,3},{8,4},{9,5},{1... | collective-permute-start | bytes 196616 | tf_op jit(solution)/shard_map/ppermute | solution.py:250
  49.5 4.1 %collective-permute-start.17 = (f32[32,512]{1,0:T(8,128)S(1)}, f32[32,512]{1,0:T(8,128)S(1)}, u32[]{:S(2)}, u32[]{:S(2)}) collective-permute-start(f32[32,512]{1,0:T(8,128)S(1)} %broadcast_select_fusion.4.refs_3_), channel_id=1, source_target_pairs={{0,28},{1,29},{2,30},{3,31},{4,0},{5,1},{6,2},{7,3},{8,4},{9,5},{1... | collective-permute-start | bytes 196616 | tf_op jit(solution)/shard_map/ppermute | solution.py:250
  53.7 0.6 gather_3_2.1
  54.3 1.0 collective-permute-done.15.refs_1_
  55.4 5.0 %collective-permute-start.18 = (f32[32,512]{1,0:T(8,128)S(1)}, f32[32,512]{1,0:T(8,128)S(1)}, u32[]{:S(2)}, u32[]{:S(2)}) collective-permute-start(f32[32,512]{1,0:T(8,128)S(1)} %get-tuple-element.94.refs_1_), channel_id=1, source_target_pairs={{0,2},{1,3},{2,0},{3,1},{4,6},{5,7},{6,4},{7,5},{8,10},{9,11},{10,... | collective-permute-start | bytes 196616 | tf_op jit(solution)/shard_map/ppermute | solution.py:247
  61.1 0.9 collective-permute-done.18
  62.1 2.1 %collective-permute-done.20 = f32[32,512]{1,0:T(8,128)S(1)} collective-permute-done((f32[32,512]{1,0:T(8,128)S(1)}, f32[32,512]{1,0:T(8,128)S(1)}, u32[]{:S(2)}, u32[]{:S(2)}) %collective-permute-start.20) | collective-permute-done | bytes 65568 | tf_op jit(solution)/shard_map/ppermute | solution.py:247
  64.3 4.1 %collective-permute-start.22 = (f32[32,512]{1,0:T(8,128)S(1)}, f32[32,512]{1,0:T(8,128)S(1)}, u32[]{:S(2)}, u32[]{:S(2)}) collective-permute-start(f32[32,512]{1,0:T(8,128)S(1)} %broadcast_select_fusion.1.refs_2_.refs_8_), channel_id=1, source_target_pairs={{0,28},{1,29},{2,30},{3,31},{4,0},{5,1},{6,2},{7,3},{8,4},{9,5},{1... | collective-permute-start | bytes 196616 | tf_op jit(solution)/shard_map/ppermute | solution.py:250
  68.4 2.1 %gather_2_3.1 = (bf16[512,1536]{1,0:T(8,128)(2,1)S(1)}, bf16[512,1536]{1,0:T(8,128)(2,1)S(1)}, bf16[512,512]{1,0:T(8,128)(2,1)S(1)}, bf16[512,512]{1,0:T(8,128)(...) custom-call(s32[26]{0:T(128)S(1)} %concatenate.21.meta_ref, ...), custom_call_target="tpu_custom_call" | custom-call | flops 536870912 | bytes 4194304 | tf_op jit(solution)/shard_map/gather_2_3/pallas_call | solution.py:188
  70.6 0.9 collective-permute-done.23.refs_5_.refs_11_
  71.5 1.8 %relax_2.3 = (f32[32,512]{1,0:T(8,128)S(1)}, f32[32,512]{1,0:T(8,128)S(1)}) custom-call(s32[8,128]{1,0:T(8,128)S(1)} %get-tuple-element.96.flag, bf16[512,1536]{1,0:T(8,128)(2,1)S(1)} %get-tuple-element.97.w_high, bf16[512,1536]{1,0:T(8,128)(2,1)S(1)} %get-tuple-element.98.w_low, bf16[512,512]{1,0:T(8,128)(2,1)S(1)} %get-tuple-element.99.d_high, ...), custom_call_target="tpu_custom_call" | custom-call | flops 536870912 | bytes 4194304 | tf_op jit(solution)/shard_map/relax_2/pallas_call | solution.py:220
  73.4 1.5 %collective-permute-start.26 = (f32[32,512]{1,0:T(8,128)S(1)}, f32[32,512]{1,0:T(8,128)S(1)}, u32[]{:S(2)}, u32[]{:S(2)}) collective-permute-start(f32[32,512]{1,0:T(8,128)S(1)} %get-tuple-element.113), channel_id=1, source_target_pairs={{0,2},{1,3},{2,0},{3,1},{4,6},{5,7},{6,4},{7,5},{8,10},{9,11},{10,... | collective-permute-start | bytes 196616 | tf_op jit(solution)/shard_map/ppermute | solution.py:247
  74.8 1.6 %collective-permute-done.24 = f32[32,512]{1,0:T(8,128)S(1)} collective-permute-done((f32[32,512]{1,0:T(8,128)S(1)}, f32[32,512]{1,0:T(8,128)S(1)}, u32[]{:S(2)}, u32[]{:S(2)}) %collective-permute-start.24) | collective-permute-done | bytes 65568 | tf_op jit(solution)/shard_map/ppermute | solution.py:247
  76.5 0.5 collective-permute-start.25
  77.0 3.7 %collective-permute-start.28 = (f32[32,512]{1,0:T(8,128)S(1)}, f32[32,512]{1,0:T(8,128)S(1)}, u32[]{:S(2)}, u32[]{:S(2)}) collective-permute-start(f32[32,512]{1,0:T(8,128)S(1)} %broadcast_select_fusion.3.refs_2_), channel_id=1, source_target_pairs={{0,28},{1,29},{2,30},{3,31},{4,0},{5,1},{6,2},{7,3},{8,4},{9,5},{1... | collective-permute-start | bytes 196616 | tf_op jit(solution)/shard_map/ppermute | solution.py:250
  80.8 4.1 %collective-permute-start.29 = (f32[32,512]{1,0:T(8,128)S(1)}, f32[32,512]{1,0:T(8,128)S(1)}, u32[]{:S(2)}, u32[]{:S(2)}) collective-permute-start(f32[32,512]{1,0:T(8,128)S(1)} %broadcast_select_fusion.2.refs_3_), channel_id=1, source_target_pairs={{0,28},{1,29},{2,30},{3,31},{4,0},{5,1},{6,2},{7,3},{8,4},{9,5},{1... | collective-permute-start | bytes 196616 | tf_op jit(solution)/shard_map/ppermute | solution.py:250
  84.9 0.6 gather_1_2.1
  85.6 1.0 collective-permute-done.27.refs_1_
  86.6 3.8 %collective-permute-start.30 = (f32[32,512]{1,0:T(8,128)S(1)}, f32[32,512]{1,0:T(8,128)S(1)}, u32[]{:S(2)}, u32[]{:S(2)}) collective-permute-start(f32[32,512]{1,0:T(8,128)S(1)} %get-tuple-element.114.refs_12_), channel_id=1, source_target_pairs={{0,2},{1,3},{2,0},{3,1},{4,6},{5,7},{6,4},{7,5},{8,10},{9,11},{10,... | collective-permute-start | bytes 196616 | tf_op jit(solution)/shard_map/ppermute | solution.py:247
  90.6 1.9 %collective-permute-done.30 = f32[32,512]{1,0:T(8,128)S(1)} collective-permute-done((f32[32,512]{1,0:T(8,128)S(1)}, f32[32,512]{1,0:T(8,128)S(1)}, u32[]{:S(2)}, u32[]{:S(2)}) %collective-permute-start.30) | collective-permute-done | bytes 65568 | tf_op jit(solution)/shard_map/ppermute | solution.py:247
  92.5 4.1 %collective-permute-start.34 = (f32[32,512]{1,0:T(8,128)S(1)}, f32[32,512]{1,0:T(8,128)S(1)}, u32[]{:S(2)}, u32[]{:S(2)}) collective-permute-start(f32[32,512]{1,0:T(8,128)S(1)} %broadcast_select_fusion.7.refs_2_), channel_id=1, source_target_pairs={{0,28},{1,29},{2,30},{3,31},{4,0},{5,1},{6,2},{7,3},{8,4},{9,5},{1... | collective-permute-start | bytes 196616 | tf_op jit(solution)/shard_map/ppermute | solution.py:250
  96.8 4.1 %collective-permute-start.35 = (f32[32,512]{1,0:T(8,128)S(1)}, f32[32,512]{1,0:T(8,128)S(1)}, u32[]{:S(2)}, u32[]{:S(2)}) collective-permute-start(f32[32,512]{1,0:T(8,128)S(1)} %broadcast_select_fusion.6.refs_3_), channel_id=1, source_target_pairs={{0,28},{1,29},{2,30},{3,31},{4,0},{5,1},{6,2},{7,3},{8,4},{9,5},{1... | collective-permute-start | bytes 196616 | tf_op jit(solution)/shard_map/ppermute | solution.py:250
  100.9 4.8 %gather_0_1.1 = (bf16[512,1536]{1,0:T(8,128)(2,1)S(1)}, bf16[512,1536]{1,0:T(8,128)(2,1)S(1)}, bf16[512,512]{1,0:T(8,128)(2,1)S(1)}, bf16[512,512]{1,0:T(8,128)(...) custom-call(s32[26]{0:T(128)S(1)} %concatenate.21.meta_ref, ...), custom_call_target="tpu_custom_call" | custom-call | flops 1342177280 | bytes 10485760 | tf_op jit(solution)/shard_map/gather_0_1/pallas_call | solution.py:188
  105.8 1.6 %relax_0.1 = (f32[32,512]{1,0:T(8,128)S(1)}, f32[32,512]{1,0:T(8,128)S(1)}) custom-call(s32[8,128]{1,0:T(8,128)S(1)} %get-tuple-element.115.flag, bf16[512,1536]{1,0:T(8,128)(2,1)S(1)} %get-tuple-element.116.w_high, bf16[512,1536]{1,0:T(8,128)(2,1)S(1)} %get-tuple-element.117.w_low, bf16[512,512]{1,0:T(8,128)(2,1)S(1)} %get-tuple-element.118.d_high, ...), custom_call_target="tpu_custom_call" | custom-call | flops 536870912 | bytes 4194304 | tf_op jit(solution)/shard_map/relax_0/pallas_call | solution.py:220
  107.4 13.9 %collective-permute-start.36 = (f32[64,512]{1,0:T(8,128)S(1)}, f32[64,512]{1,0:T(8,128)S(1)}, u32[]{:S(2)}, u32[]{:S(2)}) collective-permute-start(f32[64,512]{1,0:T(8,128)S(1)} %pad_maximum_fusion.3), channel_id=1, source_target_pairs={{0,1},{1,0},{2,3},{3,2},{4,5},{5,4},{6,7},{7,6},{8,9},{9,8},{10,11... | collective-permute-start | bytes 393224 | tf_op jit(solution)/shard_map/ppermute | solution.py:247
  121.4 1.0 collective-permute-done.36.other_ref
  122.3 0.8 last.1
  (74 shorter events, 2.3 us)
Async XLA Ops:
  0.0 20.4 %copy-start.1 = (s32[1,6]{1,0:T(1,128)S(1)}, s32[1,6]{1,0:T(1,128)}, u32[]{:S(2)}) copy-start(s32[1,6]{1,0:T(1,128)} %param.9) | copy-start | bytes 76
  0.0 6.2 %copy-start = (f32[512,512]{1,0:T(8,128)S(1)}, f32[512,512]{1,0:T(8,128)}, u32[]{:S(2)}) copy-start(f32[512,512]{1,0:T(8,128)} %own_inverse.11) | copy-start | bytes 3145732
  3.9 1.7 %collective-permute-start = (f32[72,512]{1,0:T(8,128)S(1)}, f32[72,512]{1,0:T(8,128)S(1)}, u32[]{:S(2)}, u32[]{:S(2)}) collective-permute-start(f32[72,512]{1,0:T(8,128)S(1)} %get-tuple-element.65), channel_id=1, source_target_pairs={{0,1},{1,0},{2,3},{3,2},{4,5},{5,4},{6,7},{7,6},{8,9},{9,8},{10,11... | collective-permute-start | bytes 442376 | tf_op jit(solution)/shard_map/ppermute | solution.py:247
  5.6 15.5 %collective-permute-start.4 = (f32[6,512,512]{2,1,0:T(8,128)}, f32[6,512,512]{2,1,0:T(8,128)}, u32[]{:S(2)}, u32[]{:S(2)}) collective-permute-start(f32[6,512,512]{2,1,0:T(8,128)} %bitcast.15), channel_id=1, source_target_pairs={{0,1},{1,0},{2,3},{3,2},{4,5},{5,4},{6,7},{7,6},{8,9},{9,8},{10,11... | collective-permute-start | bytes 18874376 | tf_op jit(solution)/shard_map/ppermute | solution.py:247
  6.1 5.4 %collective-permute-start.1 = (f32[72,512]{1,0:T(8,128)S(1)}, f32[72,512]{1,0:T(8,128)S(1)}, u32[]{:S(2)}, u32[]{:S(2)}) collective-permute-start(f32[72,512]{1,0:T(8,128)S(1)} %pad_maximum_fusion), channel_id=1, source_target_pairs={{0,2},{1,3},{2,0},{3,1},{4,6},{5,7},{6,4},{7,5},{8,10},{9,11},{10,... | collective-permute-start | bytes 442376 | tf_op jit(solution)/shard_map/ppermute | solution.py:247
  6.2 15.0 %collective-permute-start.5 = (f32[512,512]{1,0:T(8,128)S(1)}, f32[512,512]{1,0:T(8,128)S(1)}, u32[]{:S(2)}, u32[]{:S(2)}) collective-permute-start(f32[512,512]{1,0:T(8,128)S(1)} %copy-done), channel_id=1, source_target_pairs={{0,1},{1,0},{2,3},{3,2},{4,5},{5,4},{6,7},{7,6},{8,9},{9,8},{10,11... | collective-permute-start | bytes 3145736 | tf_op jit(solution)/shard_map/ppermute | solution.py:247
  11.6 7.4 %collective-permute-start.2 = (f32[72,512]{1,0:T(8,128)S(1)}, f32[72,512]{1,0:T(8,128)S(1)}, u32[]{:S(2)}, u32[]{:S(2)}) collective-permute-start(f32[72,512]{1,0:T(8,128)S(1)} %pad_maximum_fusion.1.refs_1_), channel_id=1, source_target_pairs={{0,4},{1,5},{2,6},{3,7},{4,8},{5,9},{6,10},{7,11},{8,12},{9,13},{1... | collective-permute-start | bytes 442376 | tf_op jit(solution)/shard_map/ppermute | solution.py:250
  13.0 7.3 %collective-permute-start.3 = (f32[72,512]{1,0:T(8,128)S(1)}, f32[72,512]{1,0:T(8,128)S(1)}, u32[]{:S(2)}, u32[]{:S(2)}) collective-permute-start(f32[72,512]{1,0:T(8,128)S(1)} %pad_maximum_fusion.1.refs_1_), channel_id=1, source_target_pairs={{0,28},{1,29},{2,30},{3,31},{4,0},{5,1},{6,2},{7,3},{8,4},{9,5},{1... | collective-permute-start | bytes 442376 | tf_op jit(solution)/shard_map/ppermute | solution.py:250
  21.8 5.3 %collective-permute-start.6 = (f32[32,512]{1,0:T(8,128)S(1)}, f32[32,512]{1,0:T(8,128)S(1)}, u32[]{:S(2)}, u32[]{:S(2)}) collective-permute-start(f32[32,512]{1,0:T(8,128)S(1)} %get-tuple-element.76.refs_3_), channel_id=1, source_target_pairs={{0,2},{1,3},{2,0},{3,1},{4,6},{5,7},{6,4},{7,5},{8,10},{9,11},{10,... | collective-permute-start | bytes 196616 | tf_op jit(solution)/shard_map/ppermute | solution.py:247
  26.1 6.0 %collective-permute-start.8 = (f32[32,512]{1,0:T(8,128)S(1)}, f32[32,512]{1,0:T(8,128)S(1)}, u32[]{:S(2)}, u32[]{:S(2)}) collective-permute-start(f32[32,512]{1,0:T(8,128)S(1)} %get-tuple-element.77), channel_id=1, source_target_pairs={{0,2},{1,3},{2,0},{3,1},{4,6},{5,7},{6,4},{7,5},{8,10},{9,11},{10,... | collective-permute-start | bytes 196616 | tf_op jit(solution)/shard_map/ppermute | solution.py:247
  27.2 13.2 %collective-permute-start.7 = (f32[32,512]{1,0:T(8,128)S(1)}, f32[32,512]{1,0:T(8,128)S(1)}, u32[]{:S(2)}, u32[]{:S(2)}) collective-permute-start(f32[32,512]{1,0:T(8,128)S(1)} %broadcast_select_fusion.9.refs_2_.refs_5_), channel_id=1, source_target_pairs={{0,4},{1,5},{2,6},{3,7},{4,8},{5,9},{6,10},{7,11},{8,12},{9,13},{1... | collective-permute-start | bytes 196616 | tf_op jit(solution)/shard_map/ppermute | solution.py:250
  27.2 13.2 %collective-permute-start.10 = (f32[32,512]{1,0:T(8,128)S(1)}, f32[32,512]{1,0:T(8,128)S(1)}, u32[]{:S(2)}, u32[]{:S(2)}) collective-permute-start(f32[32,512]{1,0:T(8,128)S(1)} %broadcast_select_fusion.9.refs_2_.refs_5_), channel_id=1, source_target_pairs={{0,28},{1,29},{2,30},{3,31},{4,0},{5,1},{6,2},{7,3},{8,4},{9,5},{1... | collective-permute-start | bytes 196616 | tf_op jit(solution)/shard_map/ppermute | solution.py:250
  32.1 8.3 %collective-permute-start.9 = (f32[32,512]{1,0:T(8,128)S(1)}, f32[32,512]{1,0:T(8,128)S(1)}, u32[]{:S(2)}, u32[]{:S(2)}) collective-permute-start(f32[32,512]{1,0:T(8,128)S(1)} %broadcast_select_fusion.8.refs_3_.refs_6_), channel_id=1, source_target_pairs={{0,4},{1,5},{2,6},{3,7},{4,8},{5,9},{6,10},{7,11},{8,12},{9,13},{1... | collective-permute-start | bytes 196616 | tf_op jit(solution)/shard_map/ppermute | solution.py:250
  32.2 8.2 %collective-permute-start.11 = (f32[32,512]{1,0:T(8,128)S(1)}, f32[32,512]{1,0:T(8,128)S(1)}, u32[]{:S(2)}, u32[]{:S(2)}) collective-permute-start(f32[32,512]{1,0:T(8,128)S(1)} %broadcast_select_fusion.8.refs_3_.refs_6_), channel_id=1, source_target_pairs={{0,28},{1,29},{2,30},{3,31},{4,0},{5,1},{6,2},{7,3},{8,4},{9,5},{1... | collective-permute-start | bytes 196616 | tf_op jit(solution)/shard_map/ppermute | solution.py:250
  42.0 3.2 %collective-permute-start.12 = (f32[32,512]{1,0:T(8,128)S(1)}, f32[32,512]{1,0:T(8,128)S(1)}, u32[]{:S(2)}, u32[]{:S(2)}) collective-permute-start(f32[32,512]{1,0:T(8,128)S(1)} %get-tuple-element.85.refs_9_), channel_id=1, source_target_pairs={{0,2},{1,3},{2,0},{3,1},{4,6},{5,7},{6,4},{7,5},{8,10},{9,11},{10,... | collective-permute-start | bytes 196616 | tf_op jit(solution)/shard_map/ppermute | solution.py:247
  42.7 6.7 %collective-permute-start.14 = (f32[32,512]{1,0:T(8,128)S(1)}, f32[32,512]{1,0:T(8,128)S(1)}, u32[]{:S(2)}, u32[]{:S(2)}) collective-permute-start(f32[32,512]{1,0:T(8,128)S(1)} %get-tuple-element.93), channel_id=1, source_target_pairs={{0,2},{1,3},{2,0},{3,1},{4,6},{5,7},{6,4},{7,5},{8,10},{9,11},{10,... | collective-permute-start | bytes 196616 | tf_op jit(solution)/shard_map/ppermute | solution.py:247
  45.2 9.1 %collective-permute-start.13 = (f32[32,512]{1,0:T(8,128)S(1)}, f32[32,512]{1,0:T(8,128)S(1)}, u32[]{:S(2)}, u32[]{:S(2)}) collective-permute-start(f32[32,512]{1,0:T(8,128)S(1)} %broadcast_select_fusion.5.refs_2_), channel_id=1, source_target_pairs={{0,4},{1,5},{2,6},{3,7},{4,8},{5,9},{6,10},{7,11},{8,12},{9,13},{1... | collective-permute-start | bytes 196616 | tf_op jit(solution)/shard_map/ppermute | solution.py:250
  45.3 10.0 %collective-permute-start.16 = (f32[32,512]{1,0:T(8,128)S(1)}, f32[32,512]{1,0:T(8,128)S(1)}, u32[]{:S(2)}, u32[]{:S(2)}) collective-permute-start(f32[32,512]{1,0:T(8,128)S(1)} %broadcast_select_fusion.5.refs_2_), channel_id=1, source_target_pairs={{0,28},{1,29},{2,30},{3,31},{4,0},{5,1},{6,2},{7,3},{8,4},{9,5},{1... | collective-permute-start | bytes 196616 | tf_op jit(solution)/shard_map/ppermute | solution.py:250
  49.5 5.9 %collective-permute-start.15 = (f32[32,512]{1,0:T(8,128)S(1)}, f32[32,512]{1,0:T(8,128)S(1)}, u32[]{:S(2)}, u32[]{:S(2)}) collective-permute-start(f32[32,512]{1,0:T(8,128)S(1)} %broadcast_select_fusion.4.refs_3_), channel_id=1, source_target_pairs={{0,4},{1,5},{2,6},{3,7},{4,8},{5,9},{6,10},{7,11},{8,12},{9,13},{1... | collective-permute-start | bytes 196616 | tf_op jit(solution)/shard_map/ppermute | solution.py:250
  49.5 5.8 %collective-permute-start.17 = (f32[32,512]{1,0:T(8,128)S(1)}, f32[32,512]{1,0:T(8,128)S(1)}, u32[]{:S(2)}, u32[]{:S(2)}) collective-permute-start(f32[32,512]{1,0:T(8,128)S(1)} %broadcast_select_fusion.4.refs_3_), channel_id=1, source_target_pairs={{0,28},{1,29},{2,30},{3,31},{4,0},{5,1},{6,2},{7,3},{8,4},{9,5},{1... | collective-permute-start | bytes 196616 | tf_op jit(solution)/shard_map/ppermute | solution.py:250
  55.4 6.6 %collective-permute-start.18 = (f32[32,512]{1,0:T(8,128)S(1)}, f32[32,512]{1,0:T(8,128)S(1)}, u32[]{:S(2)}, u32[]{:S(2)}) collective-permute-start(f32[32,512]{1,0:T(8,128)S(1)} %get-tuple-element.94.refs_1_), channel_id=1, source_target_pairs={{0,2},{1,3},{2,0},{3,1},{4,6},{5,7},{6,4},{7,5},{8,10},{9,11},{10,... | collective-permute-start | bytes 196616 | tf_op jit(solution)/shard_map/ppermute | solution.py:247
  61.0 3.2 %collective-permute-start.20 = (f32[32,512]{1,0:T(8,128)S(1)}, f32[32,512]{1,0:T(8,128)S(1)}, u32[]{:S(2)}, u32[]{:S(2)}) collective-permute-start(f32[32,512]{1,0:T(8,128)S(1)} %get-tuple-element.103), channel_id=1, source_target_pairs={{0,2},{1,3},{2,0},{3,1},{4,6},{5,7},{6,4},{7,5},{8,10},{9,11},{10,... | collective-permute-start | bytes 196616 | tf_op jit(solution)/shard_map/ppermute | solution.py:247
  62.0 8.5 %collective-permute-start.19 = (f32[32,512]{1,0:T(8,128)S(1)}, f32[32,512]{1,0:T(8,128)S(1)}, u32[]{:S(2)}, u32[]{:S(2)}) collective-permute-start(f32[32,512]{1,0:T(8,128)S(1)} %broadcast_select_fusion.1.refs_2_.refs_8_), channel_id=1, source_target_pairs={{0,4},{1,5},{2,6},{3,7},{4,8},{5,9},{6,10},{7,11},{8,12},{9,13},{1... | collective-permute-start | bytes 196616 | tf_op jit(solution)/shard_map/ppermute | solution.py:250
  64.2 6.4 %collective-permute-start.21 = (f32[32,512]{1,0:T(8,128)S(1)}, f32[32,512]{1,0:T(8,128)S(1)}, u32[]{:S(2)}, u32[]{:S(2)}) collective-permute-start(f32[32,512]{1,0:T(8,128)S(1)} %broadcast_select_fusion.refs_3_.refs_9_), channel_id=1, source_target_pairs={{0,4},{1,5},{2,6},{3,7},{4,8},{5,9},{6,10},{7,11},{8,12},{9,13},{1... | collective-permute-start | bytes 196616 | tf_op jit(solution)/shard_map/ppermute | solution.py:250
  64.3 6.3 %collective-permute-start.22 = (f32[32,512]{1,0:T(8,128)S(1)}, f32[32,512]{1,0:T(8,128)S(1)}, u32[]{:S(2)}, u32[]{:S(2)}) collective-permute-start(f32[32,512]{1,0:T(8,128)S(1)} %broadcast_select_fusion.1.refs_2_.refs_8_), channel_id=1, source_target_pairs={{0,28},{1,29},{2,30},{3,31},{4,0},{5,1},{6,2},{7,3},{8,4},{9,5},{1... | collective-permute-start | bytes 196616 | tf_op jit(solution)/shard_map/ppermute | solution.py:250
  68.4 3.1 %collective-permute-start.23 = (f32[32,512]{1,0:T(8,128)S(1)}, f32[32,512]{1,0:T(8,128)S(1)}, u32[]{:S(2)}, u32[]{:S(2)}) collective-permute-start(f32[32,512]{1,0:T(8,128)S(1)} %broadcast_select_fusion.refs_3_.refs_9_), channel_id=1, source_target_pairs={{0,28},{1,29},{2,30},{3,31},{4,0},{5,1},{6,2},{7,3},{8,4},{9,5},{1... | collective-permute-start | bytes 196616 | tf_op jit(solution)/shard_map/ppermute | solution.py:250
  73.3 3.2 %collective-permute-start.24 = (f32[32,512]{1,0:T(8,128)S(1)}, f32[32,512]{1,0:T(8,128)S(1)}, u32[]{:S(2)}, u32[]{:S(2)}) collective-permute-start(f32[32,512]{1,0:T(8,128)S(1)} %get-tuple-element.104.refs_7_), channel_id=1, source_target_pairs={{0,2},{1,3},{2,0},{3,1},{4,6},{5,7},{6,4},{7,5},{8,10},{9,11},{10,... | collective-permute-start | bytes 196616 | tf_op jit(solution)/shard_map/ppermute | solution.py:247
  73.4 7.3 %collective-permute-start.26 = (f32[32,512]{1,0:T(8,128)S(1)}, f32[32,512]{1,0:T(8,128)S(1)}, u32[]{:S(2)}, u32[]{:S(2)}) collective-permute-start(f32[32,512]{1,0:T(8,128)S(1)} %get-tuple-element.113), channel_id=1, source_target_pairs={{0,2},{1,3},{2,0},{3,1},{4,6},{5,7},{6,4},{7,5},{8,10},{9,11},{10,... | collective-permute-start | bytes 196616 | tf_op jit(solution)/shard_map/ppermute | solution.py:247
  76.5 9.1 %collective-permute-start.25 = (f32[32,512]{1,0:T(8,128)S(1)}, f32[32,512]{1,0:T(8,128)S(1)}, u32[]{:S(2)}, u32[]{:S(2)}) collective-permute-start(f32[32,512]{1,0:T(8,128)S(1)} %broadcast_select_fusion.3.refs_2_), channel_id=1, source_target_pairs={{0,4},{1,5},{2,6},{3,7},{4,8},{5,9},{6,10},{7,11},{8,12},{9,13},{1... | collective-permute-start | bytes 196616 | tf_op jit(solution)/shard_map/ppermute | solution.py:250
  77.0 9.6 %collective-permute-start.28 = (f32[32,512]{1,0:T(8,128)S(1)}, f32[32,512]{1,0:T(8,128)S(1)}, u32[]{:S(2)}, u32[]{:S(2)}) collective-permute-start(f32[32,512]{1,0:T(8,128)S(1)} %broadcast_select_fusion.3.refs_2_), channel_id=1, source_target_pairs={{0,28},{1,29},{2,30},{3,31},{4,0},{5,1},{6,2},{7,3},{8,4},{9,5},{1... | collective-permute-start | bytes 196616 | tf_op jit(solution)/shard_map/ppermute | solution.py:250
  80.7 5.9 %collective-permute-start.27 = (f32[32,512]{1,0:T(8,128)S(1)}, f32[32,512]{1,0:T(8,128)S(1)}, u32[]{:S(2)}, u32[]{:S(2)}) collective-permute-start(f32[32,512]{1,0:T(8,128)S(1)} %broadcast_select_fusion.2.refs_3_), channel_id=1, source_target_pairs={{0,4},{1,5},{2,6},{3,7},{4,8},{5,9},{6,10},{7,11},{8,12},{9,13},{1... | collective-permute-start | bytes 196616 | tf_op jit(solution)/shard_map/ppermute | solution.py:250
  80.8 5.8 %collective-permute-start.29 = (f32[32,512]{1,0:T(8,128)S(1)}, f32[32,512]{1,0:T(8,128)S(1)}, u32[]{:S(2)}, u32[]{:S(2)}) collective-permute-start(f32[32,512]{1,0:T(8,128)S(1)} %broadcast_select_fusion.2.refs_3_), channel_id=1, source_target_pairs={{0,28},{1,29},{2,30},{3,31},{4,0},{5,1},{6,2},{7,3},{8,4},{9,5},{1... | collective-permute-start | bytes 196616 | tf_op jit(solution)/shard_map/ppermute | solution.py:250
  86.6 5.8 %collective-permute-start.30 = (f32[32,512]{1,0:T(8,128)S(1)}, f32[32,512]{1,0:T(8,128)S(1)}, u32[]{:S(2)}, u32[]{:S(2)}) collective-permute-start(f32[32,512]{1,0:T(8,128)S(1)} %get-tuple-element.114.refs_12_), channel_id=1, source_target_pairs={{0,2},{1,3},{2,0},{3,1},{4,6},{5,7},{6,4},{7,5},{8,10},{9,11},{10,... | collective-permute-start | bytes 196616 | tf_op jit(solution)/shard_map/ppermute | solution.py:247
  90.5 6.2 %collective-permute-start.32 = (f32[32,512]{1,0:T(8,128)S(1)}, f32[32,512]{1,0:T(8,128)S(1)}, u32[]{:S(2)}, u32[]{:S(2)}) collective-permute-start(f32[32,512]{1,0:T(8,128)S(1)} %get-tuple-element.122), channel_id=1, source_target_pairs={{0,2},{1,3},{2,0},{3,1},{4,6},{5,7},{6,4},{7,5},{8,10},{9,11},{10,... | collective-permute-start | bytes 196616 | tf_op jit(solution)/shard_map/ppermute | solution.py:247
  92.5 13.3 %collective-permute-start.31 = (f32[32,512]{1,0:T(8,128)S(1)}, f32[32,512]{1,0:T(8,128)S(1)}, u32[]{:S(2)}, u32[]{:S(2)}) collective-permute-start(f32[32,512]{1,0:T(8,128)S(1)} %broadcast_select_fusion.7.refs_2_), channel_id=1, source_target_pairs={{0,4},{1,5},{2,6},{3,7},{4,8},{5,9},{6,10},{7,11},{8,12},{9,13},{1... | collective-permute-start | bytes 196616 | tf_op jit(solution)/shard_map/ppermute | solution.py:250
  92.5 13.2 %collective-permute-start.34 = (f32[32,512]{1,0:T(8,128)S(1)}, f32[32,512]{1,0:T(8,128)S(1)}, u32[]{:S(2)}, u32[]{:S(2)}) collective-permute-start(f32[32,512]{1,0:T(8,128)S(1)} %broadcast_select_fusion.7.refs_2_), channel_id=1, source_target_pairs={{0,28},{1,29},{2,30},{3,31},{4,0},{5,1},{6,2},{7,3},{8,4},{9,5},{1... | collective-permute-start | bytes 196616 | tf_op jit(solution)/shard_map/ppermute | solution.py:250
  96.7 9.0 %collective-permute-start.33 = (f32[32,512]{1,0:T(8,128)S(1)}, f32[32,512]{1,0:T(8,128)S(1)}, u32[]{:S(2)}, u32[]{:S(2)}) collective-permute-start(f32[32,512]{1,0:T(8,128)S(1)} %broadcast_select_fusion.6.refs_3_), channel_id=1, source_target_pairs={{0,4},{1,5},{2,6},{3,7},{4,8},{5,9},{6,10},{7,11},{8,12},{9,13},{1... | collective-permute-start | bytes 196616 | tf_op jit(solution)/shard_map/ppermute | solution.py:250
  96.8 9.0 %collective-permute-start.35 = (f32[32,512]{1,0:T(8,128)S(1)}, f32[32,512]{1,0:T(8,128)S(1)}, u32[]{:S(2)}, u32[]{:S(2)}) collective-permute-start(f32[32,512]{1,0:T(8,128)S(1)} %broadcast_select_fusion.6.refs_3_), channel_id=1, source_target_pairs={{0,28},{1,29},{2,30},{3,31},{4,0},{5,1},{6,2},{7,3},{8,4},{9,5},{1... | collective-permute-start | bytes 196616 | tf_op jit(solution)/shard_map/ppermute | solution.py:250
  107.4 14.9 %collective-permute-start.36 = (f32[64,512]{1,0:T(8,128)S(1)}, f32[64,512]{1,0:T(8,128)S(1)}, u32[]{:S(2)}, u32[]{:S(2)}) collective-permute-start(f32[64,512]{1,0:T(8,128)S(1)} %pad_maximum_fusion.3), channel_id=1, source_target_pairs={{0,1},{1,0},{2,3},{3,2},{4,5},{5,4},{6,7},{7,6},{8,9},{9,8},{10,11... | collective-permute-start | bytes 393224 | tf_op jit(solution)/shard_map/ppermute | solution.py:247

commit v3 on v2

--- a/solution.py
+++ b/solution.py
@@ -9,11 +9,12 @@
 
 COLOURS = 4
 SIDES = 3
-PIECES = 2
+CHIPS = 2
 EXTRA = 8
 OWN_COLOUR = 0
 SIB_COLOUR = 1
-TILE_START = 2
+PARITY = 2
+TILE_START = 3
 
 
 def dot_t(a, b):
@@ -60,8 +61,14 @@
     return [pltpu.with_memory_space_constraint(v, pltpu.VMEM) for v in values]
 
 
-def whole(pieces, half):
-    return jnp.concatenate([piece[: half // len(pieces), :] for piece in pieces], axis=0)
+def pick(gathered, parity, chip, side, half):
+    early, late = gathered
+    stride = early.shape[0] // (2 * CHIPS)
+    entry = chip + (2 * parity if side == 1 else CHIPS * (side // 2))
+    rows = pl.ds(pl.multiple_of(entry * stride, 8), half)
+    if side == 1:
+        return early[rows, :]
+    return jnp.where((parity == 0) == (side == 2), early[rows, :], late[rows, :])
 
 
 def first_kernel(facts_ref, inverse_hbm, residual_hbm, keep_ref, send_ref, inverse_ref, residual_ref, sems):
@@ -93,8 +100,12 @@
     out_ref[...] = jnp.transpose(jnp.concatenate([first, second], axis=0))
 
 
+def ids(tiles, side, colour):
+    return TILE_START + 2 * tiles + side * COLOURS + colour
+
+
 def tile_of(meta_ref, own, tiles, colour, side):
-    wanted = meta_ref[TILE_START + 2 * tiles + side * COLOURS + colour]
+    wanted = meta_ref[ids(tiles, side, colour)]
     start = jnp.where(own, TILE_START, TILE_START + tiles)
     found = jnp.int32(-1)
     for k in range(tiles):
@@ -102,11 +113,8 @@
     return found
 
 
-def gather_kernel(now, newest, older, counts, has_base, n_after, meta_ref, own_tiles, sib_tiles, own_inverse, sib_inverse, own_start, sib_start, *refs):
-    known = []
-    for count in counts:
-        known += [refs[side * count : (side + 1) * count] for side in range(SIDES)]
-        refs = refs[SIDES * count :]
+def gather_kernel(now, newest, older, has_base, n_after, meta_ref, own_tiles, sib_tiles, own_inverse, sib_inverse, own_start, sib_start, *refs):
+    known, refs = refs[: 2 * len(older)], refs[2 * len(older) :]
     base, refs = refs[:has_base], refs[has_base:]
     w_high, w_low, d_high, d_low, partial, begin, flag, buffer, sems = refs[n_after:]
     tiles, block = own_tiles.shape[0], own_tiles.shape[1]
@@ -114,7 +122,13 @@
     own = meta_ref[OWN_COLOUR] == now
     active = own | (meta_ref[SIB_COLOUR] == now)
     slots = [(newest, side) for side in range(SIDES)] + [(c, side) for c in older for side in range(SIDES)]
-    flag[...] = jnp.broadcast_to(active.astype(jnp.int32), flag.shape)
+    parity = meta_ref[PARITY]
+    chips = [[(meta_ref[ids(tiles, side, c)] >> 1) & 1 for side in range(SIDES)] for c in range(COLOURS)]
+    row = lax.broadcasted_iota(jnp.int32, flag.shape, 0)
+    marks = jnp.zeros(flag.shape, jnp.int32)
+    for i, mark in enumerate([active.astype(jnp.int32), parity, *chips[newest]]):
+        marks = jnp.where(row == i, mark, marks)
+    flag[...] = marks
 
     @pl.when(active)
     def _():
@@ -151,7 +165,9 @@
                     w_high[:, span] = high
                     w_low[:, span] = low
                 else:
-                    partial[...] += times(whole(known[slot - SIDES], half), high, low)
+                    at = (slot - SIDES) // SIDES * 2
+                    c, side = slots[slot]
+                    partial[...] += times(pick(known[at : at + 2], parity, chips[c][side], side, half), high, low)
 
             if slot < SIDES:
                 @pl.when(k < 0)
@@ -160,33 +176,27 @@
                     w_low[:, span] = jnp.zeros((block, block), jnp.bfloat16)
 
 
-def relax_kernel(count, flag, w_high, w_low, d_high, d_low, partial, begin, *refs):
-    latest, outs = refs[: SIDES * count], refs[SIDES * count :]
+def relax_kernel(flag, w_high, w_low, d_high, d_low, partial, begin, early, late, out, *total):
     half = begin.shape[0]
-    width = outs[0].shape[0]
 
     @pl.when(flag[0, 0] != 0)
     def _():
-        sides = [whole(latest[side * count : (side + 1) * count], half) for side in range(SIDES)]
-        value = jnp.concatenate(sides, axis=1)
-        coupled = partial[...] + times(value, w_high[...], w_low[...])
-        for ref in outs[PIECES:]:
+        sides = [pick((early, late), flag[1, 0], flag[2 + side, 0], side, half) for side in range(SIDES)]
+        coupled = partial[...] + times(jnp.concatenate(sides, axis=1), w_high[...], w_low[...])
+        for ref in total:
             ref[...] = coupled
-        result = begin[...] - times(coupled, d_high[...], d_low[...])
-        for piece in range(PIECES):
-            outs[piece][...] = result[piece * width : (piece + 1) * width]
+        out[...] = begin[...] - times(coupled, d_high[...], d_low[...])
 
 
 def gather(now, newest, older, meta, matrices, starts, known, base, after):
     tiles, block, _ = matrices[0].shape
     half = starts[0].shape[0]
     slots = SIDES * (1 + len(older)) + 1
-    operands = [piece[side] for c in older for side in range(SIDES) for piece in known[c]]
+    operands = [value for c in older for value in known[c]]
     operands = near([*starts, *operands, *base])
-    counts = [len(known[c]) for c in older]
     bf16 = jnp.bfloat16
     return pl.pallas_call(
-        functools.partial(gather_kernel, now, newest, older, counts, len(base), len(after)),
+        functools.partial(gather_kernel, now, newest, older, len(base), len(after)),
         out_shape=[
             pltpu.VMEM((block, SIDES * block), bf16),
             pltpu.VMEM((block, SIDES * block), bf16),
@@ -213,12 +223,10 @@
 def relax(now, gathered, latest, keep_sum):
     *weights, partial, begin, flag = gathered
     half, block = begin.shape
-    operands = [piece[side] for side in range(SIDES) for piece in latest]
-    operands = near([flag, *weights, partial, begin, *operands])
-    out_shape = [pltpu.VMEM((half // PIECES, block), jnp.float32)] * PIECES
-    out_shape += [pltpu.VMEM((half, block), jnp.float32)] * keep_sum
+    operands = near([flag, *weights, partial, begin, *latest])
+    out_shape = [pltpu.VMEM((half, block), jnp.float32)] * (1 + keep_sum)
     return pl.pallas_call(
-        functools.partial(relax_kernel, len(latest)),
+        relax_kernel,
         out_shape=out_shape,
         in_specs=[vmem()] * len(operands),
         out_specs=[vmem()] * len(out_shape),
@@ -246,15 +254,15 @@
     def flip(value, bit):
         return lax.ppermute(value, axis, [(i, i ^ bit) for i in range(count)])
 
-    def shift(value, by):
-        return lax.ppermute(value, axis, [(i, (i + by) % count) for i in range(count)])
-
-    def across(candidates, here_now):
-        swapped = [flip(c, 2) for c in candidates]
-        return [jnp.where(here_now, c, s) for c, s in zip(candidates, swapped)], swapped
-
-    def around(here):
-        return [[shift(h, COLOURS), h, shift(h, -COLOURS)] for h in here]
+    def spread(value):
+        gathers = []
+        for offset in range(2):
+            sets = []
+            for start in range(offset, groups + offset, 2):
+                for one in range(COLOURS // CHIPS):
+                    sets.append([(start * COLOURS + one + (COLOURS // CHIPS) * i) % count for i in range(2 * CHIPS)])
+            gathers.append(lax.all_gather(value, axis, axis_index_groups=sets, tiled=True))
+        return gathers
 
     facts = jnp.concatenate([core, colour, tile_cols[0]])
     keep, send = pl.pallas_call(
@@ -285,13 +293,18 @@
     sib_wide = arrived[half : half + 1]
     places = jnp.where(wheel == own_colour, place, 0) + jnp.where(wheel.astype(jnp.float32) == sib_wide, place ^ 1, 0)
     places = places.astype(jnp.float32)
-    here, swapped = across([jnp.concatenate([candidate, places])], (own_colour == 0) | (sib_colour == 0))
-    known = {0: around([jnp.concatenate([here[0][:half], places + swapped[0][half:]])])}
+    known = {0: spread(jnp.concatenate([candidate, places]))}
+    parity = group % 2
     blocks = []
+    tables = [g.reshape(2, CHIPS, half + EXTRA, block)[:, :, half : half + COLOURS, 0].sum(1).astype(jnp.int32) for g in known[0]]
+    found = [
+        jnp.where(parity == 0, tables[1][0], tables[0][0]),
+        jnp.where(parity == 0, tables[0][0], tables[0][1]),
+        jnp.where(parity == 0, tables[0][1], tables[1][1]),
+    ]
     for side in range(SIDES):
-        found = known[0][0][side][half : half + COLOURS, 0].astype(jnp.int32)
-        blocks.append((((group + side - 1) % groups) * COLOURS + found).astype(jnp.int32))
-    meta = jnp.concatenate([colour, sib_facts[:1], tile_cols[0], sib_facts[1:]] + blocks)
+        blocks.append((((group + side - 1) % groups) * COLOURS + found[side]).astype(jnp.int32))
+    meta = jnp.concatenate([colour, sib_facts[:1], parity.reshape(1), tile_cols[0], sib_facts[1:]] + blocks)
 
     order = list(range(1, COLOURS)) + list(range(COLOURS - 2, -1, -1))
     newest = 0
@@ -303,17 +316,16 @@
         gathered = gather(now, newest, older, meta, matrices, starts, known, sums.get(now, []), after)
         used[now] = {(c, done_at(order, c, step)) for c in known if c != now}
         outs = relax(now, gathered, known[newest], int(now in order[step + 1 :]))
-        candidates, sums[now] = outs[:PIECES], outs[PIECES:]
-        finals[now], after, newest = candidates, candidates[:1], now
+        finals[now], sums[now] = outs[0], outs[1:]
+        after, newest = [outs[0]], now
         if step < len(order) - 1:
-            here, _ = across(candidates, (own_colour == now) | (sib_colour == now))
-            known[now] = around(here)
+            known[now] = spread(outs[0])
 
     own_final, sib_final = finals[0], finals[0]
     for c in range(1, COLOURS):
-        own_final = [jnp.where(own_colour == c, a, b) for a, b in zip(finals[c], own_final)]
-        sib_final = [jnp.where(sib_colour == c, a, b) for a, b in zip(finals[c], sib_final)]
-    mine, other = jnp.concatenate(own_final), flip(jnp.concatenate(sib_final), 1)
+        own_final = jnp.where(own_colour == c, finals[c], own_final)
+        sib_final = jnp.where(sib_colour == c, finals[c], sib_final)
+    mine, other = own_final, flip(sib_final, 1)
     return pl.pallas_call(
         last_kernel,
         out_shape=jax.ShapeDtypeStruct((block, cols), jnp.float32),

time: 123 us -> 213 us (1.73)
  the two profiles are of different devices: /device:TPU:3 before, /device:TPU:0 now
where the time goes in v3:
time: 213 us
  blocking collectives  183 us (86%)
  Pallas kernels  20.9 us (10%)
  between operations  2.74 us (1%)
  waiting for transfers between devices  2.35 us (1%)
    all_gather x12, blocking collectives, spread(): lax.all_gather(value, axis, axis_index_groups=sets, tiled=True)  183 us
    pallas_call x6, Pallas kernels, gather(): pl.pallas_call(functools.partial(gather_kernel, now, newest, older, len(b...  12.8 us
    pallas_call x6, Pallas kernels, relax(): pl.pallas_call(relax_kernel, out_shape=out_shape, in_specs=[vmem()] * len...  4.91 us
  transfers between devices with their start and end apart: 4, of which 2 were waited for; matrix products, arithmetic and copies ran while one was open for 1% of the time, Pallas kernels for 0%

profile of v3, /device:TPU:0, one launch (start us, length us, event | category | flops | bytes accessed | tf_op | source)
XLA Modules:
  0.0 212.5 jit_solution(6926926592412690041)
XLA Ops:
  0.7 0.7 pad_add_fusion.facts_ref
  1.4 0.0 copy-start
  1.4 2.4 %first.1 = (f32[64,512]{1,0:T(8,128)S(1)}, f32[72,512]{1,0:T(8,128)S(1)}) custom-call(s32[8]{0:T(128)S(1)} %pad_add_fusion.facts_ref, f32[512,512]{1,0:T(8,128)} %own_inverse.11, f32[512,128]{1,0:T(8,128)} %residual_hbm.1), custom_call_target="tpu_custom_call" | custom-call | tf_op jit(solution)/shard_map/first/pallas_call | solution.py:268
  3.8 0.5 collective-permute-start
  4.3 1.0 collective-permute-done.sib_start
  5.3 0.4 collective-permute-start.1
  5.6 0.1 collective-permute-start.2
  5.8 0.1 add_convert_fusion
  5.9 20.4 %all_gather.36.late.refs_1_ = f32[288,512]{1,0:T(8,128)S(1)} all-gather(f32[72,512]{1,0:T(8,128)S(1)} %pad_maximum_fusion), channel_id=1, replica_groups={{4,6,8,10},{5,7,9,11},{12,14,16,18},{13,15,17,19},{20,22,24,26},{21,23,..., dimensions={0}, use_global_device_ids=true | all-gather | bytes 737280 | tf_op jit(solution)/shard_map/all_gather | solution.py:264
  26.3 0.1 slice_reduce_fusion.1
  26.4 12.2 %all_gather.37.early.refs_0_ = f32[288,512]{1,0:T(8,128)S(1)} all-gather(f32[72,512]{1,0:T(8,128)S(1)} %pad_maximum_fusion), channel_id=1, replica_groups={{0,2,4,6},{1,3,5,7},{8,10,12,14},{9,11,13,15},{16,18,20,22},{17,19,21,2..., dimensions={0}, use_global_device_ids=true | all-gather | bytes 737280 | tf_op jit(solution)/shard_map/all_gather | solution.py:264
  38.6 0.1 slice_reduce_fusion
  38.7 0.6 slice.43
  41.2 0.1 slice_reduce_fusion.2
  41.3 0.0 copy-done
  41.3 0.7 concatenate.11.meta_ref
  42.0 0.0 collective-permute-done.2.sib_inverse
  42.1 0.0 collective-permute-done.1.sib_tiles
  42.1 2.4 %gather_1_0.1 = (bf16[512,1536]{1,0:T(8,128)(2,1)S(1)}, bf16[512,1536]{1,0:T(8,128)(2,1)S(1)}, bf16[512,512]{1,0:T(8,128)(2,1)S(1)}, bf16[512,512]{1,0:T(8,128)(...) custom-call(s32[27]{0:T(128)S(1)} %concatenate.11.meta_ref, ...), custom_call_target="tpu_custom_call" | custom-call | flops 536870912 | bytes 4194304 | tf_op jit(solution)/shard_map/gather_1_0/pallas_call | solution.py:198
  44.5 1.6 relax_1.2
  46.1 10.8 %all_gather.38.early.refs_2_ = f32[256,512]{1,0:T(8,128)S(1)} all-gather(f32[64,512]{1,0:T(8,128)S(1)} %get-tuple-element.66.refs_2_), channel_id=1, replica_groups={{0,2,4,6},{1,3,5,7},{8,10,12,14},{9,11,13,15},{16,18,20,22},{17,19,21,2..., dimensions={0}, use_global_device_ids=true | all-gather | bytes 655360 | tf_op jit(solution)/shard_map/all_gather | solution.py:264
  56.9 17.7 %all_gather.39.late.refs_3_ = f32[256,512]{1,0:T(8,128)S(1)} all-gather(f32[64,512]{1,0:T(8,128)S(1)} %get-tuple-element.66.refs_2_), channel_id=1, replica_groups={{4,6,8,10},{5,7,9,11},{12,14,16,18},{13,15,17,19},{20,22,24,26},{21,23,..., dimensions={0}, use_global_device_ids=true | all-gather | bytes 655360 | tf_op jit(solution)/shard_map/all_gather | solution.py:264
  74.6 0.6 gather_2_1.1
  75.3 14.6 %all_gather.40.early = f32[256,512]{1,0:T(8,128)S(1)} all-gather(f32[64,512]{1,0:T(8,128)S(1)} %get-tuple-element.74.refs_4_), channel_id=1, replica_groups={{0,2,4,6},{1,3,5,7},{8,10,12,14},{9,11,13,15},{16,18,20,22},{17,19,21,2..., dimensions={0}, use_global_device_ids=true | all-gather | bytes 655360 | tf_op jit(solution)/shard_map/all_gather | solution.py:264
  89.9 17.7 %all_gather.41.late = f32[256,512]{1,0:T(8,128)S(1)} all-gather(f32[64,512]{1,0:T(8,128)S(1)} %get-tuple-element.74.refs_4_), channel_id=1, replica_groups={{4,6,8,10},{5,7,9,11},{12,14,16,18},{13,15,17,19},{20,22,24,26},{21,23,..., dimensions={0}, use_global_device_ids=true | all-gather | bytes 655360 | tf_op jit(solution)/shard_map/all_gather | solution.py:264
  107.6 0.6 gather_3_2.1
  108.3 15.1 %all_gather.42.early.refs_0_.refs_2_ = f32[256,512]{1,0:T(8,128)S(1)} all-gather(f32[64,512]{1,0:T(8,128)S(1)} %relax_3.1.refs_1_), channel_id=1, replica_groups={{0,2,4,6},{1,3,5,7},{8,10,12,14},{9,11,13,15},{16,18,20,22},{17,19,21,2..., dimensions={0}, use_global_device_ids=true | all-gather | bytes 655360 | tf_op jit(solution)/shard_map/all_gather | solution.py:264
  123.4 17.7 %all_gather.43.late.refs_1_.refs_3_ = f32[256,512]{1,0:T(8,128)S(1)} all-gather(f32[64,512]{1,0:T(8,128)S(1)} %relax_3.1.refs_1_), channel_id=1, replica_groups={{4,6,8,10},{5,7,9,11},{12,14,16,18},{13,15,17,19},{20,22,24,26},{21,23,..., dimensions={0}, use_global_device_ids=true | all-gather | bytes 655360 | tf_op jit(solution)/shard_map/all_gather | solution.py:264
  141.2 0.6 gather_2_3.1
  141.8 12.8 %all_gather.44.early.refs_0_ = f32[256,512]{1,0:T(8,128)S(1)} all-gather(f32[64,512]{1,0:T(8,128)S(1)} %relax_2.3.refs_3_), channel_id=1, replica_groups={{0,2,4,6},{1,3,5,7},{8,10,12,14},{9,11,13,15},{16,18,20,22},{17,19,21,2..., dimensions={0}, use_global_device_ids=true | all-gather | bytes 655360 | tf_op jit(solution)/shard_map/all_gather | solution.py:264
  154.6 17.8 %all_gather.45.late.refs_1_ = f32[256,512]{1,0:T(8,128)S(1)} all-gather(f32[64,512]{1,0:T(8,128)S(1)} %relax_2.3.refs_3_), channel_id=1, replica_groups={{4,6,8,10},{5,7,9,11},{12,14,16,18},{13,15,17,19},{20,22,24,26},{21,23,..., dimensions={0}, use_global_device_ids=true | all-gather | bytes 655360 | tf_op jit(solution)/shard_map/all_gather | solution.py:264
  172.5 3.9 %gather_1_2.1 = (bf16[512,1536]{1,0:T(8,128)(2,1)S(1)}, bf16[512,1536]{1,0:T(8,128)(2,1)S(1)}, bf16[512,512]{1,0:T(8,128)(2,1)S(1)}, bf16[512,512]{1,0:T(8,128)(...) custom-call(s32[27]{0:T(128)S(1)} %concatenate.11.meta_ref, ...), custom_call_target="tpu_custom_call" | custom-call | flops 939524096 | bytes 7340032 | tf_op jit(solution)/shard_map/gather_1_2/pallas_call | solution.py:198
  176.3 1.6 relax_1.3.refs_4_
  177.9 8.5 %all_gather.46.early = f32[256,512]{1,0:T(8,128)S(1)} all-gather(f32[64,512]{1,0:T(8,128)S(1)} %relax_1.3.refs_4_), channel_id=1, replica_groups={{0,2,4,6},{1,3,5,7},{8,10,12,14},{9,11,13,15},{16,18,20,22},{17,19,21,2..., dimensions={0}, use_global_device_ids=true | all-gather | bytes 655360 | tf_op jit(solution)/shard_map/all_gather | solution.py:264
  186.5 17.5 %all_gather.47.late = f32[256,512]{1,0:T(8,128)S(1)} all-gather(f32[64,512]{1,0:T(8,128)S(1)} %relax_1.3.refs_4_), channel_id=1, replica_groups={{4,6,8,10},{5,7,9,11},{12,14,16,18},{13,15,17,19},{20,22,24,26},{21,23,..., dimensions={0}, use_global_device_ids=true | all-gather | bytes 655360 | tf_op jit(solution)/shard_map/all_gather | solution.py:264
  204.0 4.6 %gather_0_1.1 = (bf16[512,1536]{1,0:T(8,128)(2,1)S(1)}, bf16[512,1536]{1,0:T(8,128)(2,1)S(1)}, bf16[512,512]{1,0:T(8,128)(2,1)S(1)}, bf16[512,512]{1,0:T(8,128)(...) custom-call(s32[27]{0:T(128)S(1)} %concatenate.11.meta_ref, ...), custom_call_target="tpu_custom_call" | custom-call | flops 1342177280 | bytes 10485760 | tf_op jit(solution)/shard_map/gather_0_1/pallas_call | solution.py:198
  208.6 1.6 relax_0.1
  210.3 0.1 collective-permute-start.3
  210.4 1.3 collective-permute-done.3.other_ref
  211.7 0.8 last.1
  (12 shorter events, 0.2 us)
Async XLA Ops:
  1.4 39.9 %copy-start = (s32[1,6]{1,0:T(1,128)S(1)}, s32[1,6]{1,0:T(1,128)}, u32[]{:S(2)}) copy-start(s32[1,6]{1,0:T(1,128)} %param.9) | copy-start | bytes 76
  3.8 1.5 collective-permute-start
  5.3 36.8 %collective-permute-start.1 = (f32[6,512,512]{2,1,0:T(8,128)}, f32[6,512,512]{2,1,0:T(8,128)}, u32[]{:S(2)}, u32[]{:S(2)}) collective-permute-start(f32[6,512,512]{2,1,0:T(8,128)} %bitcast.25), channel_id=1, source_target_pairs={{0,1},{1,0},{2,3},{3,2},{4,5},{5,4},{6,7},{7,6},{8,9},{9,8},{10,11... | collective-permute-start | bytes 18874376 | tf_op jit(solution)/shard_map/ppermute | solution.py:255
  5.6 36.4 %collective-permute-start.2 = (f32[512,512]{1,0:T(8,128)}, f32[512,512]{1,0:T(8,128)S(1)}, u32[]{:S(2)}, u32[]{:S(2)}) collective-permute-start(f32[512,512]{1,0:T(8,128)} %own_inverse.11), channel_id=1, source_target_pairs={{0,1},{1,0},{2,3},{3,2},{4,5},{5,4},{6,7},{7,6},{8,9},{9,8},{10,11... | collective-permute-start | bytes 3145736 | tf_op jit(solution)/shard_map/ppermute | solution.py:255
  210.3 1.4 collective-permute-start.3

commit v4 on v2

v4 whole, which is shorter than its diff:
```python
import functools

import jax
import jax.numpy as jnp
from jax import lax
from jax.experimental import pallas as pl
from jax.experimental.pallas import tpu as pltpu
from jax.sharding import PartitionSpec as P

COLOURS = 4
SIDES = 3
ORDER = (0, 2, 1)
PIECES = 2
EXTRA = 8
OWN_COLOUR = 0
SIB_COLOUR = 1
TILE_START = 2


def dot_t(a, b):
    return lax.dot_general(a, b, (((1,), (1,)), ((), ())), preferred_element_type=jnp.float32)


def split(value):
    high = value.astype(jnp.bfloat16)
    return high, (value - high.astype(jnp.float32)).astype(jnp.bfloat16)


def times(value, high, low):
    rows = value.shape[0]
    parts = jnp.concatenate(split(value), axis=0)
    product = dot_t(parts, high) + dot_t(parts, low)
    return product[:rows] + product[rows:]


def vmem():
    return pl.BlockSpec(memory_space=pltpu.VMEM)


def smem():
    return pl.BlockSpec(memory_space=pltpu.SMEM)


def anywhere():
    return pl.BlockSpec(memory_space=pl.ANY)


def hbm():
    return pl.BlockSpec(memory_space=pltpu.HBM)


def params(mebibytes):
    return pltpu.CompilerParams(vmem_limit_bytes=mebibytes * 1024 * 1024)


def far(values):
    return [pltpu.with_memory_space_constraint(v, pltpu.HBM) for v in values]


def near(values):
    return [pltpu.with_memory_space_constraint(v, pltpu.VMEM) for v in values]


def whole(pieces, half):
    return jnp.concatenate([piece[: half // len(pieces), :] for piece in pieces], axis=0)


def first_kernel(facts_ref, inverse_hbm, residual_hbm, keep_ref, send_ref, facts_out, inverse_ref, residual_ref, sems):
    copies = [
        pltpu.make_async_copy(residual_hbm, residual_ref, sems.at[0]),
        pltpu.make_async_copy(inverse_hbm, inverse_ref, sems.at[1]),
    ]
    for copy in copies:
        copy.start()
    for copy in copies:
        copy.wait()
    value = times(jnp.transpose(residual_ref[...]), *split(inverse_ref[...]))
    half, block = keep_ref.shape
    is_first = facts_ref[0] == 0
    keep_ref[...] = jnp.where(is_first, value[:half], value[half:])
    send_ref[:half, :] = jnp.where(is_first, value[half:], value[:half])
    row = lax.broadcasted_iota(jnp.int32, (EXTRA, block), 0)
    rows = jnp.zeros((EXTRA, block), jnp.int32)
    for i in range(1, facts_ref.shape[0]):
        rows = jnp.where(row == i - 1, facts_ref[i], rows)
    send_ref[half:, :] = rows.astype(jnp.float32)
    facts_out[...] = rows.astype(jnp.float32)


def last_kernel(core_ref, mine_ref, other_ref, out_ref):
    is_first = core_ref[0] == 0
    mine, other = mine_ref[...], other_ref[...]
    first = jnp.where(is_first, mine, other)
    second = jnp.where(is_first, other, mine)
    out_ref[...] = jnp.transpose(jnp.concatenate([first, second], axis=0))


def tile_of(meta_ref, own, tiles, colour, side):
    wanted = meta_ref[TILE_START + 2 * tiles + side * COLOURS + colour]
    start = jnp.where(own, TILE_START, TILE_START + tiles)
    found = jnp.int32(-1)
    for k in range(tiles):
        found = jnp.where(meta_ref[start + k] == wanted, k, found)
    return found


def mover(own, own_src, sib_src, dst, sem):
    def move(act):
        for is_own, src in ((own, own_src), (jnp.logical_not(own), sib_src)):
            @pl.when(is_own)
            def _(src=src):
                act(pltpu.make_async_copy(src, dst, sem))

    return move


def start(copy):
    copy.start()


def wait(copy):
    copy.wait()


def is_active(meta_ref, now):
    return (meta_ref[OWN_COLOUR] == now) | (meta_ref[SIB_COLOUR] == now)


def fetch_kernel(now, before, newest, n_after, meta_ref, own_tiles, sib_tiles, own_inverse, sib_inverse, own_start, sib_start, *refs):
    w_high, w_low, d_high, d_low, begin, mask, mask_before, buffer, sems = refs[n_after:]
    tiles, block = own_tiles.shape[0], own_tiles.shape[1]
    half = begin.shape[0]
    own = meta_ref[OWN_COLOUR] == now
    active = is_active(meta_ref, now)
    mask[...] = jnp.broadcast_to(active.astype(jnp.int32), mask.shape)
    mask_before[...] = jnp.broadcast_to(is_active(meta_ref, before).astype(jnp.int32), mask.shape)

    @pl.when(active)
    def _():
        which = [tile_of(meta_ref, own, tiles, newest, side) for side in ORDER]
        moves = [mover(own, own_tiles.at[k], sib_tiles.at[k], buffer.at[i], sems.at[i]) for i, k in enumerate(which)]
        moves.append(mover(own, own_inverse, sib_inverse, buffer.at[SIDES], sems.at[SIDES]))
        moves[-1](start)
        for k, move in zip(which, moves):
            @pl.when(k >= 0)
            def _():
                move(start)

        begin[...] = jnp.where(own, own_start[...], sib_start[:half, :])
        moves[-1](wait)
        d_high[...], d_low[...] = split(buffer[SIDES])
        for i, k in enumerate(which):
            span = pl.ds(i * block, block)

            @pl.when(k >= 0)
            def _():
                moves[i](wait)
                w_high[:, span], w_low[:, span] = split(buffer[i])

            @pl.when(k < 0)
            def _():
                w_high[:, span] = jnp.zeros((block, block), jnp.bfloat16)
                w_low[:, span] = jnp.zeros((block, block), jnp.bfloat16)


def older_kernel(now, older, counts, has_base, meta_ref, own_tiles, sib_tiles, w_high, w_low, *refs):
    *refs, partial, buffer, sems = refs
    here, refs = refs[: counts[0]], refs[counts[0] :]
    known = []
    for count in counts[1:]:
        known += [refs[side * count : (side + 1) * count] for side in range(SIDES)]
        refs = refs[SIDES * count :]
    tiles, block = own_tiles.shape[0], own_tiles.shape[1]
    half = partial.shape[0]
    own = meta_ref[OWN_COLOUR] == now

    @pl.when(is_active(meta_ref, now))
    def _():
        which = [tile_of(meta_ref, own, tiles, c, side) for c in older for side in range(SIDES)]
        moves = [mover(own, own_tiles.at[k], sib_tiles.at[k], buffer.at[i], sems.at[i]) for i, k in enumerate(which)]
        for k, move in zip(which, moves):
            @pl.when(k >= 0)
            def _():
                move(start)

        span = pl.ds((SIDES - 1) * block, block)
        total = times(whole(here, half), w_high[:, span], w_low[:, span])
        partial[...] = refs[0][...] + total if has_base else total
        for i, k in enumerate(which):
            @pl.when(k >= 0)
            def _():
                moves[i](wait)
                partial[...] += times(whole(known[i], half), *split(buffer[i]))


def relax_kernel(count, sides, mask, w_high, w_low, d_high, d_low, begin, *refs):
    latest, refs = refs[: sides * count], refs[sides * count :]
    if sides < SIDES:
        partial, *outs = refs
    else:
        partial, outs = None, refs
    half, block = begin.shape
    width = outs[0].shape[0]

    @pl.when(mask[0, 0] != 0)
    def _():
        values = [whole(latest[side * count : (side + 1) * count], half) for side in range(sides)]
        span = pl.ds(0, sides * block)
        coupled = times(jnp.concatenate(values, axis=1), w_high[:, span], w_low[:, span])
        if partial is not None:
            coupled = partial[...] + coupled
        for ref in outs[PIECES:]:
            ref[...] = coupled
        result = begin[...] - times(coupled, d_high[...], d_low[...])
        for piece in range(PIECES):
            outs[piece][...] = result[piece * width : (piece + 1) * width]


def fetch(now, before, newest, meta, matrices, starts, after):
    tiles, block, _ = matrices[0].shape
    half = starts[0].shape[0]
    bf16 = jnp.bfloat16
    return pl.pallas_call(
        functools.partial(fetch_kernel, now, before, newest, len(after)),
        out_shape=[
            pltpu.VMEM((block, SIDES * block), bf16),
            pltpu.VMEM((block, SIDES * block), bf16),
            pltpu.VMEM((block, block), bf16),
            pltpu.VMEM((block, block), bf16),
            pltpu.VMEM((half, block), jnp.float32),
            pltpu.VMEM((EXTRA, block), jnp.int32),
            pltpu.VMEM((EXTRA, block), jnp.int32),
        ],
        in_specs=[smem()] + [hbm(), anywhere()] * 2 + [vmem()] * 2 + [anywhere()] * len(after),
        out_specs=[vmem()] * 7,
        scratch_shapes=[
            pltpu.VMEM((SIDES + 1, block, block), jnp.float32),
            pltpu.SemaphoreType.DMA((SIDES + 1,)),
        ],
        compiler_params=params(16),
        cost_estimate=pl.CostEstimate(flops=0, bytes_accessed=24 * block * block, transcendentals=0),
        name=f"fetch_{now}_{newest}",
    )(meta, *matrices, *near(starts), *after)


def add_older(now, older, meta, matrices, weights, here, known, base):
    tiles, block, _ = matrices[0].shape
    operands = [piece[side] for c in older for side in range(SIDES) for piece in known[c]]
    operands = near([*weights, *here, *operands, *base])
    counts = [len(here)] + [len(known[c]) for c in older]
    slots = max(1, SIDES * len(older))
    half = sum(piece.shape[0] for piece in here)
    return pl.pallas_call(
        functools.partial(older_kernel, now, older, counts, len(base)),
        out_shape=pltpu.VMEM((half, block), jnp.float32),
        in_specs=[smem(), hbm(), anywhere()] + [vmem()] * len(operands),
        out_specs=vmem(),
        scratch_shapes=[
            pltpu.VMEM((slots, block, block), jnp.float32),
            pltpu.SemaphoreType.DMA((slots,)),
        ],
        compiler_params=params(24),
        cost_estimate=pl.CostEstimate(
            flops=4 * block * block * 128 * slots, bytes_accessed=4 * block * block * slots, transcendentals=0
        ),
        name=f"older_{now}",
    )(meta, *matrices[:2], *operands)


def relax(now, fetched, latest, partial, keep_sum):
    *weights, begin, mask, _ = fetched
    half, block = begin.shape
    sides = ORDER[: SIDES - len(partial)]
    operands = [piece[side] for side in sides for piece in latest]
    operands = near([mask, *weights, begin, *operands, *partial])
    out_shape = [pltpu.VMEM((half // PIECES, block), jnp.float32)] * PIECES
    out_shape += [pltpu.VMEM((half, block), jnp.float32)] * keep_sum
    return pl.pallas_call(
        functools.partial(relax_kernel, len(latest), len(sides)),
        out_shape=out_shape,
        in_specs=[vmem()] * len(operands),
        out_specs=[vmem()] * len(out_shape),
        compiler_params=params(16),
        cost_estimate=pl.CostEstimate(
            flops=16 * block * block * 128, bytes_accessed=16 * block * block, transcendentals=0
        ),
        name=f"relax_{now}",
    )(*operands)


def per_device(residual, inv_diag, coupling_tiles, colour, tile_cols):
    axis = "rows"
    count = lax.axis_size(axis)
    groups = count // COLOURS
    me = lax.axis_index(axis)
    core = (me % 2).reshape(1)
    place = me % COLOURS
    group = me // COLOURS
    block, cols = residual.shape
    half = cols // 2
    tiles = jnp.transpose(coupling_tiles, (1, 0, 2))
    number = tiles.shape[0]

    def flip(value, bit):
        return lax.ppermute(value, axis, [(i, i ^ bit) for i in range(count)])

    def shift(value, by):
        return lax.ppermute(value, axis, [(i, (i + by) % count) for i in range(count)])

    def around(here):
        return [shift(here, COLOURS), here, shift(here, -COLOURS)]

    facts = jnp.concatenate([core, colour, tile_cols[0]])
    keep, send, own_rows = pl.pallas_call(
        first_kernel,
        out_shape=[pltpu.VMEM((half, block), jnp.float32)]
        + [pltpu.VMEM((half + EXTRA, block), jnp.float32), pltpu.VMEM((EXTRA, block), jnp.float32)],
        in_specs=[smem(), hbm(), hbm()],
        out_specs=[vmem()] * 3,
        scratch_shapes=[
            pltpu.VMEM((block, block), jnp.float32),
            pltpu.VMEM((block, cols), jnp.float32),
            pltpu.SemaphoreType.DMA((2,)),
        ],
        compiler_params=params(16),
        name="first",
    )(facts, *far([inv_diag, residual]))
    arrived = flip(send, 1)
    starts = [keep, arrived]
    own_colour = colour[0]
    sib_facts = arrived[half : half + 1 + number, 0].astype(jnp.int32)
    sib_colour = sib_facts[0]

    late_tiles, late_inverse, _ = lax.optimization_barrier((tiles, inv_diag, arrived))
    own_tiles, own_inverse = far([tiles, inv_diag])
    matrices = [own_tiles, flip(late_tiles, 1), own_inverse, flip(late_inverse, 1)]

    own_wide, sib_wide = own_rows[:1], arrived[half : half + 1]
    candidate = jnp.where(own_wide == 0, keep, arrived[:half])
    wheel = lax.broadcasted_iota(jnp.int32, (EXTRA, block), 0).astype(jnp.float32)
    places = jnp.where(wheel == own_wide, place, 0) + jnp.where(wheel == sib_wide, place ^ 1, 0)
    places = places.astype(jnp.float32)
    sent = jnp.concatenate([candidate, places])
    swapped = flip(sent, 2)
    here = jnp.where((own_wide == 0) | (sib_wide == 0), candidate, swapped[:half])
    known = {0: [around(jnp.concatenate([here, places + swapped[half:]]))]}
    blocks = []
    for side in range(SIDES):
        found = known[0][0][side][half : half + COLOURS, 0].astype(jnp.int32)
        blocks.append((((group + side - 1) % groups) * COLOURS + found).astype(jnp.int32))
    meta = jnp.concatenate([colour, sib_facts[:1], tile_cols[0], sib_facts[1:]] + blocks)

    order = list(range(1, COLOURS)) + list(range(COLOURS - 2, -1, -1))
    newest = 0
    sums, used, finals = {}, {}, {}
    fetched, partial = fetch(order[0], 0, 0, meta, matrices, starts, []), []
    for step, now in enumerate(order):
        used[now] = {(c, done_at(order, c, step)) for c in known if c != now}
        outs = relax(now, fetched, known[newest], partial, int(now in order[step + 1 :]))
        candidates, sums[now] = outs[:PIECES], outs[PIECES:]
        finals[now] = candidates
        if step == len(order) - 1:
            break
        after = order[step + 1]
        swapped = [flip(c, 2) for c in candidates]
        before = fetched[-2]
        fetched = fetch(after, now, now, meta, matrices, starts, candidates)
        masks = [before] * (PIECES - 1) + [fetched[-1]]
        here = [jnp.where(m[:1] != 0, c, s) for m, c, s in zip(masks, candidates, swapped)]
        fresh = used.get(after, set())
        older = tuple(c for c in sorted(known) if c not in (now, after) and (c, done_at(order, c, step)) not in fresh)
        partial = [add_older(after, older, meta, matrices, fetched[:2], here, known, sums.get(after, []))]
        known[now] = [around(h) for h in here]
        newest = now

    own_final, sib_final = finals[0], finals[0]
    for c in range(1, COLOURS):
        own_final = [jnp.where(own_colour == c, a, b) for a, b in zip(finals[c], own_final)]
        sib_final = [jnp.where(sib_colour == c, a, b) for a, b in zip(finals[c], sib_final)]
    mine, other = jnp.concatenate(own_final), flip(jnp.concatenate(sib_final), 1)
    return pl.pallas_call(
        last_kernel,
        out_shape=jax.ShapeDtypeStruct((block, cols), jnp.float32),
        in_specs=[smem(), vmem(), vmem()],
        out_specs=vmem(),
        compiler_params=params(16),
        name="last",
    )(core, *near([mine, other]))


def done_at(order, colour, step):
    return max([i for i in range(step) if order[i] == colour], default=-1)


def solution(mesh):
    in_specs = (P("rows", None), P("rows", None), P("rows", None, None), P("rows"), P("rows", None))
    out_specs = P("rows", None)
    return jax.shard_map(
        per_device, mesh=mesh, in_specs=in_specs, out_specs=out_specs, check_vma=False
    )
```

time: 123 us -> 129 us (1.049)
  the two profiles are of different devices: /device:TPU:3 before, /device:TPU:0 now
where the time goes in v4:
time: 129 us; the launch traced here: 130 us
  starting transfers between devices  68.9 us (53%)
  waiting for transfers between devices  28.5 us (22%)
  Pallas kernels  26.3 us (20%)
  between operations  3.18 us (2%)
  other arithmetic  1.73 us (1%)
  local copies, waits for them, and re-layouts  1.36 us (1%)
    ppermute x22, starting transfers between devices, shift(): lax.ppermute(value, axis, [(i, (i + by) % count) for i in range(count)])  48.1 us
    ppermute x15, starting transfers between devices, flip(): return lax.ppermute(value, axis, [(i, i ^ bit) for i in range(count)])  20.8 us
    ppermute x22, waiting for transfers between devices, shift(): lax.ppermute(value, axis, [(i, (i + by) % count) for i in range(count)])  17.2 us
    ppermute x15, waiting for transfers between devices, flip(): return lax.ppermute(value, axis, [(i, i ^ bit) for i in range(count)])  11.3 us
    pallas_call x6, Pallas kernels, fetch(): pl.pallas_call(functools.partial(fetch_kernel, now, before, newest, len(a...  9.91 us
    pallas_call x5, Pallas kernels, add_older(): pl.pallas_call(functools.partial(older_kernel, now, older, counts, len(ba...  8.86 us
    pallas_call x6, Pallas kernels, relax(): pl.pallas_call(functools.partial(relax_kernel, len(latest), len(sides)),...  4.36 us
  transfers between devices with their start and end apart: 37, of which 13 were waited for; matrix products, arithmetic and copies ran while one was open for 2% of the time, Pallas kernels for 12%

profile of v4, /device:TPU:0, one launch (start us, length us, event | category | flops | bytes accessed | tf_op | source)
XLA Modules:
  0.0 130.0 jit_solution(7727830263769248459)
XLA Ops:
  0.8 0.7 pad_add_fusion.facts_ref
  1.5 2.4 %first.1 = (f32[64,512]{1,0:T(8,128)S(1)}, f32[72,512]{1,0:T(8,128)S(1)}, f32[8,512]{1,0:T(8,128)S(1)}) custom-call(s32[8]{0:T(128)S(1)} %pad_add_fusion.facts_ref, f32[512,512]{1,0:T(8,128)} %own_inverse.11, f32[512,128]{1,0:T(8,128)} %residual_hbm.1), custom_call_target="tpu_custom_call" | custom-call | tf_op jit(solution)/shard_map/first/pallas_call | solution.py:314
  3.9 0.5 collective-permute-start
  4.4 1.0 collective-permute-done.sib_start
  5.9 2.7 %collective-permute-start.1 = (f32[72,512]{1,0:T(8,128)S(1)}, f32[72,512]{1,0:T(8,128)S(1)}, u32[]{:S(2)}, u32[]{:S(2)}) collective-permute-start(f32[72,512]{1,0:T(8,128)S(1)} %pad_maximum_fusion), channel_id=1, source_target_pairs={{0,2},{1,3},{2,0},{3,1},{4,6},{5,7},{6,4},{7,5},{8,10},{9,11},{10,... | collective-permute-start | bytes 442376 | tf_op jit(solution)/shard_map/ppermute | solution.py:305
  8.7 4.3 %collective-permute-done.1 = f32[72,512]{1,0:T(8,128)S(1)} collective-permute-done((f32[72,512]{1,0:T(8,128)S(1)}, f32[72,512]{1,0:T(8,128)S(1)}, u32[]{:S(2)}, u32[]{:S(2)}) %collective-permute-start.1) | collective-permute-done | bytes 147488 | tf_op jit(solution)/shard_map/ppermute | solution.py:305
  13.1 4.9 %collective-permute-start.3 = (f32[72,512]{1,0:T(8,128)S(1)}, f32[72,512]{1,0:T(8,128)S(1)}, u32[]{:S(2)}, u32[]{:S(2)}) collective-permute-start(f32[72,512]{1,0:T(8,128)S(1)} %pad_maximum_fusion.1.refs_2_.refs_3_), channel_id=1, source_target_pairs={{0,28},{1,29},{2,30},{3,31},{4,0},{5,1},{6,2},{7,3},{8,4},{9,5},{1... | collective-permute-start | bytes 442376 | tf_op jit(solution)/shard_map/ppermute | solution.py:308
  18.1 0.5 slice.71
  20.9 7.5 %collective-permute-done.2.refs_0_.refs_2_ = f32[72,512]{1,0:T(8,128)S(1)} collective-permute-done((f32[72,512]{1,0:T(8,128)S(1)}, f32[72,512]{1,0:T(8,128)S(1)}, u32[]{:S(2)}, u32[]{:S(2)}) %collective-permute-start.2) | collective-permute-done | bytes 147488 | tf_op jit(solution)/shard_map/ppermute | solution.py:308
  28.5 0.7 concatenate.21.meta_ref
  29.3 3.2 %fetch_1_0.1 = (bf16[512,1536]{1,0:T(8,128)(2,1)S(1)}, bf16[512,1536]{1,0:T(8,128)(2,1)S(1)}, bf16[512,512]{1,0:T(8,128)(2,1)S(1)}, bf16[512,512]{1,0:T(8,128)(2...) custom-call(s32[26]{0:T(128)S(1)} %concatenate.21.meta_ref, f32[6,512,512]{2,1,0:T(8,128)} %bitcast.13, ...), custom_call_target="tpu_custom_call" | custom-call | bytes 6291456 | tf_op jit(solution)/shard_map/fetch_1_0/pallas_call | solution.py:223
  32.5 1.6 %relax_1.2 = (f32[32,512]{1,0:T(8,128)S(1)}, f32[32,512]{1,0:T(8,128)S(1)}, f32[64,512]{1,0:T(8,128)S(1)}) custom-call(s32[8,512]{1,0:T(8,128)S(1)} %get-tuple-element.70.mask, bf16[512,1536]{1,0:T(8,128)(2,1)S(1)} %get-tuple-element.71.w_high, bf16[512,1536]{1,0:T(8,128)(2,1)S(1)} %get-tuple-element.72.w_low, ...), custom_call_target="tpu_custom_call" | custom-call | flops 536870912 | bytes 4194304 | tf_op jit(solution)/shard_map/relax_1/pallas_call | solution.py:278
  34.2 2.0 %collective-permute-start.6 = (f32[32,512]{1,0:T(8,128)S(1)}, f32[32,512]{1,0:T(8,128)S(1)}, u32[]{:S(2)}, u32[]{:S(2)}) collective-permute-start(f32[32,512]{1,0:T(8,128)S(1)} %get-tuple-element.76.refs_0_), channel_id=1, source_target_pairs={{0,2},{1,3},{2,0},{3,1},{4,6},{5,7},{6,4},{7,5},{8,10},{9,11},{10,... | collective-permute-start | bytes 196616 | tf_op jit(solution)/shard_map/ppermute | solution.py:305
  36.2 0.6 fetch_2_1.1
  36.8 1.6 %collective-permute-done.8 = f32[32,512]{1,0:T(8,128)S(1)} collective-permute-done((f32[32,512]{1,0:T(8,128)S(1)}, f32[32,512]{1,0:T(8,128)S(1)}, u32[]{:S(2)}, u32[]{:S(2)}) %collective-permute-start.8) | collective-permute-done | bytes 65568 | tf_op jit(solution)/shard_map/ppermute | solution.py:305
  38.7 1.8 %collective-permute-start.9 = (f32[32,512]{1,0:T(8,128)S(1)}, f32[32,512]{1,0:T(8,128)S(1)}, u32[]{:S(2)}, u32[]{:S(2)}) collective-permute-start(f32[32,512]{1,0:T(8,128)S(1)} %broadcast_select_fusion.8.refs_1_.refs_8_), channel_id=1, source_target_pairs={{0,4},{1,5},{2,6},{3,7},{4,8},{5,9},{6,10},{7,11},{8,12},{9,13},{1... | collective-permute-start | bytes 196616 | tf_op jit(solution)/shard_map/ppermute | solution.py:308
  40.5 3.0 %collective-permute-start.10 = (f32[32,512]{1,0:T(8,128)S(1)}, f32[32,512]{1,0:T(8,128)S(1)}, u32[]{:S(2)}, u32[]{:S(2)}) collective-permute-start(f32[32,512]{1,0:T(8,128)S(1)} %broadcast_select_fusion.9.refs_0_.refs_7_), channel_id=1, source_target_pairs={{0,28},{1,29},{2,30},{3,31},{4,0},{5,1},{6,2},{7,3},{8,4},{9,5},{1... | collective-permute-start | bytes 196616 | tf_op jit(solution)/shard_map/ppermute | solution.py:308
  43.5 0.6 older_2.2.refs_4_
  44.1 1.6 %collective-permute-done.9.refs_1_.refs_6_ = f32[32,512]{1,0:T(8,128)S(1)} collective-permute-done((f32[32,512]{1,0:T(8,128)S(1)}, f32[32,512]{1,0:T(8,128)S(1)}, u32[]{:S(2)}, u32[]{:S(2)}) %collective-permute-start.9) | collective-permute-done | bytes 65568 | tf_op jit(solution)/shard_map/ppermute | solution.py:308
  46.0 4.4 %collective-permute-done.7.refs_0_.refs_5_ = f32[32,512]{1,0:T(8,128)S(1)} collective-permute-done((f32[32,512]{1,0:T(8,128)S(1)}, f32[32,512]{1,0:T(8,128)S(1)}, u32[]{:S(2)}, u32[]{:S(2)}) %collective-permute-start.7) | collective-permute-done | bytes 65568 | tf_op jit(solution)/shard_map/ppermute | solution.py:308
  50.5 3.6 %collective-permute-start.14 = (f32[32,512]{1,0:T(8,128)S(1)}, f32[32,512]{1,0:T(8,128)S(1)}, u32[]{:S(2)}, u32[]{:S(2)}) collective-permute-start(f32[32,512]{1,0:T(8,128)S(1)} %get-tuple-element.86.refs_1_), channel_id=1, source_target_pairs={{0,2},{1,3},{2,0},{3,1},{4,6},{5,7},{6,4},{7,5},{8,10},{9,11},{10,... | collective-permute-start | bytes 196616 | tf_op jit(solution)/shard_map/ppermute | solution.py:305
  54.2 0.6 fetch_3_2.1
  54.9 1.5 %collective-permute-done.14 = f32[32,512]{1,0:T(8,128)S(1)} collective-permute-done((f32[32,512]{1,0:T(8,128)S(1)}, f32[32,512]{1,0:T(8,128)S(1)}, u32[]{:S(2)}, u32[]{:S(2)}) %collective-permute-start.14) | collective-permute-done | bytes 65568 | tf_op jit(solution)/shard_map/ppermute | solution.py:305
  56.5 4.7 %collective-permute-start.17 = (f32[32,512]{1,0:T(8,128)S(1)}, f32[32,512]{1,0:T(8,128)S(1)}, u32[]{:S(2)}, u32[]{:S(2)}) collective-permute-start(f32[32,512]{1,0:T(8,128)S(1)} %broadcast_select_fusion.6.refs_1_), channel_id=1, source_target_pairs={{0,28},{1,29},{2,30},{3,31},{4,0},{5,1},{6,2},{7,3},{8,4},{9,5},{1... | collective-permute-start | bytes 196616 | tf_op jit(solution)/shard_map/ppermute | solution.py:308
  61.3 4.7 %collective-permute-start.16 = (f32[32,512]{1,0:T(8,128)S(1)}, f32[32,512]{1,0:T(8,128)S(1)}, u32[]{:S(2)}, u32[]{:S(2)}) collective-permute-start(f32[32,512]{1,0:T(8,128)S(1)} %broadcast_select_fusion.7.refs_0_), channel_id=1, source_target_pairs={{0,28},{1,29},{2,30},{3,31},{4,0},{5,1},{6,2},{7,3},{8,4},{9,5},{1... | collective-permute-start | bytes 196616 | tf_op jit(solution)/shard_map/ppermute | solution.py:308
  66.0 0.6 older_3.1.refs_4_
  66.6 1.6 %collective-permute-done.13.refs_0_ = f32[32,512]{1,0:T(8,128)S(1)} collective-permute-done((f32[32,512]{1,0:T(8,128)S(1)}, f32[32,512]{1,0:T(8,128)S(1)}, u32[]{:S(2)}, u32[]{:S(2)}) %collective-permute-start.13) | collective-permute-done | bytes 65568 | tf_op jit(solution)/shard_map/ppermute | solution.py:308
  68.3 5.6 %collective-permute-start.20 = (f32[32,512]{1,0:T(8,128)S(1)}, f32[32,512]{1,0:T(8,128)S(1)}, u32[]{:S(2)}, u32[]{:S(2)}) collective-permute-start(f32[32,512]{1,0:T(8,128)S(1)} %get-tuple-element.95.refs_1_), channel_id=1, source_target_pairs={{0,2},{1,3},{2,0},{3,1},{4,6},{5,7},{6,4},{7,5},{8,10},{9,11},{10,... | collective-permute-start | bytes 196616 | tf_op jit(solution)/shard_map/ppermute | solution.py:305
  73.9 0.6 fetch_2_3.1
  74.5 1.6 %collective-permute-done.20 = f32[32,512]{1,0:T(8,128)S(1)} collective-permute-done((f32[32,512]{1,0:T(8,128)S(1)}, f32[32,512]{1,0:T(8,128)S(1)}, u32[]{:S(2)}, u32[]{:S(2)}) %collective-permute-start.20) | collective-permute-done | bytes 65568 | tf_op jit(solution)/shard_map/ppermute | solution.py:305
  76.2 4.7 %collective-permute-start.23 = (f32[32,512]{1,0:T(8,128)S(1)}, f32[32,512]{1,0:T(8,128)S(1)}, u32[]{:S(2)}, u32[]{:S(2)}) collective-permute-start(f32[32,512]{1,0:T(8,128)S(1)} %broadcast_select_fusion.4.refs_1_.refs_5_.refs_11_), channel_id=1, source_target_pairs={{0,28},{1,29},{2,30},{3,31},{4,0},{5,1},{6,2},{7,3},{8,4},{9,5},{1... | collective-permute-start | bytes 196616 | tf_op jit(solution)/shard_map/ppermute | solution.py:308
  81.0 4.7 %collective-permute-start.22 = (f32[32,512]{1,0:T(8,128)S(1)}, f32[32,512]{1,0:T(8,128)S(1)}, u32[]{:S(2)}, u32[]{:S(2)}) collective-permute-start(f32[32,512]{1,0:T(8,128)S(1)} %broadcast_select_fusion.5.refs_0_.refs_4_.refs_10_), channel_id=1, source_target_pairs={{0,28},{1,29},{2,30},{3,31},{4,0},{5,1},{6,2},{7,3},{8,4},{9,5},{1... | collective-permute-start | bytes 196616 | tf_op jit(solution)/shard_map/ppermute | solution.py:308
  85.7 0.6 older_2.3.refs_4_
  86.3 1.6 %collective-permute-done.19.refs_0_.refs_2_.refs_8_ = f32[32,512]{1,0:T(8,128)S(1)} collective-permute-done((f32[32,512]{1,0:T(8,128)S(1)}, f32[32,512]{1,0:T(8,128)S(1)}, u32[]{:S(2)}, u32[]{:S(2)}) %collective-permute-start.19) | collective-permute-done | bytes 65568 | tf_op jit(solution)/shard_map/ppermute | solution.py:308
  88.1 3.4 %collective-permute-start.26 = (f32[32,512]{1,0:T(8,128)S(1)}, f32[32,512]{1,0:T(8,128)S(1)}, u32[]{:S(2)}, u32[]{:S(2)}) collective-permute-start(f32[32,512]{1,0:T(8,128)S(1)} %get-tuple-element.105.refs_1_), channel_id=1, source_target_pairs={{0,2},{1,3},{2,0},{3,1},{4,6},{5,7},{6,4},{7,5},{8,10},{9,11},{10,... | collective-permute-start | bytes 196616 | tf_op jit(solution)/shard_map/ppermute | solution.py:305
  91.7 2.6 %fetch_1_2.1 = (bf16[512,1536]{1,0:T(8,128)(2,1)S(1)}, bf16[512,1536]{1,0:T(8,128)(2,1)S(1)}, bf16[512,512]{1,0:T(8,128)(2,1)S(1)}, bf16[512,512]{1,0:T(8,128)(2...) custom-call(s32[26]{0:T(128)S(1)} %concatenate.21.meta_ref, f32[6,512,512]{2,1,0:T(8,128)} %bitcast.20, ...), custom_call_target="tpu_custom_call" | custom-call | bytes 6291456 | tf_op jit(solution)/shard_map/fetch_1_2/pallas_call | solution.py:223
  94.4 4.7 %collective-permute-start.29 = (f32[32,512]{1,0:T(8,128)S(1)}, f32[32,512]{1,0:T(8,128)S(1)}, u32[]{:S(2)}, u32[]{:S(2)}) collective-permute-start(f32[32,512]{1,0:T(8,128)S(1)} %broadcast_select_fusion.2.refs_1_.refs_5_), channel_id=1, source_target_pairs={{0,28},{1,29},{2,30},{3,31},{4,0},{5,1},{6,2},{7,3},{8,4},{9,5},{1... | collective-permute-start | bytes 196616 | tf_op jit(solution)/shard_map/ppermute | solution.py:308
  99.2 4.7 %collective-permute-start.28 = (f32[32,512]{1,0:T(8,128)S(1)}, f32[32,512]{1,0:T(8,128)S(1)}, u32[]{:S(2)}, u32[]{:S(2)}) collective-permute-start(f32[32,512]{1,0:T(8,128)S(1)} %broadcast_select_fusion.3.refs_0_.refs_4_), channel_id=1, source_target_pairs={{0,28},{1,29},{2,30},{3,31},{4,0},{5,1},{6,2},{7,3},{8,4},{9,5},{1... | collective-permute-start | bytes 196616 | tf_op jit(solution)/shard_map/ppermute | solution.py:308
  103.9 3.1 %older_1.1.refs_4_ = f32[64,512]{1,0:T(8,128)S(1)} custom-call(s32[26]{0:T(128)S(1)} %concatenate.21.meta_ref, f32[6,512,512]{2,1,0:T(8,128)} %bitcast.21, f32[6,512,512]{2,1,0:T(8,128)} %collective-permute-done.4.sib_tiles, bf16[512,1536]{1,0:T(8,128)(2,1)S(1)} %get-tuple-element.107.w_high, bf16[512,1536]{1,0:T(8,128)(2,1)S(1)} %get-tuple-element.108.w_low, ...), custom_call_target="tpu_custom_call" | custom-call | flops 402653184 | bytes 3145728 | tf_op jit(solution)/shard_map/older_1/pallas_call | solution.py:253
  107.0 1.2 relax_1.3
  108.3 2.0 %collective-permute-start.30 = (f32[32,512]{1,0:T(8,128)S(1)}, f32[32,512]{1,0:T(8,128)S(1)}, u32[]{:S(2)}, u32[]{:S(2)}) collective-permute-start(f32[32,512]{1,0:T(8,128)S(1)} %get-tuple-element.114.refs_0_), channel_id=1, source_target_pairs={{0,2},{1,3},{2,0},{3,1},{4,6},{5,7},{6,4},{7,5},{8,10},{9,11},{10,... | collective-permute-start | bytes 196616 | tf_op jit(solution)/shard_map/ppermute | solution.py:305
  110.3 2.4 %fetch_0_1.1 = (bf16[512,1536]{1,0:T(8,128)(2,1)S(1)}, bf16[512,1536]{1,0:T(8,128)(2,1)S(1)}, bf16[512,512]{1,0:T(8,128)(2,1)S(1)}, bf16[512,512]{1,0:T(8,128)(2...) custom-call(s32[26]{0:T(128)S(1)} %concatenate.21.meta_ref, f32[6,512,512]{2,1,0:T(8,128)} %bitcast.22, ...), custom_call_target="tpu_custom_call" | custom-call | bytes 6291456 | tf_op jit(solution)/shard_map/fetch_0_1/pallas_call | solution.py:223
  112.8 4.7 %collective-permute-start.35 = (f32[32,512]{1,0:T(8,128)S(1)}, f32[32,512]{1,0:T(8,128)S(1)}, u32[]{:S(2)}, u32[]{:S(2)}) collective-permute-start(f32[32,512]{1,0:T(8,128)S(1)} %broadcast_select_fusion.refs_1_), channel_id=1, source_target_pairs={{0,28},{1,29},{2,30},{3,31},{4,0},{5,1},{6,2},{7,3},{8,4},{9,5},{1... | collective-permute-start | bytes 196616 | tf_op jit(solution)/shard_map/ppermute | solution.py:308
  117.6 4.7 %collective-permute-start.34 = (f32[32,512]{1,0:T(8,128)S(1)}, f32[32,512]{1,0:T(8,128)S(1)}, u32[]{:S(2)}, u32[]{:S(2)}) collective-permute-start(f32[32,512]{1,0:T(8,128)S(1)} %broadcast_select_fusion.1.refs_0_), channel_id=1, source_target_pairs={{0,28},{1,29},{2,30},{3,31},{4,0},{5,1},{6,2},{7,3},{8,4},{9,5},{1... | collective-permute-start | bytes 196616 | tf_op jit(solution)/shard_map/ppermute | solution.py:308
  122.3 4.1 %older_0.1.refs_4_ = f32[64,512]{1,0:T(8,128)S(1)} custom-call(s32[26]{0:T(128)S(1)} %concatenate.21.meta_ref, f32[6,512,512]{2,1,0:T(8,128)} %bitcast.23, f32[6,512,512]{2,1,0:T(8,128)} %collective-permute-done.4.sib_tiles, bf16[512,1536]{1,0:T(8,128)(2,1)S(1)} %get-tuple-element.117.w_high, bf16[512,1536]{1,0:T(8,128)(2,1)S(1)} %get-tuple-element.118.w_low, ...), custom_call_target="tpu_custom_call" | custom-call | flops 805306368 | bytes 6291456 | tf_op jit(solution)/shard_map/older_0/pallas_call | solution.py:253
  126.4 1.2 relax_0.1
  127.9 1.3 %collective-permute-done.36.other_ref = f32[64,512]{1,0:T(8,128)S(1)} collective-permute-done((f32[64,512]{1,0:T(8,128)S(1)}, f32[64,512]{1,0:T(8,128)S(1)}, u32[]{:S(2)}, u32[]{:S(2)}) %collective-permute-start.36) | collective-permute-done | bytes 131104 | tf_op jit(solution)/shard_map/ppermute | solution.py:305
  129.2 0.8 last.1
  (90 shorter events, 3.5 us)
Async XLA Ops:
  0.0 28.5 %copy-start.1 = (s32[1,6]{1,0:T(1,128)S(1)}, s32[1,6]{1,0:T(1,128)}, u32[]{:S(2)}) copy-start(s32[1,6]{1,0:T(1,128)} %param.9) | copy-start | bytes 76
  0.0 8.6 %copy-start = (f32[512,512]{1,0:T(8,128)S(1)}, f32[512,512]{1,0:T(8,128)}, u32[]{:S(2)}) copy-start(f32[512,512]{1,0:T(8,128)} %own_inverse.11) | copy-start | bytes 3145732
  3.9 1.5 %collective-permute-start = (f32[72,512]{1,0:T(8,128)S(1)}, f32[72,512]{1,0:T(8,128)S(1)}, u32[]{:S(2)}, u32[]{:S(2)}) collective-permute-start(f32[72,512]{1,0:T(8,128)S(1)} %get-tuple-element.65), channel_id=1, source_target_pairs={{0,1},{1,0},{2,3},{3,2},{4,5},{5,4},{6,7},{7,6},{8,9},{9,8},{10,11... | collective-permute-start | bytes 442376 | tf_op jit(solution)/shard_map/ppermute | solution.py:305
  5.4 23.9 %collective-permute-start.4 = (f32[6,512,512]{2,1,0:T(8,128)}, f32[6,512,512]{2,1,0:T(8,128)}, u32[]{:S(2)}, u32[]{:S(2)}) collective-permute-start(f32[6,512,512]{2,1,0:T(8,128)} %bitcast.12), channel_id=1, source_target_pairs={{0,1},{1,0},{2,3},{3,2},{4,5},{5,4},{6,7},{7,6},{8,9},{9,8},{10,11... | collective-permute-start | bytes 18874376 | tf_op jit(solution)/shard_map/ppermute | solution.py:305
  5.9 7.1 %collective-permute-start.1 = (f32[72,512]{1,0:T(8,128)S(1)}, f32[72,512]{1,0:T(8,128)S(1)}, u32[]{:S(2)}, u32[]{:S(2)}) collective-permute-start(f32[72,512]{1,0:T(8,128)S(1)} %pad_maximum_fusion), channel_id=1, source_target_pairs={{0,2},{1,3},{2,0},{3,1},{4,6},{5,7},{6,4},{7,5},{8,10},{9,11},{10,... | collective-permute-start | bytes 442376 | tf_op jit(solution)/shard_map/ppermute | solution.py:305
  8.6 20.7 %collective-permute-start.5 = (f32[512,512]{1,0:T(8,128)S(1)}, f32[512,512]{1,0:T(8,128)S(1)}, u32[]{:S(2)}, u32[]{:S(2)}) collective-permute-start(f32[512,512]{1,0:T(8,128)S(1)} %copy-done), channel_id=1, source_target_pairs={{0,1},{1,0},{2,3},{3,2},{4,5},{5,4},{6,7},{7,6},{8,9},{9,8},{10,11... | collective-permute-start | bytes 3145736 | tf_op jit(solution)/shard_map/ppermute | solution.py:305
  13.1 7.7 %collective-permute-start.3 = (f32[72,512]{1,0:T(8,128)S(1)}, f32[72,512]{1,0:T(8,128)S(1)}, u32[]{:S(2)}, u32[]{:S(2)}) collective-permute-start(f32[72,512]{1,0:T(8,128)S(1)} %pad_maximum_fusion.1.refs_2_.refs_3_), channel_id=1, source_target_pairs={{0,28},{1,29},{2,30},{3,31},{4,0},{5,1},{6,2},{7,3},{8,4},{9,5},{1... | collective-permute-start | bytes 442376 | tf_op jit(solution)/shard_map/ppermute | solution.py:308
  20.5 7.9 %collective-permute-start.2 = (f32[72,512]{1,0:T(8,128)S(1)}, f32[72,512]{1,0:T(8,128)S(1)}, u32[]{:S(2)}, u32[]{:S(2)}) collective-permute-start(f32[72,512]{1,0:T(8,128)S(1)} %pad_maximum_fusion.1.refs_2_.refs_3_), channel_id=1, source_target_pairs={{0,4},{1,5},{2,6},{3,7},{4,8},{5,9},{6,10},{7,11},{8,12},{9,13},{1... | collective-permute-start | bytes 442376 | tf_op jit(solution)/shard_map/ppermute | solution.py:308
  34.1 4.3 %collective-permute-start.8 = (f32[32,512]{1,0:T(8,128)S(1)}, f32[32,512]{1,0:T(8,128)S(1)}, u32[]{:S(2)}, u32[]{:S(2)}) collective-permute-start(f32[32,512]{1,0:T(8,128)S(1)} %get-tuple-element.77.refs_1_), channel_id=1, source_target_pairs={{0,2},{1,3},{2,0},{3,1},{4,6},{5,7},{6,4},{7,5},{8,10},{9,11},{10,... | collective-permute-start | bytes 196616 | tf_op jit(solution)/shard_map/ppermute | solution.py:305
  34.2 6.3 %collective-permute-start.6 = (f32[32,512]{1,0:T(8,128)S(1)}, f32[32,512]{1,0:T(8,128)S(1)}, u32[]{:S(2)}, u32[]{:S(2)}) collective-permute-start(f32[32,512]{1,0:T(8,128)S(1)} %get-tuple-element.76.refs_0_), channel_id=1, source_target_pairs={{0,2},{1,3},{2,0},{3,1},{4,6},{5,7},{6,4},{7,5},{8,10},{9,11},{10,... | collective-permute-start | bytes 196616 | tf_op jit(solution)/shard_map/ppermute | solution.py:305
  38.4 5.7 %collective-permute-start.11 = (f32[32,512]{1,0:T(8,128)S(1)}, f32[32,512]{1,0:T(8,128)S(1)}, u32[]{:S(2)}, u32[]{:S(2)}) collective-permute-start(f32[32,512]{1,0:T(8,128)S(1)} %broadcast_select_fusion.8.refs_1_.refs_8_), channel_id=1, source_target_pairs={{0,28},{1,29},{2,30},{3,31},{4,0},{5,1},{6,2},{7,3},{8,4},{9,5},{1... | collective-permute-start | bytes 196616 | tf_op jit(solution)/shard_map/ppermute | solution.py:308
  38.7 7.0 %collective-permute-start.9 = (f32[32,512]{1,0:T(8,128)S(1)}, f32[32,512]{1,0:T(8,128)S(1)}, u32[]{:S(2)}, u32[]{:S(2)}) collective-permute-start(f32[32,512]{1,0:T(8,128)S(1)} %broadcast_select_fusion.8.refs_1_.refs_8_), channel_id=1, source_target_pairs={{0,4},{1,5},{2,6},{3,7},{4,8},{5,9},{6,10},{7,11},{8,12},{9,13},{1... | collective-permute-start | bytes 196616 | tf_op jit(solution)/shard_map/ppermute | solution.py:308
  40.5 5.5 %collective-permute-start.10 = (f32[32,512]{1,0:T(8,128)S(1)}, f32[32,512]{1,0:T(8,128)S(1)}, u32[]{:S(2)}, u32[]{:S(2)}) collective-permute-start(f32[32,512]{1,0:T(8,128)S(1)} %broadcast_select_fusion.9.refs_0_.refs_7_), channel_id=1, source_target_pairs={{0,28},{1,29},{2,30},{3,31},{4,0},{5,1},{6,2},{7,3},{8,4},{9,5},{1... | collective-permute-start | bytes 196616 | tf_op jit(solution)/shard_map/ppermute | solution.py:308
  43.5 7.0 %collective-permute-start.7 = (f32[32,512]{1,0:T(8,128)S(1)}, f32[32,512]{1,0:T(8,128)S(1)}, u32[]{:S(2)}, u32[]{:S(2)}) collective-permute-start(f32[32,512]{1,0:T(8,128)S(1)} %broadcast_select_fusion.9.refs_0_.refs_7_), channel_id=1, source_target_pairs={{0,4},{1,5},{2,6},{3,7},{4,8},{5,9},{6,10},{7,11},{8,12},{9,13},{1... | collective-permute-start | bytes 196616 | tf_op jit(solution)/shard_map/ppermute | solution.py:308
  50.5 5.9 %collective-permute-start.14 = (f32[32,512]{1,0:T(8,128)S(1)}, f32[32,512]{1,0:T(8,128)S(1)}, u32[]{:S(2)}, u32[]{:S(2)}) collective-permute-start(f32[32,512]{1,0:T(8,128)S(1)} %get-tuple-element.86.refs_1_), channel_id=1, source_target_pairs={{0,2},{1,3},{2,0},{3,1},{4,6},{5,7},{6,4},{7,5},{8,10},{9,11},{10,... | collective-permute-start | bytes 196616 | tf_op jit(solution)/shard_map/ppermute | solution.py:305
  54.1 7.0 %collective-permute-start.12 = (f32[32,512]{1,0:T(8,128)S(1)}, f32[32,512]{1,0:T(8,128)S(1)}, u32[]{:S(2)}, u32[]{:S(2)}) collective-permute-start(f32[32,512]{1,0:T(8,128)S(1)} %get-tuple-element.85.refs_0_), channel_id=1, source_target_pairs={{0,2},{1,3},{2,0},{3,1},{4,6},{5,7},{6,4},{7,5},{8,10},{9,11},{10,... | collective-permute-start | bytes 196616 | tf_op jit(solution)/shard_map/ppermute | solution.py:305
  56.4 10.2 %collective-permute-start.15 = (f32[32,512]{1,0:T(8,128)S(1)}, f32[32,512]{1,0:T(8,128)S(1)}, u32[]{:S(2)}, u32[]{:S(2)}) collective-permute-start(f32[32,512]{1,0:T(8,128)S(1)} %broadcast_select_fusion.6.refs_1_), channel_id=1, source_target_pairs={{0,4},{1,5},{2,6},{3,7},{4,8},{5,9},{6,10},{7,11},{8,12},{9,13},{1... | collective-permute-start | bytes 196616 | tf_op jit(solution)/shard_map/ppermute | solution.py:308
  56.5 10.1 %collective-permute-start.17 = (f32[32,512]{1,0:T(8,128)S(1)}, f32[32,512]{1,0:T(8,128)S(1)}, u32[]{:S(2)}, u32[]{:S(2)}) collective-permute-start(f32[32,512]{1,0:T(8,128)S(1)} %broadcast_select_fusion.6.refs_1_), channel_id=1, source_target_pairs={{0,28},{1,29},{2,30},{3,31},{4,0},{5,1},{6,2},{7,3},{8,4},{9,5},{1... | collective-permute-start | bytes 196616 | tf_op jit(solution)/shard_map/ppermute | solution.py:308
  61.2 7.0 %collective-permute-start.13 = (f32[32,512]{1,0:T(8,128)S(1)}, f32[32,512]{1,0:T(8,128)S(1)}, u32[]{:S(2)}, u32[]{:S(2)}) collective-permute-start(f32[32,512]{1,0:T(8,128)S(1)} %broadcast_select_fusion.7.refs_0_), channel_id=1, source_target_pairs={{0,4},{1,5},{2,6},{3,7},{4,8},{5,9},{6,10},{7,11},{8,12},{9,13},{1... | collective-permute-start | bytes 196616 | tf_op jit(solution)/shard_map/ppermute | solution.py:308
  61.3 7.0 %collective-permute-start.16 = (f32[32,512]{1,0:T(8,128)S(1)}, f32[32,512]{1,0:T(8,128)S(1)}, u32[]{:S(2)}, u32[]{:S(2)}) collective-permute-start(f32[32,512]{1,0:T(8,128)S(1)} %broadcast_select_fusion.7.refs_0_), channel_id=1, source_target_pairs={{0,28},{1,29},{2,30},{3,31},{4,0},{5,1},{6,2},{7,3},{8,4},{9,5},{1... | collective-permute-start | bytes 196616 | tf_op jit(solution)/shard_map/ppermute | solution.py:308
  68.3 7.8 %collective-permute-start.20 = (f32[32,512]{1,0:T(8,128)S(1)}, f32[32,512]{1,0:T(8,128)S(1)}, u32[]{:S(2)}, u32[]{:S(2)}) collective-permute-start(f32[32,512]{1,0:T(8,128)S(1)} %get-tuple-element.95.refs_1_), channel_id=1, source_target_pairs={{0,2},{1,3},{2,0},{3,1},{4,6},{5,7},{6,4},{7,5},{8,10},{9,11},{10,... | collective-permute-start | bytes 196616 | tf_op jit(solution)/shard_map/ppermute | solution.py:305
  73.8 7.0 %collective-permute-start.18 = (f32[32,512]{1,0:T(8,128)S(1)}, f32[32,512]{1,0:T(8,128)S(1)}, u32[]{:S(2)}, u32[]{:S(2)}) collective-permute-start(f32[32,512]{1,0:T(8,128)S(1)} %get-tuple-element.94.refs_0_), channel_id=1, source_target_pairs={{0,2},{1,3},{2,0},{3,1},{4,6},{5,7},{6,4},{7,5},{8,10},{9,11},{10,... | collective-permute-start | bytes 196616 | tf_op jit(solution)/shard_map/ppermute | solution.py:305
  76.1 10.2 %collective-permute-start.21 = (f32[32,512]{1,0:T(8,128)S(1)}, f32[32,512]{1,0:T(8,128)S(1)}, u32[]{:S(2)}, u32[]{:S(2)}) collective-permute-start(f32[32,512]{1,0:T(8,128)S(1)} %broadcast_select_fusion.4.refs_1_.refs_5_.refs_11_), channel_id=1, source_target_pairs={{0,4},{1,5},{2,6},{3,7},{4,8},{5,9},{6,10},{7,11},{8,12},{9,13},{1... | collective-permute-start | bytes 196616 | tf_op jit(solution)/shard_map/ppermute | solution.py:308
  76.2 10.1 %collective-permute-start.23 = (f32[32,512]{1,0:T(8,128)S(1)}, f32[32,512]{1,0:T(8,128)S(1)}, u32[]{:S(2)}, u32[]{:S(2)}) collective-permute-start(f32[32,512]{1,0:T(8,128)S(1)} %broadcast_select_fusion.4.refs_1_.refs_5_.refs_11_), channel_id=1, source_target_pairs={{0,28},{1,29},{2,30},{3,31},{4,0},{5,1},{6,2},{7,3},{8,4},{9,5},{1... | collective-permute-start | bytes 196616 | tf_op jit(solution)/shard_map/ppermute | solution.py:308
  80.9 7.0 %collective-permute-start.19 = (f32[32,512]{1,0:T(8,128)S(1)}, f32[32,512]{1,0:T(8,128)S(1)}, u32[]{:S(2)}, u32[]{:S(2)}) collective-permute-start(f32[32,512]{1,0:T(8,128)S(1)} %broadcast_select_fusion.5.refs_0_.refs_4_.refs_10_), channel_id=1, source_target_pairs={{0,4},{1,5},{2,6},{3,7},{4,8},{5,9},{6,10},{7,11},{8,12},{9,13},{1... | collective-permute-start | bytes 196616 | tf_op jit(solution)/shard_map/ppermute | solution.py:308
  81.0 7.0 %collective-permute-start.22 = (f32[32,512]{1,0:T(8,128)S(1)}, f32[32,512]{1,0:T(8,128)S(1)}, u32[]{:S(2)}, u32[]{:S(2)}) collective-permute-start(f32[32,512]{1,0:T(8,128)S(1)} %broadcast_select_fusion.5.refs_0_.refs_4_.refs_10_), channel_id=1, source_target_pairs={{0,28},{1,29},{2,30},{3,31},{4,0},{5,1},{6,2},{7,3},{8,4},{9,5},{1... | collective-permute-start | bytes 196616 | tf_op jit(solution)/shard_map/ppermute | solution.py:308
  88.1 6.1 %collective-permute-start.26 = (f32[32,512]{1,0:T(8,128)S(1)}, f32[32,512]{1,0:T(8,128)S(1)}, u32[]{:S(2)}, u32[]{:S(2)}) collective-permute-start(f32[32,512]{1,0:T(8,128)S(1)} %get-tuple-element.105.refs_1_), channel_id=1, source_target_pairs={{0,2},{1,3},{2,0},{3,1},{4,6},{5,7},{6,4},{7,5},{8,10},{9,11},{10,... | collective-permute-start | bytes 196616 | tf_op jit(solution)/shard_map/ppermute | solution.py:305
  91.6 7.5 %collective-permute-start.24 = (f32[32,512]{1,0:T(8,128)S(1)}, f32[32,512]{1,0:T(8,128)S(1)}, u32[]{:S(2)}, u32[]{:S(2)}) collective-permute-start(f32[32,512]{1,0:T(8,128)S(1)} %get-tuple-element.104.refs_0_), channel_id=1, source_target_pairs={{0,2},{1,3},{2,0},{3,1},{4,6},{5,7},{6,4},{7,5},{8,10},{9,11},{10,... | collective-permute-start | bytes 196616 | tf_op jit(solution)/shard_map/ppermute | solution.py:305
  94.3 12.7 %collective-permute-start.27 = (f32[32,512]{1,0:T(8,128)S(1)}, f32[32,512]{1,0:T(8,128)S(1)}, u32[]{:S(2)}, u32[]{:S(2)}) collective-permute-start(f32[32,512]{1,0:T(8,128)S(1)} %broadcast_select_fusion.2.refs_1_.refs_5_), channel_id=1, source_target_pairs={{0,4},{1,5},{2,6},{3,7},{4,8},{5,9},{6,10},{7,11},{8,12},{9,13},{1... | collective-permute-start | bytes 196616 | tf_op jit(solution)/shard_map/ppermute | solution.py:308
  94.4 12.6 %collective-permute-start.29 = (f32[32,512]{1,0:T(8,128)S(1)}, f32[32,512]{1,0:T(8,128)S(1)}, u32[]{:S(2)}, u32[]{:S(2)}) collective-permute-start(f32[32,512]{1,0:T(8,128)S(1)} %broadcast_select_fusion.2.refs_1_.refs_5_), channel_id=1, source_target_pairs={{0,28},{1,29},{2,30},{3,31},{4,0},{5,1},{6,2},{7,3},{8,4},{9,5},{1... | collective-permute-start | bytes 196616 | tf_op jit(solution)/shard_map/ppermute | solution.py:308
  99.1 7.9 %collective-permute-start.25 = (f32[32,512]{1,0:T(8,128)S(1)}, f32[32,512]{1,0:T(8,128)S(1)}, u32[]{:S(2)}, u32[]{:S(2)}) collective-permute-start(f32[32,512]{1,0:T(8,128)S(1)} %broadcast_select_fusion.3.refs_0_.refs_4_), channel_id=1, source_target_pairs={{0,4},{1,5},{2,6},{3,7},{4,8},{5,9},{6,10},{7,11},{8,12},{9,13},{1... | collective-permute-start | bytes 196616 | tf_op jit(solution)/shard_map/ppermute | solution.py:308
  99.2 7.8 %collective-permute-start.28 = (f32[32,512]{1,0:T(8,128)S(1)}, f32[32,512]{1,0:T(8,128)S(1)}, u32[]{:S(2)}, u32[]{:S(2)}) collective-permute-start(f32[32,512]{1,0:T(8,128)S(1)} %broadcast_select_fusion.3.refs_0_.refs_4_), channel_id=1, source_target_pairs={{0,28},{1,29},{2,30},{3,31},{4,0},{5,1},{6,2},{7,3},{8,4},{9,5},{1... | collective-permute-start | bytes 196616 | tf_op jit(solution)/shard_map/ppermute | solution.py:308
  108.3 4.5 %collective-permute-start.32 = (f32[32,512]{1,0:T(8,128)S(1)}, f32[32,512]{1,0:T(8,128)S(1)}, u32[]{:S(2)}, u32[]{:S(2)}) collective-permute-start(f32[32,512]{1,0:T(8,128)S(1)} %get-tuple-element.115.refs_1_), channel_id=1, source_target_pairs={{0,2},{1,3},{2,0},{3,1},{4,6},{5,7},{6,4},{7,5},{8,10},{9,11},{10,... | collective-permute-start | bytes 196616 | tf_op jit(solution)/shard_map/ppermute | solution.py:305
  108.3 9.2 %collective-permute-start.30 = (f32[32,512]{1,0:T(8,128)S(1)}, f32[32,512]{1,0:T(8,128)S(1)}, u32[]{:S(2)}, u32[]{:S(2)}) collective-permute-start(f32[32,512]{1,0:T(8,128)S(1)} %get-tuple-element.114.refs_0_), channel_id=1, source_target_pairs={{0,2},{1,3},{2,0},{3,1},{4,6},{5,7},{6,4},{7,5},{8,10},{9,11},{10,... | collective-permute-start | bytes 196616 | tf_op jit(solution)/shard_map/ppermute | solution.py:305
  112.8 13.6 %collective-permute-start.33 = (f32[32,512]{1,0:T(8,128)S(1)}, f32[32,512]{1,0:T(8,128)S(1)}, u32[]{:S(2)}, u32[]{:S(2)}) collective-permute-start(f32[32,512]{1,0:T(8,128)S(1)} %broadcast_select_fusion.refs_1_), channel_id=1, source_target_pairs={{0,4},{1,5},{2,6},{3,7},{4,8},{5,9},{6,10},{7,11},{8,12},{9,13},{1... | collective-permute-start | bytes 196616 | tf_op jit(solution)/shard_map/ppermute | solution.py:308
  112.8 13.6 %collective-permute-start.35 = (f32[32,512]{1,0:T(8,128)S(1)}, f32[32,512]{1,0:T(8,128)S(1)}, u32[]{:S(2)}, u32[]{:S(2)}) collective-permute-start(f32[32,512]{1,0:T(8,128)S(1)} %broadcast_select_fusion.refs_1_), channel_id=1, source_target_pairs={{0,28},{1,29},{2,30},{3,31},{4,0},{5,1},{6,2},{7,3},{8,4},{9,5},{1... | collective-permute-start | bytes 196616 | tf_op jit(solution)/shard_map/ppermute | solution.py:308
  117.6 8.9 %collective-permute-start.31 = (f32[32,512]{1,0:T(8,128)S(1)}, f32[32,512]{1,0:T(8,128)S(1)}, u32[]{:S(2)}, u32[]{:S(2)}) collective-permute-start(f32[32,512]{1,0:T(8,128)S(1)} %broadcast_select_fusion.1.refs_0_), channel_id=1, source_target_pairs={{0,4},{1,5},{2,6},{3,7},{4,8},{5,9},{6,10},{7,11},{8,12},{9,13},{1... | collective-permute-start | bytes 196616 | tf_op jit(solution)/shard_map/ppermute | solution.py:308
  117.6 8.8 %collective-permute-start.34 = (f32[32,512]{1,0:T(8,128)S(1)}, f32[32,512]{1,0:T(8,128)S(1)}, u32[]{:S(2)}, u32[]{:S(2)}) collective-permute-start(f32[32,512]{1,0:T(8,128)S(1)} %broadcast_select_fusion.1.refs_0_), channel_id=1, source_target_pairs={{0,28},{1,29},{2,30},{3,31},{4,0},{5,1},{6,2},{7,3},{8,4},{9,5},{1... | collective-permute-start | bytes 196616 | tf_op jit(solution)/shard_map/ppermute | solution.py:308
  127.8 1.4 %collective-permute-start.36 = (f32[64,512]{1,0:T(8,128)S(1)}, f32[64,512]{1,0:T(8,128)S(1)}, u32[]{:S(2)}, u32[]{:S(2)}) collective-permute-start(f32[64,512]{1,0:T(8,128)S(1)} %pad_maximum_fusion.3), channel_id=1, source_target_pairs={{0,1},{1,0},{2,3},{3,2},{4,5},{5,4},{6,7},{7,6},{8,9},{9,8},{10,11... | collective-permute-start | bytes 393224 | tf_op jit(solution)/shard_map/ppermute | solution.py:305

commit v5 on v4

--- a/solution.py
+++ b/solution.py
@@ -9,8 +9,7 @@
 
 COLOURS = 4
 SIDES = 3
-ORDER = (0, 2, 1)
-PIECES = 2
+INNER, OUTER, HERE = range(3)
 EXTRA = 8
 OWN_COLOUR = 0
 SIB_COLOUR = 1
@@ -59,10 +58,6 @@
 
 def near(values):
     return [pltpu.with_memory_space_constraint(v, pltpu.VMEM) for v in values]
-
-
-def whole(pieces, half):
-    return jnp.concatenate([piece[: half // len(pieces), :] for piece in pieces], axis=0)
 
 
 def first_kernel(facts_ref, inverse_hbm, residual_hbm, keep_ref, send_ref, facts_out, inverse_ref, residual_ref, sems):
@@ -137,7 +132,7 @@
 
     @pl.when(active)
     def _():
-        which = [tile_of(meta_ref, own, tiles, newest, side) for side in ORDER]
+        which = [tile_of(meta_ref, own, tiles, newest, side) for side in range(SIDES)]
         moves = [mover(own, own_tiles.at[k], sib_tiles.at[k], buffer.at[i], sems.at[i]) for i, k in enumerate(which)]
         moves.append(mover(own, own_inverse, sib_inverse, buffer.at[SIDES], sems.at[SIDES]))
         moves[-1](start)
@@ -163,13 +158,9 @@
                 w_low[:, span] = jnp.zeros((block, block), jnp.bfloat16)
 
 
-def older_kernel(now, older, counts, has_base, meta_ref, own_tiles, sib_tiles, w_high, w_low, *refs):
+def older_kernel(now, older, has_base, meta_ref, own_tiles, sib_tiles, w_high, w_low, outer, here, *refs):
     *refs, partial, buffer, sems = refs
-    here, refs = refs[: counts[0]], refs[counts[0] :]
-    known = []
-    for count in counts[1:]:
-        known += [refs[side * count : (side + 1) * count] for side in range(SIDES)]
-        refs = refs[SIDES * count :]
+    known, base = refs[: SIDES * len(older)], refs[SIDES * len(older) :]
     tiles, block = own_tiles.shape[0], own_tiles.shape[1]
     half = partial.shape[0]
     own = meta_ref[OWN_COLOUR] == now
@@ -183,37 +174,40 @@
             def _():
                 move(start)
 
-        span = pl.ds((SIDES - 1) * block, block)
-        total = times(whole(here, half), w_high[:, span], w_low[:, span])
-        partial[...] = refs[0][...] + total if has_base else total
+        span = pl.ds(OUTER * block, 2 * block)
+        newest = jnp.concatenate([outer[:half, :], here[:half, :]], axis=1)
+        total = times(newest, w_high[:, span], w_low[:, span])
+        partial[...] = base[0][...] + total if has_base else total
         for i, k in enumerate(which):
             @pl.when(k >= 0)
             def _():
                 moves[i](wait)
-                partial[...] += times(whole(known[i], half), *split(buffer[i]))
-
-
-def relax_kernel(count, sides, mask, w_high, w_low, d_high, d_low, begin, *refs):
-    latest, refs = refs[: sides * count], refs[sides * count :]
+                partial[...] += times(known[i][:half, :], *split(buffer[i]))
+
+
+def relax_kernel(sides, mask, w_high, w_low, d_high, d_low, begin, *refs):
+    latest, refs = refs[:sides], refs[sides:]
     if sides < SIDES:
-        partial, *outs = refs
+        partial, out, *total = refs
     else:
-        partial, outs = None, refs
+        partial, out, *total = None, *refs
     half, block = begin.shape
-    width = outs[0].shape[0]
-
-    @pl.when(mask[0, 0] != 0)
+    active = mask[0, 0] != 0
+
+    @pl.when(active)
     def _():
-        values = [whole(latest[side * count : (side + 1) * count], half) for side in range(sides)]
         span = pl.ds(0, sides * block)
-        coupled = times(jnp.concatenate(values, axis=1), w_high[:, span], w_low[:, span])
+        values = jnp.concatenate([ref[:half, :] for ref in latest], axis=1)
+        coupled = times(values, w_high[:, span], w_low[:, span])
         if partial is not None:
             coupled = partial[...] + coupled
-        for ref in outs[PIECES:]:
+        for ref in total:
             ref[...] = coupled
-        result = begin[...] - times(coupled, d_high[...], d_low[...])
-        for piece in range(PIECES):
-            outs[piece][...] = result[piece * width : (piece + 1) * width]
+        out[...] = begin[...] - times(coupled, d_high[...], d_low[...])
+
+    @pl.when(jnp.logical_not(active))
+    def _():
+        out[...] = jnp.zeros_like(out)
 
 
 def fetch(now, before, newest, meta, matrices, starts, after):
@@ -243,15 +237,14 @@
     )(meta, *matrices, *near(starts), *after)
 
 
-def add_older(now, older, meta, matrices, weights, here, known, base):
+def add_older(now, older, meta, matrices, weights, outer, here, known, base):
     tiles, block, _ = matrices[0].shape
-    operands = [piece[side] for c in older for side in range(SIDES) for piece in known[c]]
-    operands = near([*weights, *here, *operands, *base])
-    counts = [len(here)] + [len(known[c]) for c in older]
+    operands = [value for c in older for value in known[c]]
+    operands = near([*weights, outer, here, *operands, *base])
     slots = max(1, SIDES * len(older))
-    half = sum(piece.shape[0] for piece in here)
+    half = here.shape[0]
     return pl.pallas_call(
-        functools.partial(older_kernel, now, older, counts, len(base)),
+        functools.partial(older_kernel, now, older, len(base)),
         out_shape=pltpu.VMEM((half, block), jnp.float32),
         in_specs=[smem(), hbm(), anywhere()] + [vmem()] * len(operands),
         out_specs=vmem(),
@@ -270,13 +263,11 @@
 def relax(now, fetched, latest, partial, keep_sum):
     *weights, begin, mask, _ = fetched
     half, block = begin.shape
-    sides = ORDER[: SIDES - len(partial)]
-    operands = [piece[side] for side in sides for piece in latest]
-    operands = near([mask, *weights, begin, *operands, *partial])
-    out_shape = [pltpu.VMEM((half // PIECES, block), jnp.float32)] * PIECES
-    out_shape += [pltpu.VMEM((half, block), jnp.float32)] * keep_sum
+    sides = 1 if partial else SIDES
+    operands = near([mask, *weights, begin, *latest[:sides], *partial])
+    out_shape = [pltpu.VMEM((half, block), jnp.float32)] * (1 + keep_sum)
     return pl.pallas_call(
-        functools.partial(relax_kernel, len(latest), len(sides)),
+        functools.partial(relax_kernel, sides),
         out_shape=out_shape,
         in_specs=[vmem()] * len(operands),
         out_specs=[vmem()] * len(out_shape),
@@ -304,11 +295,12 @@
     def flip(value, bit):
         return lax.ppermute(value, axis, [(i, i ^ bit) for i in range(count)])
 
-    def shift(value, by):
-        return lax.ppermute(value, axis, [(i, (i + by) % count) for i in range(count)])
-
-    def around(here):
-        return [shift(here, COLOURS), here, shift(here, -COLOURS)]
+    def beside(value, ahead):
+        pairs = []
+        for i in range(count):
+            step = COLOURS if (i // 2) % 2 == ahead else -COLOURS
+            pairs.append((i, (i + step) % count))
+        return lax.ppermute(value, axis, pairs)
 
     facts = jnp.concatenate([core, colour, tile_cols[0]])
     keep, send, own_rows = pl.pallas_call(
@@ -327,9 +319,7 @@
     )(facts, *far([inv_diag, residual]))
     arrived = flip(send, 1)
     starts = [keep, arrived]
-    own_colour = colour[0]
     sib_facts = arrived[half : half + 1 + number, 0].astype(jnp.int32)
-    sib_colour = sib_facts[0]
 
     late_tiles, late_inverse, _ = lax.optimization_barrier((tiles, inv_diag, arrived))
     own_tiles, own_inverse = far([tiles, inv_diag])
@@ -338,16 +328,20 @@
     own_wide, sib_wide = own_rows[:1], arrived[half : half + 1]
     candidate = jnp.where(own_wide == 0, keep, arrived[:half])
     wheel = lax.broadcasted_iota(jnp.int32, (EXTRA, block), 0).astype(jnp.float32)
-    places = jnp.where(wheel == own_wide, place, 0) + jnp.where(wheel == sib_wide, place ^ 1, 0)
+    places = jnp.where(wheel == own_wide, place + 1, 0) + jnp.where(wheel == sib_wide, (place ^ 1) + 1, 0)
     places = places.astype(jnp.float32)
     sent = jnp.concatenate([candidate, places])
     swapped = flip(sent, 2)
+    outer = beside(sent, 1)
     here = jnp.where((own_wide == 0) | (sib_wide == 0), candidate, swapped[:half])
-    known = {0: [around(jnp.concatenate([here, places + swapped[half:]]))]}
+    here = jnp.concatenate([here, places + swapped[half:]])
+    known = {0: [beside(here, 0), outer, here]}
+    toward = jnp.where(place < COLOURS // 2, -1, 1)
     blocks = []
-    for side in range(SIDES):
-        found = known[0][0][side][half : half + COLOURS, 0].astype(jnp.int32)
-        blocks.append((((group + side - 1) % groups) * COLOURS + found).astype(jnp.int32))
+    for value, step in zip(known[0], (toward, -toward, 0)):
+        found = value[half : half + COLOURS, 0].astype(jnp.int32)
+        first = ((group + step) % groups) * COLOURS
+        blocks.append(jnp.where(found > 0, first + found - 1, -1).astype(jnp.int32))
     meta = jnp.concatenate([colour, sib_facts[:1], tile_cols[0], sib_facts[1:]] + blocks)
 
     order = list(range(1, COLOURS)) + list(range(COLOURS - 2, -1, -1))
@@ -357,27 +351,27 @@
     for step, now in enumerate(order):
         used[now] = {(c, done_at(order, c, step)) for c in known if c != now}
         outs = relax(now, fetched, known[newest], partial, int(now in order[step + 1 :]))
-        candidates, sums[now] = outs[:PIECES], outs[PIECES:]
-        finals[now] = candidates
+        candidate, sums[now] = outs[0], outs[1:]
+        finals[now] = candidate
         if step == len(order) - 1:
             break
         after = order[step + 1]
-        swapped = [flip(c, 2) for c in candidates]
-        before = fetched[-2]
-        fetched = fetch(after, now, now, meta, matrices, starts, candidates)
-        masks = [before] * (PIECES - 1) + [fetched[-1]]
-        here = [jnp.where(m[:1] != 0, c, s) for m, c, s in zip(masks, candidates, swapped)]
+        swapped = flip(candidate, 2)
+        outer = beside(candidate, 1)
+        fetched = fetch(after, now, now, meta, matrices, starts, [candidate])
+        here = jnp.where(fetched[-1][:1] != 0, candidate, swapped)
+        inner = beside(here, 0)
         fresh = used.get(after, set())
         older = tuple(c for c in sorted(known) if c not in (now, after) and (c, done_at(order, c, step)) not in fresh)
-        partial = [add_older(after, older, meta, matrices, fetched[:2], here, known, sums.get(after, []))]
-        known[now] = [around(h) for h in here]
+        partial = [add_older(after, older, meta, matrices, fetched[:2], outer, here, known, sums.get(after, []))]
+        known[now] = [inner, outer, here]
         newest = now
 
     own_final, sib_final = finals[0], finals[0]
     for c in range(1, COLOURS):
-        own_final = [jnp.where(own_colour == c, a, b) for a, b in zip(finals[c], own_final)]
-        sib_final = [jnp.where(sib_colour == c, a, b) for a, b in zip(finals[c], sib_final)]
-    mine, other = jnp.concatenate(own_final), flip(jnp.concatenate(sib_final), 1)
+        own_final = jnp.where(own_wide == c, finals[c], own_final)
+        sib_final = jnp.where(sib_wide == c, finals[c], sib_final)
+    mine, other = own_final, flip(sib_final, 1)
     return pl.pallas_call(
         last_kernel,
         out_shape=jax.ShapeDtypeStruct((block, cols), jnp.float32),

time: 129 us -> 104 us (0.81); the launches traced: 130 us -> 104 us
  starting transfers between devices: 68.9 us -> 35.4 us
  waiting for transfers between devices: 28.5 us -> 40.4 us
  Pallas kernels: 26.3 us -> 23.8 us
  between operations: 3.18 us -> 1.08 us
    ppermute x22 -> x12, starting transfers between devices: 48.1 us -> 27.3 us  [beside(): return lax.ppermute(value, axis, pairs)]
    ppermute x22 -> x12, waiting for transfers between devices: 17.2 us -> 35.7 us  [beside(): return lax.ppermute(value, axis, pairs)]
    ppermute x15 -> x10, starting transfers between devices: 20.8 us -> 8.07 us  [flip(): return lax.ppermute(value, axis, [(i, i ^ bit) for i in range(count)])]
    ppermute x15 -> x10, waiting for transfers between devices: 11.3 us -> 4.72 us  [flip(): return lax.ppermute(value, axis, [(i, i ^ bit) for i in range(count)])]
    pallas_call x6, Pallas kernels: 9.91 us -> 8.08 us  [fetch(): pl.pallas_call(functools.partial(fetch_kernel, now, before, newest, len(a...]
  transfers between devices with their start and end apart: 37 -> 22, of which waited for: 13 -> 13; matrix products, arithmetic and copies ran while one was open for 2% -> 2% of each run, Pallas kernels for 12% -> 17%
where the time goes in v5:
time: 104 us
  waiting for transfers between devices  40.4 us (39%)
  starting transfers between devices  35.4 us (34%)
  Pallas kernels  23.8 us (23%)
  other arithmetic  1.63 us (2%)
  local copies, waits for them, and re-layouts  1.36 us (1%)
  between operations  1.08 us (1%)
    ppermute x12, waiting for transfers between devices, beside(): return lax.ppermute(value, axis, pairs)  35.7 us
    ppermute x12, starting transfers between devices, beside(): return lax.ppermute(value, axis, pairs)  27.3 us
    pallas_call x5, Pallas kernels, add_older(): pl.pallas_call(functools.partial(older_kernel, now, older, len(base)), ou...  10.5 us
    pallas_call x6, Pallas kernels, fetch(): pl.pallas_call(functools.partial(fetch_kernel, now, before, newest, len(a...  8.08 us
    ppermute x10, starting transfers between devices, flip(): return lax.ppermute(value, axis, [(i, i ^ bit) for i in range(count)])  8.07 us
    ppermute x10, waiting for transfers between devices, flip(): return lax.ppermute(value, axis, [(i, i ^ bit) for i in range(count)])  4.72 us
    pallas_call x1, Pallas kernels, per_device(): pl.pallas_call(first_kernel, out_shape=[pltpu.VMEM((half, block), jnp.flo...  2.36 us
  transfers between devices with their start and end apart: 22, of which 13 were waited for; matrix products, arithmetic and copies ran while one was open for 2% of the time, Pallas kernels for 17%

profile of v5, /device:TPU:0, one launch (start us, length us, event | category | flops | bytes accessed | tf_op | source)
XLA Modules:
  0.0 103.6 jit_solution(14934055429396206568)
XLA Ops:
  0.8 0.7 pad_add_fusion.facts_ref
  1.5 2.4 %first.1 = (f32[64,512]{1,0:T(8,128)S(1)}, f32[72,512]{1,0:T(8,128)S(1)}, f32[8,512]{1,0:T(8,128)S(1)}) custom-call(s32[8]{0:T(128)S(1)} %pad_add_fusion.facts_ref, f32[512,512]{1,0:T(8,128)} %own_inverse.11, f32[512,128]{1,0:T(8,128)} %residual_hbm.1), custom_call_target="tpu_custom_call" | custom-call | tf_op jit(solution)/shard_map/first/pallas_call | solution.py:306
  3.9 0.5 collective-permute-start
  4.4 1.0 collective-permute-done.sib_start
  5.4 0.4 collective-permute-start.4
  5.9 2.7 %collective-permute-start.1 = (f32[72,512]{1,0:T(8,128)S(1)}, f32[72,512]{1,0:T(8,128)S(1)}, u32[]{:S(2)}, u32[]{:S(2)}) collective-permute-start(f32[72,512]{1,0:T(8,128)S(1)} %pad_maximum_fusion), channel_id=1, source_target_pairs={{0,2},{1,3},{2,0},{3,1},{4,6},{5,7},{6,4},{7,5},{8,10},{9,11},{10,... | collective-permute-start | bytes 442376 | tf_op jit(solution)/shard_map/ppermute | solution.py:296
  8.6 4.6 %collective-permute-start.3 = (f32[72,512]{1,0:T(8,128)S(1)}, f32[72,512]{1,0:T(8,128)S(1)}, u32[]{:S(2)}, u32[]{:S(2)}) collective-permute-start(f32[72,512]{1,0:T(8,128)S(1)} %pad_maximum_fusion), channel_id=1, source_target_pairs={{0,28},{1,29},{2,6},{3,7},{4,0},{5,1},{6,10},{7,11},{8,4},{9,5},{1... | collective-permute-start | bytes 442376 | tf_op jit(solution)/shard_map/ppermute | solution.py:303
  13.2 0.5 slice.56
  13.7 0.1 slice_reduce_fusion
  14.0 1.0 collective-permute-start.2
  14.9 0.1 select_reduce_fusion
  15.1 1.5 %collective-permute-done.3.refs_1_ = f32[72,512]{1,0:T(8,128)S(1)} collective-permute-done((f32[72,512]{1,0:T(8,128)S(1)}, f32[72,512]{1,0:T(8,128)S(1)}, u32[]{:S(2)}, u32[]{:S(2)}) %collective-permute-start.3) | collective-permute-done | bytes 147488 | tf_op jit(solution)/shard_map/ppermute | solution.py:303
  16.5 0.1 select_reduce_fusion.1
  16.7 6.3 %collective-permute-done.2.refs_0_ = f32[72,512]{1,0:T(8,128)S(1)} collective-permute-done((f32[72,512]{1,0:T(8,128)S(1)}, f32[72,512]{1,0:T(8,128)S(1)}, u32[]{:S(2)}, u32[]{:S(2)}) %collective-permute-start.2) | collective-permute-done | bytes 147488 | tf_op jit(solution)/shard_map/ppermute | solution.py:303
  23.0 0.1 select_reduce_fusion.2
  23.1 0.7 concatenate.15.meta_ref
  23.8 1.2 %fetch_1_0.1 = (bf16[512,1536]{1,0:T(8,128)(2,1)S(1)}, bf16[512,1536]{1,0:T(8,128)(2,1)S(1)}, bf16[512,512]{1,0:T(8,128)(2,1)S(1)}, bf16[512,512]{1,0:T(8,128)(2...) custom-call(s32[26]{0:T(128)S(1)} %concatenate.15.meta_ref, f32[6,512,512]{2,1,0:T(8,128)} %bitcast.7, ...), custom_call_target="tpu_custom_call" | custom-call | bytes 6291456 | tf_op jit(solution)/shard_map/fetch_1_0/pallas_call | solution.py:217
  25.1 2.9 %collective-permute-start.6 = (f32[64,512]{1,0:T(8,128)S(1)}, f32[64,512]{1,0:T(8,128)S(1)}, u32[]{:S(2)}, u32[]{:S(2)}) collective-permute-start(f32[64,512]{1,0:T(8,128)S(1)} %get-tuple-element.66.refs_0_), channel_id=1, source_target_pairs={{0,2},{1,3},{2,0},{3,1},{4,6},{5,7},{6,4},{7,5},{8,10},{9,11},{10,... | collective-permute-start | bytes 393224 | tf_op jit(solution)/shard_map/ppermute | solution.py:296
  28.0 5.5 %collective-permute-start.8 = (f32[64,512]{1,0:T(8,128)S(1)}, f32[64,512]{1,0:T(8,128)S(1)}, u32[]{:S(2)}, u32[]{:S(2)}) collective-permute-start(f32[64,512]{1,0:T(8,128)S(1)} %get-tuple-element.66.refs_0_), channel_id=1, source_target_pairs={{0,28},{1,29},{2,6},{3,7},{4,0},{5,1},{6,10},{7,11},{8,4},{9,5},{1... | collective-permute-start | bytes 393224 | tf_op jit(solution)/shard_map/ppermute | solution.py:303
  33.5 0.6 fetch_2_1.1
  34.2 1.8 %collective-permute-done.8.outer.refs_4_ = f32[64,512]{1,0:T(8,128)S(1)} collective-permute-done((f32[64,512]{1,0:T(8,128)S(1)}, f32[64,512]{1,0:T(8,128)S(1)}, u32[]{:S(2)}, u32[]{:S(2)}) %collective-permute-start.8) | collective-permute-done | bytes 131104 | tf_op jit(solution)/shard_map/ppermute | solution.py:303
  36.0 0.6 older_2.2.refs_1_
  36.6 5.3 %collective-permute-done.7.refs_0_.refs_3_ = f32[64,512]{1,0:T(8,128)S(1)} collective-permute-done((f32[64,512]{1,0:T(8,128)S(1)}, f32[64,512]{1,0:T(8,128)S(1)}, u32[]{:S(2)}, u32[]{:S(2)}) %collective-permute-start.7) | collective-permute-done | bytes 131104 | tf_op jit(solution)/shard_map/ppermute | solution.py:303
  41.9 1.0 collective-permute-start.9
  42.9 4.3 %collective-permute-start.11 = (f32[64,512]{1,0:T(8,128)S(1)}, f32[64,512]{1,0:T(8,128)S(1)}, u32[]{:S(2)}, u32[]{:S(2)}) collective-permute-start(f32[64,512]{1,0:T(8,128)S(1)} %get-tuple-element.74.refs_0_), channel_id=1, source_target_pairs={{0,28},{1,29},{2,6},{3,7},{4,0},{5,1},{6,10},{7,11},{8,4},{9,5},{1... | collective-permute-start | bytes 393224 | tf_op jit(solution)/shard_map/ppermute | solution.py:303
  47.2 2.4 %fetch_3_2.1 = (bf16[512,1536]{1,0:T(8,128)(2,1)S(1)}, bf16[512,1536]{1,0:T(8,128)(2,1)S(1)}, bf16[512,512]{1,0:T(8,128)(2,1)S(1)}, bf16[512,512]{1,0:T(8,128)(2...) custom-call(s32[26]{0:T(128)S(1)} %concatenate.15.meta_ref, f32[6,512,512]{2,1,0:T(8,128)} %bitcast.10, ...), custom_call_target="tpu_custom_call" | custom-call | bytes 6291456 | tf_op jit(solution)/shard_map/fetch_3_2/pallas_call | solution.py:217
  49.7 4.4 %older_3.1.refs_1_ = f32[64,512]{1,0:T(8,128)S(1)} custom-call(s32[26]{0:T(128)S(1)} %concatenate.15.meta_ref, f32[6,512,512]{2,1,0:T(8,128)} %bitcast.11, f32[6,512,512]{2,1,0:T(8,128)} %collective-permute-done.4.sib_tiles, bf16[512,1536]{1,0:T(8,128)(2,1)S(1)} %get-tuple-element.76.w_high, bf16[512,1536]{1,0:T(8,128)(2,1)S(1)} %get-tuple-element.77.w_low, ...), custom_call_target="tpu_custom_call" | custom-call | flops 805306368 | bytes 6291456 | tf_op jit(solution)/shard_map/older_3/pallas_call | solution.py:246
  54.1 3.3 %collective-permute-done.10.refs_0_ = f32[64,512]{1,0:T(8,128)S(1)} collective-permute-done((f32[64,512]{1,0:T(8,128)S(1)}, f32[64,512]{1,0:T(8,128)S(1)}, u32[]{:S(2)}, u32[]{:S(2)}) %collective-permute-start.10) | collective-permute-done | bytes 131104 | tf_op jit(solution)/shard_map/ppermute | solution.py:303
  57.5 0.9 relax_3.1.refs_0_
  58.5 2.0 %collective-permute-start.14 = (f32[64,512]{1,0:T(8,128)S(1)}, f32[64,512]{1,0:T(8,128)S(1)}, u32[]{:S(2)}, u32[]{:S(2)}) collective-permute-start(f32[64,512]{1,0:T(8,128)S(1)} %relax_3.1.refs_0_), channel_id=1, source_target_pairs={{0,28},{1,29},{2,6},{3,7},{4,0},{5,1},{6,10},{7,11},{8,4},{9,5},{1... | collective-permute-start | bytes 393224 | tf_op jit(solution)/shard_map/ppermute | solution.py:303
  60.4 0.6 fetch_2_3.1
  61.1 2.4 %collective-permute-done.12 = f32[64,512]{1,0:T(8,128)S(1)} collective-permute-done((f32[64,512]{1,0:T(8,128)S(1)}, f32[64,512]{1,0:T(8,128)S(1)}, u32[]{:S(2)}, u32[]{:S(2)}) %collective-permute-start.12) | collective-permute-done | bytes 131104 | tf_op jit(solution)/shard_map/ppermute | solution.py:296
  63.5 1.4 %collective-permute-done.14.outer.refs_1_.refs_4_ = f32[64,512]{1,0:T(8,128)S(1)} collective-permute-done((f32[64,512]{1,0:T(8,128)S(1)}, f32[64,512]{1,0:T(8,128)S(1)}, u32[]{:S(2)}, u32[]{:S(2)}) %collective-permute-start.14) | collective-permute-done | bytes 131104 | tf_op jit(solution)/shard_map/ppermute | solution.py:303
  64.9 0.6 older_2.3.refs_1_
  65.5 5.7 %collective-permute-done.13.refs_0_.refs_3_ = f32[64,512]{1,0:T(8,128)S(1)} collective-permute-done((f32[64,512]{1,0:T(8,128)S(1)}, f32[64,512]{1,0:T(8,128)S(1)}, u32[]{:S(2)}, u32[]{:S(2)}) %collective-permute-start.13) | collective-permute-done | bytes 131104 | tf_op jit(solution)/shard_map/ppermute | solution.py:303
  71.3 5.0 %collective-permute-start.17 = (f32[64,512]{1,0:T(8,128)S(1)}, f32[64,512]{1,0:T(8,128)S(1)}, u32[]{:S(2)}, u32[]{:S(2)}) collective-permute-start(f32[64,512]{1,0:T(8,128)S(1)} %relax_2.3.refs_0_), channel_id=1, source_target_pairs={{0,28},{1,29},{2,6},{3,7},{4,0},{5,1},{6,10},{7,11},{8,4},{9,5},{1... | collective-permute-start | bytes 393224 | tf_op jit(solution)/shard_map/ppermute | solution.py:303
  76.3 0.8 fetch_1_2.1
  77.2 1.6 %collective-permute-done.17.outer.refs_1_ = f32[64,512]{1,0:T(8,128)S(1)} collective-permute-done((f32[64,512]{1,0:T(8,128)S(1)}, f32[64,512]{1,0:T(8,128)S(1)}, u32[]{:S(2)}, u32[]{:S(2)}) %collective-permute-start.17) | collective-permute-done | bytes 131104 | tf_op jit(solution)/shard_map/ppermute | solution.py:303
  78.8 0.6 older_1.1.refs_1_
  79.4 5.4 %collective-permute-done.16.refs_0_ = f32[64,512]{1,0:T(8,128)S(1)} collective-permute-done((f32[64,512]{1,0:T(8,128)S(1)}, f32[64,512]{1,0:T(8,128)S(1)}, u32[]{:S(2)}, u32[]{:S(2)}) %collective-permute-start.16) | collective-permute-done | bytes 131104 | tf_op jit(solution)/shard_map/ppermute | solution.py:303
  84.9 0.3 collective-permute-start.18
  85.3 4.7 %collective-permute-start.20 = (f32[64,512]{1,0:T(8,128)S(1)}, f32[64,512]{1,0:T(8,128)S(1)}, u32[]{:S(2)}, u32[]{:S(2)}) collective-permute-start(f32[64,512]{1,0:T(8,128)S(1)} %relax_1.3.refs_0_), channel_id=1, source_target_pairs={{0,28},{1,29},{2,6},{3,7},{4,0},{5,1},{6,10},{7,11},{8,4},{9,5},{1... | collective-permute-start | bytes 393224 | tf_op jit(solution)/shard_map/ppermute | solution.py:303
  90.0 2.6 %fetch_0_1.1 = (bf16[512,1536]{1,0:T(8,128)(2,1)S(1)}, bf16[512,1536]{1,0:T(8,128)(2,1)S(1)}, bf16[512,512]{1,0:T(8,128)(2,1)S(1)}, bf16[512,512]{1,0:T(8,128)(2...) custom-call(s32[26]{0:T(128)S(1)} %concatenate.15.meta_ref, f32[6,512,512]{2,1,0:T(8,128)} %bitcast.16, ...), custom_call_target="tpu_custom_call" | custom-call | bytes 6291456 | tf_op jit(solution)/shard_map/fetch_0_1/pallas_call | solution.py:217
  92.8 4.4 %older_0.1.refs_1_ = f32[64,512]{1,0:T(8,128)S(1)} custom-call(s32[26]{0:T(128)S(1)} %concatenate.15.meta_ref, f32[6,512,512]{2,1,0:T(8,128)} %bitcast.17, f32[6,512,512]{2,1,0:T(8,128)} %collective-permute-done.4.sib_tiles, bf16[512,1536]{1,0:T(8,128)(2,1)S(1)} %get-tuple-element.99.w_high, bf16[512,1536]{1,0:T(8,128)(2,1)S(1)} %get-tuple-element.100.w_low, ...), custom_call_target="tpu_custom_call" | custom-call | flops 805306368 | bytes 6291456 | tf_op jit(solution)/shard_map/older_0/pallas_call | solution.py:246
  97.1 3.3 %collective-permute-done.19.refs_0_ = f32[64,512]{1,0:T(8,128)S(1)} collective-permute-done((f32[64,512]{1,0:T(8,128)S(1)}, f32[64,512]{1,0:T(8,128)S(1)}, u32[]{:S(2)}, u32[]{:S(2)}) %collective-permute-start.19) | collective-permute-done | bytes 131104 | tf_op jit(solution)/shard_map/ppermute | solution.py:303
  100.4 0.9 relax_0.1
  101.4 1.3 %collective-permute-done.21.other_ref = f32[64,512]{1,0:T(8,128)S(1)} collective-permute-done((f32[64,512]{1,0:T(8,128)S(1)}, f32[64,512]{1,0:T(8,128)S(1)}, u32[]{:S(2)}, u32[]{:S(2)}) %collective-permute-start.21) | collective-permute-done | bytes 131104 | tf_op jit(solution)/shard_map/ppermute | solution.py:296
  102.8 0.8 last.1
  (48 shorter events, 1.3 us)
Async XLA Ops:
  0.0 23.1 %copy-start.1 = (s32[1,6]{1,0:T(1,128)S(1)}, s32[1,6]{1,0:T(1,128)}, u32[]{:S(2)}) copy-start(s32[1,6]{1,0:T(1,128)} %param.9) | copy-start | bytes 76
  0.0 13.2 %copy-start = (f32[512,512]{1,0:T(8,128)S(1)}, f32[512,512]{1,0:T(8,128)}, u32[]{:S(2)}) copy-start(f32[512,512]{1,0:T(8,128)} %own_inverse.11) | copy-start | bytes 3145732
  3.9 1.5 %collective-permute-start = (f32[72,512]{1,0:T(8,128)S(1)}, f32[72,512]{1,0:T(8,128)S(1)}, u32[]{:S(2)}, u32[]{:S(2)}) collective-permute-start(f32[72,512]{1,0:T(8,128)S(1)} %get-tuple-element.56), channel_id=1, source_target_pairs={{0,1},{1,0},{2,3},{3,2},{4,5},{5,4},{6,7},{7,6},{8,9},{9,8},{10,11... | collective-permute-start | bytes 442376 | tf_op jit(solution)/shard_map/ppermute | solution.py:296
  5.4 18.5 %collective-permute-start.4 = (f32[6,512,512]{2,1,0:T(8,128)}, f32[6,512,512]{2,1,0:T(8,128)}, u32[]{:S(2)}, u32[]{:S(2)}) collective-permute-start(f32[6,512,512]{2,1,0:T(8,128)} %bitcast.6), channel_id=1, source_target_pairs={{0,1},{1,0},{2,3},{3,2},{4,5},{5,4},{6,7},{7,6},{8,9},{9,8},{10,11... | collective-permute-start | bytes 18874376 | tf_op jit(solution)/shard_map/ppermute | solution.py:296
  5.9 7.9 %collective-permute-start.1 = (f32[72,512]{1,0:T(8,128)S(1)}, f32[72,512]{1,0:T(8,128)S(1)}, u32[]{:S(2)}, u32[]{:S(2)}) collective-permute-start(f32[72,512]{1,0:T(8,128)S(1)} %pad_maximum_fusion), channel_id=1, source_target_pairs={{0,2},{1,3},{2,0},{3,1},{4,6},{5,7},{6,4},{7,5},{8,10},{9,11},{10,... | collective-permute-start | bytes 442376 | tf_op jit(solution)/shard_map/ppermute | solution.py:296
  8.6 7.9 %collective-permute-start.3 = (f32[72,512]{1,0:T(8,128)S(1)}, f32[72,512]{1,0:T(8,128)S(1)}, u32[]{:S(2)}, u32[]{:S(2)}) collective-permute-start(f32[72,512]{1,0:T(8,128)S(1)} %pad_maximum_fusion), channel_id=1, source_target_pairs={{0,28},{1,29},{2,6},{3,7},{4,0},{5,1},{6,10},{7,11},{8,4},{9,5},{1... | collective-permute-start | bytes 442376 | tf_op jit(solution)/shard_map/ppermute | solution.py:303
  13.2 10.6 %collective-permute-start.5 = (f32[512,512]{1,0:T(8,128)S(1)}, f32[512,512]{1,0:T(8,128)S(1)}, u32[]{:S(2)}, u32[]{:S(2)}) collective-permute-start(f32[512,512]{1,0:T(8,128)S(1)} %copy-done), channel_id=1, source_target_pairs={{0,1},{1,0},{2,3},{3,2},{4,5},{5,4},{6,7},{7,6},{8,9},{9,8},{10,11... | collective-permute-start | bytes 3145736 | tf_op jit(solution)/shard_map/ppermute | solution.py:296
  14.0 9.0 %collective-permute-start.2 = (f32[72,512]{1,0:T(8,128)S(1)}, f32[72,512]{1,0:T(8,128)S(1)}, u32[]{:S(2)}, u32[]{:S(2)}) collective-permute-start(f32[72,512]{1,0:T(8,128)S(1)} %pad_maximum_fusion.1.refs_2_), channel_id=1, source_target_pairs={{0,4},{1,5},{2,30},{3,31},{4,8},{5,9},{6,2},{7,3},{8,12},{9,13},{1... | collective-permute-start | bytes 442376 | tf_op jit(solution)/shard_map/ppermute | solution.py:303
  25.1 9.0 %collective-permute-start.6 = (f32[64,512]{1,0:T(8,128)S(1)}, f32[64,512]{1,0:T(8,128)S(1)}, u32[]{:S(2)}, u32[]{:S(2)}) collective-permute-start(f32[64,512]{1,0:T(8,128)S(1)} %get-tuple-element.66.refs_0_), channel_id=1, source_target_pairs={{0,2},{1,3},{2,0},{3,1},{4,6},{5,7},{6,4},{7,5},{8,10},{9,11},{10,... | collective-permute-start | bytes 393224 | tf_op jit(solution)/shard_map/ppermute | solution.py:296
  28.0 8.0 %collective-permute-start.8 = (f32[64,512]{1,0:T(8,128)S(1)}, f32[64,512]{1,0:T(8,128)S(1)}, u32[]{:S(2)}, u32[]{:S(2)}) collective-permute-start(f32[64,512]{1,0:T(8,128)S(1)} %get-tuple-element.66.refs_0_), channel_id=1, source_target_pairs={{0,28},{1,29},{2,6},{3,7},{4,0},{5,1},{6,10},{7,11},{8,4},{9,5},{1... | collective-permute-start | bytes 393224 | tf_op jit(solution)/shard_map/ppermute | solution.py:303
  34.2 7.7 %collective-permute-start.7 = (f32[64,512]{1,0:T(8,128)S(1)}, f32[64,512]{1,0:T(8,128)S(1)}, u32[]{:S(2)}, u32[]{:S(2)}) collective-permute-start(f32[64,512]{1,0:T(8,128)S(1)} %broadcast_select_fusion.4.here.refs_5_), channel_id=1, source_target_pairs={{0,4},{1,5},{2,30},{3,31},{4,8},{5,9},{6,2},{7,3},{8,12},{9,13},{1... | collective-permute-start | bytes 393224 | tf_op jit(solution)/shard_map/ppermute | solution.py:303
  41.9 7.7 %collective-permute-start.9 = (f32[64,512]{1,0:T(8,128)S(1)}, f32[64,512]{1,0:T(8,128)S(1)}, u32[]{:S(2)}, u32[]{:S(2)}) collective-permute-start(f32[64,512]{1,0:T(8,128)S(1)} %get-tuple-element.74.refs_0_), channel_id=1, source_target_pairs={{0,2},{1,3},{2,0},{3,1},{4,6},{5,7},{6,4},{7,5},{8,10},{9,11},{10,... | collective-permute-start | bytes 393224 | tf_op jit(solution)/shard_map/ppermute | solution.py:296
  42.9 6.8 %collective-permute-start.11 = (f32[64,512]{1,0:T(8,128)S(1)}, f32[64,512]{1,0:T(8,128)S(1)}, u32[]{:S(2)}, u32[]{:S(2)}) collective-permute-start(f32[64,512]{1,0:T(8,128)S(1)} %get-tuple-element.74.refs_0_), channel_id=1, source_target_pairs={{0,28},{1,29},{2,6},{3,7},{4,0},{5,1},{6,10},{7,11},{8,4},{9,5},{1... | collective-permute-start | bytes 393224 | tf_op jit(solution)/shard_map/ppermute | solution.py:303
  49.6 7.8 %collective-permute-start.10 = (f32[64,512]{1,0:T(8,128)S(1)}, f32[64,512]{1,0:T(8,128)S(1)}, u32[]{:S(2)}, u32[]{:S(2)}) collective-permute-start(f32[64,512]{1,0:T(8,128)S(1)} %broadcast_select_fusion.3.here), channel_id=1, source_target_pairs={{0,4},{1,5},{2,30},{3,31},{4,8},{5,9},{6,2},{7,3},{8,12},{9,13},{1... | collective-permute-start | bytes 393224 | tf_op jit(solution)/shard_map/ppermute | solution.py:303
  58.4 5.0 %collective-permute-start.12 = (f32[64,512]{1,0:T(8,128)S(1)}, f32[64,512]{1,0:T(8,128)S(1)}, u32[]{:S(2)}, u32[]{:S(2)}) collective-permute-start(f32[64,512]{1,0:T(8,128)S(1)} %relax_3.1.refs_0_), channel_id=1, source_target_pairs={{0,2},{1,3},{2,0},{3,1},{4,6},{5,7},{6,4},{7,5},{8,10},{9,11},{10,... | collective-permute-start | bytes 393224 | tf_op jit(solution)/shard_map/ppermute | solution.py:296
  58.5 6.4 %collective-permute-start.14 = (f32[64,512]{1,0:T(8,128)S(1)}, f32[64,512]{1,0:T(8,128)S(1)}, u32[]{:S(2)}, u32[]{:S(2)}) collective-permute-start(f32[64,512]{1,0:T(8,128)S(1)} %relax_3.1.refs_0_), channel_id=1, source_target_pairs={{0,28},{1,29},{2,6},{3,7},{4,0},{5,1},{6,10},{7,11},{8,4},{9,5},{1... | collective-permute-start | bytes 393224 | tf_op jit(solution)/shard_map/ppermute | solution.py:303
  63.4 7.7 %collective-permute-start.13 = (f32[64,512]{1,0:T(8,128)S(1)}, f32[64,512]{1,0:T(8,128)S(1)}, u32[]{:S(2)}, u32[]{:S(2)}) collective-permute-start(f32[64,512]{1,0:T(8,128)S(1)} %broadcast_select_fusion.2.here.refs_2_.refs_5_), channel_id=1, source_target_pairs={{0,4},{1,5},{2,30},{3,31},{4,8},{5,9},{6,2},{7,3},{8,12},{9,13},{1... | collective-permute-start | bytes 393224 | tf_op jit(solution)/shard_map/ppermute | solution.py:303
  71.2 5.9 %collective-permute-start.15 = (f32[64,512]{1,0:T(8,128)S(1)}, f32[64,512]{1,0:T(8,128)S(1)}, u32[]{:S(2)}, u32[]{:S(2)}) collective-permute-start(f32[64,512]{1,0:T(8,128)S(1)} %relax_2.3.refs_0_), channel_id=1, source_target_pairs={{0,2},{1,3},{2,0},{3,1},{4,6},{5,7},{6,4},{7,5},{8,10},{9,11},{10,... | collective-permute-start | bytes 393224 | tf_op jit(solution)/shard_map/ppermute | solution.py:296
  71.3 7.5 %collective-permute-start.17 = (f32[64,512]{1,0:T(8,128)S(1)}, f32[64,512]{1,0:T(8,128)S(1)}, u32[]{:S(2)}, u32[]{:S(2)}) collective-permute-start(f32[64,512]{1,0:T(8,128)S(1)} %relax_2.3.refs_0_), channel_id=1, source_target_pairs={{0,28},{1,29},{2,6},{3,7},{4,0},{5,1},{6,10},{7,11},{8,4},{9,5},{1... | collective-permute-start | bytes 393224 | tf_op jit(solution)/shard_map/ppermute | solution.py:303
  77.2 7.7 %collective-permute-start.16 = (f32[64,512]{1,0:T(8,128)S(1)}, f32[64,512]{1,0:T(8,128)S(1)}, u32[]{:S(2)}, u32[]{:S(2)}) collective-permute-start(f32[64,512]{1,0:T(8,128)S(1)} %broadcast_select_fusion.1.here.refs_2_), channel_id=1, source_target_pairs={{0,4},{1,5},{2,30},{3,31},{4,8},{5,9},{6,2},{7,3},{8,12},{9,13},{1... | collective-permute-start | bytes 393224 | tf_op jit(solution)/shard_map/ppermute | solution.py:303
  84.9 7.7 %collective-permute-start.18 = (f32[64,512]{1,0:T(8,128)S(1)}, f32[64,512]{1,0:T(8,128)S(1)}, u32[]{:S(2)}, u32[]{:S(2)}) collective-permute-start(f32[64,512]{1,0:T(8,128)S(1)} %relax_1.3.refs_0_), channel_id=1, source_target_pairs={{0,2},{1,3},{2,0},{3,1},{4,6},{5,7},{6,4},{7,5},{8,10},{9,11},{10,... | collective-permute-start | bytes 393224 | tf_op jit(solution)/shard_map/ppermute | solution.py:296
  85.3 7.5 %collective-permute-start.20 = (f32[64,512]{1,0:T(8,128)S(1)}, f32[64,512]{1,0:T(8,128)S(1)}, u32[]{:S(2)}, u32[]{:S(2)}) collective-permute-start(f32[64,512]{1,0:T(8,128)S(1)} %relax_1.3.refs_0_), channel_id=1, source_target_pairs={{0,28},{1,29},{2,6},{3,7},{4,0},{5,1},{6,10},{7,11},{8,4},{9,5},{1... | collective-permute-start | bytes 393224 | tf_op jit(solution)/shard_map/ppermute | solution.py:303
  92.7 7.7 %collective-permute-start.19 = (f32[64,512]{1,0:T(8,128)S(1)}, f32[64,512]{1,0:T(8,128)S(1)}, u32[]{:S(2)}, u32[]{:S(2)}) collective-permute-start(f32[64,512]{1,0:T(8,128)S(1)} %broadcast_select_fusion.here), channel_id=1, source_target_pairs={{0,4},{1,5},{2,30},{3,31},{4,8},{5,9},{6,2},{7,3},{8,12},{9,13},{1... | collective-permute-start | bytes 393224 | tf_op jit(solution)/shard_map/ppermute | solution.py:303
  101.4 1.4 %collective-permute-start.21 = (f32[64,512]{1,0:T(8,128)S(1)}, f32[64,512]{1,0:T(8,128)S(1)}, u32[]{:S(2)}, u32[]{:S(2)}) collective-permute-start(f32[64,512]{1,0:T(8,128)S(1)} %get-tuple-element.113), channel_id=1, source_target_pairs={{0,1},{1,0},{2,3},{3,2},{4,5},{5,4},{6,7},{7,6},{8,9},{9,8},{10,11... | collective-permute-start | bytes 393224 | tf_op jit(solution)/shard_map/ppermute | solution.py:296

commit v6 on v5

v6 whole, which is shorter than its diff:
```python
import functools

import jax
import jax.numpy as jnp
from jax import lax
from jax.experimental import pallas as pl
from jax.experimental.pallas import tpu as pltpu
from jax.sharding import PartitionSpec as P

COLOURS = 4
SIDES = 3
INNER, OUTER, HERE = range(3)
EXTRA = 8
LANES = 128
ACTIVE, IS_OWN, TILE = range(3)


def dot_t(a, b):
    return lax.dot_general(a, b, (((1,), (1,)), ((), ())), preferred_element_type=jnp.float32)


def split(value):
    high = value.astype(jnp.bfloat16)
    return high, (value - high.astype(jnp.float32)).astype(jnp.bfloat16)


def times(value, high, low):
    rows = value.shape[0]
    parts = jnp.concatenate(split(value), axis=0)
    product = dot_t(parts, high) + dot_t(parts, low)
    return product[:rows] + product[rows:]


def vmem():
    return pl.BlockSpec(memory_space=pltpu.VMEM)


def smem():
    return pl.BlockSpec(memory_space=pltpu.SMEM)


def anywhere():
    return pl.BlockSpec(memory_space=pl.ANY)


def hbm():
    return pl.BlockSpec(memory_space=pltpu.HBM)


def params(mebibytes):
    return pltpu.CompilerParams(vmem_limit_bytes=mebibytes * 1024 * 1024)


def far(values):
    return [pltpu.with_memory_space_constraint(v, pltpu.HBM) for v in values]


def near(values):
    return [pltpu.with_memory_space_constraint(v, pltpu.VMEM) for v in values]


def first_kernel(core_ref, colour_ref, tile_cols_ref, inverse_hbm, residual_hbm, keep_ref, send_ref, facts_out, inverse_ref, residual_ref, sems):
    copies = [
        pltpu.make_async_copy(residual_hbm, residual_ref, sems.at[0]),
        pltpu.make_async_copy(inverse_hbm, inverse_ref, sems.at[1]),
    ]
    for copy in copies:
        copy.start()
    for copy in copies:
        copy.wait()
    value = times(jnp.transpose(residual_ref[...]), *split(inverse_ref[...]))
    half, block = keep_ref.shape
    is_first = core_ref[0] == 0
    keep_ref[...] = jnp.where(is_first, value[:half], value[half:])
    send_ref[:half, :] = jnp.where(is_first, value[half:], value[:half])
    row = lax.broadcasted_iota(jnp.int32, (EXTRA, block), 0)
    rows = jnp.where(row == 0, colour_ref[0], 0)
    for k in range(tile_cols_ref.shape[1]):
        rows = jnp.where(row == k + 1, tile_cols_ref[0, k], rows)
    send_ref[half:, :] = rows.astype(jnp.float32)
    facts_out[...] = rows.astype(jnp.float32)


def last_kernel(core_ref, mine_ref, other_ref, out_ref):
    is_first = core_ref[0] == 0
    mine, other = mine_ref[...], other_ref[...]
    first = jnp.where(is_first, mine, other)
    second = jnp.where(is_first, other, mine)
    out_ref[...] = jnp.transpose(jnp.concatenate([first, second], axis=0))


def parts_kernel(tiles_ref, inverse_ref, w_high, w_low, zeros, buffer, sems):
    zeros[...] = jnp.zeros_like(zeros)
    tiles = tiles_ref.shape[0]
    copies = [pltpu.make_async_copy(tiles_ref.at[k], buffer.at[k], sems.at[k]) for k in range(tiles)]
    copies.append(pltpu.make_async_copy(inverse_ref, buffer.at[tiles], sems.at[tiles]))
    for copy in copies:
        copy.start()
    for k, copy in enumerate(copies):
        copy.wait()
        w_high[k], w_low[k] = split(buffer[k])


def plan_kernel(tiles, firsts_ref, _, own_rows, arrived, inner, outer, here, *outs):
    half = arrived.shape[0] - EXTRA
    lanes = pl.ds(0, LANES)
    own = own_rows[:, lanes].astype(jnp.int32)
    sib = arrived[half:, lanes].astype(jnp.int32)
    wanted = []
    for side, ref in enumerate((inner, outer, here)):
        found = ref[half:, lanes].astype(jnp.int32)
        wanted.append(jnp.where(found > 0, firsts_ref[side] + found - 1, -1))
    rows = outs[0].shape[0]
    row = lax.broadcasted_iota(jnp.int32, (rows, LANES), 0)
    for now in range(COLOURS):
        is_own, is_sib = own[:1] == now, sib[:1] == now
        active = (is_own | is_sib).astype(jnp.int32)
        plan = jnp.where(row == ACTIVE, active, is_own.astype(jnp.int32))
        listed = [jnp.where(is_own, own[k + 1 : k + 2], sib[k + 1 : k + 2]) for k in range(tiles)]
        for side in range(SIDES):
            found = jnp.full((EXTRA, LANES), -1, jnp.int32)
            for k in range(tiles):
                found = jnp.where(wanted[side] == listed[k], k, found)
            for c in range(COLOURS):
                plan = jnp.where(row == TILE + side * COLOURS + c, found[c : c + 1], plan)
        outs[now][...] = plan
        mask = outs[COLOURS + now]
        mask[...] = jnp.concatenate([jnp.broadcast_to(active, (EXTRA, LANES))] * (mask.shape[1] // LANES), axis=1)


def chosen(plan, body, own, sib):
    active, is_own = plan[ACTIVE, 0] != 0, plan[IS_OWN, 0] != 0

    @pl.when(active & is_own)
    def _():
        body(*own)

    @pl.when(active & jnp.logical_not(is_own))
    def _():
        body(*sib)


def older_kernel(newest, older, has_base, plan, own_high, own_low, sib_high, sib_low, outer, here, *refs):
    *refs, partial = refs
    known, base = refs[: SIDES * len(older)], refs[SIDES * len(older) :]
    half = partial.shape[0]
    slots = [(newest, OUTER, outer), (newest, HERE, here)]
    slots += [(c, side, known[SIDES * i + side]) for i, c in enumerate(older) for side in range(SIDES)]

    def body(w_high, w_low):
        partial[...] = base[0][...] if has_base else jnp.zeros_like(partial)
        for c, side, ref in slots:
            k = plan[TILE + side * COLOURS + c, 0]

            @pl.when(k >= 0)
            def _():
                partial[...] += times(ref[:half, :], w_high[k], w_low[k])

    chosen(plan, body, (own_high, own_low), (sib_high, sib_low))


def relax_kernel(newest, sides, plan, own_high, own_low, sib_high, sib_low, own_start, sib_start, *refs):
    latest, refs = refs[:sides], refs[sides:]
    base, refs = refs[: int(sides < SIDES)], refs[int(sides < SIDES) :]
    out, total = refs[:2]
    half = out.shape[0]

    def body(w_high, w_low, begin):
        total[...] = base[0][...] if base else jnp.zeros_like(total)
        for side, ref in enumerate(latest):
            k = plan[TILE + side * COLOURS + newest, 0]

            @pl.when(k >= 0)
            def _():
                total[...] += times(ref[:half, :], w_high[k], w_low[k])

        last = w_high.shape[0] - 1
        out[...] = begin[:half, :] - times(total[...], w_high[last], w_low[last])

    chosen(plan, body, (own_high, own_low, own_start), (sib_high, sib_low, sib_start))

    @pl.when(plan[ACTIVE, 0] == 0)
    def _():
        out[...] = jnp.zeros_like(out)


def parts(tiles, inverse, name):
    count, block, _ = tiles.shape
    return pl.pallas_call(
        parts_kernel,
        out_shape=[pltpu.VMEM((count + 1, block, block), jnp.bfloat16)] * 2 + [pltpu.VMEM((EXTRA, block), jnp.float32)],
        in_specs=[anywhere()] * 2,
        out_specs=[vmem()] * 3,
        scratch_shapes=[
            pltpu.VMEM((count + 1, block, block), jnp.float32),
            pltpu.SemaphoreType.DMA((count + 1,)),
        ],
        compiler_params=params(12),
        cost_estimate=pl.CostEstimate(flops=0, bytes_accessed=8 * count * block * block, transcendentals=0),
        name=name,
    )(tiles, inverse)


def make_plans(tiles, firsts, own_rows, arrived, first_known, zeros):
    block = own_rows.shape[1]
    rows = -(-(TILE + SIDES * COLOURS) // EXTRA) * EXTRA
    outs = pl.pallas_call(
        functools.partial(plan_kernel, tiles),
        out_shape=[pltpu.VMEM((rows, LANES), jnp.int32)] * COLOURS + [pltpu.VMEM((EXTRA, block), jnp.int32)] * COLOURS,
        in_specs=[smem()] + [vmem()] * 6,
        out_specs=[vmem()] * (2 * COLOURS),
        compiler_params=params(8),
        name="plan",
    )(firsts, *near([zeros, own_rows, arrived, *first_known]))
    return outs[:COLOURS], outs[COLOURS:]


def add_older(now, newest, older, plan, matrices, outer, here, known, base):
    half, block = here.shape
    operands = near([plan, *matrices, outer, here, *[value for c in older for value in known[c]], *base])
    slots = 2 + SIDES * len(older)
    return pl.pallas_call(
        functools.partial(older_kernel, newest, older, len(base)),
        out_shape=pltpu.VMEM((half, block), jnp.float32),
        in_specs=[vmem()] * len(operands),
        out_specs=vmem(),
        compiler_params=params(8),
        cost_estimate=pl.CostEstimate(
            flops=4 * block * block * LANES * slots, bytes_accessed=4 * block * block * slots, transcendentals=0
        ),
        name=f"older_{now}",
    )(*operands)


def relax(now, newest, plan, matrices, starts, latest, partial, keep_sum):
    half, block = starts[0].shape
    sides = 1 if partial else SIDES
    operands = near([plan, *matrices, *starts, *latest[:sides], *partial])
    value = pltpu.VMEM((half, block), jnp.float32)
    return pl.pallas_call(
        functools.partial(relax_kernel, newest, sides),
        out_shape=[value] * (1 + keep_sum),
        in_specs=[vmem()] * len(operands),
        out_specs=[vmem()] * (1 + keep_sum),
        scratch_shapes=[value] * (1 - keep_sum),
        compiler_params=params(8),
        cost_estimate=pl.CostEstimate(
            flops=16 * block * block * LANES, bytes_accessed=16 * block * block, transcendentals=0
        ),
        name=f"relax_{now}",
    )(*operands)


def per_device(residual, inv_diag, coupling_tiles, colour, tile_cols):
    axis = "rows"
    count = lax.axis_size(axis)
    groups = count // COLOURS
    me = lax.axis_index(axis)
    core = (me % 2).reshape(1)
    place = me % COLOURS
    group = me // COLOURS
    block, cols = residual.shape
    half = cols // 2
    tiles = jnp.transpose(coupling_tiles, (1, 0, 2))
    number = tiles.shape[0]

    def flip(value, bit):
        return lax.ppermute(value, axis, [(i, i ^ bit) for i in range(count)])

    def beside(value, ahead):
        pairs = []
        for i in range(count):
            step = COLOURS if (i // 2) % 2 == ahead else -COLOURS
            pairs.append((i, (i + step) % count))
        return lax.ppermute(value, axis, pairs)

    keep, send, own_rows = pl.pallas_call(
        first_kernel,
        out_shape=[pltpu.VMEM((half, block), jnp.float32)]
        + [pltpu.VMEM((half + EXTRA, block), jnp.float32), pltpu.VMEM((EXTRA, block), jnp.float32)],
        in_specs=[smem(), smem(), smem(), hbm(), hbm()],
        out_specs=[vmem()] * 3,
        scratch_shapes=[
            pltpu.VMEM((block, block), jnp.float32),
            pltpu.VMEM((block, cols), jnp.float32),
            pltpu.SemaphoreType.DMA((2,)),
        ],
        compiler_params=params(16),
        name="first",
    )(core, colour, tile_cols, *far([inv_diag, residual]))
    arrived = flip(send, 1)
    starts = [keep, arrived]

    late_tiles, late_inverse, _ = lax.optimization_barrier((tiles, inv_diag, arrived))
    sib_tiles, sib_inverse = flip(late_tiles, 1), flip(late_inverse, 1)

    own_wide, sib_wide = own_rows[:1], arrived[half : half + 1]
    candidate = jnp.where(own_wide == 0, keep, arrived[:half])
    wheel = lax.broadcasted_iota(jnp.int32, (EXTRA, block), 0).astype(jnp.float32)
    places = jnp.where(wheel == own_wide, place + 1, 0) + jnp.where(wheel == sib_wide, (place ^ 1) + 1, 0)
    places = places.astype(jnp.float32)
    sent = jnp.concatenate([candidate, places])
    swapped = flip(sent, 2)
    outer = beside(sent, 1)
    far_tiles, far_inverse, _ = lax.optimization_barrier((tiles, inv_diag, sent))
    *own_parts, zeros = parts(*far([far_tiles, far_inverse]), "own_parts")
    here = jnp.where((own_wide + zeros[:1] == 0) | (sib_wide == 0), candidate, swapped[:half])
    here = jnp.concatenate([here, places + swapped[half:]])
    known = {0: [beside(here, 0), outer, here]}
    toward = jnp.where(place < COLOURS // 2, -1, 1)
    firsts = jnp.stack([((group + step) % groups) * COLOURS for step in (toward, -toward, 0 * toward)]).astype(jnp.int32)
    *sib_parts, zeros = parts(sib_tiles, sib_inverse, "sib_parts")
    matrices = [*own_parts, *sib_parts]
    plans, masks = make_plans(number, firsts, own_rows, arrived, known[0], zeros)

    order = list(range(1, COLOURS)) + list(range(COLOURS - 2, -1, -1))
    newest = 0
    sums, used, finals = {}, {}, {}
    partial = []
    for step, now in enumerate(order):
        used[now] = {(c, done_at(order, c, step)) for c in known if c != now}
        outs = relax(now, newest, plans[now], matrices, starts, known[newest], partial, int(now in order[step + 1 :]))
        candidate, sums[now] = outs[0], outs[1:]
        finals[now] = candidate
        if step == len(order) - 1:
            break
        after = order[step + 1]
        swapped = flip(candidate, 2)
        outer = beside(candidate, 1)
        here = jnp.where(masks[now][:1] != 0, candidate, swapped)
        inner = beside(here, 0)
        fresh = used.get(after, set())
        older = tuple(c for c in sorted(known) if c not in (now, after) and (c, done_at(order, c, step)) not in fresh)
        partial = [add_older(after, now, older, plans[after], matrices, outer, here, known, sums.get(after, []))]
        known[now] = [inner, outer, here]
        newest = now

    own_final, sib_final = finals[0], finals[0]
    for c in range(1, COLOURS):
        own_final = jnp.where(own_wide == c, finals[c], own_final)
        sib_final = jnp.where(sib_wide == c, finals[c], sib_final)
    mine, other = own_final, flip(sib_final, 1)
    return pl.pallas_call(
        last_kernel,
        out_shape=jax.ShapeDtypeStruct((block, cols), jnp.float32),
        in_specs=[smem(), vmem(), vmem()],
        out_specs=vmem(),
        compiler_params=params(16),
        name="last",
    )(core, *near([mine, other]))


def done_at(order, colour, step):
    return max([i for i in range(step) if order[i] == colour], default=-1)


def solution(mesh):
    in_specs = (P("rows", None), P("rows", None), P("rows", None, None), P("rows"), P("rows", None))
    out_specs = P("rows", None)
    return jax.shard_map(
        per_device, mesh=mesh, in_specs=in_specs, out_specs=out_specs, check_vma=False
    )
```

time: 104 us -> 100 us (0.962); the launches traced: 104 us -> 101 us
  starting transfers between devices: 35.4 us -> 18.1 us
  waiting for transfers between devices: 40.4 us -> 56.9 us
  Pallas kernels: 23.8 us -> 19.7 us
  local copies, waits for them, and re-layouts: 1.36 us -> 4.44 us
    ppermute x12, starting transfers between devices: 27.3 us -> 13 us  [beside(): return lax.ppermute(value, axis, pairs)]
    ppermute x10, waiting for transfers between devices: 4.72 us -> 18.3 us  [flip(): return lax.ppermute(value, axis, [(i, i ^ bit) for i in range(count)])]
    unnamed x4 -> x10, local copies, waits for them, and re-layouts: 0.01 us -> 4.43 us
    pallas_call x17 -> x14, Pallas kernels: 20.6 us -> 16.5 us  [the longest x2 6.59 us: parts(): pl.pallas_call(parts_kernel, out_shape=[pltpu.VMEM((count + 1, block, blo...]
    ppermute x12, waiting for transfers between devices: 35.7 us -> 38.7 us  [beside(): return lax.ppermute(value, axis, pairs)]
    ppermute x10, starting transfers between devices: 8.07 us -> 5.09 us  [flip(): return lax.ppermute(value, axis, [(i, i ^ bit) for i in range(count)])]
  transfers between devices with their start and end apart: 22 -> 22, of which waited for: 13 -> 15; matrix products, arithmetic and copies ran while one was open for 2% -> 1% of each run, Pallas kernels for 17% -> 12%
where the time goes in v6:
time: 100 us; the launch traced here: 101 us
  waiting for transfers between devices  56.9 us (57%)
  Pallas kernels  19.7 us (20%)
  starting transfers between devices  18.1 us (18%)
  local copies, waits for them, and re-layouts  4.44 us (4%)
  between operations  1.05 us (1%)
    ppermute x12, waiting for transfers between devices, beside(): return lax.ppermute(value, axis, pairs)  38.7 us
    ppermute x10, waiting for transfers between devices, flip(): return lax.ppermute(value, axis, [(i, i ^ bit) for i in range(count)])  18.3 us
    ppermute x12, starting transfers between devices, beside(): return lax.ppermute(value, axis, pairs)  13 us
    pallas_call x2, Pallas kernels, parts(): pl.pallas_call(parts_kernel, out_shape=[pltpu.VMEM((count + 1, block, blo...  6.59 us
    pallas_call x5, Pallas kernels, add_older(): pl.pallas_call(functools.partial(older_kernel, newest, older, len(base)),...  5.11 us
    ppermute x10, starting transfers between devices, flip(): return lax.ppermute(value, axis, [(i, i ^ bit) for i in range(count)])  5.09 us
    unnamed x10, local copies, waits for them, and re-layouts  4.43 us
    pallas_call x6, Pallas kernels, relax(): pl.pallas_call(functools.partial(relax_kernel, newest, sides), out_shape=...  3.68 us
  transfers between devices with their start and end apart: 22, of which 15 were waited for; matrix products, arithmetic and copies ran while one was open for 1% of the time, Pallas kernels for 12%

profile of v6, /device:TPU:0, one launch (start us, length us, event | category | flops | bytes accessed | tf_op | source)
XLA Modules:
  0.0 100.9 jit_solution(14593898070947161690)
XLA Ops:
  0.7 0.6 copy-done.4
  1.3 2.4 %first.1 = (f32[64,512]{1,0:T(8,128)S(1)}, f32[72,512]{1,0:T(8,128)S(1)}, f32[8,512]{1,0:T(8,128)S(1)}) custom-call(s32[1]{0:T(128)} %bitcast.core_ref, s32[1]{0:T(128)S(6)} %copy.6.colour_ref, s32[1,6]{1,0:T(1,128)S(1)} %copy-done.4, f32[512,512]{1,0:T(8,128)} %inverse_ref, f32[512,128]{1,0:T(8,128)} %residual_hbm.1), custom_call_target="tpu_custom_call" | custom-call | tf_op jit(solution)/shard_map/first/pallas_call | solution.py:277
  3.7 0.5 collective-permute-start
  4.2 1.0 collective-permute-done.arrived.sib_start
  5.2 0.4 collective-permute-start.1
  5.6 0.2 collective-permute-start.2
  5.8 0.1 add_convert_fusion
  5.9 2.9 %collective-permute-start.3 = (f32[72,512]{1,0:T(8,128)S(1)}, f32[72,512]{1,0:T(8,128)S(1)}, u32[]{:S(2)}, u32[]{:S(2)}) collective-permute-start(f32[72,512]{1,0:T(8,128)S(1)} %pad_maximum_fusion), channel_id=1, source_target_pairs={{0,2},{1,3},{2,0},{3,1},{4,6},{5,7},{6,4},{7,5},{8,10},{9,11},{10,... | collective-permute-start | bytes 442376 | tf_op jit(solution)/shard_map/ppermute | solution.py:268
  8.8 4.5 %collective-permute-start.5 = (f32[72,512]{1,0:T(8,128)S(1)}, f32[72,512]{1,0:T(8,128)S(1)}, u32[]{:S(2)}, u32[]{:S(2)}) collective-permute-start(f32[72,512]{1,0:T(8,128)S(1)} %pad_maximum_fusion), channel_id=1, source_target_pairs={{0,28},{1,29},{2,6},{3,7},{4,0},{5,1},{6,10},{7,11},{8,4},{9,5},{1... | collective-permute-start | bytes 442376 | tf_op jit(solution)/shard_map/ppermute | solution.py:275
  13.4 3.3 %own_parts.1 = (bf16[7,512,512]{2,1,0:T(8,128)(2,1)S(1)}, bf16[7,512,512]{2,1,0:T(8,128)(2,1)S(1)}, f32[8,512]{1,0:T(8,128)S(1)}) custom-call(f32[6,512,512]{2,1,0:T(8,128)} %bitcast.8, f32[512,512]{1,0:T(8,128)} %inverse_ref), custom_call_target="tpu_custom_call" | custom-call | bytes 12582912 | tf_op jit(solution)/shard_map/own_parts/pallas_call | solution.py:189
  16.7 1.9 %copy-done = bf16[7,512,512]{2,1,0:T(8,128)(2,1)} copy-done((bf16[7,512,512]{2,1,0:T(8,128)(2,1)}, bf16[7,512,512]{2,1,0:T(8,128)(2,1)S(1)}, u32[]{:S(2)}) %copy-start) | copy-done | bytes 3670040
  18.6 1.9 %copy-done.2 = bf16[7,512,512]{2,1,0:T(8,128)(2,1)} copy-done((bf16[7,512,512]{2,1,0:T(8,128)(2,1)}, bf16[7,512,512]{2,1,0:T(8,128)(2,1)S(1)}, u32[]{:S(2)}) %copy-start.2) | copy-done | bytes 3670040
  20.5 0.1 slice_add_fusion
  20.8 0.1 pad_add_fusion.firsts_ref
  20.9 3.3 %sib_parts.1 = (bf16[7,512,512]{2,1,0:T(8,128)(2,1)S(1)}, bf16[7,512,512]{2,1,0:T(8,128)(2,1)S(1)}, f32[8,512]{1,0:T(8,128)S(1)}) custom-call(f32[6,512,512]{2,1,0:T(8,128)} %collective-permute-done.1.tiles_ref, f32[512,512]{1,0:T(8,128)S(1)} %collective-permute-done.2.inverse_ref), custom_call_target="tpu_custom_call" | custom-call | bytes 12582912 | tf_op jit(solution)/shard_map/sib_parts/pallas_call | solution.py:189
  24.2 4.6 %collective-permute-done.4.inner.refs_0_ = f32[72,512]{1,0:T(8,128)S(1)} collective-permute-done((f32[72,512]{1,0:T(8,128)S(1)}, f32[72,512]{1,0:T(8,128)S(1)}, u32[]{:S(2)}, u32[]{:S(2)}) %collective-permute-start.4) | collective-permute-done | bytes 147488 | tf_op jit(solution)/shard_map/ppermute | solution.py:275
  28.8 1.2 %plan.1 = (s32[16,128]{1,0:T(8,128)S(1)}, s32[16,128]{1,0:T(8,128)S(1)}, s32[16,128]{1,0:T(8,128)S(1)}, s32[16,128]{1,0:T(8,128)S(1)}, s32[8,512]{1,0:T(8,128)},...) custom-call(s32[3]{0:T(128)S(1)} %pad_add_fusion.firsts_ref, f32[8,512]{1,0:T(8,128)S(1)} %get-tuple-element.33._, ...), custom_call_target="tpu_custom_call" | custom-call | tf_op jit(solution)/shard_map/plan/pallas_call | solution.py:207
  29.9 0.1 relax_1.2
  30.0 0.1 collective-permute-start.6
  30.1 2.2 %collective-permute-start.8 = (f32[64,512]{1,0:T(8,128)S(1)}, f32[64,512]{1,0:T(8,128)S(1)}, u32[]{:S(2)}, u32[]{:S(2)}) collective-permute-start(f32[64,512]{1,0:T(8,128)S(1)} %get-tuple-element.47), channel_id=1, source_target_pairs={{0,28},{1,29},{2,6},{3,7},{4,0},{5,1},{6,10},{7,11},{8,4},{9,5},{1... | collective-permute-start | bytes 393224 | tf_op jit(solution)/shard_map/ppermute | solution.py:275
  32.3 2.7 %collective-permute-done.6 = f32[64,512]{1,0:T(8,128)S(1)} collective-permute-done((f32[64,512]{1,0:T(8,128)S(1)}, f32[64,512]{1,0:T(8,128)S(1)}, u32[]{:S(2)}, u32[]{:S(2)}) %collective-permute-start.6) | collective-permute-done | bytes 131104 | tf_op jit(solution)/shard_map/ppermute | solution.py:268
  35.1 1.7 %older_2.2.refs_1_ = f32[64,512]{1,0:T(8,128)S(1)} custom-call(s32[16,128]{1,0:T(8,128)S(1)} %get-tuple-element.44.plan, bf16[7,512,512]{2,1,0:T(8,128)(2,1)S(1)} %copy-done.1, bf16[7,512,512]{2,1,0:T(8,128)(2,1)S(1)} %copy-done.3, bf16[7,512,512]{2,1,0:T(8,128)(2,1)S(1)} %get-tuple-element.41.sib_high, bf16[7,512,512]{2,1,0:T(8,128)(2,1)S(1)} %get-tuple-element.42.sib_low, ...), custom_call_target="tpu_custom_call" | custom-call | flops 671088640 | bytes 5242880 | tf_op jit(solution)/shard_map/older_2/pallas_call | solution.py:222
  36.8 6.0 %collective-permute-done.7.refs_0_.refs_3_ = f32[64,512]{1,0:T(8,128)S(1)} collective-permute-done((f32[64,512]{1,0:T(8,128)S(1)}, f32[64,512]{1,0:T(8,128)S(1)}, u32[]{:S(2)}, u32[]{:S(2)}) %collective-permute-start.7) | collective-permute-done | bytes 131104 | tf_op jit(solution)/shard_map/ppermute | solution.py:275
  42.8 1.1 %relax_2.2 = (f32[64,512]{1,0:T(8,128)S(1)}, f32[64,512]{1,0:T(8,128)S(1)}) custom-call(s32[16,128]{1,0:T(8,128)S(1)} %get-tuple-element.44.plan, bf16[7,512,512]{2,1,0:T(8,128)(2,1)S(1)} %copy-done.1, bf16[7,512,512]{2,1,0:T(8,128)(2,1)S(1)} %copy-done.3, bf16[7,512,512]{2,1,0:T(8,128)(2,1)S(1)} %get-tuple-element.41.sib_high, ...), custom_call_target="tpu_custom_call" | custom-call | flops 536870912 | bytes 4194304 | tf_op jit(solution)/shard_map/relax_2/pallas_call | solution.py:240
  43.9 0.1 collective-permute-start.9
  44.0 2.3 %collective-permute-start.11 = (f32[64,512]{1,0:T(8,128)S(1)}, f32[64,512]{1,0:T(8,128)S(1)}, u32[]{:S(2)}, u32[]{:S(2)}) collective-permute-start(f32[64,512]{1,0:T(8,128)S(1)} %get-tuple-element.48), channel_id=1, source_target_pairs={{0,28},{1,29},{2,6},{3,7},{4,0},{5,1},{6,10},{7,11},{8,4},{9,5},{1... | collective-permute-start | bytes 393224 | tf_op jit(solution)/shard_map/ppermute | solution.py:275
  46.2 2.7 %collective-permute-done.9 = f32[64,512]{1,0:T(8,128)S(1)} collective-permute-done((f32[64,512]{1,0:T(8,128)S(1)}, f32[64,512]{1,0:T(8,128)S(1)}, u32[]{:S(2)}, u32[]{:S(2)}) %collective-permute-start.9) | collective-permute-done | bytes 131104 | tf_op jit(solution)/shard_map/ppermute | solution.py:268
  49.0 2.7 %older_3.1.refs_1_ = f32[64,512]{1,0:T(8,128)S(1)} custom-call(s32[16,128]{1,0:T(8,128)S(1)} %get-tuple-element.38.plan, bf16[7,512,512]{2,1,0:T(8,128)(2,1)S(1)} %copy-done.1, bf16[7,512,512]{2,1,0:T(8,128)(2,1)S(1)} %copy-done.3, bf16[7,512,512]{2,1,0:T(8,128)(2,1)S(1)} %get-tuple-element.41.sib_high, bf16[7,512,512]{2,1,0:T(8,128)(2,1)S(1)} %get-tuple-element.42.sib_low, ...), custom_call_target="tpu_custom_call" | custom-call | flops 1073741824 | bytes 8388608 | tf_op jit(solution)/shard_map/older_3/pallas_call | solution.py:222
  51.7 5.0 %collective-permute-done.10.refs_0_ = f32[64,512]{1,0:T(8,128)S(1)} collective-permute-done((f32[64,512]{1,0:T(8,128)S(1)}, f32[64,512]{1,0:T(8,128)S(1)}, u32[]{:S(2)}, u32[]{:S(2)}) %collective-permute-start.10) | collective-permute-done | bytes 131104 | tf_op jit(solution)/shard_map/ppermute | solution.py:275
  56.8 1.3 %relax_3.1 = f32[64,512]{1,0:T(8,128)S(1)} custom-call(s32[16,128]{1,0:T(8,128)S(1)} %get-tuple-element.38.plan, bf16[7,512,512]{2,1,0:T(8,128)(2,1)S(1)} %copy-done.1, bf16[7,512,512]{2,1,0:T(8,128)(2,1)S(1)} %copy-done.3, bf16[7,512,512]{2,1,0:T(8,128)(2,1)S(1)} %get-tuple-element.41.sib_high, bf16[7,512,512]{2,1,0:T(8,128)(2,1)S(1)} %get-tuple-element.42.sib_low, ...), custom_call_target="tpu_custom_call" | custom-call | flops 536870912 | bytes 4194304 | tf_op jit(solution)/shard_map/relax_3/pallas_call | solution.py:240
  58.1 1.2 %collective-permute-start.14 = (f32[64,512]{1,0:T(8,128)S(1)}, f32[64,512]{1,0:T(8,128)S(1)}, u32[]{:S(2)}, u32[]{:S(2)}) collective-permute-start(f32[64,512]{1,0:T(8,128)S(1)} %relax_3.1), channel_id=1, source_target_pairs={{0,28},{1,29},{2,6},{3,7},{4,0},{5,1},{6,10},{7,11},{8,4},{9,5},{1... | collective-permute-start | bytes 393224 | tf_op jit(solution)/shard_map/ppermute | solution.py:275
  59.3 3.7 %collective-permute-done.12 = f32[64,512]{1,0:T(8,128)S(1)} collective-permute-done((f32[64,512]{1,0:T(8,128)S(1)}, f32[64,512]{1,0:T(8,128)S(1)}, u32[]{:S(2)}, u32[]{:S(2)}) %collective-permute-start.12) | collective-permute-done | bytes 131104 | tf_op jit(solution)/shard_map/ppermute | solution.py:268
  63.2 1.2 %collective-permute-done.14.outer.refs_1_.refs_4_ = f32[64,512]{1,0:T(8,128)S(1)} collective-permute-done((f32[64,512]{1,0:T(8,128)S(1)}, f32[64,512]{1,0:T(8,128)S(1)}, u32[]{:S(2)}, u32[]{:S(2)}) %collective-permute-start.14) | collective-permute-done | bytes 131104 | tf_op jit(solution)/shard_map/ppermute | solution.py:275
  64.4 0.6 older_2.3.refs_1_
  65.0 5.8 %collective-permute-done.13.refs_0_.refs_3_ = f32[64,512]{1,0:T(8,128)S(1)} collective-permute-done((f32[64,512]{1,0:T(8,128)S(1)}, f32[64,512]{1,0:T(8,128)S(1)}, u32[]{:S(2)}, u32[]{:S(2)}) %collective-permute-start.13) | collective-permute-done | bytes 131104 | tf_op jit(solution)/shard_map/ppermute | solution.py:275
  70.8 1.1 %relax_2.3 = f32[64,512]{1,0:T(8,128)S(1)} custom-call(s32[16,128]{1,0:T(8,128)S(1)} %get-tuple-element.44.plan, bf16[7,512,512]{2,1,0:T(8,128)(2,1)S(1)} %copy-done.1, bf16[7,512,512]{2,1,0:T(8,128)(2,1)S(1)} %copy-done.3, bf16[7,512,512]{2,1,0:T(8,128)(2,1)S(1)} %get-tuple-element.41.sib_high, bf16[7,512,512]{2,1,0:T(8,128)(2,1)S(1)} %get-tuple-element.42.sib_low, ...), custom_call_target="tpu_custom_call" | custom-call | flops 536870912 | bytes 4194304 | tf_op jit(solution)/shard_map/relax_2/pallas_call | solution.py:240
  72.0 1.8 %collective-permute-start.17 = (f32[64,512]{1,0:T(8,128)S(1)}, f32[64,512]{1,0:T(8,128)S(1)}, u32[]{:S(2)}, u32[]{:S(2)}) collective-permute-start(f32[64,512]{1,0:T(8,128)S(1)} %relax_2.3), channel_id=1, source_target_pairs={{0,28},{1,29},{2,6},{3,7},{4,0},{5,1},{6,10},{7,11},{8,4},{9,5},{1... | collective-permute-start | bytes 393224 | tf_op jit(solution)/shard_map/ppermute | solution.py:275
  73.8 3.1 %collective-permute-done.15 = f32[64,512]{1,0:T(8,128)S(1)} collective-permute-done((f32[64,512]{1,0:T(8,128)S(1)}, f32[64,512]{1,0:T(8,128)S(1)}, u32[]{:S(2)}, u32[]{:S(2)}) %collective-permute-start.15) | collective-permute-done | bytes 131104 | tf_op jit(solution)/shard_map/ppermute | solution.py:268
  77.1 8.5 %collective-permute-done.16.refs_0_ = f32[64,512]{1,0:T(8,128)S(1)} collective-permute-done((f32[64,512]{1,0:T(8,128)S(1)}, f32[64,512]{1,0:T(8,128)S(1)}, u32[]{:S(2)}, u32[]{:S(2)}) %collective-permute-start.16) | collective-permute-done | bytes 131104 | tf_op jit(solution)/shard_map/ppermute | solution.py:275
  85.6 0.1 relax_1.3
  85.7 0.7 collective-permute-start.18
  86.4 0.6 collective-permute-start.20
  87.0 3.7 %collective-permute-done.18 = f32[64,512]{1,0:T(8,128)S(1)} collective-permute-done((f32[64,512]{1,0:T(8,128)S(1)}, f32[64,512]{1,0:T(8,128)S(1)}, u32[]{:S(2)}, u32[]{:S(2)}) %collective-permute-start.18) | collective-permute-done | bytes 131104 | tf_op jit(solution)/shard_map/ppermute | solution.py:268
  90.8 0.6 collective-permute-done.20.outer
  91.4 7.0 %collective-permute-done.19.refs_0_ = f32[64,512]{1,0:T(8,128)S(1)} collective-permute-done((f32[64,512]{1,0:T(8,128)S(1)}, f32[64,512]{1,0:T(8,128)S(1)}, u32[]{:S(2)}, u32[]{:S(2)}) %collective-permute-start.19) | collective-permute-done | bytes 131104 | tf_op jit(solution)/shard_map/ppermute | solution.py:275
  98.5 0.1 relax_0.1
  98.7 1.3 %collective-permute-done.21.other_ref = f32[64,512]{1,0:T(8,128)S(1)} collective-permute-done((f32[64,512]{1,0:T(8,128)S(1)}, f32[64,512]{1,0:T(8,128)S(1)}, u32[]{:S(2)}, u32[]{:S(2)}) %collective-permute-start.21) | collective-permute-done | bytes 131104 | tf_op jit(solution)/shard_map/ppermute | solution.py:268
  100.0 0.8 last.1
  (43 shorter events, 1.1 us)
Async XLA Ops:
  0.7 0.7 copy-start.4
  3.7 1.5 %collective-permute-start = (f32[72,512]{1,0:T(8,128)S(1)}, f32[72,512]{1,0:T(8,128)S(1)}, u32[]{:S(2)}, u32[]{:S(2)}) collective-permute-start(f32[72,512]{1,0:T(8,128)S(1)} %get-tuple-element.30), channel_id=1, source_target_pairs={{0,1},{1,0},{2,3},{3,2},{4,5},{5,4},{6,7},{7,6},{8,9},{9,8},{10,11... | collective-permute-start | bytes 442376 | tf_op jit(solution)/shard_map/ppermute | solution.py:268
  5.2 15.7 %collective-permute-start.1 = (f32[6,512,512]{2,1,0:T(8,128)}, f32[6,512,512]{2,1,0:T(8,128)}, u32[]{:S(2)}, u32[]{:S(2)}) collective-permute-start(f32[6,512,512]{2,1,0:T(8,128)} %bitcast.7), channel_id=1, source_target_pairs={{0,1},{1,0},{2,3},{3,2},{4,5},{5,4},{6,7},{7,6},{8,9},{9,8},{10,11... | collective-permute-start | bytes 18874376 | tf_op jit(solution)/shard_map/ppermute | solution.py:268
  5.6 15.3 %collective-permute-start.2 = (f32[512,512]{1,0:T(8,128)}, f32[512,512]{1,0:T(8,128)S(1)}, u32[]{:S(2)}, u32[]{:S(2)}) collective-permute-start(f32[512,512]{1,0:T(8,128)} %inverse_ref), channel_id=1, source_target_pairs={{0,1},{1,0},{2,3},{3,2},{4,5},{5,4},{6,7},{7,6},{8,9},{9,8},{10,11... | collective-permute-start | bytes 3145736 | tf_op jit(solution)/shard_map/ppermute | solution.py:268
  5.9 14.6 %collective-permute-start.3 = (f32[72,512]{1,0:T(8,128)S(1)}, f32[72,512]{1,0:T(8,128)S(1)}, u32[]{:S(2)}, u32[]{:S(2)}) collective-permute-start(f32[72,512]{1,0:T(8,128)S(1)} %pad_maximum_fusion), channel_id=1, source_target_pairs={{0,2},{1,3},{2,0},{3,1},{4,6},{5,7},{6,4},{7,5},{8,10},{9,11},{10,... | collective-permute-start | bytes 442376 | tf_op jit(solution)/shard_map/ppermute | solution.py:268
  8.8 15.4 %collective-permute-start.5 = (f32[72,512]{1,0:T(8,128)S(1)}, f32[72,512]{1,0:T(8,128)S(1)}, u32[]{:S(2)}, u32[]{:S(2)}) collective-permute-start(f32[72,512]{1,0:T(8,128)S(1)} %pad_maximum_fusion), channel_id=1, source_target_pairs={{0,28},{1,29},{2,6},{3,7},{4,0},{5,1},{6,10},{7,11},{8,4},{9,5},{1... | collective-permute-start | bytes 442376 | tf_op jit(solution)/shard_map/ppermute | solution.py:275
  16.7 1.9 %copy-start = (bf16[7,512,512]{2,1,0:T(8,128)(2,1)}, bf16[7,512,512]{2,1,0:T(8,128)(2,1)S(1)}, u32[]{:S(2)}) copy-start(bf16[7,512,512]{2,1,0:T(8,128)(2,1)S(1)} %get-tuple-element.39.own_high) | copy-start | bytes 11010052
  18.6 1.9 %copy-start.2 = (bf16[7,512,512]{2,1,0:T(8,128)(2,1)}, bf16[7,512,512]{2,1,0:T(8,128)(2,1)S(1)}, u32[]{:S(2)}) copy-start(bf16[7,512,512]{2,1,0:T(8,128)(2,1)S(1)} %get-tuple-element.40.own_low) | copy-start | bytes 11010052
  20.7 8.1 %collective-permute-start.4 = (f32[72,512]{1,0:T(8,128)S(1)}, f32[72,512]{1,0:T(8,128)S(1)}, u32[]{:S(2)}, u32[]{:S(2)}) collective-permute-start(f32[72,512]{1,0:T(8,128)S(1)} %pad_maximum_fusion.1.here.refs_2_), channel_id=1, source_target_pairs={{0,4},{1,5},{2,30},{3,31},{4,8},{5,9},{6,2},{7,3},{8,12},{9,13},{1... | collective-permute-start | bytes 442376 | tf_op jit(solution)/shard_map/ppermute | solution.py:275
  20.9 9.0 %copy-start.1 = (bf16[7,512,512]{2,1,0:T(8,128)(2,1)S(1)}, bf16[7,512,512]{2,1,0:T(8,128)(2,1)}, u32[]{:S(2)}) copy-start(bf16[7,512,512]{2,1,0:T(8,128)(2,1)} %copy-done) | copy-start | bytes 11010052
  20.9 9.0 %copy-start.3 = (bf16[7,512,512]{2,1,0:T(8,128)(2,1)S(1)}, bf16[7,512,512]{2,1,0:T(8,128)(2,1)}, u32[]{:S(2)}) copy-start(bf16[7,512,512]{2,1,0:T(8,128)(2,1)} %copy-done.2) | copy-start | bytes 11010052
  30.0 5.0 %collective-permute-start.6 = (f32[64,512]{1,0:T(8,128)S(1)}, f32[64,512]{1,0:T(8,128)S(1)}, u32[]{:S(2)}, u32[]{:S(2)}) collective-permute-start(f32[64,512]{1,0:T(8,128)S(1)} %get-tuple-element.47), channel_id=1, source_target_pairs={{0,2},{1,3},{2,0},{3,1},{4,6},{5,7},{6,4},{7,5},{8,10},{9,11},{10,... | collective-permute-start | bytes 393224 | tf_op jit(solution)/shard_map/ppermute | solution.py:268
  30.1 5.0 %collective-permute-start.8 = (f32[64,512]{1,0:T(8,128)S(1)}, f32[64,512]{1,0:T(8,128)S(1)}, u32[]{:S(2)}, u32[]{:S(2)}) collective-permute-start(f32[64,512]{1,0:T(8,128)S(1)} %get-tuple-element.47), channel_id=1, source_target_pairs={{0,28},{1,29},{2,6},{3,7},{4,0},{5,1},{6,10},{7,11},{8,4},{9,5},{1... | collective-permute-start | bytes 393224 | tf_op jit(solution)/shard_map/ppermute | solution.py:275
  35.1 7.7 %collective-permute-start.7 = (f32[64,512]{1,0:T(8,128)S(1)}, f32[64,512]{1,0:T(8,128)S(1)}, u32[]{:S(2)}, u32[]{:S(2)}) collective-permute-start(f32[64,512]{1,0:T(8,128)S(1)} %broadcast_select_fusion.2.here.refs_5_), channel_id=1, source_target_pairs={{0,4},{1,5},{2,30},{3,31},{4,8},{5,9},{6,2},{7,3},{8,12},{9,13},{1... | collective-permute-start | bytes 393224 | tf_op jit(solution)/shard_map/ppermute | solution.py:275
  43.9 5.0 %collective-permute-start.9 = (f32[64,512]{1,0:T(8,128)S(1)}, f32[64,512]{1,0:T(8,128)S(1)}, u32[]{:S(2)}, u32[]{:S(2)}) collective-permute-start(f32[64,512]{1,0:T(8,128)S(1)} %get-tuple-element.48), channel_id=1, source_target_pairs={{0,2},{1,3},{2,0},{3,1},{4,6},{5,7},{6,4},{7,5},{8,10},{9,11},{10,... | collective-permute-start | bytes 393224 | tf_op jit(solution)/shard_map/ppermute | solution.py:268
  44.0 5.0 %collective-permute-start.11 = (f32[64,512]{1,0:T(8,128)S(1)}, f32[64,512]{1,0:T(8,128)S(1)}, u32[]{:S(2)}, u32[]{:S(2)}) collective-permute-start(f32[64,512]{1,0:T(8,128)S(1)} %get-tuple-element.48), channel_id=1, source_target_pairs={{0,28},{1,29},{2,6},{3,7},{4,0},{5,1},{6,10},{7,11},{8,4},{9,5},{1... | collective-permute-start | bytes 393224 | tf_op jit(solution)/shard_map/ppermute | solution.py:275
  48.9 7.8 %collective-permute-start.10 = (f32[64,512]{1,0:T(8,128)S(1)}, f32[64,512]{1,0:T(8,128)S(1)}, u32[]{:S(2)}, u32[]{:S(2)}) collective-permute-start(f32[64,512]{1,0:T(8,128)S(1)} %broadcast_select_fusion.4.here), channel_id=1, source_target_pairs={{0,4},{1,5},{2,30},{3,31},{4,8},{5,9},{6,2},{7,3},{8,12},{9,13},{1... | collective-permute-start | bytes 393224 | tf_op jit(solution)/shard_map/ppermute | solution.py:275
  58.0 5.0 %collective-permute-start.12 = (f32[64,512]{1,0:T(8,128)S(1)}, f32[64,512]{1,0:T(8,128)S(1)}, u32[]{:S(2)}, u32[]{:S(2)}) collective-permute-start(f32[64,512]{1,0:T(8,128)S(1)} %relax_3.1), channel_id=1, source_target_pairs={{0,2},{1,3},{2,0},{3,1},{4,6},{5,7},{6,4},{7,5},{8,10},{9,11},{10,... | collective-permute-start | bytes 393224 | tf_op jit(solution)/shard_map/ppermute | solution.py:268
  58.1 6.2 %collective-permute-start.14 = (f32[64,512]{1,0:T(8,128)S(1)}, f32[64,512]{1,0:T(8,128)S(1)}, u32[]{:S(2)}, u32[]{:S(2)}) collective-permute-start(f32[64,512]{1,0:T(8,128)S(1)} %relax_3.1), channel_id=1, source_target_pairs={{0,28},{1,29},{2,6},{3,7},{4,0},{5,1},{6,10},{7,11},{8,4},{9,5},{1... | collective-permute-start | bytes 393224 | tf_op jit(solution)/shard_map/ppermute | solution.py:275
  63.1 7.7 %collective-permute-start.13 = (f32[64,512]{1,0:T(8,128)S(1)}, f32[64,512]{1,0:T(8,128)S(1)}, u32[]{:S(2)}, u32[]{:S(2)}) collective-permute-start(f32[64,512]{1,0:T(8,128)S(1)} %broadcast_select_fusion.here.refs_2_.refs_5_), channel_id=1, source_target_pairs={{0,4},{1,5},{2,30},{3,31},{4,8},{5,9},{6,2},{7,3},{8,12},{9,13},{1... | collective-permute-start | bytes 393224 | tf_op jit(solution)/shard_map/ppermute | solution.py:275
  71.9 5.0 %collective-permute-start.15 = (f32[64,512]{1,0:T(8,128)S(1)}, f32[64,512]{1,0:T(8,128)S(1)}, u32[]{:S(2)}, u32[]{:S(2)}) collective-permute-start(f32[64,512]{1,0:T(8,128)S(1)} %relax_2.3), channel_id=1, source_target_pairs={{0,2},{1,3},{2,0},{3,1},{4,6},{5,7},{6,4},{7,5},{8,10},{9,11},{10,... | collective-permute-start | bytes 393224 | tf_op jit(solution)/shard_map/ppermute | solution.py:268
  72.0 5.1 %collective-permute-start.17 = (f32[64,512]{1,0:T(8,128)S(1)}, f32[64,512]{1,0:T(8,128)S(1)}, u32[]{:S(2)}, u32[]{:S(2)}) collective-permute-start(f32[64,512]{1,0:T(8,128)S(1)} %relax_2.3), channel_id=1, source_target_pairs={{0,28},{1,29},{2,6},{3,7},{4,0},{5,1},{6,10},{7,11},{8,4},{9,5},{1... | collective-permute-start | bytes 393224 | tf_op jit(solution)/shard_map/ppermute | solution.py:275
  76.9 8.7 %collective-permute-start.16 = (f32[64,512]{1,0:T(8,128)S(1)}, f32[64,512]{1,0:T(8,128)S(1)}, u32[]{:S(2)}, u32[]{:S(2)}) collective-permute-start(f32[64,512]{1,0:T(8,128)S(1)} %broadcast_select_fusion.3.here.refs_2_), channel_id=1, source_target_pairs={{0,4},{1,5},{2,30},{3,31},{4,8},{5,9},{6,2},{7,3},{8,12},{9,13},{1... | collective-permute-start | bytes 393224 | tf_op jit(solution)/shard_map/ppermute | solution.py:275
  85.7 5.0 %collective-permute-start.18 = (f32[64,512]{1,0:T(8,128)S(1)}, f32[64,512]{1,0:T(8,128)S(1)}, u32[]{:S(2)}, u32[]{:S(2)}) collective-permute-start(f32[64,512]{1,0:T(8,128)S(1)} %relax_1.3), channel_id=1, source_target_pairs={{0,2},{1,3},{2,0},{3,1},{4,6},{5,7},{6,4},{7,5},{8,10},{9,11},{10,... | collective-permute-start | bytes 393224 | tf_op jit(solution)/shard_map/ppermute | solution.py:268
  86.4 5.0 %collective-permute-start.20 = (f32[64,512]{1,0:T(8,128)S(1)}, f32[64,512]{1,0:T(8,128)S(1)}, u32[]{:S(2)}, u32[]{:S(2)}) collective-permute-start(f32[64,512]{1,0:T(8,128)S(1)} %relax_1.3), channel_id=1, source_target_pairs={{0,28},{1,29},{2,6},{3,7},{4,0},{5,1},{6,10},{7,11},{8,4},{9,5},{1... | collective-permute-start | bytes 393224 | tf_op jit(solution)/shard_map/ppermute | solution.py:275
  90.8 7.7 %collective-permute-start.19 = (f32[64,512]{1,0:T(8,128)S(1)}, f32[64,512]{1,0:T(8,128)S(1)}, u32[]{:S(2)}, u32[]{:S(2)}) collective-permute-start(f32[64,512]{1,0:T(8,128)S(1)} %broadcast_select_fusion.1.here), channel_id=1, source_target_pairs={{0,4},{1,5},{2,30},{3,31},{4,8},{5,9},{6,2},{7,3},{8,12},{9,13},{1... | collective-permute-start | bytes 393224 | tf_op jit(solution)/shard_map/ppermute | solution.py:275
  98.6 1.4 %collective-permute-start.21 = (f32[64,512]{1,0:T(8,128)S(1)}, f32[64,512]{1,0:T(8,128)S(1)}, u32[]{:S(2)}, u32[]{:S(2)}) collective-permute-start(f32[64,512]{1,0:T(8,128)S(1)} %get-tuple-element.60), channel_id=1, source_target_pairs={{0,1},{1,0},{2,3},{3,2},{4,5},{5,4},{6,7},{7,6},{8,9},{9,8},{10,11... | collective-permute-start | bytes 393224 | tf_op jit(solution)/shard_map/ppermute | solution.py:268

commit v7 on v6

--- a/solution.py
+++ b/solution.py
@@ -89,19 +89,28 @@
     out_ref[...] = jnp.transpose(jnp.concatenate([first, second], axis=0))
 
 
-def parts_kernel(tiles_ref, inverse_ref, w_high, w_low, zeros, buffer, sems):
+def parts_kernel(stored, tiles_ref, inverse_ref, w_high, w_low, zeros, buffer, sems, *held):
     zeros[...] = jnp.zeros_like(zeros)
     tiles = tiles_ref.shape[0]
-    copies = [pltpu.make_async_copy(tiles_ref.at[k], buffer.at[k], sems.at[k]) for k in range(tiles)]
-    copies.append(pltpu.make_async_copy(inverse_ref, buffer.at[tiles], sems.at[tiles]))
+    copies = [pltpu.make_async_copy(tiles_ref.at[k], buffer.at[k], sems.at[0, k]) for k in range(tiles)]
+    copies.append(pltpu.make_async_copy(inverse_ref, buffer.at[tiles], sems.at[0, tiles]))
     for copy in copies:
         copy.start()
+    high, low = held if stored else (w_high, w_low)
+    stores = []
     for k, copy in enumerate(copies):
         copy.wait()
-        w_high[k], w_low[k] = split(buffer[k])
-
-
-def plan_kernel(tiles, firsts_ref, _, own_rows, arrived, inner, outer, here, *outs):
+        high[k], low[k] = split(buffer[k])
+        if stored:
+            stores.append(pltpu.make_async_copy(high.at[k], w_high.at[k], sems.at[1, k]))
+            stores.append(pltpu.make_async_copy(low.at[k], w_low.at[k], sems.at[2, k]))
+            stores[-2].start()
+            stores[-1].start()
+    for store in stores:
+        store.wait()
+
+
+def plan_kernel(tiles, colours, firsts_ref, _, own_rows, arrived, inner, outer, here, *outs):
     half = arrived.shape[0] - EXTRA
     lanes = pl.ds(0, LANES)
     own = own_rows[:, lanes].astype(jnp.int32)
@@ -112,7 +121,7 @@
         wanted.append(jnp.where(found > 0, firsts_ref[side] + found - 1, -1))
     rows = outs[0].shape[0]
     row = lax.broadcasted_iota(jnp.int32, (rows, LANES), 0)
-    for now in range(COLOURS):
+    for i, now in enumerate(colours):
         is_own, is_sib = own[:1] == now, sib[:1] == now
         active = (is_own | is_sib).astype(jnp.int32)
         plan = jnp.where(row == ACTIVE, active, is_own.astype(jnp.int32))
@@ -123,8 +132,8 @@
                 found = jnp.where(wanted[side] == listed[k], k, found)
             for c in range(COLOURS):
                 plan = jnp.where(row == TILE + side * COLOURS + c, found[c : c + 1], plan)
-        outs[now][...] = plan
-        mask = outs[COLOURS + now]
+        outs[i][...] = plan
+        mask = outs[len(colours) + i]
         mask[...] = jnp.concatenate([jnp.broadcast_to(active, (EXTRA, LANES))] * (mask.shape[1] // LANES), axis=1)
 
 
@@ -184,35 +193,36 @@
         out[...] = jnp.zeros_like(out)
 
 
-def parts(tiles, inverse, name):
+def parts(tiles, inverse, stored, name):
     count, block, _ = tiles.shape
+    shape = (count + 1, block, block)
+    space = pltpu.HBM if stored else pltpu.VMEM
     return pl.pallas_call(
-        parts_kernel,
-        out_shape=[pltpu.VMEM((count + 1, block, block), jnp.bfloat16)] * 2 + [pltpu.VMEM((EXTRA, block), jnp.float32)],
+        functools.partial(parts_kernel, stored),
+        out_shape=[space(shape, jnp.bfloat16)] * 2 + [pltpu.VMEM((EXTRA, block), jnp.float32)],
         in_specs=[anywhere()] * 2,
-        out_specs=[vmem()] * 3,
-        scratch_shapes=[
-            pltpu.VMEM((count + 1, block, block), jnp.float32),
-            pltpu.SemaphoreType.DMA((count + 1,)),
-        ],
-        compiler_params=params(12),
+        out_specs=[hbm() if stored else vmem()] * 2 + [vmem()],
+        scratch_shapes=[pltpu.VMEM(shape, jnp.float32), pltpu.SemaphoreType.DMA((3, count + 1))]
+        + [pltpu.VMEM(shape, jnp.bfloat16)] * (2 * stored),
+        compiler_params=params(20 if stored else 12),
         cost_estimate=pl.CostEstimate(flops=0, bytes_accessed=8 * count * block * block, transcendentals=0),
         name=name,
     )(tiles, inverse)
 
 
-def make_plans(tiles, firsts, own_rows, arrived, first_known, zeros):
+def make_plans(tiles, colours, firsts, own_rows, arrived, first_known, zeros):
     block = own_rows.shape[1]
     rows = -(-(TILE + SIDES * COLOURS) // EXTRA) * EXTRA
+    number = len(colours)
     outs = pl.pallas_call(
-        functools.partial(plan_kernel, tiles),
-        out_shape=[pltpu.VMEM((rows, LANES), jnp.int32)] * COLOURS + [pltpu.VMEM((EXTRA, block), jnp.int32)] * COLOURS,
+        functools.partial(plan_kernel, tiles, colours),
+        out_shape=[pltpu.VMEM((rows, LANES), jnp.int32)] * number + [pltpu.VMEM((EXTRA, block), jnp.int32)] * number,
         in_specs=[smem()] + [vmem()] * 6,
-        out_specs=[vmem()] * (2 * COLOURS),
+        out_specs=[vmem()] * (2 * number),
         compiler_params=params(8),
-        name="plan",
+        name=f"plan_{number}",
     )(firsts, *near([zeros, own_rows, arrived, *first_known]))
-    return outs[:COLOURS], outs[COLOURS:]
+    return dict(zip(colours, outs[:number])), dict(zip(colours, outs[number:]))
 
 
 def add_older(now, newest, older, plan, matrices, outer, here, known, base):
@@ -303,17 +313,17 @@
     swapped = flip(sent, 2)
     outer = beside(sent, 1)
     far_tiles, far_inverse, _ = lax.optimization_barrier((tiles, inv_diag, sent))
-    *own_parts, zeros = parts(*far([far_tiles, far_inverse]), "own_parts")
+    *own_parts, zeros = parts(*far([far_tiles, far_inverse]), 1, "own_parts")
     here = jnp.where((own_wide + zeros[:1] == 0) | (sib_wide == 0), candidate, swapped[:half])
     here = jnp.concatenate([here, places + swapped[half:]])
     known = {0: [beside(here, 0), outer, here]}
     toward = jnp.where(place < COLOURS // 2, -1, 1)
     firsts = jnp.stack([((group + step) % groups) * COLOURS for step in (toward, -toward, 0 * toward)]).astype(jnp.int32)
-    *sib_parts, zeros = parts(sib_tiles, sib_inverse, "sib_parts")
+    *sib_parts, zeros = parts(sib_tiles, sib_inverse, 0, "sib_parts")
     matrices = [*own_parts, *sib_parts]
-    plans, masks = make_plans(number, firsts, own_rows, arrived, known[0], zeros)
-
+    facts = (firsts, own_rows, arrived, known[0])
     order = list(range(1, COLOURS)) + list(range(COLOURS - 2, -1, -1))
+    plans, masks = make_plans(number, order[:1], *facts, zeros)
     newest = 0
     sums, used, finals = {}, {}, {}
     partial = []
@@ -324,6 +334,10 @@
         finals[now] = candidate
         if step == len(order) - 1:
             break
+        if step == 0:
+            rest = [c for c in range(COLOURS) if c not in plans]
+            for table, more in zip((plans, masks), make_plans(number, rest, *facts, candidate)):
+                table.update(more)
         after = order[step + 1]
         swapped = flip(candidate, 2)
         outer = beside(candidate, 1)

time: 100 us -> 98.8 us (0.988); the launches traced: 101 us -> 98.2 us
  local copies, waits for them, and re-layouts: 4.44 us -> 0.66 us
  Pallas kernels: 19.7 us -> 23.3 us
  waiting for transfers between devices: 56.9 us -> 55.6 us
  starting transfers between devices: 18.1 us -> 16.9 us
    unnamed x10 -> x6, local copies, waits for them, and re-layouts: 4.43 us -> 0.66 us
    pallas_call x3 -> x4, Pallas kernels: 7.74 us -> 11.4 us  [the longest x2 9.64 us: parts(): pl.pallas_call(functools.partial(parts_kernel, stored), out_shape=[space(...]
    ppermute x12, waiting for transfers between devices: 38.7 us -> 36.1 us  [beside(): return lax.ppermute(value, axis, pairs)]
    ppermute x10, waiting for transfers between devices: 18.3 us -> 19.5 us  [flip(): return lax.ppermute(value, axis, [(i, i ^ bit) for i in range(count)])]
  transfers between devices with their start and end apart: 22 -> 22, of which waited for: 15 -> 14; matrix products, arithmetic and copies ran while one was open for 1% -> 1% of each run, Pallas kernels for 12% -> 17%
where the time goes in v7:
time: 98.8 us; the launch traced here: 98.2 us
  waiting for transfers between devices  55.6 us (56%)
  Pallas kernels  23.3 us (24%)
  starting transfers between devices  16.9 us (17%)
  between operations  1.07 us (1%)
    ppermute x12, waiting for transfers between devices, beside(): return lax.ppermute(value, axis, pairs)  36.1 us
    ppermute x10, waiting for transfers between devices, flip(): return lax.ppermute(value, axis, [(i, i ^ bit) for i in range(count)])  19.5 us
    ppermute x12, starting transfers between devices, beside(): return lax.ppermute(value, axis, pairs)  12.5 us
    pallas_call x2, Pallas kernels, parts(): pl.pallas_call(functools.partial(parts_kernel, stored), out_shape=[space(...  9.64 us
    pallas_call x5, Pallas kernels, add_older(): pl.pallas_call(functools.partial(older_kernel, newest, older, len(base)),...  5.5 us
    ppermute x10, starting transfers between devices, flip(): return lax.ppermute(value, axis, [(i, i ^ bit) for i in range(count)])  4.43 us
    pallas_call x6, Pallas kernels, relax(): pl.pallas_call(functools.partial(relax_kernel, newest, sides), out_shape=...  3.29 us
    pallas_call x1, Pallas kernels, per_device(): pl.pallas_call(first_kernel, out_shape=[pltpu.VMEM((half, block), jnp.flo...  2.35 us
  transfers between devices with their start and end apart: 22, of which 14 were waited for; matrix products, arithmetic and copies ran while one was open for 1% of the time, Pallas kernels for 17%

profile of v7, /device:TPU:0, one launch (start us, length us, event | category | flops | bytes accessed | tf_op | source)
XLA Modules:
  0.0 98.2 jit_solution(13920923371920105187)
XLA Ops:
  0.7 0.6 copy-done.2
  1.3 2.4 %first.1 = (f32[64,512]{1,0:T(8,128)S(1)}, f32[72,512]{1,0:T(8,128)S(1)}, f32[8,512]{1,0:T(8,128)S(1)}) custom-call(s32[1]{0:T(128)} %bitcast.core_ref, s32[1]{0:T(128)S(6)} %copy.6.colour_ref, s32[1,6]{1,0:T(1,128)S(1)} %copy-done.2, f32[512,512]{1,0:T(8,128)} %inverse_ref, f32[512,128]{1,0:T(8,128)} %residual_hbm.1), custom_call_target="tpu_custom_call" | custom-call | tf_op jit(solution)/shard_map/first/pallas_call | solution.py:287
  3.7 0.5 collective-permute-start
  4.2 1.0 %collective-permute-done.arrived.sib_start = f32[72,512]{1,0:T(8,128)S(1)} collective-permute-done((f32[72,512]{1,0:T(8,128)S(1)}, f32[72,512]{1,0:T(8,128)S(1)}, u32[]{:S(2)}, u32[]{:S(2)}) %collective-permute-start) | collective-permute-done | bytes 147488 | tf_op jit(solution)/shard_map/ppermute | solution.py:278
  5.2 0.4 collective-permute-start.1
  5.6 0.2 collective-permute-start.2
  5.8 0.1 add_convert_fusion
  5.9 2.9 %collective-permute-start.3 = (f32[72,512]{1,0:T(8,128)S(1)}, f32[72,512]{1,0:T(8,128)S(1)}, u32[]{:S(2)}, u32[]{:S(2)}) collective-permute-start(f32[72,512]{1,0:T(8,128)S(1)} %pad_maximum_fusion), channel_id=1, source_target_pairs={{0,2},{1,3},{2,0},{3,1},{4,6},{5,7},{6,4},{7,5},{8,10},{9,11},{10,... | collective-permute-start | bytes 442376 | tf_op jit(solution)/shard_map/ppermute | solution.py:278
  8.8 4.5 %collective-permute-start.5 = (f32[72,512]{1,0:T(8,128)S(1)}, f32[72,512]{1,0:T(8,128)S(1)}, u32[]{:S(2)}, u32[]{:S(2)}) collective-permute-start(f32[72,512]{1,0:T(8,128)S(1)} %pad_maximum_fusion), channel_id=1, source_target_pairs={{0,28},{1,29},{2,6},{3,7},{4,0},{5,1},{6,10},{7,11},{8,4},{9,5},{1... | collective-permute-start | bytes 442376 | tf_op jit(solution)/shard_map/ppermute | solution.py:285
  13.4 6.2 %own_parts.1 = (bf16[7,512,512]{2,1,0:T(8,128)(2,1)}, bf16[7,512,512]{2,1,0:T(8,128)(2,1)}, f32[8,512]{1,0:T(8,128)S(1)}) custom-call(f32[6,512,512]{2,1,0:T(8,128)} %bitcast.8, f32[512,512]{1,0:T(8,128)} %inverse_ref), custom_call_target="tpu_custom_call" | custom-call | bytes 12582912 | tf_op jit(solution)/shard_map/own_parts/pallas_call | solution.py:200
  19.7 0.1 slice_add_fusion
  19.9 0.1 pad_add_fusion.firsts_ref
  20.0 3.4 %sib_parts.1 = (bf16[7,512,512]{2,1,0:T(8,128)(2,1)S(1)}, bf16[7,512,512]{2,1,0:T(8,128)(2,1)S(1)}, f32[8,512]{1,0:T(8,128)S(1)}) custom-call(f32[6,512,512]{2,1,0:T(8,128)} %collective-permute-done.1.tiles_ref, f32[512,512]{1,0:T(8,128)S(1)} %collective-permute-done.2.inverse_ref), custom_call_target="tpu_custom_call" | custom-call | bytes 12582912 | tf_op jit(solution)/shard_map/sib_parts/pallas_call | solution.py:200
  23.5 4.4 %collective-permute-done.4.inner.refs_0_ = f32[72,512]{1,0:T(8,128)S(1)} collective-permute-done((f32[72,512]{1,0:T(8,128)S(1)}, f32[72,512]{1,0:T(8,128)S(1)}, u32[]{:S(2)}, u32[]{:S(2)}) %collective-permute-start.4) | collective-permute-done | bytes 147488 | tf_op jit(solution)/shard_map/ppermute | solution.py:285
  27.9 0.6 plan_1.1
  28.5 1.2 %relax_1.2 = (f32[64,512]{1,0:T(8,128)S(1)}, f32[64,512]{1,0:T(8,128)S(1)}) custom-call(s32[16,128]{1,0:T(8,128)S(1)} %get-tuple-element.38.plan, bf16[7,512,512]{2,1,0:T(8,128)(2,1)S(1)} %copy-done, bf16[7,512,512]{2,1,0:T(8,128)(2,1)S(1)} %copy-done.1, bf16[7,512,512]{2,1,0:T(8,128)(2,1)S(1)} %get-tuple-element.41.sib_high, ...), custom_call_target="tpu_custom_call" | custom-call | flops 536870912 | bytes 4194304 | tf_op jit(solution)/shard_map/relax_1/pallas_call | solution.py:250
  29.7 0.1 collective-permute-start.6
  29.7 1.3 %collective-permute-start.8 = (f32[64,512]{1,0:T(8,128)S(1)}, f32[64,512]{1,0:T(8,128)S(1)}, u32[]{:S(2)}, u32[]{:S(2)}) collective-permute-start(f32[64,512]{1,0:T(8,128)S(1)} %get-tuple-element.43._), channel_id=1, source_target_pairs={{0,28},{1,29},{2,6},{3,7},{4,0},{5,1},{6,10},{7,11},{8,4},{9,5},{1... | collective-permute-start | bytes 393224 | tf_op jit(solution)/shard_map/ppermute | solution.py:285
  31.0 3.6 %collective-permute-done.6 = f32[64,512]{1,0:T(8,128)S(1)} collective-permute-done((f32[64,512]{1,0:T(8,128)S(1)}, f32[64,512]{1,0:T(8,128)S(1)}, u32[]{:S(2)}, u32[]{:S(2)}) %collective-permute-start.6) | collective-permute-done | bytes 131104 | tf_op jit(solution)/shard_map/ppermute | solution.py:278
  34.8 1.2 %plan_3.1 = (s32[16,128]{1,0:T(8,128)S(1)}, s32[16,128]{1,0:T(8,128)S(1)}, s32[16,128]{1,0:T(8,128)S(1)}, s32[8,512]{1,0:T(8,128)}, s32[8,512]{1,0:T(8,128)S(1)}, /*index=5*/s32[8,512]{1,0:T(8,128)S(1)}) custom-call(s32[3]{0:T(128)S(1)} %pad_add_fusion.firsts_ref, f32[64,512]{1,0:T(8,128)S(1)} %get-tuple-element.43._, ...), custom_call_target="tpu_custom_call" | custom-call | tf_op jit(solution)/shard_map/plan_3/pallas_call | solution.py:217
  36.0 6.5 %collective-permute-done.7.refs_0_.refs_3_ = f32[64,512]{1,0:T(8,128)S(1)} collective-permute-done((f32[64,512]{1,0:T(8,128)S(1)}, f32[64,512]{1,0:T(8,128)S(1)}, u32[]{:S(2)}, u32[]{:S(2)}) %collective-permute-start.7) | collective-permute-done | bytes 131104 | tf_op jit(solution)/shard_map/ppermute | solution.py:285
  42.5 0.1 relax_2.2
  42.6 0.1 collective-permute-start.9
  42.7 1.8 %collective-permute-start.11 = (f32[64,512]{1,0:T(8,128)S(1)}, f32[64,512]{1,0:T(8,128)S(1)}, u32[]{:S(2)}, u32[]{:S(2)}) collective-permute-start(f32[64,512]{1,0:T(8,128)S(1)} %get-tuple-element.48), channel_id=1, source_target_pairs={{0,28},{1,29},{2,6},{3,7},{4,0},{5,1},{6,10},{7,11},{8,4},{9,5},{1... | collective-permute-start | bytes 393224 | tf_op jit(solution)/shard_map/ppermute | solution.py:285
  44.5 3.1 %collective-permute-done.9 = f32[64,512]{1,0:T(8,128)S(1)} collective-permute-done((f32[64,512]{1,0:T(8,128)S(1)}, f32[64,512]{1,0:T(8,128)S(1)}, u32[]{:S(2)}, u32[]{:S(2)}) %collective-permute-start.9) | collective-permute-done | bytes 131104 | tf_op jit(solution)/shard_map/ppermute | solution.py:278
  47.7 3.2 %older_3.1.refs_1_ = f32[64,512]{1,0:T(8,128)S(1)} custom-call(s32[16,128]{1,0:T(8,128)S(1)} %get-tuple-element.44.plan, bf16[7,512,512]{2,1,0:T(8,128)(2,1)S(1)} %copy-done, bf16[7,512,512]{2,1,0:T(8,128)(2,1)S(1)} %copy-done.1, bf16[7,512,512]{2,1,0:T(8,128)(2,1)S(1)} %get-tuple-element.41.sib_high, bf16[7,512,512]{2,1,0:T(8,128)(2,1)S(1)} %get-tuple-element.42.sib_low, ...), custom_call_target="tpu_custom_call" | custom-call | flops 1073741824 | bytes 8388608 | tf_op jit(solution)/shard_map/older_3/pallas_call | solution.py:232
  50.9 4.5 %collective-permute-done.10.refs_0_ = f32[64,512]{1,0:T(8,128)S(1)} collective-permute-done((f32[64,512]{1,0:T(8,128)S(1)}, f32[64,512]{1,0:T(8,128)S(1)}, u32[]{:S(2)}, u32[]{:S(2)}) %collective-permute-start.10) | collective-permute-done | bytes 131104 | tf_op jit(solution)/shard_map/ppermute | solution.py:285
  55.4 0.8 relax_3.1
  56.2 0.1 collective-permute-start.12
  56.3 1.3 %collective-permute-start.14 = (f32[64,512]{1,0:T(8,128)S(1)}, f32[64,512]{1,0:T(8,128)S(1)}, u32[]{:S(2)}, u32[]{:S(2)}) collective-permute-start(f32[64,512]{1,0:T(8,128)S(1)} %relax_3.1), channel_id=1, source_target_pairs={{0,28},{1,29},{2,6},{3,7},{4,0},{5,1},{6,10},{7,11},{8,4},{9,5},{1... | collective-permute-start | bytes 393224 | tf_op jit(solution)/shard_map/ppermute | solution.py:285
  57.6 3.6 %collective-permute-done.12 = f32[64,512]{1,0:T(8,128)S(1)} collective-permute-done((f32[64,512]{1,0:T(8,128)S(1)}, f32[64,512]{1,0:T(8,128)S(1)}, u32[]{:S(2)}, u32[]{:S(2)}) %collective-permute-start.12) | collective-permute-done | bytes 131104 | tf_op jit(solution)/shard_map/ppermute | solution.py:278
  61.4 1.2 %collective-permute-done.14.outer.refs_1_.refs_4_ = f32[64,512]{1,0:T(8,128)S(1)} collective-permute-done((f32[64,512]{1,0:T(8,128)S(1)}, f32[64,512]{1,0:T(8,128)S(1)}, u32[]{:S(2)}, u32[]{:S(2)}) %collective-permute-start.14) | collective-permute-done | bytes 131104 | tf_op jit(solution)/shard_map/ppermute | solution.py:285
  62.6 6.4 %collective-permute-done.13.refs_0_.refs_3_ = f32[64,512]{1,0:T(8,128)S(1)} collective-permute-done((f32[64,512]{1,0:T(8,128)S(1)}, f32[64,512]{1,0:T(8,128)S(1)}, u32[]{:S(2)}, u32[]{:S(2)}) %collective-permute-start.13) | collective-permute-done | bytes 131104 | tf_op jit(solution)/shard_map/ppermute | solution.py:285
  69.0 0.1 relax_2.3
  69.1 0.1 collective-permute-start.15
  69.2 1.8 %collective-permute-start.17 = (f32[64,512]{1,0:T(8,128)S(1)}, f32[64,512]{1,0:T(8,128)S(1)}, u32[]{:S(2)}, u32[]{:S(2)}) collective-permute-start(f32[64,512]{1,0:T(8,128)S(1)} %relax_2.3), channel_id=1, source_target_pairs={{0,28},{1,29},{2,6},{3,7},{4,0},{5,1},{6,10},{7,11},{8,4},{9,5},{1... | collective-permute-start | bytes 393224 | tf_op jit(solution)/shard_map/ppermute | solution.py:285
  71.0 3.1 %collective-permute-done.15 = f32[64,512]{1,0:T(8,128)S(1)} collective-permute-done((f32[64,512]{1,0:T(8,128)S(1)}, f32[64,512]{1,0:T(8,128)S(1)}, u32[]{:S(2)}, u32[]{:S(2)}) %collective-permute-start.15) | collective-permute-done | bytes 131104 | tf_op jit(solution)/shard_map/ppermute | solution.py:278
  74.3 2.1 %older_1.1.refs_1_ = f32[64,512]{1,0:T(8,128)S(1)} custom-call(s32[16,128]{1,0:T(8,128)S(1)} %get-tuple-element.38.plan, bf16[7,512,512]{2,1,0:T(8,128)(2,1)S(1)} %copy-done, bf16[7,512,512]{2,1,0:T(8,128)(2,1)S(1)} %copy-done.1, bf16[7,512,512]{2,1,0:T(8,128)(2,1)S(1)} %get-tuple-element.41.sib_high, bf16[7,512,512]{2,1,0:T(8,128)(2,1)S(1)} %get-tuple-element.42.sib_low, ...), custom_call_target="tpu_custom_call" | custom-call | flops 671088640 | bytes 5242880 | tf_op jit(solution)/shard_map/older_1/pallas_call | solution.py:232
  76.4 5.5 %collective-permute-done.16.refs_0_ = f32[64,512]{1,0:T(8,128)S(1)} collective-permute-done((f32[64,512]{1,0:T(8,128)S(1)}, f32[64,512]{1,0:T(8,128)S(1)}, u32[]{:S(2)}, u32[]{:S(2)}) %collective-permute-start.16) | collective-permute-done | bytes 131104 | tf_op jit(solution)/shard_map/ppermute | solution.py:285
  81.9 1.1 %relax_1.3 = f32[64,512]{1,0:T(8,128)S(1)} custom-call(s32[16,128]{1,0:T(8,128)S(1)} %get-tuple-element.38.plan, bf16[7,512,512]{2,1,0:T(8,128)(2,1)S(1)} %copy-done, bf16[7,512,512]{2,1,0:T(8,128)(2,1)S(1)} %copy-done.1, bf16[7,512,512]{2,1,0:T(8,128)(2,1)S(1)} %get-tuple-element.41.sib_high, bf16[7,512,512]{2,1,0:T(8,128)(2,1)S(1)} %get-tuple-element.42.sib_low, ...), custom_call_target="tpu_custom_call" | custom-call | flops 536870912 | bytes 4194304 | tf_op jit(solution)/shard_map/relax_1/pallas_call | solution.py:250
  83.0 0.1 collective-permute-start.18
  83.1 1.4 %collective-permute-start.20 = (f32[64,512]{1,0:T(8,128)S(1)}, f32[64,512]{1,0:T(8,128)S(1)}, u32[]{:S(2)}, u32[]{:S(2)}) collective-permute-start(f32[64,512]{1,0:T(8,128)S(1)} %relax_1.3), channel_id=1, source_target_pairs={{0,28},{1,29},{2,6},{3,7},{4,0},{5,1},{6,10},{7,11},{8,4},{9,5},{1... | collective-permute-start | bytes 393224 | tf_op jit(solution)/shard_map/ppermute | solution.py:285
  84.4 3.6 %collective-permute-done.18 = f32[64,512]{1,0:T(8,128)S(1)} collective-permute-done((f32[64,512]{1,0:T(8,128)S(1)}, f32[64,512]{1,0:T(8,128)S(1)}, u32[]{:S(2)}, u32[]{:S(2)}) %collective-permute-start.18) | collective-permute-done | bytes 131104 | tf_op jit(solution)/shard_map/ppermute | solution.py:278
  88.2 7.6 %collective-permute-done.19.refs_0_ = f32[64,512]{1,0:T(8,128)S(1)} collective-permute-done((f32[64,512]{1,0:T(8,128)S(1)}, f32[64,512]{1,0:T(8,128)S(1)}, u32[]{:S(2)}, u32[]{:S(2)}) %collective-permute-start.19) | collective-permute-done | bytes 131104 | tf_op jit(solution)/shard_map/ppermute | solution.py:285
  95.8 0.1 relax_0.1
  95.9 0.1 collective-permute-start.21
  96.0 1.3 %collective-permute-done.21.other_ref = f32[64,512]{1,0:T(8,128)S(1)} collective-permute-done((f32[64,512]{1,0:T(8,128)S(1)}, f32[64,512]{1,0:T(8,128)S(1)}, u32[]{:S(2)}, u32[]{:S(2)}) %collective-permute-start.21) | collective-permute-done | bytes 131104 | tf_op jit(solution)/shard_map/ppermute | solution.py:278
  97.3 0.8 last.1
  (40 shorter events, 0.9 us)
Async XLA Ops:
  0.7 0.7 copy-start.2
  3.7 1.5 %collective-permute-start = (f32[72,512]{1,0:T(8,128)S(1)}, f32[72,512]{1,0:T(8,128)S(1)}, u32[]{:S(2)}, u32[]{:S(2)}) collective-permute-start(f32[72,512]{1,0:T(8,128)S(1)} %get-tuple-element.30), channel_id=1, source_target_pairs={{0,1},{1,0},{2,3},{3,2},{4,5},{5,4},{6,7},{7,6},{8,9},{9,8},{10,11... | collective-permute-start | bytes 442376 | tf_op jit(solution)/shard_map/ppermute | solution.py:278
  5.2 14.8 %collective-permute-start.1 = (f32[6,512,512]{2,1,0:T(8,128)}, f32[6,512,512]{2,1,0:T(8,128)}, u32[]{:S(2)}, u32[]{:S(2)}) collective-permute-start(f32[6,512,512]{2,1,0:T(8,128)} %bitcast.7), channel_id=1, source_target_pairs={{0,1},{1,0},{2,3},{3,2},{4,5},{5,4},{6,7},{7,6},{8,9},{9,8},{10,11... | collective-permute-start | bytes 18874376 | tf_op jit(solution)/shard_map/ppermute | solution.py:278
  5.6 14.4 %collective-permute-start.2 = (f32[512,512]{1,0:T(8,128)}, f32[512,512]{1,0:T(8,128)S(1)}, u32[]{:S(2)}, u32[]{:S(2)}) collective-permute-start(f32[512,512]{1,0:T(8,128)} %inverse_ref), channel_id=1, source_target_pairs={{0,1},{1,0},{2,3},{3,2},{4,5},{5,4},{6,7},{7,6},{8,9},{9,8},{10,11... | collective-permute-start | bytes 3145736 | tf_op jit(solution)/shard_map/ppermute | solution.py:278
  5.9 13.8 %collective-permute-start.3 = (f32[72,512]{1,0:T(8,128)S(1)}, f32[72,512]{1,0:T(8,128)S(1)}, u32[]{:S(2)}, u32[]{:S(2)}) collective-permute-start(f32[72,512]{1,0:T(8,128)S(1)} %pad_maximum_fusion), channel_id=1, source_target_pairs={{0,2},{1,3},{2,0},{3,1},{4,6},{5,7},{6,4},{7,5},{8,10},{9,11},{10,... | collective-permute-start | bytes 442376 | tf_op jit(solution)/shard_map/ppermute | solution.py:278
  8.8 14.6 %collective-permute-start.5 = (f32[72,512]{1,0:T(8,128)S(1)}, f32[72,512]{1,0:T(8,128)S(1)}, u32[]{:S(2)}, u32[]{:S(2)}) collective-permute-start(f32[72,512]{1,0:T(8,128)S(1)} %pad_maximum_fusion), channel_id=1, source_target_pairs={{0,28},{1,29},{2,6},{3,7},{4,0},{5,1},{6,10},{7,11},{8,4},{9,5},{1... | collective-permute-start | bytes 442376 | tf_op jit(solution)/shard_map/ppermute | solution.py:285
  19.8 8.1 %collective-permute-start.4 = (f32[72,512]{1,0:T(8,128)S(1)}, f32[72,512]{1,0:T(8,128)S(1)}, u32[]{:S(2)}, u32[]{:S(2)}) collective-permute-start(f32[72,512]{1,0:T(8,128)S(1)} %pad_maximum_fusion.1.here.refs_2_), channel_id=1, source_target_pairs={{0,4},{1,5},{2,30},{3,31},{4,8},{5,9},{6,2},{7,3},{8,12},{9,13},{1... | collective-permute-start | bytes 442376 | tf_op jit(solution)/shard_map/ppermute | solution.py:285
  20.0 8.5 %copy-start = (bf16[7,512,512]{2,1,0:T(8,128)(2,1)S(1)}, bf16[7,512,512]{2,1,0:T(8,128)(2,1)}, u32[]{:S(2)}) copy-start(bf16[7,512,512]{2,1,0:T(8,128)(2,1)} %get-tuple-element.39.own_high) | copy-start | bytes 11010052
  20.0 8.5 %copy-start.1 = (bf16[7,512,512]{2,1,0:T(8,128)(2,1)S(1)}, bf16[7,512,512]{2,1,0:T(8,128)(2,1)}, u32[]{:S(2)}) copy-start(bf16[7,512,512]{2,1,0:T(8,128)(2,1)} %get-tuple-element.40.own_low) | copy-start | bytes 11010052
  29.7 5.0 %collective-permute-start.6 = (f32[64,512]{1,0:T(8,128)S(1)}, f32[64,512]{1,0:T(8,128)S(1)}, u32[]{:S(2)}, u32[]{:S(2)}) collective-permute-start(f32[64,512]{1,0:T(8,128)S(1)} %get-tuple-element.43._), channel_id=1, source_target_pairs={{0,2},{1,3},{2,0},{3,1},{4,6},{5,7},{6,4},{7,5},{8,10},{9,11},{10,... | collective-permute-start | bytes 393224 | tf_op jit(solution)/shard_map/ppermute | solution.py:278
  29.7 6.2 %collective-permute-start.8 = (f32[64,512]{1,0:T(8,128)S(1)}, f32[64,512]{1,0:T(8,128)S(1)}, u32[]{:S(2)}, u32[]{:S(2)}) collective-permute-start(f32[64,512]{1,0:T(8,128)S(1)} %get-tuple-element.43._), channel_id=1, source_target_pairs={{0,28},{1,29},{2,6},{3,7},{4,0},{5,1},{6,10},{7,11},{8,4},{9,5},{1... | collective-permute-start | bytes 393224 | tf_op jit(solution)/shard_map/ppermute | solution.py:285
  34.7 7.8 %collective-permute-start.7 = (f32[64,512]{1,0:T(8,128)S(1)}, f32[64,512]{1,0:T(8,128)S(1)}, u32[]{:S(2)}, u32[]{:S(2)}) collective-permute-start(f32[64,512]{1,0:T(8,128)S(1)} %broadcast_select_fusion.2.here.refs_5_), channel_id=1, source_target_pairs={{0,4},{1,5},{2,30},{3,31},{4,8},{5,9},{6,2},{7,3},{8,12},{9,13},{1... | collective-permute-start | bytes 393224 | tf_op jit(solution)/shard_map/ppermute | solution.py:285
  42.6 5.0 %collective-permute-start.9 = (f32[64,512]{1,0:T(8,128)S(1)}, f32[64,512]{1,0:T(8,128)S(1)}, u32[]{:S(2)}, u32[]{:S(2)}) collective-permute-start(f32[64,512]{1,0:T(8,128)S(1)} %get-tuple-element.48), channel_id=1, source_target_pairs={{0,2},{1,3},{2,0},{3,1},{4,6},{5,7},{6,4},{7,5},{8,10},{9,11},{10,... | collective-permute-start | bytes 393224 | tf_op jit(solution)/shard_map/ppermute | solution.py:278
  42.7 5.0 %collective-permute-start.11 = (f32[64,512]{1,0:T(8,128)S(1)}, f32[64,512]{1,0:T(8,128)S(1)}, u32[]{:S(2)}, u32[]{:S(2)}) collective-permute-start(f32[64,512]{1,0:T(8,128)S(1)} %get-tuple-element.48), channel_id=1, source_target_pairs={{0,28},{1,29},{2,6},{3,7},{4,0},{5,1},{6,10},{7,11},{8,4},{9,5},{1... | collective-permute-start | bytes 393224 | tf_op jit(solution)/shard_map/ppermute | solution.py:285
  47.6 7.8 %collective-permute-start.10 = (f32[64,512]{1,0:T(8,128)S(1)}, f32[64,512]{1,0:T(8,128)S(1)}, u32[]{:S(2)}, u32[]{:S(2)}) collective-permute-start(f32[64,512]{1,0:T(8,128)S(1)} %broadcast_select_fusion.4.here), channel_id=1, source_target_pairs={{0,4},{1,5},{2,30},{3,31},{4,8},{5,9},{6,2},{7,3},{8,12},{9,13},{1... | collective-permute-start | bytes 393224 | tf_op jit(solution)/shard_map/ppermute | solution.py:285
  56.2 5.0 %collective-permute-start.12 = (f32[64,512]{1,0:T(8,128)S(1)}, f32[64,512]{1,0:T(8,128)S(1)}, u32[]{:S(2)}, u32[]{:S(2)}) collective-permute-start(f32[64,512]{1,0:T(8,128)S(1)} %relax_3.1), channel_id=1, source_target_pairs={{0,2},{1,3},{2,0},{3,1},{4,6},{5,7},{6,4},{7,5},{8,10},{9,11},{10,... | collective-permute-start | bytes 393224 | tf_op jit(solution)/shard_map/ppermute | solution.py:278
  56.3 6.2 %collective-permute-start.14 = (f32[64,512]{1,0:T(8,128)S(1)}, f32[64,512]{1,0:T(8,128)S(1)}, u32[]{:S(2)}, u32[]{:S(2)}) collective-permute-start(f32[64,512]{1,0:T(8,128)S(1)} %relax_3.1), channel_id=1, source_target_pairs={{0,28},{1,29},{2,6},{3,7},{4,0},{5,1},{6,10},{7,11},{8,4},{9,5},{1... | collective-permute-start | bytes 393224 | tf_op jit(solution)/shard_map/ppermute | solution.py:285
  61.3 7.7 %collective-permute-start.13 = (f32[64,512]{1,0:T(8,128)S(1)}, f32[64,512]{1,0:T(8,128)S(1)}, u32[]{:S(2)}, u32[]{:S(2)}) collective-permute-start(f32[64,512]{1,0:T(8,128)S(1)} %broadcast_select_fusion.here.refs_2_.refs_5_), channel_id=1, source_target_pairs={{0,4},{1,5},{2,30},{3,31},{4,8},{5,9},{6,2},{7,3},{8,12},{9,13},{1... | collective-permute-start | bytes 393224 | tf_op jit(solution)/shard_map/ppermute | solution.py:285
  69.1 5.0 %collective-permute-start.15 = (f32[64,512]{1,0:T(8,128)S(1)}, f32[64,512]{1,0:T(8,128)S(1)}, u32[]{:S(2)}, u32[]{:S(2)}) collective-permute-start(f32[64,512]{1,0:T(8,128)S(1)} %relax_2.3), channel_id=1, source_target_pairs={{0,2},{1,3},{2,0},{3,1},{4,6},{5,7},{6,4},{7,5},{8,10},{9,11},{10,... | collective-permute-start | bytes 393224 | tf_op jit(solution)/shard_map/ppermute | solution.py:278
  69.2 5.1 %collective-permute-start.17 = (f32[64,512]{1,0:T(8,128)S(1)}, f32[64,512]{1,0:T(8,128)S(1)}, u32[]{:S(2)}, u32[]{:S(2)}) collective-permute-start(f32[64,512]{1,0:T(8,128)S(1)} %relax_2.3), channel_id=1, source_target_pairs={{0,28},{1,29},{2,6},{3,7},{4,0},{5,1},{6,10},{7,11},{8,4},{9,5},{1... | collective-permute-start | bytes 393224 | tf_op jit(solution)/shard_map/ppermute | solution.py:285
  74.2 7.7 %collective-permute-start.16 = (f32[64,512]{1,0:T(8,128)S(1)}, f32[64,512]{1,0:T(8,128)S(1)}, u32[]{:S(2)}, u32[]{:S(2)}) collective-permute-start(f32[64,512]{1,0:T(8,128)S(1)} %broadcast_select_fusion.3.here.refs_2_), channel_id=1, source_target_pairs={{0,4},{1,5},{2,30},{3,31},{4,8},{5,9},{6,2},{7,3},{8,12},{9,13},{1... | collective-permute-start | bytes 393224 | tf_op jit(solution)/shard_map/ppermute | solution.py:285
  83.0 5.0 %collective-permute-start.18 = (f32[64,512]{1,0:T(8,128)S(1)}, f32[64,512]{1,0:T(8,128)S(1)}, u32[]{:S(2)}, u32[]{:S(2)}) collective-permute-start(f32[64,512]{1,0:T(8,128)S(1)} %relax_1.3), channel_id=1, source_target_pairs={{0,2},{1,3},{2,0},{3,1},{4,6},{5,7},{6,4},{7,5},{8,10},{9,11},{10,... | collective-permute-start | bytes 393224 | tf_op jit(solution)/shard_map/ppermute | solution.py:278
  83.1 5.1 %collective-permute-start.20 = (f32[64,512]{1,0:T(8,128)S(1)}, f32[64,512]{1,0:T(8,128)S(1)}, u32[]{:S(2)}, u32[]{:S(2)}) collective-permute-start(f32[64,512]{1,0:T(8,128)S(1)} %relax_1.3), channel_id=1, source_target_pairs={{0,28},{1,29},{2,6},{3,7},{4,0},{5,1},{6,10},{7,11},{8,4},{9,5},{1... | collective-permute-start | bytes 393224 | tf_op jit(solution)/shard_map/ppermute | solution.py:285
  88.1 7.7 %collective-permute-start.19 = (f32[64,512]{1,0:T(8,128)S(1)}, f32[64,512]{1,0:T(8,128)S(1)}, u32[]{:S(2)}, u32[]{:S(2)}) collective-permute-start(f32[64,512]{1,0:T(8,128)S(1)} %broadcast_select_fusion.1.here), channel_id=1, source_target_pairs={{0,4},{1,5},{2,30},{3,31},{4,8},{5,9},{6,2},{7,3},{8,12},{9,13},{1... | collective-permute-start | bytes 393224 | tf_op jit(solution)/shard_map/ppermute | solution.py:285
  95.9 1.4 %collective-permute-start.21 = (f32[64,512]{1,0:T(8,128)S(1)}, f32[64,512]{1,0:T(8,128)S(1)}, u32[]{:S(2)}, u32[]{:S(2)}) collective-permute-start(f32[64,512]{1,0:T(8,128)S(1)} %get-tuple-element.60), channel_id=1, source_target_pairs={{0,1},{1,0},{2,3},{3,2},{4,5},{5,4},{6,7},{7,6},{8,9},{9,8},{10,11... | collective-permute-start | bytes 393224 | tf_op jit(solution)/shard_map/ppermute | solution.py:278

commit v8 on v7

--- a/solution.py
+++ b/solution.py
@@ -9,6 +9,7 @@
 
 COLOURS = 4
 SIDES = 3
+ARRIVALS = 3
 INNER, OUTER, HERE = range(3)
 EXTRA = 8
 LANES = 128
@@ -89,35 +90,32 @@
     out_ref[...] = jnp.transpose(jnp.concatenate([first, second], axis=0))
 
 
-def parts_kernel(stored, tiles_ref, inverse_ref, w_high, w_low, zeros, buffer, sems, *held):
+def arrived_inner(inner, rows):
+    return sum((ref[rows, :] for ref in inner[1:]), inner[0][rows, :])
+
+
+def parts_kernel(tiles_ref, inverse_ref, _, w_high, w_low, zeros, buffer, sems):
     zeros[...] = jnp.zeros_like(zeros)
     tiles = tiles_ref.shape[0]
-    copies = [pltpu.make_async_copy(tiles_ref.at[k], buffer.at[k], sems.at[0, k]) for k in range(tiles)]
-    copies.append(pltpu.make_async_copy(inverse_ref, buffer.at[tiles], sems.at[0, tiles]))
+    copies = [pltpu.make_async_copy(tiles_ref.at[k], buffer.at[k], sems.at[k]) for k in range(tiles)]
+    copies.append(pltpu.make_async_copy(inverse_ref, buffer.at[tiles], sems.at[tiles]))
     for copy in copies:
         copy.start()
-    high, low = held if stored else (w_high, w_low)
-    stores = []
     for k, copy in enumerate(copies):
         copy.wait()
-        high[k], low[k] = split(buffer[k])
-        if stored:
-            stores.append(pltpu.make_async_copy(high.at[k], w_high.at[k], sems.at[1, k]))
-            stores.append(pltpu.make_async_copy(low.at[k], w_low.at[k], sems.at[2, k]))
-            stores[-2].start()
-            stores[-1].start()
-    for store in stores:
-        store.wait()
-
-
-def plan_kernel(tiles, colours, firsts_ref, _, own_rows, arrived, inner, outer, here, *outs):
+        w_high[k], w_low[k] = split(buffer[k])
+
+
+def plan_kernel(tiles, colours, firsts_ref, _, own_rows, arrived, *refs):
+    inner, (outer, here), outs = refs[:ARRIVALS], refs[ARRIVALS : ARRIVALS + 2], refs[ARRIVALS + 2 :]
     half = arrived.shape[0] - EXTRA
     lanes = pl.ds(0, LANES)
     own = own_rows[:, lanes].astype(jnp.int32)
     sib = arrived[half:, lanes].astype(jnp.int32)
     wanted = []
-    for side, ref in enumerate((inner, outer, here)):
-        found = ref[half:, lanes].astype(jnp.int32)
+    rows_of = [arrived_inner(inner, pl.ds(half, EXTRA)), outer[half:, :], here[half:, :]]
+    for side, value in enumerate(rows_of):
+        found = value[:, :LANES].astype(jnp.int32)
         wanted.append(jnp.where(found > 0, firsts_ref[side] + found - 1, -1))
     rows = outs[0].shape[0]
     row = lax.broadcasted_iota(jnp.int32, (rows, LANES), 0)
@@ -151,37 +149,41 @@
 
 def older_kernel(newest, older, has_base, plan, own_high, own_low, sib_high, sib_low, outer, here, *refs):
     *refs, partial = refs
-    known, base = refs[: SIDES * len(older)], refs[SIDES * len(older) :]
+    each = ARRIVALS + 2
+    known, base = refs[: each * len(older)], refs[each * len(older) :]
     half = partial.shape[0]
-    slots = [(newest, OUTER, outer), (newest, HERE, here)]
-    slots += [(c, side, known[SIDES * i + side]) for i, c in enumerate(older) for side in range(SIDES)]
+    slots = [(newest, OUTER, [outer]), (newest, HERE, [here])]
+    for i, c in enumerate(older):
+        *inner, old_outer, old_here = known[each * i : each * (i + 1)]
+        slots += [(c, INNER, inner), (c, OUTER, [old_outer]), (c, HERE, [old_here])]
 
     def body(w_high, w_low):
         partial[...] = base[0][...] if has_base else jnp.zeros_like(partial)
-        for c, side, ref in slots:
+        for c, side, values in slots:
             k = plan[TILE + side * COLOURS + c, 0]
 
             @pl.when(k >= 0)
             def _():
-                partial[...] += times(ref[:half, :], w_high[k], w_low[k])
+                partial[...] += times(arrived_inner(values, pl.ds(0, half)), w_high[k], w_low[k])
 
     chosen(plan, body, (own_high, own_low), (sib_high, sib_low))
 
 
 def relax_kernel(newest, sides, plan, own_high, own_low, sib_high, sib_low, own_start, sib_start, *refs):
-    latest, refs = refs[:sides], refs[sides:]
+    inner, refs = refs[:ARRIVALS], refs[ARRIVALS:]
+    others, refs = refs[: sides - 1], refs[sides - 1 :]
     base, refs = refs[: int(sides < SIDES)], refs[int(sides < SIDES) :]
     out, total = refs[:2]
     half = out.shape[0]
 
     def body(w_high, w_low, begin):
         total[...] = base[0][...] if base else jnp.zeros_like(total)
-        for side, ref in enumerate(latest):
+        for side, values in enumerate([inner] + [[ref] for ref in others]):
             k = plan[TILE + side * COLOURS + newest, 0]
 
             @pl.when(k >= 0)
             def _():
-                total[...] += times(ref[:half, :], w_high[k], w_low[k])
+                total[...] += times(arrived_inner(values, pl.ds(0, half)), w_high[k], w_low[k])
 
         last = w_high.shape[0] - 1
         out[...] = begin[:half, :] - times(total[...], w_high[last], w_low[last])
@@ -193,21 +195,24 @@
         out[...] = jnp.zeros_like(out)
 
 
-def parts(tiles, inverse, stored, name):
+def parts(tiles, inverse, after, name):
     count, block, _ = tiles.shape
     shape = (count + 1, block, block)
-    space = pltpu.HBM if stored else pltpu.VMEM
     return pl.pallas_call(
-        functools.partial(parts_kernel, stored),
-        out_shape=[space(shape, jnp.bfloat16)] * 2 + [pltpu.VMEM((EXTRA, block), jnp.float32)],
-        in_specs=[anywhere()] * 2,
-        out_specs=[hbm() if stored else vmem()] * 2 + [vmem()],
-        scratch_shapes=[pltpu.VMEM(shape, jnp.float32), pltpu.SemaphoreType.DMA((3, count + 1))]
-        + [pltpu.VMEM(shape, jnp.bfloat16)] * (2 * stored),
-        compiler_params=params(20 if stored else 12),
+        parts_kernel,
+        out_shape=[pltpu.VMEM(shape, jnp.bfloat16)] * 2 + [pltpu.VMEM((EXTRA, block), jnp.float32)],
+        in_specs=[anywhere()] * 3,
+        out_specs=[vmem()] * 3,
+        scratch_shapes=[pltpu.VMEM(shape, jnp.float32), pltpu.SemaphoreType.DMA((count + 1,))],
+        compiler_params=params(12),
         cost_estimate=pl.CostEstimate(flops=0, bytes_accessed=8 * count * block * block, transcendentals=0),
         name=name,
-    )(tiles, inverse)
+    )(tiles, inverse, *after)
+
+
+def flat(sides):
+    inner, outer, here = sides
+    return [*inner, outer, here]
 
 
 def make_plans(tiles, colours, firsts, own_rows, arrived, first_known, zeros):
@@ -217,17 +222,17 @@
     outs = pl.pallas_call(
         functools.partial(plan_kernel, tiles, colours),
         out_shape=[pltpu.VMEM((rows, LANES), jnp.int32)] * number + [pltpu.VMEM((EXTRA, block), jnp.int32)] * number,
-        in_specs=[smem()] + [vmem()] * 6,
+        in_specs=[smem()] + [vmem()] * (5 + ARRIVALS),
         out_specs=[vmem()] * (2 * number),
         compiler_params=params(8),
         name=f"plan_{number}",
-    )(firsts, *near([zeros, own_rows, arrived, *first_known]))
+    )(firsts, *near([zeros, own_rows, arrived, *flat(first_known)]))
     return dict(zip(colours, outs[:number])), dict(zip(colours, outs[number:]))
 
 
 def add_older(now, newest, older, plan, matrices, outer, here, known, base):
     half, block = here.shape
-    operands = near([plan, *matrices, outer, here, *[value for c in older for value in known[c]], *base])
+    operands = near([plan, *matrices, outer, here, *[value for c in older for value in flat(known[c])], *base])
     slots = 2 + SIDES * len(older)
     return pl.pallas_call(
         functools.partial(older_kernel, newest, older, len(base)),
@@ -245,7 +250,7 @@
 def relax(now, newest, plan, matrices, starts, latest, partial, keep_sum):
     half, block = starts[0].shape
     sides = 1 if partial else SIDES
-    operands = near([plan, *matrices, *starts, *latest[:sides], *partial])
+    operands = near([plan, *matrices, *starts, *flat(latest)[: ARRIVALS - 1 + sides], *partial])
     value = pltpu.VMEM((half, block), jnp.float32)
     return pl.pallas_call(
         functools.partial(relax_kernel, newest, sides),
@@ -277,11 +282,23 @@
     def flip(value, bit):
         return lax.ppermute(value, axis, [(i, i ^ bit) for i in range(count)])
 
-    def beside(value, ahead):
+    def is_wrap(i, target):
+        return abs(i // COLOURS - target // COLOURS) > 1
+
+    def beside(value, ahead, with_wrap):
         pairs = []
         for i in range(count):
             step = COLOURS if (i // 2) % 2 == ahead else -COLOURS
             pairs.append((i, (i + step) % count))
+        return lax.ppermute(value, axis, [p for p in pairs if with_wrap or not is_wrap(*p)])
+
+    def around_wrap(value, change):
+        pairs = []
+        for i in range(count):
+            target_chip = (i // 2) % 2 ^ change
+            target = (i ^ (2 * change)) + (COLOURS if target_chip == 0 else -COLOURS)
+            if not 0 <= target < count:
+                pairs.append((i, target % count))
         return lax.ppermute(value, axis, pairs)
 
     keep, send, own_rows = pl.pallas_call(
@@ -301,25 +318,26 @@
     arrived = flip(send, 1)
     starts = [keep, arrived]
 
-    late_tiles, late_inverse, _ = lax.optimization_barrier((tiles, inv_diag, arrived))
-    sib_tiles, sib_inverse = flip(late_tiles, 1), flip(late_inverse, 1)
+    late_tiles, _ = lax.optimization_barrier((tiles, arrived))
+    sib_tiles, sib_inverse = flip(late_tiles, 1), flip(inv_diag, 1)
 
     own_wide, sib_wide = own_rows[:1], arrived[half : half + 1]
-    candidate = jnp.where(own_wide == 0, keep, arrived[:half])
+    candidate = jnp.where(own_wide == 0, keep, jnp.where(sib_wide == 0, arrived[:half], 0.0))
     wheel = lax.broadcasted_iota(jnp.int32, (EXTRA, block), 0).astype(jnp.float32)
     places = jnp.where(wheel == own_wide, place + 1, 0) + jnp.where(wheel == sib_wide, (place ^ 1) + 1, 0)
     places = places.astype(jnp.float32)
     sent = jnp.concatenate([candidate, places])
     swapped = flip(sent, 2)
-    outer = beside(sent, 1)
-    far_tiles, far_inverse, _ = lax.optimization_barrier((tiles, inv_diag, sent))
-    *own_parts, zeros = parts(*far([far_tiles, far_inverse]), 1, "own_parts")
-    here = jnp.where((own_wide + zeros[:1] == 0) | (sib_wide == 0), candidate, swapped[:half])
+    outer = beside(sent, 1, True)
+    here = jnp.where((own_wide == 0) | (sib_wide == 0), candidate, swapped[:half])
     here = jnp.concatenate([here, places + swapped[half:]])
-    known = {0: [beside(here, 0), outer, here]}
+    none = jnp.zeros_like(here)
+    known = {0: [[beside(here, 0, True), none, none], outer, here]}
     toward = jnp.where(place < COLOURS // 2, -1, 1)
     firsts = jnp.stack([((group + step) % groups) * COLOURS for step in (toward, -toward, 0 * toward)]).astype(jnp.int32)
-    *sib_parts, zeros = parts(sib_tiles, sib_inverse, 0, "sib_parts")
+    far_tiles, far_inverse, _ = lax.optimization_barrier((tiles, inv_diag, here))
+    *own_parts, zeros = parts(*far([far_tiles, far_inverse]), [here], "own_parts")
+    *sib_parts, zeros = parts(sib_tiles, sib_inverse, [zeros], "sib_parts")
     matrices = [*own_parts, *sib_parts]
     facts = (firsts, own_rows, arrived, known[0])
     order = list(range(1, COLOURS)) + list(range(COLOURS - 2, -1, -1))
@@ -340,9 +358,10 @@
                 table.update(more)
         after = order[step + 1]
         swapped = flip(candidate, 2)
-        outer = beside(candidate, 1)
+        outer = beside(candidate, 1, True)
+        wraps = [around_wrap(candidate, change) for change in range(2)]
         here = jnp.where(masks[now][:1] != 0, candidate, swapped)
-        inner = beside(here, 0)
+        inner = [beside(here, 0, False), *wraps]
         fresh = used.get(after, set())
         older = tuple(c for c in sorted(known) if c not in (now, after) and (c, done_at(order, c, step)) not in fresh)
         partial = [add_older(after, now, older, plans[after], matrices, outer, here, known, sums.get(after, []))]

time: 98.8 us -> 118 us (1.19)
  starting transfers between devices: 16.9 us -> 68.6 us
  waiting for transfers between devices: 55.6 us -> 25.2 us
  Pallas kernels: 23.3 us -> 20.2 us
    ppermute x12 -> x22, starting transfers between devices: 12.5 us -> 57.3 us  [the longest x10 31.4 us: around_wrap(): return lax.ppermute(value, axis, pairs)]
    ppermute x10, waiting for transfers between devices: 19.5 us -> 2.36 us  [flip(): return lax.ppermute(value, axis, [(i, i ^ bit) for i in range(count)])]
    ppermute x12 -> x22, waiting for transfers between devices: 36.1 us -> 22.8 us  [the longest x12 22.8 us: beside(): lax.ppermute(value, axis, [p for p in pairs if with_wrap or not is_wrap(*...]
    ppermute x10, starting transfers between devices: 4.43 us -> 11.3 us  [flip(): return lax.ppermute(value, axis, [(i, i ^ bit) for i in range(count)])]
    pallas_call x2, Pallas kernels: 9.64 us -> 6.45 us  [parts(): pl.pallas_call(parts_kernel, out_shape=[pltpu.VMEM(shape, jnp.bfloat16)]...]
    pallas_call x6, Pallas kernels: 3.29 us -> 4.74 us  [relax(): pl.pallas_call(functools.partial(relax_kernel, newest, sides), out_shape=...]
    pallas_call x5, Pallas kernels: 5.5 us -> 4.09 us  [add_older(): pl.pallas_call(functools.partial(older_kernel, newest, older, len(base)),...]
  transfers between devices with their start and end apart: 22 -> 32, of which waited for: 14 -> 8; matrix products, arithmetic and copies ran while one was open for 1% -> 0% of each run, Pallas kernels for 17% -> 10%
where the time goes in v8:
time: 118 us; the launch traced here: 116 us
  starting transfers between devices  68.6 us (58%)
  waiting for transfers between devices  25.2 us (21%)
  Pallas kernels  20.2 us (17%)
    ppermute x10, starting transfers between devices, around_wrap(): return lax.ppermute(value, axis, pairs)  31.4 us
    ppermute x12, starting transfers between devices, beside(): lax.ppermute(value, axis, [p for p in pairs if with_wrap or not is_wrap(*...  25.9 us
    ppermute x12, waiting for transfers between devices, beside(): lax.ppermute(value, axis, [p for p in pairs if with_wrap or not is_wrap(*...  22.8 us
    ppermute x10, starting transfers between devices, flip(): return lax.ppermute(value, axis, [(i, i ^ bit) for i in range(count)])  11.3 us
    pallas_call x2, Pallas kernels, parts(): pl.pallas_call(parts_kernel, out_shape=[pltpu.VMEM(shape, jnp.bfloat16)]...  6.45 us
    pallas_call x6, Pallas kernels, relax(): pl.pallas_call(functools.partial(relax_kernel, newest, sides), out_shape=...  4.74 us
    pallas_call x5, Pallas kernels, add_older(): pl.pallas_call(functools.partial(older_kernel, newest, older, len(base)),...  4.09 us
    ppermute x10, waiting for transfers between devices, flip(): return lax.ppermute(value, axis, [(i, i ^ bit) for i in range(count)])  2.36 us
  transfers between devices with their start and end apart: 32, of which 8 were waited for; matrix products, arithmetic and copies ran while one was open for 0% of the time, Pallas kernels for 10%

profile of v8, /device:TPU:0, one launch (start us, length us, event | category | flops | bytes accessed | tf_op | source)
XLA Modules:
  0.0 116.4 jit_solution(7417430189507488578)
XLA Ops:
  0.7 0.6 copy-done
  1.3 2.4 %first.1 = (f32[64,512]{1,0:T(8,128)S(1)}, f32[72,512]{1,0:T(8,128)S(1)}, f32[8,512]{1,0:T(8,128)S(1)}) custom-call(s32[1]{0:T(128)} %bitcast.core_ref, s32[1]{0:T(128)S(6)} %copy.6.colour_ref, s32[1,6]{1,0:T(1,128)S(1)} %copy-done, f32[512,512]{1,0:T(8,128)} %inverse_ref, f32[512,128]{1,0:T(8,128)} %residual_hbm.1), custom_call_target="tpu_custom_call" | custom-call | tf_op jit(solution)/shard_map/first/pallas_call | solution.py:304
  3.7 0.5 collective-permute-start
  4.2 1.0 collective-permute-done.arrived.sib_start
  5.2 0.4 collective-permute-start.1
  5.6 0.1 collective-permute-start.2
  5.9 2.9 %collective-permute-start.3 = (f32[72,512]{1,0:T(8,128)S(1)}, f32[72,512]{1,0:T(8,128)S(1)}, u32[]{:S(2)}, u32[]{:S(2)}) collective-permute-start(f32[72,512]{1,0:T(8,128)S(1)} %pad_maximum_fusion), channel_id=1, source_target_pairs={{0,2},{1,3},{2,0},{3,1},{4,6},{5,7},{6,4},{7,5},{8,10},{9,11},{10,... | collective-permute-start | bytes 442376 | tf_op jit(solution)/shard_map/ppermute | solution.py:283
  8.8 4.5 %collective-permute-start.5 = (f32[72,512]{1,0:T(8,128)S(1)}, f32[72,512]{1,0:T(8,128)S(1)}, u32[]{:S(2)}, u32[]{:S(2)}) collective-permute-start(f32[72,512]{1,0:T(8,128)S(1)} %pad_maximum_fusion), channel_id=1, source_target_pairs={{0,28},{1,29},{2,6},{3,7},{4,0},{5,1},{6,10},{7,11},{8,4},{9,5},{1... | collective-permute-start | bytes 442376 | tf_op jit(solution)/shard_map/ppermute | solution.py:293
  13.5 1.4 %collective-permute-start.4 = (f32[72,512]{1,0:T(8,128)S(1)}, f32[72,512]{1,0:T(8,128)S(1)}, u32[]{:S(2)}, u32[]{:S(2)}) collective-permute-start(f32[72,512]{1,0:T(8,128)S(1)} %pad_maximum_fusion.1._.refs_4_), channel_id=1, source_target_pairs={{0,4},{1,5},{2,30},{3,31},{4,8},{5,9},{6,2},{7,3},{8,12},{9,13},{1... | collective-permute-start | bytes 442376 | tf_op jit(solution)/shard_map/ppermute | solution.py:293
  15.0 3.3 %own_parts.1 = (bf16[7,512,512]{2,1,0:T(8,128)(2,1)S(1)}, bf16[7,512,512]{2,1,0:T(8,128)(2,1)S(1)}, f32[8,512]{1,0:T(8,128)S(1)}) custom-call(f32[6,512,512]{2,1,0:T(8,128)} %bitcast.8, f32[512,512]{1,0:T(8,128)} %inverse_ref, f32[72,512]{1,0:T(8,128)S(1)} %pad_maximum_fusion.1._.refs_4_), custom_call_target="tpu_custom_call" | custom-call | bytes 12582912 | tf_op jit(solution)/shard_map/own_parts/pallas_call | solution.py:201
  18.3 3.1 %sib_parts.1 = (bf16[7,512,512]{2,1,0:T(8,128)(2,1)S(1)}, bf16[7,512,512]{2,1,0:T(8,128)(2,1)S(1)}, f32[8,512]{1,0:T(8,128)S(1)}) custom-call(f32[6,512,512]{2,1,0:T(8,128)} %collective-permute-done.1.tiles_ref, f32[512,512]{1,0:T(8,128)S(1)} %collective-permute-done.2.inverse_ref, f32[8,512]{1,0:T(8,128)S(1)} %get-tuple-element.34._), custom_call_target="tpu_custom_call" | custom-call | bytes 12582912 | tf_op jit(solution)/shard_map/sib_parts/pallas_call | solution.py:201
  21.6 0.6 plan_1.1
  22.2 2.1 %relax_1.2 = (f32[64,512]{1,0:T(8,128)S(1)}, f32[64,512]{1,0:T(8,128)S(1)}) custom-call(s32[16,128]{1,0:T(8,128)S(1)} %get-tuple-element.36.plan, bf16[7,512,512]{2,1,0:T(8,128)(2,1)S(1)} %get-tuple-element.37.own_high, bf16[7,512,512]{2,1,0:T(8,128)(2,1)S(1)} %get-tuple-element.38.own_low, bf16[7,512,512]{2,1,0:T(8,128)(2,1)S(1)} %get-tuple-element.39.sib_high, ...), custom_call_target="tpu_custom_call" | custom-call | flops 536870912 | bytes 4194304 | tf_op jit(solution)/shard_map/relax_1/pallas_call | solution.py:255
  24.3 2.5 %collective-permute-start.6 = (f32[64,512]{1,0:T(8,128)S(1)}, f32[64,512]{1,0:T(8,128)S(1)}, u32[]{:S(2)}, u32[]{:S(2)}) collective-permute-start(f32[64,512]{1,0:T(8,128)S(1)} %get-tuple-element.41._), channel_id=1, source_target_pairs={{0,2},{1,3},{2,0},{3,1},{4,6},{5,7},{6,4},{7,5},{8,10},{9,11},{10,... | collective-permute-start | bytes 393224 | tf_op jit(solution)/shard_map/ppermute | solution.py:283
  26.8 1.3 %collective-permute-start.8 = (f32[64,512]{1,0:T(8,128)S(1)}, f32[64,512]{1,0:T(8,128)S(1)}, u32[]{:S(2)}, u32[]{:S(2)}) collective-permute-start(f32[64,512]{1,0:T(8,128)S(1)} %get-tuple-element.41._), channel_id=1, source_target_pairs={{2,30},{3,31},{28,0},{29,1}} | collective-permute-start | bytes 393224 | tf_op jit(solution)/shard_map/ppermute | solution.py:302
  28.1 5.2 %collective-permute-start.9 = (f32[64,512]{1,0:T(8,128)S(1)}, f32[64,512]{1,0:T(8,128)S(1)}, u32[]{:S(2)}, u32[]{:S(2)}) collective-permute-start(f32[64,512]{1,0:T(8,128)S(1)} %get-tuple-element.41._), channel_id=1, source_target_pairs={{0,30},{1,31},{30,0},{31,1}} | collective-permute-start | bytes 393224 | tf_op jit(solution)/shard_map/ppermute | solution.py:302
  33.3 0.9 collective-permute-start.10
  34.2 3.1 %collective-permute-start.7 = (f32[64,512]{1,0:T(8,128)S(1)}, f32[64,512]{1,0:T(8,128)S(1)}, u32[]{:S(2)}, u32[]{:S(2)}) collective-permute-start(f32[64,512]{1,0:T(8,128)S(1)} %broadcast_select_fusion.2.here.refs_9_), channel_id=1, source_target_pairs={{0,4},{1,5},{4,8},{5,9},{6,2},{7,3},{8,12},{9,13},{10,6},{11,7},{1... | collective-permute-start | bytes 393224 | tf_op jit(solution)/shard_map/ppermute | solution.py:293
  37.3 1.2 plan_3.1
  38.5 3.5 %collective-permute-done.10.outer.refs_8_ = f32[64,512]{1,0:T(8,128)S(1)} collective-permute-done((f32[64,512]{1,0:T(8,128)S(1)}, f32[64,512]{1,0:T(8,128)S(1)}, u32[]{:S(2)}, u32[]{:S(2)}) %collective-permute-start.10) | collective-permute-done | bytes 131104 | tf_op jit(solution)/shard_map/ppermute | solution.py:293
  42.1 2.7 %collective-permute-start.11 = (f32[64,512]{1,0:T(8,128)S(1)}, f32[64,512]{1,0:T(8,128)S(1)}, u32[]{:S(2)}, u32[]{:S(2)}) collective-permute-start(f32[64,512]{1,0:T(8,128)S(1)} %get-tuple-element.46), channel_id=1, source_target_pairs={{0,2},{1,3},{2,0},{3,1},{4,6},{5,7},{6,4},{7,5},{8,10},{9,11},{10,... | collective-permute-start | bytes 393224 | tf_op jit(solution)/shard_map/ppermute | solution.py:283
  44.9 1.3 %collective-permute-start.13 = (f32[64,512]{1,0:T(8,128)S(1)}, f32[64,512]{1,0:T(8,128)S(1)}, u32[]{:S(2)}, u32[]{:S(2)}) collective-permute-start(f32[64,512]{1,0:T(8,128)S(1)} %get-tuple-element.46), channel_id=1, source_target_pairs={{2,30},{3,31},{28,0},{29,1}} | collective-permute-start | bytes 393224 | tf_op jit(solution)/shard_map/ppermute | solution.py:302
  46.2 5.1 %collective-permute-start.14 = (f32[64,512]{1,0:T(8,128)S(1)}, f32[64,512]{1,0:T(8,128)S(1)}, u32[]{:S(2)}, u32[]{:S(2)}) collective-permute-start(f32[64,512]{1,0:T(8,128)S(1)} %get-tuple-element.46), channel_id=1, source_target_pairs={{0,30},{1,31},{30,0},{31,1}} | collective-permute-start | bytes 393224 | tf_op jit(solution)/shard_map/ppermute | solution.py:302
  51.3 0.9 collective-permute-start.15
  52.3 3.0 %collective-permute-start.12 = (f32[64,512]{1,0:T(8,128)S(1)}, f32[64,512]{1,0:T(8,128)S(1)}, u32[]{:S(2)}, u32[]{:S(2)}) collective-permute-start(f32[64,512]{1,0:T(8,128)S(1)} %broadcast_select_fusion.4.here), channel_id=1, source_target_pairs={{0,4},{1,5},{4,8},{5,9},{6,2},{7,3},{8,12},{9,13},{10,6},{11,7},{1... | collective-permute-start | bytes 393224 | tf_op jit(solution)/shard_map/ppermute | solution.py:293
  55.3 4.7 %collective-permute-done.15.outer = f32[64,512]{1,0:T(8,128)S(1)} collective-permute-done((f32[64,512]{1,0:T(8,128)S(1)}, f32[64,512]{1,0:T(8,128)S(1)}, u32[]{:S(2)}, u32[]{:S(2)}) %collective-permute-start.15) | collective-permute-done | bytes 131104 | tf_op jit(solution)/shard_map/ppermute | solution.py:293
  60.0 2.7 %older_3.1.refs_3_ = f32[64,512]{1,0:T(8,128)S(1)} custom-call(s32[16,128]{1,0:T(8,128)S(1)} %get-tuple-element.42.plan, bf16[7,512,512]{2,1,0:T(8,128)(2,1)S(1)} %get-tuple-element.37.own_high, bf16[7,512,512]{2,1,0:T(8,128)(2,1)S(1)} %get-tuple-element.38.own_low, bf16[7,512,512]{2,1,0:T(8,128)(2,1)S(1)} %get-tuple-element.39.sib_high, ...), custom_call_target="tpu_custom_call" | custom-call | flops 1073741824 | bytes 8388608 | tf_op jit(solution)/shard_map/older_3/pallas_call | solution.py:237
  62.8 1.3 %relax_3.1 = f32[64,512]{1,0:T(8,128)S(1)} custom-call(s32[16,128]{1,0:T(8,128)S(1)} %get-tuple-element.42.plan, bf16[7,512,512]{2,1,0:T(8,128)(2,1)S(1)} %get-tuple-element.37.own_high, bf16[7,512,512]{2,1,0:T(8,128)(2,1)S(1)} %get-tuple-element.38.own_low, bf16[7,512,512]{2,1,0:T(8,128)(2,1)S(1)} %get-tuple-element.39.sib_high, ...), custom_call_target="tpu_custom_call" | custom-call | flops 536870912 | bytes 4194304 | tf_op jit(solution)/shard_map/relax_3/pallas_call | solution.py:255
  64.1 1.3 %collective-permute-start.18 = (f32[64,512]{1,0:T(8,128)S(1)}, f32[64,512]{1,0:T(8,128)S(1)}, u32[]{:S(2)}, u32[]{:S(2)}) collective-permute-start(f32[64,512]{1,0:T(8,128)S(1)} %relax_3.1), channel_id=1, source_target_pairs={{2,30},{3,31},{28,0},{29,1}} | collective-permute-start | bytes 393224 | tf_op jit(solution)/shard_map/ppermute | solution.py:302
  65.4 5.2 %collective-permute-start.19 = (f32[64,512]{1,0:T(8,128)S(1)}, f32[64,512]{1,0:T(8,128)S(1)}, u32[]{:S(2)}, u32[]{:S(2)}) collective-permute-start(f32[64,512]{1,0:T(8,128)S(1)} %relax_3.1), channel_id=1, source_target_pairs={{0,30},{1,31},{30,0},{31,1}} | collective-permute-start | bytes 393224 | tf_op jit(solution)/shard_map/ppermute | solution.py:302
  70.7 0.8 collective-permute-start.20
  71.5 3.2 %collective-permute-start.17 = (f32[64,512]{1,0:T(8,128)S(1)}, f32[64,512]{1,0:T(8,128)S(1)}, u32[]{:S(2)}, u32[]{:S(2)}) collective-permute-start(f32[64,512]{1,0:T(8,128)S(1)} %broadcast_select_fusion.here.refs_4_.refs_9_), channel_id=1, source_target_pairs={{0,4},{1,5},{4,8},{5,9},{6,2},{7,3},{8,12},{9,13},{10,6},{11,7},{1... | collective-permute-start | bytes 393224 | tf_op jit(solution)/shard_map/ppermute | solution.py:293
  74.7 4.8 %collective-permute-done.20.outer.refs_3_.refs_8_ = f32[64,512]{1,0:T(8,128)S(1)} collective-permute-done((f32[64,512]{1,0:T(8,128)S(1)}, f32[64,512]{1,0:T(8,128)S(1)}, u32[]{:S(2)}, u32[]{:S(2)}) %collective-permute-start.20) | collective-permute-done | bytes 131104 | tf_op jit(solution)/shard_map/ppermute | solution.py:293
  79.7 1.9 %collective-permute-start.21 = (f32[64,512]{1,0:T(8,128)S(1)}, f32[64,512]{1,0:T(8,128)S(1)}, u32[]{:S(2)}, u32[]{:S(2)}) collective-permute-start(f32[64,512]{1,0:T(8,128)S(1)} %relax_2.3), channel_id=1, source_target_pairs={{0,2},{1,3},{2,0},{3,1},{4,6},{5,7},{6,4},{7,5},{8,10},{9,11},{10,... | collective-permute-start | bytes 393224 | tf_op jit(solution)/shard_map/ppermute | solution.py:283
  81.6 1.3 %collective-permute-start.23 = (f32[64,512]{1,0:T(8,128)S(1)}, f32[64,512]{1,0:T(8,128)S(1)}, u32[]{:S(2)}, u32[]{:S(2)}) collective-permute-start(f32[64,512]{1,0:T(8,128)S(1)} %relax_2.3), channel_id=1, source_target_pairs={{2,30},{3,31},{28,0},{29,1}} | collective-permute-start | bytes 393224 | tf_op jit(solution)/shard_map/ppermute | solution.py:302
  82.9 4.0 %collective-permute-start.24 = (f32[64,512]{1,0:T(8,128)S(1)}, f32[64,512]{1,0:T(8,128)S(1)}, u32[]{:S(2)}, u32[]{:S(2)}) collective-permute-start(f32[64,512]{1,0:T(8,128)S(1)} %relax_2.3), channel_id=1, source_target_pairs={{0,30},{1,31},{30,0},{31,1}} | collective-permute-start | bytes 393224 | tf_op jit(solution)/shard_map/ppermute | solution.py:302
  86.9 2.1 %collective-permute-start.25 = (f32[64,512]{1,0:T(8,128)S(1)}, f32[64,512]{1,0:T(8,128)S(1)}, u32[]{:S(2)}, u32[]{:S(2)}) collective-permute-start(f32[64,512]{1,0:T(8,128)S(1)} %relax_2.3), channel_id=1, source_target_pairs={{0,28},{1,29},{2,6},{3,7},{4,0},{5,1},{6,10},{7,11},{8,4},{9,5},{1... | collective-permute-start | bytes 393224 | tf_op jit(solution)/shard_map/ppermute | solution.py:293
  89.0 1.9 %collective-permute-start.22 = (f32[64,512]{1,0:T(8,128)S(1)}, f32[64,512]{1,0:T(8,128)S(1)}, u32[]{:S(2)}, u32[]{:S(2)}) collective-permute-start(f32[64,512]{1,0:T(8,128)S(1)} %broadcast_select_fusion.3.here.refs_4_), channel_id=1, source_target_pairs={{0,4},{1,5},{4,8},{5,9},{6,2},{7,3},{8,12},{9,13},{10,6},{11,7},{1... | collective-permute-start | bytes 393224 | tf_op jit(solution)/shard_map/ppermute | solution.py:293
  91.0 5.4 %collective-permute-done.25.outer.refs_3_ = f32[64,512]{1,0:T(8,128)S(1)} collective-permute-done((f32[64,512]{1,0:T(8,128)S(1)}, f32[64,512]{1,0:T(8,128)S(1)}, u32[]{:S(2)}, u32[]{:S(2)}) %collective-permute-start.25) | collective-permute-done | bytes 131104 | tf_op jit(solution)/shard_map/ppermute | solution.py:293
  96.3 1.2 %older_1.1.refs_3_ = f32[64,512]{1,0:T(8,128)S(1)} custom-call(s32[16,128]{1,0:T(8,128)S(1)} %get-tuple-element.36.plan, bf16[7,512,512]{2,1,0:T(8,128)(2,1)S(1)} %get-tuple-element.37.own_high, bf16[7,512,512]{2,1,0:T(8,128)(2,1)S(1)} %get-tuple-element.38.own_low, bf16[7,512,512]{2,1,0:T(8,128)(2,1)S(1)} %get-tuple-element.39.sib_high, ...), custom_call_target="tpu_custom_call" | custom-call | flops 671088640 | bytes 5242880 | tf_op jit(solution)/shard_map/older_1/pallas_call | solution.py:237
  97.6 1.1 relax_1.3
  98.8 1.3 %collective-permute-start.28 = (f32[64,512]{1,0:T(8,128)S(1)}, f32[64,512]{1,0:T(8,128)S(1)}, u32[]{:S(2)}, u32[]{:S(2)}) collective-permute-start(f32[64,512]{1,0:T(8,128)S(1)} %relax_1.3), channel_id=1, source_target_pairs={{2,30},{3,31},{28,0},{29,1}} | collective-permute-start | bytes 393224 | tf_op jit(solution)/shard_map/ppermute | solution.py:302
  100.0 5.4 %collective-permute-start.29 = (f32[64,512]{1,0:T(8,128)S(1)}, f32[64,512]{1,0:T(8,128)S(1)}, u32[]{:S(2)}, u32[]{:S(2)}) collective-permute-start(f32[64,512]{1,0:T(8,128)S(1)} %relax_1.3), channel_id=1, source_target_pairs={{0,30},{1,31},{30,0},{31,1}} | collective-permute-start | bytes 393224 | tf_op jit(solution)/shard_map/ppermute | solution.py:302
  105.5 0.6 collective-permute-start.30
  106.1 3.3 %collective-permute-start.27 = (f32[64,512]{1,0:T(8,128)S(1)}, f32[64,512]{1,0:T(8,128)S(1)}, u32[]{:S(2)}, u32[]{:S(2)}) collective-permute-start(f32[64,512]{1,0:T(8,128)S(1)} %broadcast_select_fusion.1.here), channel_id=1, source_target_pairs={{0,4},{1,5},{4,8},{5,9},{6,2},{7,3},{8,12},{9,13},{10,6},{11,7},{1... | collective-permute-start | bytes 393224 | tf_op jit(solution)/shard_map/ppermute | solution.py:293
  109.5 4.4 %collective-permute-done.30.outer = f32[64,512]{1,0:T(8,128)S(1)} collective-permute-done((f32[64,512]{1,0:T(8,128)S(1)}, f32[64,512]{1,0:T(8,128)S(1)}, u32[]{:S(2)}, u32[]{:S(2)}) %collective-permute-start.30) | collective-permute-done | bytes 131104 | tf_op jit(solution)/shard_map/ppermute | solution.py:293
  114.2 1.3 %collective-permute-done.31.other_ref = f32[64,512]{1,0:T(8,128)S(1)} collective-permute-done((f32[64,512]{1,0:T(8,128)S(1)}, f32[64,512]{1,0:T(8,128)S(1)}, u32[]{:S(2)}, u32[]{:S(2)}) %collective-permute-start.31) | collective-permute-done | bytes 131104 | tf_op jit(solution)/shard_map/ppermute | solution.py:283
  115.5 0.8 last.1
  (56 shorter events, 1.4 us)
Async XLA Ops:
  0.7 0.7 copy-start
  3.7 1.5 %collective-permute-start = (f32[72,512]{1,0:T(8,128)S(1)}, f32[72,512]{1,0:T(8,128)S(1)}, u32[]{:S(2)}, u32[]{:S(2)}) collective-permute-start(f32[72,512]{1,0:T(8,128)S(1)} %get-tuple-element.29), channel_id=1, source_target_pairs={{0,1},{1,0},{2,3},{3,2},{4,5},{5,4},{6,7},{7,6},{8,9},{9,8},{10,11... | collective-permute-start | bytes 442376 | tf_op jit(solution)/shard_map/ppermute | solution.py:283
  5.2 13.1 %collective-permute-start.1 = (f32[6,512,512]{2,1,0:T(8,128)}, f32[6,512,512]{2,1,0:T(8,128)}, u32[]{:S(2)}, u32[]{:S(2)}) collective-permute-start(f32[6,512,512]{2,1,0:T(8,128)} %bitcast.7), channel_id=1, source_target_pairs={{0,1},{1,0},{2,3},{3,2},{4,5},{5,4},{6,7},{7,6},{8,9},{9,8},{10,11... | collective-permute-start | bytes 18874376 | tf_op jit(solution)/shard_map/ppermute | solution.py:283
  5.6 12.8 %collective-permute-start.2 = (f32[512,512]{1,0:T(8,128)}, f32[512,512]{1,0:T(8,128)S(1)}, u32[]{:S(2)}, u32[]{:S(2)}) collective-permute-start(f32[512,512]{1,0:T(8,128)} %inverse_ref), channel_id=1, source_target_pairs={{0,1},{1,0},{2,3},{3,2},{4,5},{5,4},{6,7},{7,6},{8,9},{9,8},{10,11... | collective-permute-start | bytes 3145736 | tf_op jit(solution)/shard_map/ppermute | solution.py:283
  5.9 7.5 %collective-permute-start.3 = (f32[72,512]{1,0:T(8,128)S(1)}, f32[72,512]{1,0:T(8,128)S(1)}, u32[]{:S(2)}, u32[]{:S(2)}) collective-permute-start(f32[72,512]{1,0:T(8,128)S(1)} %pad_maximum_fusion), channel_id=1, source_target_pairs={{0,2},{1,3},{2,0},{3,1},{4,6},{5,7},{6,4},{7,5},{8,10},{9,11},{10,... | collective-permute-start | bytes 442376 | tf_op jit(solution)/shard_map/ppermute | solution.py:283
  8.8 12.7 %collective-permute-start.5 = (f32[72,512]{1,0:T(8,128)S(1)}, f32[72,512]{1,0:T(8,128)S(1)}, u32[]{:S(2)}, u32[]{:S(2)}) collective-permute-start(f32[72,512]{1,0:T(8,128)S(1)} %pad_maximum_fusion), channel_id=1, source_target_pairs={{0,28},{1,29},{2,6},{3,7},{4,0},{5,1},{6,10},{7,11},{8,4},{9,5},{1... | collective-permute-start | bytes 442376 | tf_op jit(solution)/shard_map/ppermute | solution.py:293
  13.5 8.1 %collective-permute-start.4 = (f32[72,512]{1,0:T(8,128)S(1)}, f32[72,512]{1,0:T(8,128)S(1)}, u32[]{:S(2)}, u32[]{:S(2)}) collective-permute-start(f32[72,512]{1,0:T(8,128)S(1)} %pad_maximum_fusion.1._.refs_4_), channel_id=1, source_target_pairs={{0,4},{1,5},{2,30},{3,31},{4,8},{5,9},{6,2},{7,3},{8,12},{9,13},{1... | collective-permute-start | bytes 442376 | tf_op jit(solution)/shard_map/ppermute | solution.py:293
  24.3 9.9 %collective-permute-start.6 = (f32[64,512]{1,0:T(8,128)S(1)}, f32[64,512]{1,0:T(8,128)S(1)}, u32[]{:S(2)}, u32[]{:S(2)}) collective-permute-start(f32[64,512]{1,0:T(8,128)S(1)} %get-tuple-element.41._), channel_id=1, source_target_pairs={{0,2},{1,3},{2,0},{3,1},{4,6},{5,7},{6,4},{7,5},{8,10},{9,11},{10,... | collective-permute-start | bytes 393224 | tf_op jit(solution)/shard_map/ppermute | solution.py:283
  26.8 15.2 %collective-permute-start.8 = (f32[64,512]{1,0:T(8,128)S(1)}, f32[64,512]{1,0:T(8,128)S(1)}, u32[]{:S(2)}, u32[]{:S(2)}) collective-permute-start(f32[64,512]{1,0:T(8,128)S(1)} %get-tuple-element.41._), channel_id=1, source_target_pairs={{2,30},{3,31},{28,0},{29,1}} | collective-permute-start | bytes 393224 | tf_op jit(solution)/shard_map/ppermute | solution.py:302
  28.1 13.9 %collective-permute-start.9 = (f32[64,512]{1,0:T(8,128)S(1)}, f32[64,512]{1,0:T(8,128)S(1)}, u32[]{:S(2)}, u32[]{:S(2)}) collective-permute-start(f32[64,512]{1,0:T(8,128)S(1)} %get-tuple-element.41._), channel_id=1, source_target_pairs={{0,30},{1,31},{30,0},{31,1}} | collective-permute-start | bytes 393224 | tf_op jit(solution)/shard_map/ppermute | solution.py:302
  33.3 8.7 %collective-permute-start.10 = (f32[64,512]{1,0:T(8,128)S(1)}, f32[64,512]{1,0:T(8,128)S(1)}, u32[]{:S(2)}, u32[]{:S(2)}) collective-permute-start(f32[64,512]{1,0:T(8,128)S(1)} %get-tuple-element.41._), channel_id=1, source_target_pairs={{0,28},{1,29},{2,6},{3,7},{4,0},{5,1},{6,10},{7,11},{8,4},{9,5},{1... | collective-permute-start | bytes 393224 | tf_op jit(solution)/shard_map/ppermute | solution.py:293
  34.2 7.8 %collective-permute-start.7 = (f32[64,512]{1,0:T(8,128)S(1)}, f32[64,512]{1,0:T(8,128)S(1)}, u32[]{:S(2)}, u32[]{:S(2)}) collective-permute-start(f32[64,512]{1,0:T(8,128)S(1)} %broadcast_select_fusion.2.here.refs_9_), channel_id=1, source_target_pairs={{0,4},{1,5},{4,8},{5,9},{6,2},{7,3},{8,12},{9,13},{10,6},{11,7},{1... | collective-permute-start | bytes 393224 | tf_op jit(solution)/shard_map/ppermute | solution.py:293
  42.1 10.1 %collective-permute-start.11 = (f32[64,512]{1,0:T(8,128)S(1)}, f32[64,512]{1,0:T(8,128)S(1)}, u32[]{:S(2)}, u32[]{:S(2)}) collective-permute-start(f32[64,512]{1,0:T(8,128)S(1)} %get-tuple-element.46), channel_id=1, source_target_pairs={{0,2},{1,3},{2,0},{3,1},{4,6},{5,7},{6,4},{7,5},{8,10},{9,11},{10,... | collective-permute-start | bytes 393224 | tf_op jit(solution)/shard_map/ppermute | solution.py:283
  44.9 17.9 %collective-permute-start.13 = (f32[64,512]{1,0:T(8,128)S(1)}, f32[64,512]{1,0:T(8,128)S(1)}, u32[]{:S(2)}, u32[]{:S(2)}) collective-permute-start(f32[64,512]{1,0:T(8,128)S(1)} %get-tuple-element.46), channel_id=1, source_target_pairs={{2,30},{3,31},{28,0},{29,1}} | collective-permute-start | bytes 393224 | tf_op jit(solution)/shard_map/ppermute | solution.py:302
  46.2 16.6 %collective-permute-start.14 = (f32[64,512]{1,0:T(8,128)S(1)}, f32[64,512]{1,0:T(8,128)S(1)}, u32[]{:S(2)}, u32[]{:S(2)}) collective-permute-start(f32[64,512]{1,0:T(8,128)S(1)} %get-tuple-element.46), channel_id=1, source_target_pairs={{0,30},{1,31},{30,0},{31,1}} | collective-permute-start | bytes 393224 | tf_op jit(solution)/shard_map/ppermute | solution.py:302
  51.3 8.7 %collective-permute-start.15 = (f32[64,512]{1,0:T(8,128)S(1)}, f32[64,512]{1,0:T(8,128)S(1)}, u32[]{:S(2)}, u32[]{:S(2)}) collective-permute-start(f32[64,512]{1,0:T(8,128)S(1)} %get-tuple-element.46), channel_id=1, source_target_pairs={{0,28},{1,29},{2,6},{3,7},{4,0},{5,1},{6,10},{7,11},{8,4},{9,5},{1... | collective-permute-start | bytes 393224 | tf_op jit(solution)/shard_map/ppermute | solution.py:293
  52.3 10.5 %collective-permute-start.12 = (f32[64,512]{1,0:T(8,128)S(1)}, f32[64,512]{1,0:T(8,128)S(1)}, u32[]{:S(2)}, u32[]{:S(2)}) collective-permute-start(f32[64,512]{1,0:T(8,128)S(1)} %broadcast_select_fusion.4.here), channel_id=1, source_target_pairs={{0,4},{1,5},{4,8},{5,9},{6,2},{7,3},{8,12},{9,13},{10,6},{11,7},{1... | collective-permute-start | bytes 393224 | tf_op jit(solution)/shard_map/ppermute | solution.py:293
  64.0 7.5 %collective-permute-start.16 = (f32[64,512]{1,0:T(8,128)S(1)}, f32[64,512]{1,0:T(8,128)S(1)}, u32[]{:S(2)}, u32[]{:S(2)}) collective-permute-start(f32[64,512]{1,0:T(8,128)S(1)} %relax_3.1), channel_id=1, source_target_pairs={{0,2},{1,3},{2,0},{3,1},{4,6},{5,7},{6,4},{7,5},{8,10},{9,11},{10,... | collective-permute-start | bytes 393224 | tf_op jit(solution)/shard_map/ppermute | solution.py:283
  64.1 15.4 %collective-permute-start.18 = (f32[64,512]{1,0:T(8,128)S(1)}, f32[64,512]{1,0:T(8,128)S(1)}, u32[]{:S(2)}, u32[]{:S(2)}) collective-permute-start(f32[64,512]{1,0:T(8,128)S(1)} %relax_3.1), channel_id=1, source_target_pairs={{2,30},{3,31},{28,0},{29,1}} | collective-permute-start | bytes 393224 | tf_op jit(solution)/shard_map/ppermute | solution.py:302
  65.4 14.1 %collective-permute-start.19 = (f32[64,512]{1,0:T(8,128)S(1)}, f32[64,512]{1,0:T(8,128)S(1)}, u32[]{:S(2)}, u32[]{:S(2)}) collective-permute-start(f32[64,512]{1,0:T(8,128)S(1)} %relax_3.1), channel_id=1, source_target_pairs={{0,30},{1,31},{30,0},{31,1}} | collective-permute-start | bytes 393224 | tf_op jit(solution)/shard_map/ppermute | solution.py:302
  70.7 8.8 %collective-permute-start.20 = (f32[64,512]{1,0:T(8,128)S(1)}, f32[64,512]{1,0:T(8,128)S(1)}, u32[]{:S(2)}, u32[]{:S(2)}) collective-permute-start(f32[64,512]{1,0:T(8,128)S(1)} %relax_3.1), channel_id=1, source_target_pairs={{0,28},{1,29},{2,6},{3,7},{4,0},{5,1},{6,10},{7,11},{8,4},{9,5},{1... | collective-permute-start | bytes 393224 | tf_op jit(solution)/shard_map/ppermute | solution.py:293
  71.5 8.0 %collective-permute-start.17 = (f32[64,512]{1,0:T(8,128)S(1)}, f32[64,512]{1,0:T(8,128)S(1)}, u32[]{:S(2)}, u32[]{:S(2)}) collective-permute-start(f32[64,512]{1,0:T(8,128)S(1)} %broadcast_select_fusion.here.refs_4_.refs_9_), channel_id=1, source_target_pairs={{0,4},{1,5},{4,8},{5,9},{6,2},{7,3},{8,12},{9,13},{10,6},{11,7},{1... | collective-permute-start | bytes 393224 | tf_op jit(solution)/shard_map/ppermute | solution.py:293
  79.7 9.3 %collective-permute-start.21 = (f32[64,512]{1,0:T(8,128)S(1)}, f32[64,512]{1,0:T(8,128)S(1)}, u32[]{:S(2)}, u32[]{:S(2)}) collective-permute-start(f32[64,512]{1,0:T(8,128)S(1)} %relax_2.3), channel_id=1, source_target_pairs={{0,2},{1,3},{2,0},{3,1},{4,6},{5,7},{6,4},{7,5},{8,10},{9,11},{10,... | collective-permute-start | bytes 393224 | tf_op jit(solution)/shard_map/ppermute | solution.py:283
  81.6 15.9 %collective-permute-start.23 = (f32[64,512]{1,0:T(8,128)S(1)}, f32[64,512]{1,0:T(8,128)S(1)}, u32[]{:S(2)}, u32[]{:S(2)}) collective-permute-start(f32[64,512]{1,0:T(8,128)S(1)} %relax_2.3), channel_id=1, source_target_pairs={{2,30},{3,31},{28,0},{29,1}} | collective-permute-start | bytes 393224 | tf_op jit(solution)/shard_map/ppermute | solution.py:302
  82.9 14.6 %collective-permute-start.24 = (f32[64,512]{1,0:T(8,128)S(1)}, f32[64,512]{1,0:T(8,128)S(1)}, u32[]{:S(2)}, u32[]{:S(2)}) collective-permute-start(f32[64,512]{1,0:T(8,128)S(1)} %relax_2.3), channel_id=1, source_target_pairs={{0,30},{1,31},{30,0},{31,1}} | collective-permute-start | bytes 393224 | tf_op jit(solution)/shard_map/ppermute | solution.py:302
  86.9 9.4 %collective-permute-start.25 = (f32[64,512]{1,0:T(8,128)S(1)}, f32[64,512]{1,0:T(8,128)S(1)}, u32[]{:S(2)}, u32[]{:S(2)}) collective-permute-start(f32[64,512]{1,0:T(8,128)S(1)} %relax_2.3), channel_id=1, source_target_pairs={{0,28},{1,29},{2,6},{3,7},{4,0},{5,1},{6,10},{7,11},{8,4},{9,5},{1... | collective-permute-start | bytes 393224 | tf_op jit(solution)/shard_map/ppermute | solution.py:293
  89.0 8.6 %collective-permute-start.22 = (f32[64,512]{1,0:T(8,128)S(1)}, f32[64,512]{1,0:T(8,128)S(1)}, u32[]{:S(2)}, u32[]{:S(2)}) collective-permute-start(f32[64,512]{1,0:T(8,128)S(1)} %broadcast_select_fusion.3.here.refs_4_), channel_id=1, source_target_pairs={{0,4},{1,5},{4,8},{5,9},{6,2},{7,3},{8,12},{9,13},{10,6},{11,7},{1... | collective-permute-start | bytes 393224 | tf_op jit(solution)/shard_map/ppermute | solution.py:293
  98.7 7.5 %collective-permute-start.26 = (f32[64,512]{1,0:T(8,128)S(1)}, f32[64,512]{1,0:T(8,128)S(1)}, u32[]{:S(2)}, u32[]{:S(2)}) collective-permute-start(f32[64,512]{1,0:T(8,128)S(1)} %relax_1.3), channel_id=1, source_target_pairs={{0,2},{1,3},{2,0},{3,1},{4,6},{5,7},{6,4},{7,5},{8,10},{9,11},{10,... | collective-permute-start | bytes 393224 | tf_op jit(solution)/shard_map/ppermute | solution.py:283
  98.8 15.2 %collective-permute-start.28 = (f32[64,512]{1,0:T(8,128)S(1)}, f32[64,512]{1,0:T(8,128)S(1)}, u32[]{:S(2)}, u32[]{:S(2)}) collective-permute-start(f32[64,512]{1,0:T(8,128)S(1)} %relax_1.3), channel_id=1, source_target_pairs={{2,30},{3,31},{28,0},{29,1}} | collective-permute-start | bytes 393224 | tf_op jit(solution)/shard_map/ppermute | solution.py:302
  100.0 13.9 %collective-permute-start.29 = (f32[64,512]{1,0:T(8,128)S(1)}, f32[64,512]{1,0:T(8,128)S(1)}, u32[]{:S(2)}, u32[]{:S(2)}) collective-permute-start(f32[64,512]{1,0:T(8,128)S(1)} %relax_1.3), channel_id=1, source_target_pairs={{0,30},{1,31},{30,0},{31,1}} | collective-permute-start | bytes 393224 | tf_op jit(solution)/shard_map/ppermute | solution.py:302
  105.5 8.4 %collective-permute-start.30 = (f32[64,512]{1,0:T(8,128)S(1)}, f32[64,512]{1,0:T(8,128)S(1)}, u32[]{:S(2)}, u32[]{:S(2)}) collective-permute-start(f32[64,512]{1,0:T(8,128)S(1)} %relax_1.3), channel_id=1, source_target_pairs={{0,28},{1,29},{2,6},{3,7},{4,0},{5,1},{6,10},{7,11},{8,4},{9,5},{1... | collective-permute-start | bytes 393224 | tf_op jit(solution)/shard_map/ppermute | solution.py:293
  106.1 7.8 %collective-permute-start.27 = (f32[64,512]{1,0:T(8,128)S(1)}, f32[64,512]{1,0:T(8,128)S(1)}, u32[]{:S(2)}, u32[]{:S(2)}) collective-permute-start(f32[64,512]{1,0:T(8,128)S(1)} %broadcast_select_fusion.1.here), channel_id=1, source_target_pairs={{0,4},{1,5},{4,8},{5,9},{6,2},{7,3},{8,12},{9,13},{10,6},{11,7},{1... | collective-permute-start | bytes 393224 | tf_op jit(solution)/shard_map/ppermute | solution.py:293
  114.1 1.4 %collective-permute-start.31 = (f32[64,512]{1,0:T(8,128)S(1)}, f32[64,512]{1,0:T(8,128)S(1)}, u32[]{:S(2)}, u32[]{:S(2)}) collective-permute-start(f32[64,512]{1,0:T(8,128)S(1)} %get-tuple-element.60), channel_id=1, source_target_pairs={{0,1},{1,0},{2,3},{3,2},{4,5},{5,4},{6,7},{7,6},{8,9},{9,8},{10,11... | collective-permute-start | bytes 393224 | tf_op jit(solution)/shard_map/ppermute | solution.py:283

commit v9 on v7

--- a/solution.py
+++ b/solution.py
@@ -89,25 +89,16 @@
     out_ref[...] = jnp.transpose(jnp.concatenate([first, second], axis=0))
 
 
-def parts_kernel(stored, tiles_ref, inverse_ref, w_high, w_low, zeros, buffer, sems, *held):
+def parts_kernel(tiles_ref, inverse_ref, _, w_high, w_low, zeros, buffer, sems):
     zeros[...] = jnp.zeros_like(zeros)
     tiles = tiles_ref.shape[0]
-    copies = [pltpu.make_async_copy(tiles_ref.at[k], buffer.at[k], sems.at[0, k]) for k in range(tiles)]
-    copies.append(pltpu.make_async_copy(inverse_ref, buffer.at[tiles], sems.at[0, tiles]))
+    copies = [pltpu.make_async_copy(tiles_ref.at[k], buffer.at[k], sems.at[k]) for k in range(tiles)]
+    copies.append(pltpu.make_async_copy(inverse_ref, buffer.at[tiles], sems.at[tiles]))
     for copy in copies:
         copy.start()
-    high, low = held if stored else (w_high, w_low)
-    stores = []
     for k, copy in enumerate(copies):
         copy.wait()
-        high[k], low[k] = split(buffer[k])
-        if stored:
-            stores.append(pltpu.make_async_copy(high.at[k], w_high.at[k], sems.at[1, k]))
-            stores.append(pltpu.make_async_copy(low.at[k], w_low.at[k], sems.at[2, k]))
-            stores[-2].start()
-            stores[-1].start()
-    for store in stores:
-        store.wait()
+        w_high[k], w_low[k] = split(buffer[k])
 
 
 def plan_kernel(tiles, colours, firsts_ref, _, own_rows, arrived, inner, outer, here, *outs):
@@ -193,21 +184,19 @@
         out[...] = jnp.zeros_like(out)
 
 
-def parts(tiles, inverse, stored, name):
+def parts(tiles, inverse, after, name):
     count, block, _ = tiles.shape
     shape = (count + 1, block, block)
-    space = pltpu.HBM if stored else pltpu.VMEM
     return pl.pallas_call(
-        functools.partial(parts_kernel, stored),
-        out_shape=[space(shape, jnp.bfloat16)] * 2 + [pltpu.VMEM((EXTRA, block), jnp.float32)],
-        in_specs=[anywhere()] * 2,
-        out_specs=[hbm() if stored else vmem()] * 2 + [vmem()],
-        scratch_shapes=[pltpu.VMEM(shape, jnp.float32), pltpu.SemaphoreType.DMA((3, count + 1))]
-        + [pltpu.VMEM(shape, jnp.bfloat16)] * (2 * stored),
-        compiler_params=params(20 if stored else 12),
+        parts_kernel,
+        out_shape=[pltpu.VMEM(shape, jnp.bfloat16)] * 2 + [pltpu.VMEM((EXTRA, block), jnp.float32)],
+        in_specs=[anywhere()] * 3,
+        out_specs=[vmem()] * 3,
+        scratch_shapes=[pltpu.VMEM(shape, jnp.float32), pltpu.SemaphoreType.DMA((count + 1,))],
+        compiler_params=params(12),
         cost_estimate=pl.CostEstimate(flops=0, bytes_accessed=8 * count * block * block, transcendentals=0),
         name=name,
-    )(tiles, inverse)
+    )(tiles, inverse, *after)
 
 
 def make_plans(tiles, colours, firsts, own_rows, arrived, first_known, zeros):
@@ -301,25 +290,25 @@
     arrived = flip(send, 1)
     starts = [keep, arrived]
 
-    late_tiles, late_inverse, _ = lax.optimization_barrier((tiles, inv_diag, arrived))
-    sib_tiles, sib_inverse = flip(late_tiles, 1), flip(late_inverse, 1)
+    late_tiles, _ = lax.optimization_barrier((tiles, arrived))
+    sib_tiles, sib_inverse = flip(late_tiles, 1), flip(inv_diag, 1)
 
     own_wide, sib_wide = own_rows[:1], arrived[half : half + 1]
-    candidate = jnp.where(own_wide == 0, keep, arrived[:half])
+    candidate = jnp.where(own_wide == 0, keep, jnp.where(sib_wide == 0, arrived[:half], 0.0))
     wheel = lax.broadcasted_iota(jnp.int32, (EXTRA, block), 0).astype(jnp.float32)
     places = jnp.where(wheel == own_wide, place + 1, 0) + jnp.where(wheel == sib_wide, (place ^ 1) + 1, 0)
     places = places.astype(jnp.float32)
     sent = jnp.concatenate([candidate, places])
     swapped = flip(sent, 2)
     outer = beside(sent, 1)
-    far_tiles, far_inverse, _ = lax.optimization_barrier((tiles, inv_diag, sent))
-    *own_parts, zeros = parts(*far([far_tiles, far_inverse]), 1, "own_parts")
-    here = jnp.where((own_wide + zeros[:1] == 0) | (sib_wide == 0), candidate, swapped[:half])
+    here = jnp.where((own_wide == 0) | (sib_wide == 0), candidate, swapped[:half])
     here = jnp.concatenate([here, places + swapped[half:]])
     known = {0: [beside(here, 0), outer, here]}
     toward = jnp.where(place < COLOURS // 2, -1, 1)
     firsts = jnp.stack([((group + step) % groups) * COLOURS for step in (toward, -toward, 0 * toward)]).astype(jnp.int32)
-    *sib_parts, zeros = parts(sib_tiles, sib_inverse, 0, "sib_parts")
+    far_tiles, far_inverse, _ = lax.optimization_barrier((tiles, inv_diag, here))
+    *own_parts, zeros = parts(*far([far_tiles, far_inverse]), [here], "own_parts")
+    *sib_parts, zeros = parts(sib_tiles, sib_inverse, [zeros], "sib_parts")
     matrices = [*own_parts, *sib_parts]
     facts = (firsts, own_rows, arrived, known[0])
     order = list(range(1, COLOURS)) + list(range(COLOURS - 2, -1, -1))

time: 98.8 us -> 95.6 us (0.968); the launches traced: 98.2 us -> 96.2 us
  starting transfers between devices: 16.9 us -> 32.1 us
  waiting for transfers between devices: 55.6 us -> 41.8 us
  Pallas kernels: 23.3 us -> 20.1 us
    ppermute x10, waiting for transfers between devices: 19.5 us -> 9.61 us  [flip(): return lax.ppermute(value, axis, [(i, i ^ bit) for i in range(count)])]
    ppermute x12, starting transfers between devices: 12.5 us -> 20.8 us  [beside(): return lax.ppermute(value, axis, pairs)]
    ppermute x10, starting transfers between devices: 4.43 us -> 11.2 us  [flip(): return lax.ppermute(value, axis, [(i, i ^ bit) for i in range(count)])]
    ppermute x12, waiting for transfers between devices: 36.1 us -> 32.2 us  [beside(): return lax.ppermute(value, axis, pairs)]
    pallas_call x2, Pallas kernels: 9.64 us -> 6.45 us  [parts(): pl.pallas_call(parts_kernel, out_shape=[pltpu.VMEM(shape, jnp.bfloat16)]...]
  transfers between devices with their start and end apart: 22 -> 22, of which waited for: 14 -> 18; matrix products, arithmetic and copies ran while one was open for 1% -> 1% of each run, Pallas kernels for 17% -> 13%
where the time goes in v9:
time: 95.6 us; the launch traced here: 96.2 us
  waiting for transfers between devices  41.8 us (44%)
  starting transfers between devices  32.1 us (34%)
  Pallas kernels  20.1 us (21%)
    ppermute x12, waiting for transfers between devices, beside(): return lax.ppermute(value, axis, pairs)  32.2 us
    ppermute x12, starting transfers between devices, beside(): return lax.ppermute(value, axis, pairs)  20.8 us
    ppermute x10, starting transfers between devices, flip(): return lax.ppermute(value, axis, [(i, i ^ bit) for i in range(count)])  11.2 us
    ppermute x10, waiting for transfers between devices, flip(): return lax.ppermute(value, axis, [(i, i ^ bit) for i in range(count)])  9.61 us
    pallas_call x2, Pallas kernels, parts(): pl.pallas_call(parts_kernel, out_shape=[pltpu.VMEM(shape, jnp.bfloat16)]...  6.45 us
    pallas_call x5, Pallas kernels, add_older(): pl.pallas_call(functools.partial(older_kernel, newest, older, len(base)),...  5.1 us
    pallas_call x6, Pallas kernels, relax(): pl.pallas_call(functools.partial(relax_kernel, newest, sides), out_shape=...  3.69 us
    pallas_call x1, Pallas kernels, per_device(): pl.pallas_call(first_kernel, out_shape=[pltpu.VMEM((half, block), jnp.flo...  2.35 us
  transfers between devices with their start and end apart: 22, of which 18 were waited for; matrix products, arithmetic and copies ran while one was open for 1% of the time, Pallas kernels for 13%

profile of v9, /device:TPU:0, one launch (start us, length us, event | category | flops | bytes accessed | tf_op | source)
XLA Modules:
  0.0 96.2 jit_solution(13913573224218582620)
XLA Ops:
  0.7 0.6 copy-done
  1.3 2.4 %first.1 = (f32[64,512]{1,0:T(8,128)S(1)}, f32[72,512]{1,0:T(8,128)S(1)}, f32[8,512]{1,0:T(8,128)S(1)}) custom-call(s32[1]{0:T(128)} %bitcast.core_ref, s32[1]{0:T(128)S(6)} %copy.6.colour_ref, s32[1,6]{1,0:T(1,128)S(1)} %copy-done, f32[512,512]{1,0:T(8,128)} %inverse_ref, f32[512,128]{1,0:T(8,128)} %residual_hbm.1), custom_call_target="tpu_custom_call" | custom-call | tf_op jit(solution)/shard_map/first/pallas_call | solution.py:276
  3.7 0.5 collective-permute-start
  4.2 1.0 %collective-permute-done.arrived.sib_start = f32[72,512]{1,0:T(8,128)S(1)} collective-permute-done((f32[72,512]{1,0:T(8,128)S(1)}, f32[72,512]{1,0:T(8,128)S(1)}, u32[]{:S(2)}, u32[]{:S(2)}) %collective-permute-start) | collective-permute-done | bytes 147488 | tf_op jit(solution)/shard_map/ppermute | solution.py:267
  5.2 0.4 collective-permute-start.1
  5.6 0.1 collective-permute-start.2
  5.8 0.1 add_convert_fusion
  5.9 2.9 %collective-permute-start.3 = (f32[72,512]{1,0:T(8,128)S(1)}, f32[72,512]{1,0:T(8,128)S(1)}, u32[]{:S(2)}, u32[]{:S(2)}) collective-permute-start(f32[72,512]{1,0:T(8,128)S(1)} %pad_maximum_fusion), channel_id=1, source_target_pairs={{0,2},{1,3},{2,0},{3,1},{4,6},{5,7},{6,4},{7,5},{8,10},{9,11},{10,... | collective-permute-start | bytes 442376 | tf_op jit(solution)/shard_map/ppermute | solution.py:267
  8.8 4.5 %collective-permute-start.5 = (f32[72,512]{1,0:T(8,128)S(1)}, f32[72,512]{1,0:T(8,128)S(1)}, u32[]{:S(2)}, u32[]{:S(2)}) collective-permute-start(f32[72,512]{1,0:T(8,128)S(1)} %pad_maximum_fusion), channel_id=1, source_target_pairs={{0,28},{1,29},{2,6},{3,7},{4,0},{5,1},{6,10},{7,11},{8,4},{9,5},{1... | collective-permute-start | bytes 442376 | tf_op jit(solution)/shard_map/ppermute | solution.py:274
  13.5 1.4 %collective-permute-start.4 = (f32[72,512]{1,0:T(8,128)S(1)}, f32[72,512]{1,0:T(8,128)S(1)}, u32[]{:S(2)}, u32[]{:S(2)}) collective-permute-start(f32[72,512]{1,0:T(8,128)S(1)} %pad_maximum_fusion.1._.here.refs_2_), channel_id=1, source_target_pairs={{0,4},{1,5},{2,30},{3,31},{4,8},{5,9},{6,2},{7,3},{8,12},{9,13},{1... | collective-permute-start | bytes 442376 | tf_op jit(solution)/shard_map/ppermute | solution.py:274
  15.0 3.3 %own_parts.1 = (bf16[7,512,512]{2,1,0:T(8,128)(2,1)S(1)}, bf16[7,512,512]{2,1,0:T(8,128)(2,1)S(1)}, f32[8,512]{1,0:T(8,128)S(1)}) custom-call(f32[6,512,512]{2,1,0:T(8,128)} %bitcast.8, f32[512,512]{1,0:T(8,128)} %inverse_ref, f32[72,512]{1,0:T(8,128)S(1)} %pad_maximum_fusion.1._.here.refs_2_), custom_call_target="tpu_custom_call" | custom-call | bytes 12582912 | tf_op jit(solution)/shard_map/own_parts/pallas_call | solution.py:190
  18.3 3.1 %sib_parts.1 = (bf16[7,512,512]{2,1,0:T(8,128)(2,1)S(1)}, bf16[7,512,512]{2,1,0:T(8,128)(2,1)S(1)}, f32[8,512]{1,0:T(8,128)S(1)}) custom-call(f32[6,512,512]{2,1,0:T(8,128)} %collective-permute-done.1.tiles_ref, f32[512,512]{1,0:T(8,128)S(1)} %collective-permute-done.2.inverse_ref, f32[8,512]{1,0:T(8,128)S(1)} %get-tuple-element.34._), custom_call_target="tpu_custom_call" | custom-call | bytes 12582912 | tf_op jit(solution)/shard_map/sib_parts/pallas_call | solution.py:190
  21.5 0.1 collective-permute-done.4.inner.refs_0_
  21.6 0.6 plan_1.1
  22.2 0.1 relax_1.2
  22.3 6.1 %collective-permute-start.6 = (f32[64,512]{1,0:T(8,128)S(1)}, f32[64,512]{1,0:T(8,128)S(1)}, u32[]{:S(2)}, u32[]{:S(2)}) collective-permute-start(f32[64,512]{1,0:T(8,128)S(1)} %get-tuple-element.41._), channel_id=1, source_target_pairs={{0,2},{1,3},{2,0},{3,1},{4,6},{5,7},{6,4},{7,5},{8,10},{9,11},{10,... | collective-permute-start | bytes 393224 | tf_op jit(solution)/shard_map/ppermute | solution.py:267
  28.3 0.8 collective-permute-start.8
  29.1 2.2 %collective-permute-done.6 = f32[64,512]{1,0:T(8,128)S(1)} collective-permute-done((f32[64,512]{1,0:T(8,128)S(1)}, f32[64,512]{1,0:T(8,128)S(1)}, u32[]{:S(2)}, u32[]{:S(2)}) %collective-permute-start.6) | collective-permute-done | bytes 131104 | tf_op jit(solution)/shard_map/ppermute | solution.py:267
  31.4 1.2 %plan_3.1 = (s32[16,128]{1,0:T(8,128)S(1)}, s32[16,128]{1,0:T(8,128)S(1)}, s32[16,128]{1,0:T(8,128)S(1)}, s32[8,512]{1,0:T(8,128)}, s32[8,512]{1,0:T(8,128)S(1)}, /*index=5*/s32[8,512]{1,0:T(8,128)S(1)}) custom-call(s32[3]{0:T(128)S(1)} %pad_add_fusion.firsts_ref, f32[64,512]{1,0:T(8,128)S(1)} %get-tuple-element.41._, ...), custom_call_target="tpu_custom_call" | custom-call | tf_op jit(solution)/shard_map/plan_3/pallas_call | solution.py:206
  32.5 0.8 collective-permute-done.8.outer.refs_4_
  33.3 1.7 %older_2.2.refs_1_ = f32[64,512]{1,0:T(8,128)S(1)} custom-call(s32[16,128]{1,0:T(8,128)S(1)} %get-tuple-element.44.plan, bf16[7,512,512]{2,1,0:T(8,128)(2,1)S(1)} %get-tuple-element.37.own_high, bf16[7,512,512]{2,1,0:T(8,128)(2,1)S(1)} %get-tuple-element.38.own_low, bf16[7,512,512]{2,1,0:T(8,128)(2,1)S(1)} %get-tuple-element.39.sib_high, ...), custom_call_target="tpu_custom_call" | custom-call | flops 671088640 | bytes 5242880 | tf_op jit(solution)/shard_map/older_2/pallas_call | solution.py:221
  35.0 4.0 %collective-permute-done.7.refs_0_.refs_3_ = f32[64,512]{1,0:T(8,128)S(1)} collective-permute-done((f32[64,512]{1,0:T(8,128)S(1)}, f32[64,512]{1,0:T(8,128)S(1)}, u32[]{:S(2)}, u32[]{:S(2)}) %collective-permute-start.7) | collective-permute-done | bytes 131104 | tf_op jit(solution)/shard_map/ppermute | solution.py:274
  39.0 1.1 %relax_2.2 = (f32[64,512]{1,0:T(8,128)S(1)}, f32[64,512]{1,0:T(8,128)S(1)}) custom-call(s32[16,128]{1,0:T(8,128)S(1)} %get-tuple-element.44.plan, bf16[7,512,512]{2,1,0:T(8,128)(2,1)S(1)} %get-tuple-element.37.own_high, bf16[7,512,512]{2,1,0:T(8,128)(2,1)S(1)} %get-tuple-element.38.own_low, bf16[7,512,512]{2,1,0:T(8,128)(2,1)S(1)} %get-tuple-element.39.sib_high, ...), custom_call_target="tpu_custom_call" | custom-call | flops 536870912 | bytes 4194304 | tf_op jit(solution)/shard_map/relax_2/pallas_call | solution.py:239
  40.2 3.7 %collective-permute-start.11 = (f32[64,512]{1,0:T(8,128)S(1)}, f32[64,512]{1,0:T(8,128)S(1)}, u32[]{:S(2)}, u32[]{:S(2)}) collective-permute-start(f32[64,512]{1,0:T(8,128)S(1)} %get-tuple-element.46), channel_id=1, source_target_pairs={{0,28},{1,29},{2,6},{3,7},{4,0},{5,1},{6,10},{7,11},{8,4},{9,5},{1... | collective-permute-start | bytes 393224 | tf_op jit(solution)/shard_map/ppermute | solution.py:274
  43.9 1.2 %collective-permute-done.9 = f32[64,512]{1,0:T(8,128)S(1)} collective-permute-done((f32[64,512]{1,0:T(8,128)S(1)}, f32[64,512]{1,0:T(8,128)S(1)}, u32[]{:S(2)}, u32[]{:S(2)}) %collective-permute-start.9) | collective-permute-done | bytes 131104 | tf_op jit(solution)/shard_map/ppermute | solution.py:267
  45.2 1.2 %collective-permute-done.11.outer = f32[64,512]{1,0:T(8,128)S(1)} collective-permute-done((f32[64,512]{1,0:T(8,128)S(1)}, f32[64,512]{1,0:T(8,128)S(1)}, u32[]{:S(2)}, u32[]{:S(2)}) %collective-permute-start.11) | collective-permute-done | bytes 131104 | tf_op jit(solution)/shard_map/ppermute | solution.py:274
  46.5 6.4 %collective-permute-done.10.refs_0_ = f32[64,512]{1,0:T(8,128)S(1)} collective-permute-done((f32[64,512]{1,0:T(8,128)S(1)}, f32[64,512]{1,0:T(8,128)S(1)}, u32[]{:S(2)}, u32[]{:S(2)}) %collective-permute-start.10) | collective-permute-done | bytes 131104 | tf_op jit(solution)/shard_map/ppermute | solution.py:274
  52.9 0.3 relax_3.1
  53.2 0.9 collective-permute-start.12
  54.1 2.8 %collective-permute-start.14 = (f32[64,512]{1,0:T(8,128)S(1)}, f32[64,512]{1,0:T(8,128)S(1)}, u32[]{:S(2)}, u32[]{:S(2)}) collective-permute-start(f32[64,512]{1,0:T(8,128)S(1)} %relax_3.1), channel_id=1, source_target_pairs={{0,28},{1,29},{2,6},{3,7},{4,0},{5,1},{6,10},{7,11},{8,4},{9,5},{1... | collective-permute-start | bytes 393224 | tf_op jit(solution)/shard_map/ppermute | solution.py:274
  57.0 1.2 %collective-permute-done.12 = f32[64,512]{1,0:T(8,128)S(1)} collective-permute-done((f32[64,512]{1,0:T(8,128)S(1)}, f32[64,512]{1,0:T(8,128)S(1)}, u32[]{:S(2)}, u32[]{:S(2)}) %collective-permute-start.12) | collective-permute-done | bytes 131104 | tf_op jit(solution)/shard_map/ppermute | solution.py:267
  58.3 2.2 %collective-permute-done.14.outer.refs_1_.refs_4_ = f32[64,512]{1,0:T(8,128)S(1)} collective-permute-done((f32[64,512]{1,0:T(8,128)S(1)}, f32[64,512]{1,0:T(8,128)S(1)}, u32[]{:S(2)}, u32[]{:S(2)}) %collective-permute-start.14) | collective-permute-done | bytes 131104 | tf_op jit(solution)/shard_map/ppermute | solution.py:274
  60.5 0.6 older_2.3.refs_1_
  61.2 4.9 %collective-permute-done.13.refs_0_.refs_3_ = f32[64,512]{1,0:T(8,128)S(1)} collective-permute-done((f32[64,512]{1,0:T(8,128)S(1)}, f32[64,512]{1,0:T(8,128)S(1)}, u32[]{:S(2)}, u32[]{:S(2)}) %collective-permute-start.13) | collective-permute-done | bytes 131104 | tf_op jit(solution)/shard_map/ppermute | solution.py:274
  66.1 1.1 %relax_2.3 = f32[64,512]{1,0:T(8,128)S(1)} custom-call(s32[16,128]{1,0:T(8,128)S(1)} %get-tuple-element.44.plan, bf16[7,512,512]{2,1,0:T(8,128)(2,1)S(1)} %get-tuple-element.37.own_high, bf16[7,512,512]{2,1,0:T(8,128)(2,1)S(1)} %get-tuple-element.38.own_low, bf16[7,512,512]{2,1,0:T(8,128)(2,1)S(1)} %get-tuple-element.39.sib_high, ...), custom_call_target="tpu_custom_call" | custom-call | flops 536870912 | bytes 4194304 | tf_op jit(solution)/shard_map/relax_2/pallas_call | solution.py:239
  67.2 3.6 %collective-permute-start.17 = (f32[64,512]{1,0:T(8,128)S(1)}, f32[64,512]{1,0:T(8,128)S(1)}, u32[]{:S(2)}, u32[]{:S(2)}) collective-permute-start(f32[64,512]{1,0:T(8,128)S(1)} %relax_2.3), channel_id=1, source_target_pairs={{0,28},{1,29},{2,6},{3,7},{4,0},{5,1},{6,10},{7,11},{8,4},{9,5},{1... | collective-permute-start | bytes 393224 | tf_op jit(solution)/shard_map/ppermute | solution.py:274
  70.9 1.3 %collective-permute-done.15 = f32[64,512]{1,0:T(8,128)S(1)} collective-permute-done((f32[64,512]{1,0:T(8,128)S(1)}, f32[64,512]{1,0:T(8,128)S(1)}, u32[]{:S(2)}, u32[]{:S(2)}) %collective-permute-start.15) | collective-permute-done | bytes 131104 | tf_op jit(solution)/shard_map/ppermute | solution.py:267
  72.3 1.1 %collective-permute-done.17.outer.refs_1_ = f32[64,512]{1,0:T(8,128)S(1)} collective-permute-done((f32[64,512]{1,0:T(8,128)S(1)}, f32[64,512]{1,0:T(8,128)S(1)}, u32[]{:S(2)}, u32[]{:S(2)}) %collective-permute-start.17) | collective-permute-done | bytes 131104 | tf_op jit(solution)/shard_map/ppermute | solution.py:274
  73.4 6.5 %collective-permute-done.16.refs_0_ = f32[64,512]{1,0:T(8,128)S(1)} collective-permute-done((f32[64,512]{1,0:T(8,128)S(1)}, f32[64,512]{1,0:T(8,128)S(1)}, u32[]{:S(2)}, u32[]{:S(2)}) %collective-permute-start.16) | collective-permute-done | bytes 131104 | tf_op jit(solution)/shard_map/ppermute | solution.py:274
  79.9 0.1 relax_1.3
  80.1 3.6 %collective-permute-start.20 = (f32[64,512]{1,0:T(8,128)S(1)}, f32[64,512]{1,0:T(8,128)S(1)}, u32[]{:S(2)}, u32[]{:S(2)}) collective-permute-start(f32[64,512]{1,0:T(8,128)S(1)} %relax_1.3), channel_id=1, source_target_pairs={{0,28},{1,29},{2,6},{3,7},{4,0},{5,1},{6,10},{7,11},{8,4},{9,5},{1... | collective-permute-start | bytes 393224 | tf_op jit(solution)/shard_map/ppermute | solution.py:274
  83.7 1.3 %collective-permute-done.18 = f32[64,512]{1,0:T(8,128)S(1)} collective-permute-done((f32[64,512]{1,0:T(8,128)S(1)}, f32[64,512]{1,0:T(8,128)S(1)}, u32[]{:S(2)}, u32[]{:S(2)}) %collective-permute-start.18) | collective-permute-done | bytes 131104 | tf_op jit(solution)/shard_map/ppermute | solution.py:267
  85.1 1.1 %collective-permute-done.20.outer = f32[64,512]{1,0:T(8,128)S(1)} collective-permute-done((f32[64,512]{1,0:T(8,128)S(1)}, f32[64,512]{1,0:T(8,128)S(1)}, u32[]{:S(2)}, u32[]{:S(2)}) %collective-permute-start.20) | collective-permute-done | bytes 131104 | tf_op jit(solution)/shard_map/ppermute | solution.py:274
  86.3 2.7 %older_0.1.refs_1_ = f32[64,512]{1,0:T(8,128)S(1)} custom-call(s32[16,128]{1,0:T(8,128)S(1)} %get-tuple-element.50.plan, bf16[7,512,512]{2,1,0:T(8,128)(2,1)S(1)} %get-tuple-element.37.own_high, bf16[7,512,512]{2,1,0:T(8,128)(2,1)S(1)} %get-tuple-element.38.own_low, bf16[7,512,512]{2,1,0:T(8,128)(2,1)S(1)} %get-tuple-element.39.sib_high, ...), custom_call_target="tpu_custom_call" | custom-call | flops 1073741824 | bytes 8388608 | tf_op jit(solution)/shard_map/older_0/pallas_call | solution.py:221
  89.0 3.8 %collective-permute-done.19.refs_0_ = f32[64,512]{1,0:T(8,128)S(1)} collective-permute-done((f32[64,512]{1,0:T(8,128)S(1)}, f32[64,512]{1,0:T(8,128)S(1)}, u32[]{:S(2)}, u32[]{:S(2)}) %collective-permute-start.19) | collective-permute-done | bytes 131104 | tf_op jit(solution)/shard_map/ppermute | solution.py:274
  92.8 1.1 %relax_0.1 = f32[64,512]{1,0:T(8,128)S(1)} custom-call(s32[16,128]{1,0:T(8,128)S(1)} %get-tuple-element.50.plan, bf16[7,512,512]{2,1,0:T(8,128)(2,1)S(1)} %get-tuple-element.37.own_high, bf16[7,512,512]{2,1,0:T(8,128)(2,1)S(1)} %get-tuple-element.38.own_low, bf16[7,512,512]{2,1,0:T(8,128)(2,1)S(1)} %get-tuple-element.39.sib_high, ...), custom_call_target="tpu_custom_call" | custom-call | flops 536870912 | bytes 4194304 | tf_op jit(solution)/shard_map/relax_0/pallas_call | solution.py:239
  94.0 1.3 %collective-permute-done.21.other_ref = f32[64,512]{1,0:T(8,128)S(1)} collective-permute-done((f32[64,512]{1,0:T(8,128)S(1)}, f32[64,512]{1,0:T(8,128)S(1)}, u32[]{:S(2)}, u32[]{:S(2)}) %collective-permute-start.21) | collective-permute-done | bytes 131104 | tf_op jit(solution)/shard_map/ppermute | solution.py:267
  95.4 0.8 last.1
  (35 shorter events, 1.2 us)
Async XLA Ops:
  0.7 0.7 copy-start
  3.7 1.5 %collective-permute-start = (f32[72,512]{1,0:T(8,128)S(1)}, f32[72,512]{1,0:T(8,128)S(1)}, u32[]{:S(2)}, u32[]{:S(2)}) collective-permute-start(f32[72,512]{1,0:T(8,128)S(1)} %get-tuple-element.29), channel_id=1, source_target_pairs={{0,1},{1,0},{2,3},{3,2},{4,5},{5,4},{6,7},{7,6},{8,9},{9,8},{10,11... | collective-permute-start | bytes 442376 | tf_op jit(solution)/shard_map/ppermute | solution.py:267
  5.2 13.1 %collective-permute-start.1 = (f32[6,512,512]{2,1,0:T(8,128)}, f32[6,512,512]{2,1,0:T(8,128)}, u32[]{:S(2)}, u32[]{:S(2)}) collective-permute-start(f32[6,512,512]{2,1,0:T(8,128)} %bitcast.7), channel_id=1, source_target_pairs={{0,1},{1,0},{2,3},{3,2},{4,5},{5,4},{6,7},{7,6},{8,9},{9,8},{10,11... | collective-permute-start | bytes 18874376 | tf_op jit(solution)/shard_map/ppermute | solution.py:267
  5.6 12.8 %collective-permute-start.2 = (f32[512,512]{1,0:T(8,128)}, f32[512,512]{1,0:T(8,128)S(1)}, u32[]{:S(2)}, u32[]{:S(2)}) collective-permute-start(f32[512,512]{1,0:T(8,128)} %inverse_ref), channel_id=1, source_target_pairs={{0,1},{1,0},{2,3},{3,2},{4,5},{5,4},{6,7},{7,6},{8,9},{9,8},{10,11... | collective-permute-start | bytes 3145736 | tf_op jit(solution)/shard_map/ppermute | solution.py:267
  5.9 7.5 %collective-permute-start.3 = (f32[72,512]{1,0:T(8,128)S(1)}, f32[72,512]{1,0:T(8,128)S(1)}, u32[]{:S(2)}, u32[]{:S(2)}) collective-permute-start(f32[72,512]{1,0:T(8,128)S(1)} %pad_maximum_fusion), channel_id=1, source_target_pairs={{0,2},{1,3},{2,0},{3,1},{4,6},{5,7},{6,4},{7,5},{8,10},{9,11},{10,... | collective-permute-start | bytes 442376 | tf_op jit(solution)/shard_map/ppermute | solution.py:267
  8.8 12.7 %collective-permute-start.5 = (f32[72,512]{1,0:T(8,128)S(1)}, f32[72,512]{1,0:T(8,128)S(1)}, u32[]{:S(2)}, u32[]{:S(2)}) collective-permute-start(f32[72,512]{1,0:T(8,128)S(1)} %pad_maximum_fusion), channel_id=1, source_target_pairs={{0,28},{1,29},{2,6},{3,7},{4,0},{5,1},{6,10},{7,11},{8,4},{9,5},{1... | collective-permute-start | bytes 442376 | tf_op jit(solution)/shard_map/ppermute | solution.py:274
  13.5 8.1 %collective-permute-start.4 = (f32[72,512]{1,0:T(8,128)S(1)}, f32[72,512]{1,0:T(8,128)S(1)}, u32[]{:S(2)}, u32[]{:S(2)}) collective-permute-start(f32[72,512]{1,0:T(8,128)S(1)} %pad_maximum_fusion.1._.here.refs_2_), channel_id=1, source_target_pairs={{0,4},{1,5},{2,30},{3,31},{4,8},{5,9},{6,2},{7,3},{8,12},{9,13},{1... | collective-permute-start | bytes 442376 | tf_op jit(solution)/shard_map/ppermute | solution.py:274
  22.3 9.0 %collective-permute-start.6 = (f32[64,512]{1,0:T(8,128)S(1)}, f32[64,512]{1,0:T(8,128)S(1)}, u32[]{:S(2)}, u32[]{:S(2)}) collective-permute-start(f32[64,512]{1,0:T(8,128)S(1)} %get-tuple-element.41._), channel_id=1, source_target_pairs={{0,2},{1,3},{2,0},{3,1},{4,6},{5,7},{6,4},{7,5},{8,10},{9,11},{10,... | collective-permute-start | bytes 393224 | tf_op jit(solution)/shard_map/ppermute | solution.py:267
  28.3 5.0 %collective-permute-start.8 = (f32[64,512]{1,0:T(8,128)S(1)}, f32[64,512]{1,0:T(8,128)S(1)}, u32[]{:S(2)}, u32[]{:S(2)}) collective-permute-start(f32[64,512]{1,0:T(8,128)S(1)} %get-tuple-element.41._), channel_id=1, source_target_pairs={{0,28},{1,29},{2,6},{3,7},{4,0},{5,1},{6,10},{7,11},{8,4},{9,5},{1... | collective-permute-start | bytes 393224 | tf_op jit(solution)/shard_map/ppermute | solution.py:274
  31.3 7.7 %collective-permute-start.7 = (f32[64,512]{1,0:T(8,128)S(1)}, f32[64,512]{1,0:T(8,128)S(1)}, u32[]{:S(2)}, u32[]{:S(2)}) collective-permute-start(f32[64,512]{1,0:T(8,128)S(1)} %broadcast_select_fusion.2.here.refs_5_), channel_id=1, source_target_pairs={{0,4},{1,5},{2,30},{3,31},{4,8},{5,9},{6,2},{7,3},{8,12},{9,13},{1... | collective-permute-start | bytes 393224 | tf_op jit(solution)/shard_map/ppermute | solution.py:274
  40.1 5.0 %collective-permute-start.9 = (f32[64,512]{1,0:T(8,128)S(1)}, f32[64,512]{1,0:T(8,128)S(1)}, u32[]{:S(2)}, u32[]{:S(2)}) collective-permute-start(f32[64,512]{1,0:T(8,128)S(1)} %get-tuple-element.46), channel_id=1, source_target_pairs={{0,2},{1,3},{2,0},{3,1},{4,6},{5,7},{6,4},{7,5},{8,10},{9,11},{10,... | collective-permute-start | bytes 393224 | tf_op jit(solution)/shard_map/ppermute | solution.py:267
  40.2 6.2 %collective-permute-start.11 = (f32[64,512]{1,0:T(8,128)S(1)}, f32[64,512]{1,0:T(8,128)S(1)}, u32[]{:S(2)}, u32[]{:S(2)}) collective-permute-start(f32[64,512]{1,0:T(8,128)S(1)} %get-tuple-element.46), channel_id=1, source_target_pairs={{0,28},{1,29},{2,6},{3,7},{4,0},{5,1},{6,10},{7,11},{8,4},{9,5},{1... | collective-permute-start | bytes 393224 | tf_op jit(solution)/shard_map/ppermute | solution.py:274
  45.2 7.7 %collective-permute-start.10 = (f32[64,512]{1,0:T(8,128)S(1)}, f32[64,512]{1,0:T(8,128)S(1)}, u32[]{:S(2)}, u32[]{:S(2)}) collective-permute-start(f32[64,512]{1,0:T(8,128)S(1)} %broadcast_select_fusion.4.here), channel_id=1, source_target_pairs={{0,4},{1,5},{2,30},{3,31},{4,8},{5,9},{6,2},{7,3},{8,12},{9,13},{1... | collective-permute-start | bytes 393224 | tf_op jit(solution)/shard_map/ppermute | solution.py:274
  53.2 5.0 %collective-permute-start.12 = (f32[64,512]{1,0:T(8,128)S(1)}, f32[64,512]{1,0:T(8,128)S(1)}, u32[]{:S(2)}, u32[]{:S(2)}) collective-permute-start(f32[64,512]{1,0:T(8,128)S(1)} %relax_3.1), channel_id=1, source_target_pairs={{0,2},{1,3},{2,0},{3,1},{4,6},{5,7},{6,4},{7,5},{8,10},{9,11},{10,... | collective-permute-start | bytes 393224 | tf_op jit(solution)/shard_map/ppermute | solution.py:267
  54.1 6.4 %collective-permute-start.14 = (f32[64,512]{1,0:T(8,128)S(1)}, f32[64,512]{1,0:T(8,128)S(1)}, u32[]{:S(2)}, u32[]{:S(2)}) collective-permute-start(f32[64,512]{1,0:T(8,128)S(1)} %relax_3.1), channel_id=1, source_target_pairs={{0,28},{1,29},{2,6},{3,7},{4,0},{5,1},{6,10},{7,11},{8,4},{9,5},{1... | collective-permute-start | bytes 393224 | tf_op jit(solution)/shard_map/ppermute | solution.py:274
  58.2 7.8 %collective-permute-start.13 = (f32[64,512]{1,0:T(8,128)S(1)}, f32[64,512]{1,0:T(8,128)S(1)}, u32[]{:S(2)}, u32[]{:S(2)}) collective-permute-start(f32[64,512]{1,0:T(8,128)S(1)} %broadcast_select_fusion.here.refs_2_.refs_5_), channel_id=1, source_target_pairs={{0,4},{1,5},{2,30},{3,31},{4,8},{5,9},{6,2},{7,3},{8,12},{9,13},{1... | collective-permute-start | bytes 393224 | tf_op jit(solution)/shard_map/ppermute | solution.py:274
  67.1 5.0 %collective-permute-start.15 = (f32[64,512]{1,0:T(8,128)S(1)}, f32[64,512]{1,0:T(8,128)S(1)}, u32[]{:S(2)}, u32[]{:S(2)}) collective-permute-start(f32[64,512]{1,0:T(8,128)S(1)} %relax_2.3), channel_id=1, source_target_pairs={{0,2},{1,3},{2,0},{3,1},{4,6},{5,7},{6,4},{7,5},{8,10},{9,11},{10,... | collective-permute-start | bytes 393224 | tf_op jit(solution)/shard_map/ppermute | solution.py:267
  67.2 6.2 %collective-permute-start.17 = (f32[64,512]{1,0:T(8,128)S(1)}, f32[64,512]{1,0:T(8,128)S(1)}, u32[]{:S(2)}, u32[]{:S(2)}) collective-permute-start(f32[64,512]{1,0:T(8,128)S(1)} %relax_2.3), channel_id=1, source_target_pairs={{0,28},{1,29},{2,6},{3,7},{4,0},{5,1},{6,10},{7,11},{8,4},{9,5},{1... | collective-permute-start | bytes 393224 | tf_op jit(solution)/shard_map/ppermute | solution.py:274
  72.2 7.7 %collective-permute-start.16 = (f32[64,512]{1,0:T(8,128)S(1)}, f32[64,512]{1,0:T(8,128)S(1)}, u32[]{:S(2)}, u32[]{:S(2)}) collective-permute-start(f32[64,512]{1,0:T(8,128)S(1)} %broadcast_select_fusion.3.here.refs_2_), channel_id=1, source_target_pairs={{0,4},{1,5},{2,30},{3,31},{4,8},{5,9},{6,2},{7,3},{8,12},{9,13},{1... | collective-permute-start | bytes 393224 | tf_op jit(solution)/shard_map/ppermute | solution.py:274
  80.0 5.0 %collective-permute-start.18 = (f32[64,512]{1,0:T(8,128)S(1)}, f32[64,512]{1,0:T(8,128)S(1)}, u32[]{:S(2)}, u32[]{:S(2)}) collective-permute-start(f32[64,512]{1,0:T(8,128)S(1)} %relax_1.3), channel_id=1, source_target_pairs={{0,2},{1,3},{2,0},{3,1},{4,6},{5,7},{6,4},{7,5},{8,10},{9,11},{10,... | collective-permute-start | bytes 393224 | tf_op jit(solution)/shard_map/ppermute | solution.py:267
  80.1 6.2 %collective-permute-start.20 = (f32[64,512]{1,0:T(8,128)S(1)}, f32[64,512]{1,0:T(8,128)S(1)}, u32[]{:S(2)}, u32[]{:S(2)}) collective-permute-start(f32[64,512]{1,0:T(8,128)S(1)} %relax_1.3), channel_id=1, source_target_pairs={{0,28},{1,29},{2,6},{3,7},{4,0},{5,1},{6,10},{7,11},{8,4},{9,5},{1... | collective-permute-start | bytes 393224 | tf_op jit(solution)/shard_map/ppermute | solution.py:274
  85.1 7.7 %collective-permute-start.19 = (f32[64,512]{1,0:T(8,128)S(1)}, f32[64,512]{1,0:T(8,128)S(1)}, u32[]{:S(2)}, u32[]{:S(2)}) collective-permute-start(f32[64,512]{1,0:T(8,128)S(1)} %broadcast_select_fusion.1.here), channel_id=1, source_target_pairs={{0,4},{1,5},{2,30},{3,31},{4,8},{5,9},{6,2},{7,3},{8,12},{9,13},{1... | collective-permute-start | bytes 393224 | tf_op jit(solution)/shard_map/ppermute | solution.py:274
  94.0 1.4 %collective-permute-start.21 = (f32[64,512]{1,0:T(8,128)S(1)}, f32[64,512]{1,0:T(8,128)S(1)}, u32[]{:S(2)}, u32[]{:S(2)}) collective-permute-start(f32[64,512]{1,0:T(8,128)S(1)} %get-tuple-element.60), channel_id=1, source_target_pairs={{0,1},{1,0},{2,3},{3,2},{4,5},{5,4},{6,7},{7,6},{8,9},{9,8},{10,11... | collective-permute-start | bytes 393224 | tf_op jit(solution)/shard_map/ppermute | solution.py:267

commit v10 on v9

--- a/solution.py
+++ b/solution.py
@@ -17,6 +17,10 @@
 
 def dot_t(a, b):
     return lax.dot_general(a, b, (((1,), (1,)), ((), ())), preferred_element_type=jnp.float32)
+
+
+def dot(a, b):
+    return jnp.dot(a, b, preferred_element_type=jnp.float32)
 
 
 def split(value):
@@ -140,14 +144,22 @@
         body(*sib)
 
 
-def older_kernel(newest, older, has_base, plan, own_high, own_low, sib_high, sib_low, outer, here, *refs):
-    *refs, partial = refs
-    known, base = refs[: SIDES * len(older)], refs[SIDES * len(older) :]
+def older_kernel(newest, slots, has_base, plan, own_high, own_low, sib_high, sib_low, own_start, sib_start, outer, here, *refs):
+    *refs, partial, begin, m_high, m_low = refs
+    known, base = refs[: len(slots)], refs[len(slots) :]
     half = partial.shape[0]
-    slots = [(newest, OUTER, outer), (newest, HERE, here)]
-    slots += [(c, side, known[SIDES * i + side]) for i, c in enumerate(older) for side in range(SIDES)]
-
-    def body(w_high, w_low):
+    slots = [(newest, OUTER, outer), (newest, HERE, here)] + [(*slot, ref) for slot, ref in zip(slots, known)]
+
+    def body(w_high, w_low, start):
+        last = w_high.shape[0] - 1
+        inner = plan[TILE + INNER * COLOURS + newest, 0]
+
+        @pl.when(inner >= 0)
+        def _():
+            high, low = w_high[last], w_low[last]
+            tile_high, tile_low = w_high[inner], w_low[inner]
+            m_high[...], m_low[...] = split(dot(high, tile_high) + (dot(high, tile_low) + dot(low, tile_high)))
+
         partial[...] = base[0][...] if has_base else jnp.zeros_like(partial)
         for c, side, ref in slots:
             k = plan[TILE + side * COLOURS + c, 0]
@@ -156,17 +168,34 @@
             def _():
                 partial[...] += times(ref[:half, :], w_high[k], w_low[k])
 
-    chosen(plan, body, (own_high, own_low), (sib_high, sib_low))
-
-
-def relax_kernel(newest, sides, plan, own_high, own_low, sib_high, sib_low, own_start, sib_start, *refs):
-    latest, refs = refs[:sides], refs[sides:]
-    base, refs = refs[: int(sides < SIDES)], refs[int(sides < SIDES) :]
-    out, total = refs[:2]
+        begin[...] = start[:half, :] - times(partial[...], w_high[last], w_low[last])
+
+    chosen(plan, body, (own_high, own_low, own_start), (sib_high, sib_low, sib_start))
+
+
+def relax_kernel(newest, plan, inner, begin, m_high, m_low, out):
+    active = plan[ACTIVE, 0] != 0
+    meets = plan[TILE + INNER * COLOURS + newest, 0] >= 0
+
+    @pl.when(active & meets)
+    def _():
+        out[...] = begin[...] - times(inner[...], m_high[...], m_low[...])
+
+    @pl.when(active & jnp.logical_not(meets))
+    def _():
+        out[...] = begin[...]
+
+    @pl.when(jnp.logical_not(active))
+    def _():
+        out[...] = jnp.zeros_like(out)
+
+
+def first_relax_kernel(newest, plan, own_high, own_low, sib_high, sib_low, own_start, sib_start, *refs):
+    *latest, out, total = refs
     half = out.shape[0]
 
     def body(w_high, w_low, begin):
-        total[...] = base[0][...] if base else jnp.zeros_like(total)
+        total[...] = jnp.zeros_like(total)
         for side, ref in enumerate(latest):
             k = plan[TILE + side * COLOURS + newest, 0]
 
@@ -214,40 +243,35 @@
     return dict(zip(colours, outs[:number])), dict(zip(colours, outs[number:]))
 
 
-def add_older(now, newest, older, plan, matrices, outer, here, known, base):
-    half, block = here.shape
-    operands = near([plan, *matrices, outer, here, *[value for c in older for value in known[c]], *base])
-    slots = 2 + SIDES * len(older)
+def add_older(now, newest, slots, plan, matrices, starts, outer, here, known, base):
+    half, block = starts[0].shape
+    operands = near([plan, *matrices, *starts, outer, here, *[known[c][side] for c, side in slots], *base])
+    value, matrix = pltpu.VMEM((half, block), jnp.float32), pltpu.VMEM((block, block), jnp.bfloat16)
     return pl.pallas_call(
-        functools.partial(older_kernel, newest, older, len(base)),
-        out_shape=pltpu.VMEM((half, block), jnp.float32),
+        functools.partial(older_kernel, newest, slots, len(base)),
+        out_shape=[value, value, matrix, matrix],
         in_specs=[vmem()] * len(operands),
-        out_specs=vmem(),
-        compiler_params=params(8),
+        out_specs=[vmem()] * 4,
+        compiler_params=params(16),
         cost_estimate=pl.CostEstimate(
-            flops=4 * block * block * LANES * slots, bytes_accessed=4 * block * block * slots, transcendentals=0
+            flops=4 * block * block * LANES * (2 + len(slots)), bytes_accessed=24 * block * block, transcendentals=0
         ),
         name=f"older_{now}",
     )(*operands)
 
 
-def relax(now, newest, plan, matrices, starts, latest, partial, keep_sum):
-    half, block = starts[0].shape
-    sides = 1 if partial else SIDES
-    operands = near([plan, *matrices, *starts, *latest[:sides], *partial])
-    value = pltpu.VMEM((half, block), jnp.float32)
+def run_relax(name, kernel, operands, half, block, outs):
     return pl.pallas_call(
-        functools.partial(relax_kernel, newest, sides),
-        out_shape=[value] * (1 + keep_sum),
+        kernel,
+        out_shape=[pltpu.VMEM((half, block), jnp.float32)] * outs,
         in_specs=[vmem()] * len(operands),
-        out_specs=[vmem()] * (1 + keep_sum),
-        scratch_shapes=[value] * (1 - keep_sum),
+        out_specs=[vmem()] * outs,
         compiler_params=params(8),
         cost_estimate=pl.CostEstimate(
             flops=16 * block * block * LANES, bytes_accessed=16 * block * block, transcendentals=0
         ),
-        name=f"relax_{now}",
-    )(*operands)
+        name=name,
+    )(*near(operands))
 
 
 def per_device(residual, inv_diag, coupling_tiles, colour, tile_cols):
@@ -314,12 +338,17 @@
     order = list(range(1, COLOURS)) + list(range(COLOURS - 2, -1, -1))
     plans, masks = make_plans(number, order[:1], *facts, zeros)
     newest = 0
-    sums, used, finals = {}, {}, {}
-    partial = []
+    bases, included, finals = {}, {}, {}
     for step, now in enumerate(order):
-        used[now] = {(c, done_at(order, c, step)) for c in known if c != now}
-        outs = relax(now, newest, plans[now], matrices, starts, known[newest], partial, int(now in order[step + 1 :]))
-        candidate, sums[now] = outs[0], outs[1:]
+        if step == 0:
+            operands = [plans[now], *matrices, *starts, *known[newest]]
+            kernel = functools.partial(first_relax_kernel, newest)
+            candidate, bases[now] = run_relax(f"relax_{now}", kernel, operands, half, block, 2)
+            included[now] = {(newest, -1, side) for side in range(SIDES)}
+        else:
+            operands = [plans[now], known[newest][INNER], *update]
+            kernel = functools.partial(relax_kernel, newest)
+            (candidate,) = run_relax(f"relax_{now}", kernel, operands, half, block, 1)
         finals[now] = candidate
         if step == len(order) - 1:
             break
@@ -332,9 +361,17 @@
         outer = beside(candidate, 1)
         here = jnp.where(masks[now][:1] != 0, candidate, swapped)
         inner = beside(here, 0)
-        fresh = used.get(after, set())
-        older = tuple(c for c in sorted(known) if c not in (now, after) and (c, done_at(order, c, step)) not in fresh)
-        partial = [add_older(after, now, older, plans[after], matrices, outer, here, known, sums.get(after, []))]
+        have = included.get(after, set())
+        slots, all_slots = [], {(now, step, OUTER), (now, step, HERE)}
+        for c in sorted(known):
+            for side in range(SIDES):
+                if c not in (now, after):
+                    all_slots.add((c, done_at(order, c, step), side))
+                    if (c, done_at(order, c, step), side) not in have:
+                        slots.append((c, side))
+        base = [bases[after]] if after in bases else []
+        partial, *update = add_older(after, now, slots, plans[after], matrices, starts, outer, here, known, base)
+        bases[after], included[after] = partial, all_slots
         known[now] = [inner, outer, here]
         newest = now
 

time: 95.6 us -> 93.7 us (0.980); the launches traced: 96.2 us -> 93.4 us
  waiting for transfers between devices: 41.8 us -> 35.7 us
  Pallas kernels: 20.1 us -> 23.6 us
    ppermute x12, waiting for transfers between devices: 32.2 us -> 25.9 us  [beside(): return lax.ppermute(value, axis, pairs)]
    pallas_call x11, Pallas kernels: 8.79 us -> 12.2 us  [the longest x5 11.4 us: add_older(): pl.pallas_call(functools.partial(older_kernel, newest, slots, len(base)),...]
    ppermute x12, starting transfers between devices: 20.8 us -> 18.5 us  [beside(): return lax.ppermute(value, axis, pairs)]
    ppermute x10, starting transfers between devices: 11.2 us -> 13.4 us  [flip(): return lax.ppermute(value, axis, [(i, i ^ bit) for i in range(count)])]
  transfers between devices with their start and end apart: 22 -> 22, of which waited for: 18 -> 18; matrix products, arithmetic and copies ran while one was open for 1% -> 1% of each run, Pallas kernels for 13% -> 20%
where the time goes in v10:
time: 93.7 us; the launch traced here: 93.4 us
  waiting for transfers between devices  35.7 us (38%)
  starting transfers between devices  31.9 us (34%)
  Pallas kernels  23.6 us (25%)
    ppermute x12, waiting for transfers between devices, beside(): return lax.ppermute(value, axis, pairs)  25.9 us
    ppermute x12, starting transfers between devices, beside(): return lax.ppermute(value, axis, pairs)  18.5 us
    ppermute x10, starting transfers between devices, flip(): return lax.ppermute(value, axis, [(i, i ^ bit) for i in range(count)])  13.4 us
    pallas_call x5, Pallas kernels, add_older(): pl.pallas_call(functools.partial(older_kernel, newest, slots, len(base)),...  11.4 us
    ppermute x10, waiting for transfers between devices, flip(): return lax.ppermute(value, axis, [(i, i ^ bit) for i in range(count)])  9.79 us
    pallas_call x2, Pallas kernels, parts(): pl.pallas_call(parts_kernel, out_shape=[pltpu.VMEM(shape, jnp.bfloat16)]...  6.45 us
    pallas_call x1, Pallas kernels, per_device(): pl.pallas_call(first_kernel, out_shape=[pltpu.VMEM((half, block), jnp.flo...  2.35 us
  transfers between devices with their start and end apart: 22, of which 18 were waited for; matrix products, arithmetic and copies ran while one was open for 1% of the time, Pallas kernels for 20%

profile of v10, /device:TPU:0, one launch (start us, length us, event | category | flops | bytes accessed | tf_op | source)
XLA Modules:
  0.0 93.4 jit_solution(10242539412721436897)
XLA Ops:
  0.7 0.6 copy-done
  1.3 2.4 %first.1 = (f32[64,512]{1,0:T(8,128)S(1)}, f32[72,512]{1,0:T(8,128)S(1)}, f32[8,512]{1,0:T(8,128)S(1)}) custom-call(s32[1]{0:T(128)} %bitcast.core_ref, s32[1]{0:T(128)S(6)} %copy.6.colour_ref, s32[1,6]{1,0:T(1,128)S(1)} %copy-done, f32[512,512]{1,0:T(8,128)} %inverse_ref, f32[512,128]{1,0:T(8,128)} %residual_hbm.1), custom_call_target="tpu_custom_call" | custom-call | tf_op jit(solution)/shard_map/first/pallas_call | solution.py:300
  3.7 0.5 collective-permute-start
  4.2 1.0 %collective-permute-done.arrived.sib_start = f32[72,512]{1,0:T(8,128)S(1)} collective-permute-done((f32[72,512]{1,0:T(8,128)S(1)}, f32[72,512]{1,0:T(8,128)S(1)}, u32[]{:S(2)}, u32[]{:S(2)}) %collective-permute-start) | collective-permute-done | bytes 147488 | tf_op jit(solution)/shard_map/ppermute | solution.py:291
  5.2 0.4 collective-permute-start.1
  5.6 0.1 collective-permute-start.2
  5.8 0.1 add_convert_fusion
  5.9 2.9 %collective-permute-start.3 = (f32[72,512]{1,0:T(8,128)S(1)}, f32[72,512]{1,0:T(8,128)S(1)}, u32[]{:S(2)}, u32[]{:S(2)}) collective-permute-start(f32[72,512]{1,0:T(8,128)S(1)} %pad_maximum_fusion), channel_id=1, source_target_pairs={{0,2},{1,3},{2,0},{3,1},{4,6},{5,7},{6,4},{7,5},{8,10},{9,11},{10,... | collective-permute-start | bytes 442376 | tf_op jit(solution)/shard_map/ppermute | solution.py:291
  8.8 4.5 %collective-permute-start.5 = (f32[72,512]{1,0:T(8,128)S(1)}, f32[72,512]{1,0:T(8,128)S(1)}, u32[]{:S(2)}, u32[]{:S(2)}) collective-permute-start(f32[72,512]{1,0:T(8,128)S(1)} %pad_maximum_fusion), channel_id=1, source_target_pairs={{0,28},{1,29},{2,6},{3,7},{4,0},{5,1},{6,10},{7,11},{8,4},{9,5},{1... | collective-permute-start | bytes 442376 | tf_op jit(solution)/shard_map/ppermute | solution.py:298
  13.4 0.1 slice_add_fusion
  13.5 1.4 %collective-permute-start.4 = (f32[72,512]{1,0:T(8,128)S(1)}, f32[72,512]{1,0:T(8,128)S(1)}, u32[]{:S(2)}, u32[]{:S(2)}) collective-permute-start(f32[72,512]{1,0:T(8,128)S(1)} %pad_maximum_fusion.1._.here.refs_2_), channel_id=1, source_target_pairs={{0,4},{1,5},{2,30},{3,31},{4,8},{5,9},{6,2},{7,3},{8,12},{9,13},{1... | collective-permute-start | bytes 442376 | tf_op jit(solution)/shard_map/ppermute | solution.py:298
  15.0 3.3 %own_parts.1 = (bf16[7,512,512]{2,1,0:T(8,128)(2,1)S(1)}, bf16[7,512,512]{2,1,0:T(8,128)(2,1)S(1)}, f32[8,512]{1,0:T(8,128)S(1)}) custom-call(f32[6,512,512]{2,1,0:T(8,128)} %bitcast.8, f32[512,512]{1,0:T(8,128)} %inverse_ref, f32[72,512]{1,0:T(8,128)S(1)} %pad_maximum_fusion.1._.here.refs_2_), custom_call_target="tpu_custom_call" | custom-call | bytes 12582912 | tf_op jit(solution)/shard_map/own_parts/pallas_call | solution.py:219
  18.3 3.1 %sib_parts.1 = (bf16[7,512,512]{2,1,0:T(8,128)(2,1)S(1)}, bf16[7,512,512]{2,1,0:T(8,128)(2,1)S(1)}, f32[8,512]{1,0:T(8,128)S(1)}) custom-call(f32[6,512,512]{2,1,0:T(8,128)} %collective-permute-done.1.tiles_ref, f32[512,512]{1,0:T(8,128)S(1)} %collective-permute-done.2.inverse_ref, f32[8,512]{1,0:T(8,128)S(1)} %get-tuple-element.48._), custom_call_target="tpu_custom_call" | custom-call | bytes 12582912 | tf_op jit(solution)/shard_map/sib_parts/pallas_call | solution.py:219
  21.5 0.1 collective-permute-done.4.inner.refs_0_
  21.6 0.6 plan_1.1
  22.2 0.1 relax_1.2
  22.3 6.1 %collective-permute-start.6 = (f32[64,512]{1,0:T(8,128)S(1)}, f32[64,512]{1,0:T(8,128)S(1)}, u32[]{:S(2)}, u32[]{:S(2)}) collective-permute-start(f32[64,512]{1,0:T(8,128)S(1)} %get-tuple-element.55._), channel_id=1, source_target_pairs={{0,2},{1,3},{2,0},{3,1},{4,6},{5,7},{6,4},{7,5},{8,10},{9,11},{10,... | collective-permute-start | bytes 393224 | tf_op jit(solution)/shard_map/ppermute | solution.py:291
  28.3 0.2 collective-permute-start.8
  28.5 2.7 %collective-permute-done.6 = f32[64,512]{1,0:T(8,128)S(1)} collective-permute-done((f32[64,512]{1,0:T(8,128)S(1)}, f32[64,512]{1,0:T(8,128)S(1)}, u32[]{:S(2)}, u32[]{:S(2)}) %collective-permute-start.6) | collective-permute-done | bytes 131104 | tf_op jit(solution)/shard_map/ppermute | solution.py:291
  31.4 1.2 %plan_3.1 = (s32[16,128]{1,0:T(8,128)S(1)}, s32[16,128]{1,0:T(8,128)S(1)}, s32[16,128]{1,0:T(8,128)S(1)}, s32[8,512]{1,0:T(8,128)}, s32[8,512]{1,0:T(8,128)S(1)}, /*index=5*/s32[8,512]{1,0:T(8,128)S(1)}) custom-call(s32[3]{0:T(128)S(1)} %pad_add_fusion.firsts_ref, f32[64,512]{1,0:T(8,128)S(1)} %get-tuple-element.55._, ...), custom_call_target="tpu_custom_call" | custom-call | tf_op jit(solution)/shard_map/plan_3/pallas_call | solution.py:235
  32.5 0.8 collective-permute-done.8.outer.refs_4_
  33.3 2.7 %older_2.2 = (f32[64,512]{1,0:T(8,128)S(1)}, f32[64,512]{1,0:T(8,128)S(1)}, bf16[512,512]{1,0:T(8,128)(2,1)S(1)}, bf16[512,512]{1,0:T(8,128)(2,1)S(1)}) custom-call(s32[16,128]{1,0:T(8,128)S(1)} %get-tuple-element.58.plan, bf16[7,512,512]{2,1,0:T(8,128)(2,1)S(1)} %get-tuple-element.51.own_high, bf16[7,512,512]{2,1,0:T(8,128)(2,1)S(1)} %get-tuple-element.52.own_low, ...), custom_call_target="tpu_custom_call" | custom-call | flops 671088640 | bytes 6291456 | tf_op jit(solution)/shard_map/older_2/pallas_call | solution.py:250
  36.0 3.1 %collective-permute-done.7.inner.refs_3_.refs_0_ = f32[64,512]{1,0:T(8,128)S(1)} collective-permute-done((f32[64,512]{1,0:T(8,128)S(1)}, f32[64,512]{1,0:T(8,128)S(1)}, u32[]{:S(2)}, u32[]{:S(2)}) %collective-permute-start.7) | collective-permute-done | bytes 131104 | tf_op jit(solution)/shard_map/ppermute | solution.py:298
  39.2 3.3 %collective-permute-start.11 = (f32[64,512]{1,0:T(8,128)S(1)}, f32[64,512]{1,0:T(8,128)S(1)}, u32[]{:S(2)}, u32[]{:S(2)}) collective-permute-start(f32[64,512]{1,0:T(8,128)S(1)} %relax_2.2), channel_id=1, source_target_pairs={{0,28},{1,29},{2,6},{3,7},{4,0},{5,1},{6,10},{7,11},{8,4},{9,5},{1... | collective-permute-start | bytes 393224 | tf_op jit(solution)/shard_map/ppermute | solution.py:298
  42.5 1.6 %collective-permute-done.9 = f32[64,512]{1,0:T(8,128)S(1)} collective-permute-done((f32[64,512]{1,0:T(8,128)S(1)}, f32[64,512]{1,0:T(8,128)S(1)}, u32[]{:S(2)}, u32[]{:S(2)}) %collective-permute-start.9) | collective-permute-done | bytes 131104 | tf_op jit(solution)/shard_map/ppermute | solution.py:291
  44.2 0.8 collective-permute-done.11.outer
  45.0 0.9 older_3.1
  45.9 6.0 %collective-permute-done.10.inner = f32[64,512]{1,0:T(8,128)S(1)} collective-permute-done((f32[64,512]{1,0:T(8,128)S(1)}, f32[64,512]{1,0:T(8,128)S(1)}, u32[]{:S(2)}, u32[]{:S(2)}) %collective-permute-start.10) | collective-permute-done | bytes 131104 | tf_op jit(solution)/shard_map/ppermute | solution.py:298
  51.9 1.8 %collective-permute-start.12 = (f32[64,512]{1,0:T(8,128)S(1)}, f32[64,512]{1,0:T(8,128)S(1)}, u32[]{:S(2)}, u32[]{:S(2)}) collective-permute-start(f32[64,512]{1,0:T(8,128)S(1)} %relax_3.1), channel_id=1, source_target_pairs={{0,2},{1,3},{2,0},{3,1},{4,6},{5,7},{6,4},{7,5},{8,10},{9,11},{10,... | collective-permute-start | bytes 393224 | tf_op jit(solution)/shard_map/ppermute | solution.py:291
  53.7 2.3 %collective-permute-start.14 = (f32[64,512]{1,0:T(8,128)S(1)}, f32[64,512]{1,0:T(8,128)S(1)}, u32[]{:S(2)}, u32[]{:S(2)}) collective-permute-start(f32[64,512]{1,0:T(8,128)S(1)} %relax_3.1), channel_id=1, source_target_pairs={{0,28},{1,29},{2,6},{3,7},{4,0},{5,1},{6,10},{7,11},{8,4},{9,5},{1... | collective-permute-start | bytes 393224 | tf_op jit(solution)/shard_map/ppermute | solution.py:298
  56.0 1.0 %collective-permute-done.12 = f32[64,512]{1,0:T(8,128)S(1)} collective-permute-done((f32[64,512]{1,0:T(8,128)S(1)}, f32[64,512]{1,0:T(8,128)S(1)}, u32[]{:S(2)}, u32[]{:S(2)}) %collective-permute-start.12) | collective-permute-done | bytes 131104 | tf_op jit(solution)/shard_map/ppermute | solution.py:291
  57.1 3.1 %collective-permute-done.14.outer.refs_1_.refs_4_ = f32[64,512]{1,0:T(8,128)S(1)} collective-permute-done((f32[64,512]{1,0:T(8,128)S(1)}, f32[64,512]{1,0:T(8,128)S(1)}, u32[]{:S(2)}, u32[]{:S(2)}) %collective-permute-start.14) | collective-permute-done | bytes 131104 | tf_op jit(solution)/shard_map/ppermute | solution.py:298
  60.1 2.8 %older_2.3 = (f32[64,512]{1,0:T(8,128)}, f32[64,512]{1,0:T(8,128)S(1)}, bf16[512,512]{1,0:T(8,128)(2,1)S(1)}, bf16[512,512]{1,0:T(8,128)(2,1)S(1)}) custom-call(s32[16,128]{1,0:T(8,128)S(1)} %get-tuple-element.58.plan, bf16[7,512,512]{2,1,0:T(8,128)(2,1)S(1)} %get-tuple-element.51.own_high, bf16[7,512,512]{2,1,0:T(8,128)(2,1)S(1)} %get-tuple-element.52.own_low, ...), custom_call_target="tpu_custom_call" | custom-call | flops 402653184 | bytes 6291456 | tf_op jit(solution)/shard_map/older_2/pallas_call | solution.py:250
  62.9 1.9 %collective-permute-done.13.inner.refs_0_.refs_3_ = f32[64,512]{1,0:T(8,128)S(1)} collective-permute-done((f32[64,512]{1,0:T(8,128)S(1)}, f32[64,512]{1,0:T(8,128)S(1)}, u32[]{:S(2)}, u32[]{:S(2)}) %collective-permute-start.13) | collective-permute-done | bytes 131104 | tf_op jit(solution)/shard_map/ppermute | solution.py:298
  64.8 0.5 relax_2.3
  65.4 3.9 %collective-permute-start.17 = (f32[64,512]{1,0:T(8,128)S(1)}, f32[64,512]{1,0:T(8,128)S(1)}, u32[]{:S(2)}, u32[]{:S(2)}) collective-permute-start(f32[64,512]{1,0:T(8,128)S(1)} %relax_2.3), channel_id=1, source_target_pairs={{0,28},{1,29},{2,6},{3,7},{4,0},{5,1},{6,10},{7,11},{8,4},{9,5},{1... | collective-permute-start | bytes 393224 | tf_op jit(solution)/shard_map/ppermute | solution.py:298
  69.3 1.1 %collective-permute-done.15 = f32[64,512]{1,0:T(8,128)S(1)} collective-permute-done((f32[64,512]{1,0:T(8,128)S(1)}, f32[64,512]{1,0:T(8,128)S(1)}, u32[]{:S(2)}, u32[]{:S(2)}) %collective-permute-start.15) | collective-permute-done | bytes 131104 | tf_op jit(solution)/shard_map/ppermute | solution.py:291
  70.5 1.4 %collective-permute-done.17.outer.refs_1_ = f32[64,512]{1,0:T(8,128)S(1)} collective-permute-done((f32[64,512]{1,0:T(8,128)S(1)}, f32[64,512]{1,0:T(8,128)S(1)}, u32[]{:S(2)}, u32[]{:S(2)}) %collective-permute-start.17) | collective-permute-done | bytes 131104 | tf_op jit(solution)/shard_map/ppermute | solution.py:298
  71.9 0.7 older_1.1
  72.6 5.6 %collective-permute-done.16.inner.refs_0_ = f32[64,512]{1,0:T(8,128)S(1)} collective-permute-done((f32[64,512]{1,0:T(8,128)S(1)}, f32[64,512]{1,0:T(8,128)S(1)}, u32[]{:S(2)}, u32[]{:S(2)}) %collective-permute-start.16) | collective-permute-done | bytes 131104 | tf_op jit(solution)/shard_map/ppermute | solution.py:298
  78.2 1.4 %collective-permute-start.18 = (f32[64,512]{1,0:T(8,128)S(1)}, f32[64,512]{1,0:T(8,128)S(1)}, u32[]{:S(2)}, u32[]{:S(2)}) collective-permute-start(f32[64,512]{1,0:T(8,128)S(1)} %relax_1.3), channel_id=1, source_target_pairs={{0,2},{1,3},{2,0},{3,1},{4,6},{5,7},{6,4},{7,5},{8,10},{9,11},{10,... | collective-permute-start | bytes 393224 | tf_op jit(solution)/shard_map/ppermute | solution.py:291
  79.6 2.6 %collective-permute-start.20 = (f32[64,512]{1,0:T(8,128)S(1)}, f32[64,512]{1,0:T(8,128)S(1)}, u32[]{:S(2)}, u32[]{:S(2)}) collective-permute-start(f32[64,512]{1,0:T(8,128)S(1)} %relax_1.3), channel_id=1, source_target_pairs={{0,28},{1,29},{2,6},{3,7},{4,0},{5,1},{6,10},{7,11},{8,4},{9,5},{1... | collective-permute-start | bytes 393224 | tf_op jit(solution)/shard_map/ppermute | solution.py:298
  82.3 1.0 %collective-permute-done.18 = f32[64,512]{1,0:T(8,128)S(1)} collective-permute-done((f32[64,512]{1,0:T(8,128)S(1)}, f32[64,512]{1,0:T(8,128)S(1)}, u32[]{:S(2)}, u32[]{:S(2)}) %collective-permute-start.18) | collective-permute-done | bytes 131104 | tf_op jit(solution)/shard_map/ppermute | solution.py:291
  83.3 1.5 %collective-permute-done.20.outer = f32[64,512]{1,0:T(8,128)S(1)} collective-permute-done((f32[64,512]{1,0:T(8,128)S(1)}, f32[64,512]{1,0:T(8,128)S(1)}, u32[]{:S(2)}, u32[]{:S(2)}) %collective-permute-start.20) | collective-permute-done | bytes 131104 | tf_op jit(solution)/shard_map/ppermute | solution.py:298
  84.8 4.4 %older_0.1 = (f32[64,512]{1,0:T(8,128)}, f32[64,512]{1,0:T(8,128)S(1)}, bf16[512,512]{1,0:T(8,128)(2,1)S(1)}, bf16[512,512]{1,0:T(8,128)(2,1)S(1)}) custom-call(s32[16,128]{1,0:T(8,128)S(1)} %get-tuple-element.75.plan, bf16[7,512,512]{2,1,0:T(8,128)(2,1)S(1)} %get-tuple-element.51.own_high, bf16[7,512,512]{2,1,0:T(8,128)(2,1)S(1)} %get-tuple-element.52.own_low, ...), custom_call_target="tpu_custom_call" | custom-call | flops 1073741824 | bytes 6291456 | tf_op jit(solution)/shard_map/older_0/pallas_call | solution.py:250
  89.2 1.8 %collective-permute-done.19.inner = f32[64,512]{1,0:T(8,128)S(1)} collective-permute-done((f32[64,512]{1,0:T(8,128)S(1)}, f32[64,512]{1,0:T(8,128)S(1)}, u32[]{:S(2)}, u32[]{:S(2)}) %collective-permute-start.19) | collective-permute-done | bytes 131104 | tf_op jit(solution)/shard_map/ppermute | solution.py:298
  91.2 1.3 %collective-permute-done.21.other_ref = f32[64,512]{1,0:T(8,128)S(1)} collective-permute-done((f32[64,512]{1,0:T(8,128)S(1)}, f32[64,512]{1,0:T(8,128)S(1)}, u32[]{:S(2)}, u32[]{:S(2)}) %collective-permute-start.21) | collective-permute-done | bytes 131104 | tf_op jit(solution)/shard_map/ppermute | solution.py:291
  92.5 0.8 last.1
  (35 shorter events, 1.2 us)
Async XLA Ops:
  0.7 0.7 copy-start
  3.7 1.5 %collective-permute-start = (f32[72,512]{1,0:T(8,128)S(1)}, f32[72,512]{1,0:T(8,128)S(1)}, u32[]{:S(2)}, u32[]{:S(2)}) collective-permute-start(f32[72,512]{1,0:T(8,128)S(1)} %get-tuple-element.43), channel_id=1, source_target_pairs={{0,1},{1,0},{2,3},{3,2},{4,5},{5,4},{6,7},{7,6},{8,9},{9,8},{10,11... | collective-permute-start | bytes 442376 | tf_op jit(solution)/shard_map/ppermute | solution.py:291
  5.2 13.1 %collective-permute-start.1 = (f32[6,512,512]{2,1,0:T(8,128)}, f32[6,512,512]{2,1,0:T(8,128)}, u32[]{:S(2)}, u32[]{:S(2)}) collective-permute-start(f32[6,512,512]{2,1,0:T(8,128)} %bitcast.7), channel_id=1, source_target_pairs={{0,1},{1,0},{2,3},{3,2},{4,5},{5,4},{6,7},{7,6},{8,9},{9,8},{10,11... | collective-permute-start | bytes 18874376 | tf_op jit(solution)/shard_map/ppermute | solution.py:291
  5.6 12.8 %collective-permute-start.2 = (f32[512,512]{1,0:T(8,128)}, f32[512,512]{1,0:T(8,128)S(1)}, u32[]{:S(2)}, u32[]{:S(2)}) collective-permute-start(f32[512,512]{1,0:T(8,128)} %inverse_ref), channel_id=1, source_target_pairs={{0,1},{1,0},{2,3},{3,2},{4,5},{5,4},{6,7},{7,6},{8,9},{9,8},{10,11... | collective-permute-start | bytes 3145736 | tf_op jit(solution)/shard_map/ppermute | solution.py:291
  5.9 7.5 %collective-permute-start.3 = (f32[72,512]{1,0:T(8,128)S(1)}, f32[72,512]{1,0:T(8,128)S(1)}, u32[]{:S(2)}, u32[]{:S(2)}) collective-permute-start(f32[72,512]{1,0:T(8,128)S(1)} %pad_maximum_fusion), channel_id=1, source_target_pairs={{0,2},{1,3},{2,0},{3,1},{4,6},{5,7},{6,4},{7,5},{8,10},{9,11},{10,... | collective-permute-start | bytes 442376 | tf_op jit(solution)/shard_map/ppermute | solution.py:291
  8.8 12.7 %collective-permute-start.5 = (f32[72,512]{1,0:T(8,128)S(1)}, f32[72,512]{1,0:T(8,128)S(1)}, u32[]{:S(2)}, u32[]{:S(2)}) collective-permute-start(f32[72,512]{1,0:T(8,128)S(1)} %pad_maximum_fusion), channel_id=1, source_target_pairs={{0,28},{1,29},{2,6},{3,7},{4,0},{5,1},{6,10},{7,11},{8,4},{9,5},{1... | collective-permute-start | bytes 442376 | tf_op jit(solution)/shard_map/ppermute | solution.py:298
  13.5 8.1 %collective-permute-start.4 = (f32[72,512]{1,0:T(8,128)S(1)}, f32[72,512]{1,0:T(8,128)S(1)}, u32[]{:S(2)}, u32[]{:S(2)}) collective-permute-start(f32[72,512]{1,0:T(8,128)S(1)} %pad_maximum_fusion.1._.here.refs_2_), channel_id=1, source_target_pairs={{0,4},{1,5},{2,30},{3,31},{4,8},{5,9},{6,2},{7,3},{8,12},{9,13},{1... | collective-permute-start | bytes 442376 | tf_op jit(solution)/shard_map/ppermute | solution.py:298
  22.3 9.0 %collective-permute-start.6 = (f32[64,512]{1,0:T(8,128)S(1)}, f32[64,512]{1,0:T(8,128)S(1)}, u32[]{:S(2)}, u32[]{:S(2)}) collective-permute-start(f32[64,512]{1,0:T(8,128)S(1)} %get-tuple-element.55._), channel_id=1, source_target_pairs={{0,2},{1,3},{2,0},{3,1},{4,6},{5,7},{6,4},{7,5},{8,10},{9,11},{10,... | collective-permute-start | bytes 393224 | tf_op jit(solution)/shard_map/ppermute | solution.py:291
  28.3 5.0 %collective-permute-start.8 = (f32[64,512]{1,0:T(8,128)S(1)}, f32[64,512]{1,0:T(8,128)S(1)}, u32[]{:S(2)}, u32[]{:S(2)}) collective-permute-start(f32[64,512]{1,0:T(8,128)S(1)} %get-tuple-element.55._), channel_id=1, source_target_pairs={{0,28},{1,29},{2,6},{3,7},{4,0},{5,1},{6,10},{7,11},{8,4},{9,5},{1... | collective-permute-start | bytes 393224 | tf_op jit(solution)/shard_map/ppermute | solution.py:298
  31.3 7.7 %collective-permute-start.7 = (f32[64,512]{1,0:T(8,128)S(1)}, f32[64,512]{1,0:T(8,128)S(1)}, u32[]{:S(2)}, u32[]{:S(2)}) collective-permute-start(f32[64,512]{1,0:T(8,128)S(1)} %broadcast_select_fusion.2.here.refs_5_), channel_id=1, source_target_pairs={{0,4},{1,5},{2,30},{3,31},{4,8},{5,9},{6,2},{7,3},{8,12},{9,13},{1... | collective-permute-start | bytes 393224 | tf_op jit(solution)/shard_map/ppermute | solution.py:298
  39.1 5.0 %collective-permute-start.9 = (f32[64,512]{1,0:T(8,128)S(1)}, f32[64,512]{1,0:T(8,128)S(1)}, u32[]{:S(2)}, u32[]{:S(2)}) collective-permute-start(f32[64,512]{1,0:T(8,128)S(1)} %relax_2.2), channel_id=1, source_target_pairs={{0,2},{1,3},{2,0},{3,1},{4,6},{5,7},{6,4},{7,5},{8,10},{9,11},{10,... | collective-permute-start | bytes 393224 | tf_op jit(solution)/shard_map/ppermute | solution.py:291
  39.2 5.8 %collective-permute-start.11 = (f32[64,512]{1,0:T(8,128)S(1)}, f32[64,512]{1,0:T(8,128)S(1)}, u32[]{:S(2)}, u32[]{:S(2)}) collective-permute-start(f32[64,512]{1,0:T(8,128)S(1)} %relax_2.2), channel_id=1, source_target_pairs={{0,28},{1,29},{2,6},{3,7},{4,0},{5,1},{6,10},{7,11},{8,4},{9,5},{1... | collective-permute-start | bytes 393224 | tf_op jit(solution)/shard_map/ppermute | solution.py:298
  44.1 7.7 %collective-permute-start.10 = (f32[64,512]{1,0:T(8,128)S(1)}, f32[64,512]{1,0:T(8,128)S(1)}, u32[]{:S(2)}, u32[]{:S(2)}) collective-permute-start(f32[64,512]{1,0:T(8,128)S(1)} %broadcast_select_fusion.4.here), channel_id=1, source_target_pairs={{0,4},{1,5},{2,30},{3,31},{4,8},{5,9},{6,2},{7,3},{8,12},{9,13},{1... | collective-permute-start | bytes 393224 | tf_op jit(solution)/shard_map/ppermute | solution.py:298
  51.9 5.0 %collective-permute-start.12 = (f32[64,512]{1,0:T(8,128)S(1)}, f32[64,512]{1,0:T(8,128)S(1)}, u32[]{:S(2)}, u32[]{:S(2)}) collective-permute-start(f32[64,512]{1,0:T(8,128)S(1)} %relax_3.1), channel_id=1, source_target_pairs={{0,2},{1,3},{2,0},{3,1},{4,6},{5,7},{6,4},{7,5},{8,10},{9,11},{10,... | collective-permute-start | bytes 393224 | tf_op jit(solution)/shard_map/ppermute | solution.py:291
  53.7 6.4 %collective-permute-start.14 = (f32[64,512]{1,0:T(8,128)S(1)}, f32[64,512]{1,0:T(8,128)S(1)}, u32[]{:S(2)}, u32[]{:S(2)}) collective-permute-start(f32[64,512]{1,0:T(8,128)S(1)} %relax_3.1), channel_id=1, source_target_pairs={{0,28},{1,29},{2,6},{3,7},{4,0},{5,1},{6,10},{7,11},{8,4},{9,5},{1... | collective-permute-start | bytes 393224 | tf_op jit(solution)/shard_map/ppermute | solution.py:298
  57.0 7.8 %collective-permute-start.13 = (f32[64,512]{1,0:T(8,128)S(1)}, f32[64,512]{1,0:T(8,128)S(1)}, u32[]{:S(2)}, u32[]{:S(2)}) collective-permute-start(f32[64,512]{1,0:T(8,128)S(1)} %broadcast_select_fusion.here.refs_2_.refs_5_), channel_id=1, source_target_pairs={{0,4},{1,5},{2,30},{3,31},{4,8},{5,9},{6,2},{7,3},{8,12},{9,13},{1... | collective-permute-start | bytes 393224 | tf_op jit(solution)/shard_map/ppermute | solution.py:298
  65.4 5.0 %collective-permute-start.15 = (f32[64,512]{1,0:T(8,128)S(1)}, f32[64,512]{1,0:T(8,128)S(1)}, u32[]{:S(2)}, u32[]{:S(2)}) collective-permute-start(f32[64,512]{1,0:T(8,128)S(1)} %relax_2.3), channel_id=1, source_target_pairs={{0,2},{1,3},{2,0},{3,1},{4,6},{5,7},{6,4},{7,5},{8,10},{9,11},{10,... | collective-permute-start | bytes 393224 | tf_op jit(solution)/shard_map/ppermute | solution.py:291
  65.4 6.4 %collective-permute-start.17 = (f32[64,512]{1,0:T(8,128)S(1)}, f32[64,512]{1,0:T(8,128)S(1)}, u32[]{:S(2)}, u32[]{:S(2)}) collective-permute-start(f32[64,512]{1,0:T(8,128)S(1)} %relax_2.3), channel_id=1, source_target_pairs={{0,28},{1,29},{2,6},{3,7},{4,0},{5,1},{6,10},{7,11},{8,4},{9,5},{1... | collective-permute-start | bytes 393224 | tf_op jit(solution)/shard_map/ppermute | solution.py:298
  70.4 7.7 %collective-permute-start.16 = (f32[64,512]{1,0:T(8,128)S(1)}, f32[64,512]{1,0:T(8,128)S(1)}, u32[]{:S(2)}, u32[]{:S(2)}) collective-permute-start(f32[64,512]{1,0:T(8,128)S(1)} %broadcast_select_fusion.3.here.refs_2_), channel_id=1, source_target_pairs={{0,4},{1,5},{2,30},{3,31},{4,8},{5,9},{6,2},{7,3},{8,12},{9,13},{1... | collective-permute-start | bytes 393224 | tf_op jit(solution)/shard_map/ppermute | solution.py:298
  78.2 5.0 %collective-permute-start.18 = (f32[64,512]{1,0:T(8,128)S(1)}, f32[64,512]{1,0:T(8,128)S(1)}, u32[]{:S(2)}, u32[]{:S(2)}) collective-permute-start(f32[64,512]{1,0:T(8,128)S(1)} %relax_1.3), channel_id=1, source_target_pairs={{0,2},{1,3},{2,0},{3,1},{4,6},{5,7},{6,4},{7,5},{8,10},{9,11},{10,... | collective-permute-start | bytes 393224 | tf_op jit(solution)/shard_map/ppermute | solution.py:291
  79.6 5.2 %collective-permute-start.20 = (f32[64,512]{1,0:T(8,128)S(1)}, f32[64,512]{1,0:T(8,128)S(1)}, u32[]{:S(2)}, u32[]{:S(2)}) collective-permute-start(f32[64,512]{1,0:T(8,128)S(1)} %relax_1.3), channel_id=1, source_target_pairs={{0,28},{1,29},{2,6},{3,7},{4,0},{5,1},{6,10},{7,11},{8,4},{9,5},{1... | collective-permute-start | bytes 393224 | tf_op jit(solution)/shard_map/ppermute | solution.py:298
  83.3 7.7 %collective-permute-start.19 = (f32[64,512]{1,0:T(8,128)S(1)}, f32[64,512]{1,0:T(8,128)S(1)}, u32[]{:S(2)}, u32[]{:S(2)}) collective-permute-start(f32[64,512]{1,0:T(8,128)S(1)} %broadcast_select_fusion.1.here), channel_id=1, source_target_pairs={{0,4},{1,5},{2,30},{3,31},{4,8},{5,9},{6,2},{7,3},{8,12},{9,13},{1... | collective-permute-start | bytes 393224 | tf_op jit(solution)/shard_map/ppermute | solution.py:298
  91.1 1.4 %collective-permute-start.21 = (f32[64,512]{1,0:T(8,128)S(1)}, f32[64,512]{1,0:T(8,128)S(1)}, u32[]{:S(2)}, u32[]{:S(2)}) collective-permute-start(f32[64,512]{1,0:T(8,128)S(1)} %get-tuple-element.88), channel_id=1, source_target_pairs={{0,1},{1,0},{2,3},{3,2},{4,5},{5,4},{6,7},{7,6},{8,9},{9,8},{10,11... | collective-permute-start | bytes 393224 | tf_op jit(solution)/shard_map/ppermute | solution.py:291

commit v11 on v10

--- a/solution.py
+++ b/solution.py
@@ -353,7 +353,7 @@
         if step == len(order) - 1:
             break
         if step == 0:
-            rest = [c for c in range(COLOURS) if c not in plans]
+            rest = list(range(COLOURS))
             for table, more in zip((plans, masks), make_plans(number, rest, *facts, candidate)):
                 table.update(more)
         after = order[step + 1]

time: 93.7 us -> 95.4 us (1.018)
  Pallas kernels: 23.6 us -> 26.1 us
  waiting for transfers between devices: 35.7 us -> 33.3 us
  starting transfers between devices: 31.9 us -> 33.5 us
    ppermute x12, starting transfers between devices: 18.5 us -> 23.1 us  [beside(): return lax.ppermute(value, axis, pairs)]
    ppermute x10, waiting for transfers between devices: 9.79 us -> 6.65 us  [flip(): return lax.ppermute(value, axis, [(i, i ^ bit) for i in range(count)])]
    ppermute x10, starting transfers between devices: 13.4 us -> 10.4 us  [flip(): return lax.ppermute(value, axis, [(i, i ^ bit) for i in range(count)])]
    pallas_call x6, Pallas kernels: 0.83 us -> 2.35 us  [run_relax(): pl.pallas_call(kernel, out_shape=[pltpu.VMEM((half, block), jnp.float32)]...]
  transfers between devices with their start and end apart: 22 -> 22, of which waited for: 18 -> 17; matrix products, arithmetic and copies ran while one was open for 1% -> 1% of each run, Pallas kernels for 20% -> 20%
where the time goes in v11:
time: 95.4 us; the launch traced here: 95 us
  starting transfers between devices  33.5 us (35%)
  waiting for transfers between devices  33.3 us (35%)
  Pallas kernels  26.1 us (27%)
    ppermute x12, waiting for transfers between devices, beside(): return lax.ppermute(value, axis, pairs)  26.6 us
    ppermute x12, starting transfers between devices, beside(): return lax.ppermute(value, axis, pairs)  23.1 us
    pallas_call x5, Pallas kernels, add_older(): pl.pallas_call(functools.partial(older_kernel, newest, slots, len(base)),...  11.8 us
    ppermute x10, starting transfers between devices, flip(): return lax.ppermute(value, axis, [(i, i ^ bit) for i in range(count)])  10.4 us
    ppermute x10, waiting for transfers between devices, flip(): return lax.ppermute(value, axis, [(i, i ^ bit) for i in range(count)])  6.65 us
    pallas_call x2, Pallas kernels, parts(): pl.pallas_call(parts_kernel, out_shape=[pltpu.VMEM(shape, jnp.bfloat16)]...  6.45 us
    pallas_call x1, Pallas kernels, per_device(): pl.pallas_call(first_kernel, out_shape=[pltpu.VMEM((half, block), jnp.flo...  2.35 us
    pallas_call x6, Pallas kernels, run_relax(): pl.pallas_call(kernel, out_shape=[pltpu.VMEM((half, block), jnp.float32)]...  2.35 us
  transfers between devices with their start and end apart: 22, of which 17 were waited for; matrix products, arithmetic and copies ran while one was open for 1% of the time, Pallas kernels for 20%

profile of v11, /device:TPU:0, one launch (start us, length us, event | category | flops | bytes accessed | tf_op | source)
XLA Modules:
  0.0 95.0 jit_solution(1322503148442284053)
XLA Ops:
  0.7 0.6 copy-done
  1.3 2.4 %first.1 = (f32[64,512]{1,0:T(8,128)S(1)}, f32[72,512]{1,0:T(8,128)S(1)}, f32[8,512]{1,0:T(8,128)S(1)}) custom-call(s32[1]{0:T(128)} %bitcast.core_ref, s32[1]{0:T(128)S(6)} %copy.6.colour_ref, s32[1,6]{1,0:T(1,128)S(1)} %copy-done, f32[512,512]{1,0:T(8,128)} %inverse_ref, f32[512,128]{1,0:T(8,128)} %residual_hbm.1), custom_call_target="tpu_custom_call" | custom-call | tf_op jit(solution)/shard_map/first/pallas_call | solution.py:300
  3.7 0.5 collective-permute-start
  4.2 1.0 %collective-permute-done.arrived.sib_start = f32[72,512]{1,0:T(8,128)S(1)} collective-permute-done((f32[72,512]{1,0:T(8,128)S(1)}, f32[72,512]{1,0:T(8,128)S(1)}, u32[]{:S(2)}, u32[]{:S(2)}) %collective-permute-start) | collective-permute-done | bytes 147488 | tf_op jit(solution)/shard_map/ppermute | solution.py:291
  5.2 0.4 collective-permute-start.1
  5.6 0.1 collective-permute-start.2
  5.8 0.1 add_convert_fusion
  5.9 2.9 %collective-permute-start.3 = (f32[72,512]{1,0:T(8,128)S(1)}, f32[72,512]{1,0:T(8,128)S(1)}, u32[]{:S(2)}, u32[]{:S(2)}) collective-permute-start(f32[72,512]{1,0:T(8,128)S(1)} %pad_maximum_fusion), channel_id=1, source_target_pairs={{0,2},{1,3},{2,0},{3,1},{4,6},{5,7},{6,4},{7,5},{8,10},{9,11},{10,... | collective-permute-start | bytes 442376 | tf_op jit(solution)/shard_map/ppermute | solution.py:291
  8.8 4.5 %collective-permute-start.5 = (f32[72,512]{1,0:T(8,128)S(1)}, f32[72,512]{1,0:T(8,128)S(1)}, u32[]{:S(2)}, u32[]{:S(2)}) collective-permute-start(f32[72,512]{1,0:T(8,128)S(1)} %pad_maximum_fusion), channel_id=1, source_target_pairs={{0,28},{1,29},{2,6},{3,7},{4,0},{5,1},{6,10},{7,11},{8,4},{9,5},{1... | collective-permute-start | bytes 442376 | tf_op jit(solution)/shard_map/ppermute | solution.py:298
  13.4 0.1 slice_add_fusion
  13.5 1.4 %collective-permute-start.4 = (f32[72,512]{1,0:T(8,128)S(1)}, f32[72,512]{1,0:T(8,128)S(1)}, u32[]{:S(2)}, u32[]{:S(2)}) collective-permute-start(f32[72,512]{1,0:T(8,128)S(1)} %pad_maximum_fusion.1._.here.refs_2_), channel_id=1, source_target_pairs={{0,4},{1,5},{2,30},{3,31},{4,8},{5,9},{6,2},{7,3},{8,12},{9,13},{1... | collective-permute-start | bytes 442376 | tf_op jit(solution)/shard_map/ppermute | solution.py:298
  15.0 3.3 %own_parts.1 = (bf16[7,512,512]{2,1,0:T(8,128)(2,1)S(1)}, bf16[7,512,512]{2,1,0:T(8,128)(2,1)S(1)}, f32[8,512]{1,0:T(8,128)S(1)}) custom-call(f32[6,512,512]{2,1,0:T(8,128)} %bitcast.8, f32[512,512]{1,0:T(8,128)} %inverse_ref, f32[72,512]{1,0:T(8,128)S(1)} %pad_maximum_fusion.1._.here.refs_2_), custom_call_target="tpu_custom_call" | custom-call | bytes 12582912 | tf_op jit(solution)/shard_map/own_parts/pallas_call | solution.py:219
  18.3 3.1 %sib_parts.1 = (bf16[7,512,512]{2,1,0:T(8,128)(2,1)S(1)}, bf16[7,512,512]{2,1,0:T(8,128)(2,1)S(1)}, f32[8,512]{1,0:T(8,128)S(1)}) custom-call(f32[6,512,512]{2,1,0:T(8,128)} %collective-permute-done.1.tiles_ref, f32[512,512]{1,0:T(8,128)S(1)} %collective-permute-done.2.inverse_ref, f32[8,512]{1,0:T(8,128)S(1)} %get-tuple-element.49._), custom_call_target="tpu_custom_call" | custom-call | bytes 12582912 | tf_op jit(solution)/shard_map/sib_parts/pallas_call | solution.py:219
  21.5 0.1 collective-permute-done.4.inner.refs_0_
  21.6 1.2 %plan_1.1 = (s32[16,128]{1,0:T(8,128)S(1)}, s32[8,512]{1,0:T(8,128)}) custom-call(s32[3]{0:T(128)S(1)} %pad_add_fusion.firsts_ref, f32[8,512]{1,0:T(8,128)S(1)} %get-tuple-element.50._, f32[8,512]{1,0:T(8,128)S(1)} %get-tuple-element.43.own_rows, f32[72,512]{1,0:T(8,128)S(1)} %collective-permute-done.arrived.sib_start, ...), custom_call_target="tpu_custom_call" | custom-call | tf_op jit(solution)/shard_map/plan_1/pallas_call | solution.py:235
  22.7 1.1 %relax_1.2 = (f32[64,512]{1,0:T(8,128)S(1)}, f32[64,512]{1,0:T(8,128)S(1)}) custom-call(s32[16,128]{1,0:T(8,128)S(1)} %get-tuple-element.51.plan, bf16[7,512,512]{2,1,0:T(8,128)(2,1)S(1)} %get-tuple-element.52.own_high, bf16[7,512,512]{2,1,0:T(8,128)(2,1)S(1)} %get-tuple-element.53.own_low, bf16[7,512,512]{2,1,0:T(8,128)(2,1)S(1)} %get-tuple-element.54.sib_high, ...), custom_call_target="tpu_custom_call" | custom-call | flops 536870912 | bytes 4194304 | tf_op jit(solution)/shard_map/relax_1/pallas_call | solution.py:264
  23.9 3.4 %collective-permute-start.6 = (f32[64,512]{1,0:T(8,128)S(1)}, f32[64,512]{1,0:T(8,128)S(1)}, u32[]{:S(2)}, u32[]{:S(2)}) collective-permute-start(f32[64,512]{1,0:T(8,128)S(1)} %get-tuple-element.56._), channel_id=1, source_target_pairs={{0,2},{1,3},{2,0},{3,1},{4,6},{5,7},{6,4},{7,5},{8,10},{9,11},{10,... | collective-permute-start | bytes 393224 | tf_op jit(solution)/shard_map/ppermute | solution.py:291
  27.4 3.3 %collective-permute-start.8 = (f32[64,512]{1,0:T(8,128)S(1)}, f32[64,512]{1,0:T(8,128)S(1)}, u32[]{:S(2)}, u32[]{:S(2)}) collective-permute-start(f32[64,512]{1,0:T(8,128)S(1)} %get-tuple-element.56._), channel_id=1, source_target_pairs={{0,28},{1,29},{2,6},{3,7},{4,0},{5,1},{6,10},{7,11},{8,4},{9,5},{1... | collective-permute-start | bytes 393224 | tf_op jit(solution)/shard_map/ppermute | solution.py:298
  30.6 1.2 %plan_4.1 = (s32[16,128]{1,0:T(8,128)S(1)}, s32[16,128]{1,0:T(8,128)S(1)}, s32[16,128]{1,0:T(8,128)S(1)}, s32[16,128]{1,0:T(8,128)S(1)}, s32[8,512]{1,0:T(8,128)...) custom-call(s32[3]{0:T(128)S(1)} %pad_add_fusion.firsts_ref, ...), custom_call_target="tpu_custom_call" | custom-call | tf_op jit(solution)/shard_map/plan_4/pallas_call | solution.py:235
  31.8 0.1 collective-permute-start.7
  32.0 1.5 %collective-permute-done.8.outer.refs_4_ = f32[64,512]{1,0:T(8,128)S(1)} collective-permute-done((f32[64,512]{1,0:T(8,128)S(1)}, f32[64,512]{1,0:T(8,128)S(1)}, u32[]{:S(2)}, u32[]{:S(2)}) %collective-permute-start.8) | collective-permute-done | bytes 131104 | tf_op jit(solution)/shard_map/ppermute | solution.py:298
  33.4 3.6 %older_2.2 = (f32[64,512]{1,0:T(8,128)S(1)}, f32[64,512]{1,0:T(8,128)S(1)}, bf16[512,512]{1,0:T(8,128)(2,1)S(1)}, bf16[512,512]{1,0:T(8,128)(2,1)S(1)}) custom-call(s32[16,128]{1,0:T(8,128)S(1)} %get-tuple-element.59.plan, bf16[7,512,512]{2,1,0:T(8,128)(2,1)S(1)} %get-tuple-element.52.own_high, bf16[7,512,512]{2,1,0:T(8,128)(2,1)S(1)} %get-tuple-element.53.own_low, ...), custom_call_target="tpu_custom_call" | custom-call | flops 671088640 | bytes 6291456 | tf_op jit(solution)/shard_map/older_2/pallas_call | solution.py:250
  37.1 2.5 %collective-permute-done.7.inner.refs_3_.refs_0_ = f32[64,512]{1,0:T(8,128)S(1)} collective-permute-done((f32[64,512]{1,0:T(8,128)S(1)}, f32[64,512]{1,0:T(8,128)S(1)}, u32[]{:S(2)}, u32[]{:S(2)}) %collective-permute-start.7) | collective-permute-done | bytes 131104 | tf_op jit(solution)/shard_map/ppermute | solution.py:298
  39.6 0.5 relax_2.2
  40.2 3.9 %collective-permute-start.11 = (f32[64,512]{1,0:T(8,128)S(1)}, f32[64,512]{1,0:T(8,128)S(1)}, u32[]{:S(2)}, u32[]{:S(2)}) collective-permute-start(f32[64,512]{1,0:T(8,128)S(1)} %relax_2.2), channel_id=1, source_target_pairs={{0,28},{1,29},{2,6},{3,7},{4,0},{5,1},{6,10},{7,11},{8,4},{9,5},{1... | collective-permute-start | bytes 393224 | tf_op jit(solution)/shard_map/ppermute | solution.py:298
  44.1 1.0 %collective-permute-done.9 = f32[64,512]{1,0:T(8,128)S(1)} collective-permute-done((f32[64,512]{1,0:T(8,128)S(1)}, f32[64,512]{1,0:T(8,128)S(1)}, u32[]{:S(2)}, u32[]{:S(2)}) %collective-permute-start.9) | collective-permute-done | bytes 131104 | tf_op jit(solution)/shard_map/ppermute | solution.py:291
  45.2 1.4 %collective-permute-done.11.outer = f32[64,512]{1,0:T(8,128)S(1)} collective-permute-done((f32[64,512]{1,0:T(8,128)S(1)}, f32[64,512]{1,0:T(8,128)S(1)}, u32[]{:S(2)}, u32[]{:S(2)}) %collective-permute-start.11) | collective-permute-done | bytes 131104 | tf_op jit(solution)/shard_map/ppermute | solution.py:298
  46.6 0.9 older_3.1
  47.5 5.4 %collective-permute-done.10.inner = f32[64,512]{1,0:T(8,128)S(1)} collective-permute-done((f32[64,512]{1,0:T(8,128)S(1)}, f32[64,512]{1,0:T(8,128)S(1)}, u32[]{:S(2)}, u32[]{:S(2)}) %collective-permute-start.10) | collective-permute-done | bytes 131104 | tf_op jit(solution)/shard_map/ppermute | solution.py:298
  52.9 2.8 %collective-permute-start.12 = (f32[64,512]{1,0:T(8,128)S(1)}, f32[64,512]{1,0:T(8,128)S(1)}, u32[]{:S(2)}, u32[]{:S(2)}) collective-permute-start(f32[64,512]{1,0:T(8,128)S(1)} %relax_3.1), channel_id=1, source_target_pairs={{0,2},{1,3},{2,0},{3,1},{4,6},{5,7},{6,4},{7,5},{8,10},{9,11},{10,... | collective-permute-start | bytes 393224 | tf_op jit(solution)/shard_map/ppermute | solution.py:291
  55.7 1.9 %collective-permute-start.14 = (f32[64,512]{1,0:T(8,128)S(1)}, f32[64,512]{1,0:T(8,128)S(1)}, u32[]{:S(2)}, u32[]{:S(2)}) collective-permute-start(f32[64,512]{1,0:T(8,128)S(1)} %relax_3.1), channel_id=1, source_target_pairs={{0,28},{1,29},{2,6},{3,7},{4,0},{5,1},{6,10},{7,11},{8,4},{9,5},{1... | collective-permute-start | bytes 393224 | tf_op jit(solution)/shard_map/ppermute | solution.py:298
  57.6 1.0 %collective-permute-done.12 = f32[64,512]{1,0:T(8,128)S(1)} collective-permute-done((f32[64,512]{1,0:T(8,128)S(1)}, f32[64,512]{1,0:T(8,128)S(1)}, u32[]{:S(2)}, u32[]{:S(2)}) %collective-permute-start.12) | collective-permute-done | bytes 131104 | tf_op jit(solution)/shard_map/ppermute | solution.py:291
  58.7 3.4 %collective-permute-done.14.outer.refs_1_.refs_4_ = f32[64,512]{1,0:T(8,128)S(1)} collective-permute-done((f32[64,512]{1,0:T(8,128)S(1)}, f32[64,512]{1,0:T(8,128)S(1)}, u32[]{:S(2)}, u32[]{:S(2)}) %collective-permute-start.14) | collective-permute-done | bytes 131104 | tf_op jit(solution)/shard_map/ppermute | solution.py:298
  62.1 2.3 %older_2.3 = (f32[64,512]{1,0:T(8,128)}, f32[64,512]{1,0:T(8,128)S(1)}, bf16[512,512]{1,0:T(8,128)(2,1)S(1)}, bf16[512,512]{1,0:T(8,128)(2,1)S(1)}) custom-call(s32[16,128]{1,0:T(8,128)S(1)} %get-tuple-element.59.plan, bf16[7,512,512]{2,1,0:T(8,128)(2,1)S(1)} %get-tuple-element.52.own_high, bf16[7,512,512]{2,1,0:T(8,128)(2,1)S(1)} %get-tuple-element.53.own_low, ...), custom_call_target="tpu_custom_call" | custom-call | flops 402653184 | bytes 6291456 | tf_op jit(solution)/shard_map/older_2/pallas_call | solution.py:250
  64.4 2.1 %collective-permute-done.13.inner.refs_0_.refs_3_ = f32[64,512]{1,0:T(8,128)S(1)} collective-permute-done((f32[64,512]{1,0:T(8,128)S(1)}, f32[64,512]{1,0:T(8,128)S(1)}, u32[]{:S(2)}, u32[]{:S(2)}) %collective-permute-start.13) | collective-permute-done | bytes 131104 | tf_op jit(solution)/shard_map/ppermute | solution.py:298
  66.6 3.8 %collective-permute-start.17 = (f32[64,512]{1,0:T(8,128)S(1)}, f32[64,512]{1,0:T(8,128)S(1)}, u32[]{:S(2)}, u32[]{:S(2)}) collective-permute-start(f32[64,512]{1,0:T(8,128)S(1)} %relax_2.3), channel_id=1, source_target_pairs={{0,28},{1,29},{2,6},{3,7},{4,0},{5,1},{6,10},{7,11},{8,4},{9,5},{1... | collective-permute-start | bytes 393224 | tf_op jit(solution)/shard_map/ppermute | solution.py:298
  70.5 1.1 %collective-permute-done.15 = f32[64,512]{1,0:T(8,128)S(1)} collective-permute-done((f32[64,512]{1,0:T(8,128)S(1)}, f32[64,512]{1,0:T(8,128)S(1)}, u32[]{:S(2)}, u32[]{:S(2)}) %collective-permute-start.15) | collective-permute-done | bytes 131104 | tf_op jit(solution)/shard_map/ppermute | solution.py:291
  71.7 1.4 %collective-permute-done.17.outer.refs_1_ = f32[64,512]{1,0:T(8,128)S(1)} collective-permute-done((f32[64,512]{1,0:T(8,128)S(1)}, f32[64,512]{1,0:T(8,128)S(1)}, u32[]{:S(2)}, u32[]{:S(2)}) %collective-permute-start.17) | collective-permute-done | bytes 131104 | tf_op jit(solution)/shard_map/ppermute | solution.py:298
  73.1 4.3 %older_1.1 = (f32[64,512]{1,0:T(8,128)}, f32[64,512]{1,0:T(8,128)S(1)}, bf16[512,512]{1,0:T(8,128)(2,1)S(1)}, bf16[512,512]{1,0:T(8,128)(2,1)S(1)}) custom-call(s32[16,128]{1,0:T(8,128)S(1)} %get-tuple-element.72.plan, bf16[7,512,512]{2,1,0:T(8,128)(2,1)S(1)} %get-tuple-element.52.own_high, bf16[7,512,512]{2,1,0:T(8,128)(2,1)S(1)} %get-tuple-element.53.own_low, ...), custom_call_target="tpu_custom_call" | custom-call | flops 671088640 | bytes 6291456 | tf_op jit(solution)/shard_map/older_1/pallas_call | solution.py:250
  77.4 2.0 %collective-permute-done.16.inner.refs_0_ = f32[64,512]{1,0:T(8,128)S(1)} collective-permute-done((f32[64,512]{1,0:T(8,128)S(1)}, f32[64,512]{1,0:T(8,128)S(1)}, u32[]{:S(2)}, u32[]{:S(2)}) %collective-permute-start.16) | collective-permute-done | bytes 131104 | tf_op jit(solution)/shard_map/ppermute | solution.py:298
  79.3 0.5 relax_1.3
  79.9 3.8 %collective-permute-start.20 = (f32[64,512]{1,0:T(8,128)S(1)}, f32[64,512]{1,0:T(8,128)S(1)}, u32[]{:S(2)}, u32[]{:S(2)}) collective-permute-start(f32[64,512]{1,0:T(8,128)S(1)} %relax_1.3), channel_id=1, source_target_pairs={{0,28},{1,29},{2,6},{3,7},{4,0},{5,1},{6,10},{7,11},{8,4},{9,5},{1... | collective-permute-start | bytes 393224 | tf_op jit(solution)/shard_map/ppermute | solution.py:298
  83.8 1.1 %collective-permute-done.18 = f32[64,512]{1,0:T(8,128)S(1)} collective-permute-done((f32[64,512]{1,0:T(8,128)S(1)}, f32[64,512]{1,0:T(8,128)S(1)}, u32[]{:S(2)}, u32[]{:S(2)}) %collective-permute-start.18) | collective-permute-done | bytes 131104 | tf_op jit(solution)/shard_map/ppermute | solution.py:291
  85.0 1.3 %collective-permute-done.20.outer = f32[64,512]{1,0:T(8,128)S(1)} collective-permute-done((f32[64,512]{1,0:T(8,128)S(1)}, f32[64,512]{1,0:T(8,128)S(1)}, u32[]{:S(2)}, u32[]{:S(2)}) %collective-permute-start.20) | collective-permute-done | bytes 131104 | tf_op jit(solution)/shard_map/ppermute | solution.py:298
  86.3 0.7 older_0.1
  87.0 5.6 %collective-permute-done.19.inner = f32[64,512]{1,0:T(8,128)S(1)} collective-permute-done((f32[64,512]{1,0:T(8,128)S(1)}, f32[64,512]{1,0:T(8,128)S(1)}, u32[]{:S(2)}, u32[]{:S(2)}) %collective-permute-start.19) | collective-permute-done | bytes 131104 | tf_op jit(solution)/shard_map/ppermute | solution.py:298
  92.8 1.3 %collective-permute-done.21.other_ref = f32[64,512]{1,0:T(8,128)S(1)} collective-permute-done((f32[64,512]{1,0:T(8,128)S(1)}, f32[64,512]{1,0:T(8,128)S(1)}, u32[]{:S(2)}, u32[]{:S(2)}) %collective-permute-start.21) | collective-permute-done | bytes 131104 | tf_op jit(solution)/shard_map/ppermute | solution.py:291
  94.2 0.8 last.1
  (35 shorter events, 1.1 us)
Async XLA Ops:
  0.7 0.7 copy-start
  3.7 1.5 %collective-permute-start = (f32[72,512]{1,0:T(8,128)S(1)}, f32[72,512]{1,0:T(8,128)S(1)}, u32[]{:S(2)}, u32[]{:S(2)}) collective-permute-start(f32[72,512]{1,0:T(8,128)S(1)} %get-tuple-element.44), channel_id=1, source_target_pairs={{0,1},{1,0},{2,3},{3,2},{4,5},{5,4},{6,7},{7,6},{8,9},{9,8},{10,11... | collective-permute-start | bytes 442376 | tf_op jit(solution)/shard_map/ppermute | solution.py:291
  5.2 13.1 %collective-permute-start.1 = (f32[6,512,512]{2,1,0:T(8,128)}, f32[6,512,512]{2,1,0:T(8,128)}, u32[]{:S(2)}, u32[]{:S(2)}) collective-permute-start(f32[6,512,512]{2,1,0:T(8,128)} %bitcast.7), channel_id=1, source_target_pairs={{0,1},{1,0},{2,3},{3,2},{4,5},{5,4},{6,7},{7,6},{8,9},{9,8},{10,11... | collective-permute-start | bytes 18874376 | tf_op jit(solution)/shard_map/ppermute | solution.py:291
  5.6 12.8 %collective-permute-start.2 = (f32[512,512]{1,0:T(8,128)}, f32[512,512]{1,0:T(8,128)S(1)}, u32[]{:S(2)}, u32[]{:S(2)}) collective-permute-start(f32[512,512]{1,0:T(8,128)} %inverse_ref), channel_id=1, source_target_pairs={{0,1},{1,0},{2,3},{3,2},{4,5},{5,4},{6,7},{7,6},{8,9},{9,8},{10,11... | collective-permute-start | bytes 3145736 | tf_op jit(solution)/shard_map/ppermute | solution.py:291
  5.9 7.5 %collective-permute-start.3 = (f32[72,512]{1,0:T(8,128)S(1)}, f32[72,512]{1,0:T(8,128)S(1)}, u32[]{:S(2)}, u32[]{:S(2)}) collective-permute-start(f32[72,512]{1,0:T(8,128)S(1)} %pad_maximum_fusion), channel_id=1, source_target_pairs={{0,2},{1,3},{2,0},{3,1},{4,6},{5,7},{6,4},{7,5},{8,10},{9,11},{10,... | collective-permute-start | bytes 442376 | tf_op jit(solution)/shard_map/ppermute | solution.py:291
  8.8 12.7 %collective-permute-start.5 = (f32[72,512]{1,0:T(8,128)S(1)}, f32[72,512]{1,0:T(8,128)S(1)}, u32[]{:S(2)}, u32[]{:S(2)}) collective-permute-start(f32[72,512]{1,0:T(8,128)S(1)} %pad_maximum_fusion), channel_id=1, source_target_pairs={{0,28},{1,29},{2,6},{3,7},{4,0},{5,1},{6,10},{7,11},{8,4},{9,5},{1... | collective-permute-start | bytes 442376 | tf_op jit(solution)/shard_map/ppermute | solution.py:298
  13.5 8.1 %collective-permute-start.4 = (f32[72,512]{1,0:T(8,128)S(1)}, f32[72,512]{1,0:T(8,128)S(1)}, u32[]{:S(2)}, u32[]{:S(2)}) collective-permute-start(f32[72,512]{1,0:T(8,128)S(1)} %pad_maximum_fusion.1._.here.refs_2_), channel_id=1, source_target_pairs={{0,4},{1,5},{2,30},{3,31},{4,8},{5,9},{6,2},{7,3},{8,12},{9,13},{1... | collective-permute-start | bytes 442376 | tf_op jit(solution)/shard_map/ppermute | solution.py:298
  23.9 7.9 %collective-permute-start.6 = (f32[64,512]{1,0:T(8,128)S(1)}, f32[64,512]{1,0:T(8,128)S(1)}, u32[]{:S(2)}, u32[]{:S(2)}) collective-permute-start(f32[64,512]{1,0:T(8,128)S(1)} %get-tuple-element.56._), channel_id=1, source_target_pairs={{0,2},{1,3},{2,0},{3,1},{4,6},{5,7},{6,4},{7,5},{8,10},{9,11},{10,... | collective-permute-start | bytes 393224 | tf_op jit(solution)/shard_map/ppermute | solution.py:291
  27.4 6.1 %collective-permute-start.8 = (f32[64,512]{1,0:T(8,128)S(1)}, f32[64,512]{1,0:T(8,128)S(1)}, u32[]{:S(2)}, u32[]{:S(2)}) collective-permute-start(f32[64,512]{1,0:T(8,128)S(1)} %get-tuple-element.56._), channel_id=1, source_target_pairs={{0,28},{1,29},{2,6},{3,7},{4,0},{5,1},{6,10},{7,11},{8,4},{9,5},{1... | collective-permute-start | bytes 393224 | tf_op jit(solution)/shard_map/ppermute | solution.py:298
  31.8 7.7 %collective-permute-start.7 = (f32[64,512]{1,0:T(8,128)S(1)}, f32[64,512]{1,0:T(8,128)S(1)}, u32[]{:S(2)}, u32[]{:S(2)}) collective-permute-start(f32[64,512]{1,0:T(8,128)S(1)} %broadcast_select_fusion.2.here.refs_5_), channel_id=1, source_target_pairs={{0,4},{1,5},{2,30},{3,31},{4,8},{5,9},{6,2},{7,3},{8,12},{9,13},{1... | collective-permute-start | bytes 393224 | tf_op jit(solution)/shard_map/ppermute | solution.py:298
  40.1 5.0 %collective-permute-start.9 = (f32[64,512]{1,0:T(8,128)S(1)}, f32[64,512]{1,0:T(8,128)S(1)}, u32[]{:S(2)}, u32[]{:S(2)}) collective-permute-start(f32[64,512]{1,0:T(8,128)S(1)} %relax_2.2), channel_id=1, source_target_pairs={{0,2},{1,3},{2,0},{3,1},{4,6},{5,7},{6,4},{7,5},{8,10},{9,11},{10,... | collective-permute-start | bytes 393224 | tf_op jit(solution)/shard_map/ppermute | solution.py:291
  40.2 6.4 %collective-permute-start.11 = (f32[64,512]{1,0:T(8,128)S(1)}, f32[64,512]{1,0:T(8,128)S(1)}, u32[]{:S(2)}, u32[]{:S(2)}) collective-permute-start(f32[64,512]{1,0:T(8,128)S(1)} %relax_2.2), channel_id=1, source_target_pairs={{0,28},{1,29},{2,6},{3,7},{4,0},{5,1},{6,10},{7,11},{8,4},{9,5},{1... | collective-permute-start | bytes 393224 | tf_op jit(solution)/shard_map/ppermute | solution.py:298
  45.2 7.7 %collective-permute-start.10 = (f32[64,512]{1,0:T(8,128)S(1)}, f32[64,512]{1,0:T(8,128)S(1)}, u32[]{:S(2)}, u32[]{:S(2)}) collective-permute-start(f32[64,512]{1,0:T(8,128)S(1)} %broadcast_select_fusion.4.here), channel_id=1, source_target_pairs={{0,4},{1,5},{2,30},{3,31},{4,8},{5,9},{6,2},{7,3},{8,12},{9,13},{1... | collective-permute-start | bytes 393224 | tf_op jit(solution)/shard_map/ppermute | solution.py:298
  52.9 5.7 %collective-permute-start.12 = (f32[64,512]{1,0:T(8,128)S(1)}, f32[64,512]{1,0:T(8,128)S(1)}, u32[]{:S(2)}, u32[]{:S(2)}) collective-permute-start(f32[64,512]{1,0:T(8,128)S(1)} %relax_3.1), channel_id=1, source_target_pairs={{0,2},{1,3},{2,0},{3,1},{4,6},{5,7},{6,4},{7,5},{8,10},{9,11},{10,... | collective-permute-start | bytes 393224 | tf_op jit(solution)/shard_map/ppermute | solution.py:291
  55.7 6.4 %collective-permute-start.14 = (f32[64,512]{1,0:T(8,128)S(1)}, f32[64,512]{1,0:T(8,128)S(1)}, u32[]{:S(2)}, u32[]{:S(2)}) collective-permute-start(f32[64,512]{1,0:T(8,128)S(1)} %relax_3.1), channel_id=1, source_target_pairs={{0,28},{1,29},{2,6},{3,7},{4,0},{5,1},{6,10},{7,11},{8,4},{9,5},{1... | collective-permute-start | bytes 393224 | tf_op jit(solution)/shard_map/ppermute | solution.py:298
  58.7 7.8 %collective-permute-start.13 = (f32[64,512]{1,0:T(8,128)S(1)}, f32[64,512]{1,0:T(8,128)S(1)}, u32[]{:S(2)}, u32[]{:S(2)}) collective-permute-start(f32[64,512]{1,0:T(8,128)S(1)} %broadcast_select_fusion.here.refs_2_.refs_5_), channel_id=1, source_target_pairs={{0,4},{1,5},{2,30},{3,31},{4,8},{5,9},{6,2},{7,3},{8,12},{9,13},{1... | collective-permute-start | bytes 393224 | tf_op jit(solution)/shard_map/ppermute | solution.py:298
  66.6 5.0 %collective-permute-start.15 = (f32[64,512]{1,0:T(8,128)S(1)}, f32[64,512]{1,0:T(8,128)S(1)}, u32[]{:S(2)}, u32[]{:S(2)}) collective-permute-start(f32[64,512]{1,0:T(8,128)S(1)} %relax_2.3), channel_id=1, source_target_pairs={{0,2},{1,3},{2,0},{3,1},{4,6},{5,7},{6,4},{7,5},{8,10},{9,11},{10,... | collective-permute-start | bytes 393224 | tf_op jit(solution)/shard_map/ppermute | solution.py:291
  66.6 6.4 %collective-permute-start.17 = (f32[64,512]{1,0:T(8,128)S(1)}, f32[64,512]{1,0:T(8,128)S(1)}, u32[]{:S(2)}, u32[]{:S(2)}) collective-permute-start(f32[64,512]{1,0:T(8,128)S(1)} %relax_2.3), channel_id=1, source_target_pairs={{0,28},{1,29},{2,6},{3,7},{4,0},{5,1},{6,10},{7,11},{8,4},{9,5},{1... | collective-permute-start | bytes 393224 | tf_op jit(solution)/shard_map/ppermute | solution.py:298
  71.6 7.7 %collective-permute-start.16 = (f32[64,512]{1,0:T(8,128)S(1)}, f32[64,512]{1,0:T(8,128)S(1)}, u32[]{:S(2)}, u32[]{:S(2)}) collective-permute-start(f32[64,512]{1,0:T(8,128)S(1)} %broadcast_select_fusion.3.here.refs_2_), channel_id=1, source_target_pairs={{0,4},{1,5},{2,30},{3,31},{4,8},{5,9},{6,2},{7,3},{8,12},{9,13},{1... | collective-permute-start | bytes 393224 | tf_op jit(solution)/shard_map/ppermute | solution.py:298
  79.9 5.0 %collective-permute-start.18 = (f32[64,512]{1,0:T(8,128)S(1)}, f32[64,512]{1,0:T(8,128)S(1)}, u32[]{:S(2)}, u32[]{:S(2)}) collective-permute-start(f32[64,512]{1,0:T(8,128)S(1)} %relax_1.3), channel_id=1, source_target_pairs={{0,2},{1,3},{2,0},{3,1},{4,6},{5,7},{6,4},{7,5},{8,10},{9,11},{10,... | collective-permute-start | bytes 393224 | tf_op jit(solution)/shard_map/ppermute | solution.py:291
  79.9 6.3 %collective-permute-start.20 = (f32[64,512]{1,0:T(8,128)S(1)}, f32[64,512]{1,0:T(8,128)S(1)}, u32[]{:S(2)}, u32[]{:S(2)}) collective-permute-start(f32[64,512]{1,0:T(8,128)S(1)} %relax_1.3), channel_id=1, source_target_pairs={{0,28},{1,29},{2,6},{3,7},{4,0},{5,1},{6,10},{7,11},{8,4},{9,5},{1... | collective-permute-start | bytes 393224 | tf_op jit(solution)/shard_map/ppermute | solution.py:298
  84.9 7.7 %collective-permute-start.19 = (f32[64,512]{1,0:T(8,128)S(1)}, f32[64,512]{1,0:T(8,128)S(1)}, u32[]{:S(2)}, u32[]{:S(2)}) collective-permute-start(f32[64,512]{1,0:T(8,128)S(1)} %broadcast_select_fusion.1.here), channel_id=1, source_target_pairs={{0,4},{1,5},{2,30},{3,31},{4,8},{5,9},{6,2},{7,3},{8,12},{9,13},{1... | collective-permute-start | bytes 393224 | tf_op jit(solution)/shard_map/ppermute | solution.py:298
  92.8 1.4 %collective-permute-start.21 = (f32[64,512]{1,0:T(8,128)S(1)}, f32[64,512]{1,0:T(8,128)S(1)}, u32[]{:S(2)}, u32[]{:S(2)}) collective-permute-start(f32[64,512]{1,0:T(8,128)S(1)} %get-tuple-element.90), channel_id=1, source_target_pairs={{0,1},{1,0},{2,3},{3,2},{4,5},{5,4},{6,7},{7,6},{8,9},{9,8},{10,11... | collective-permute-start | bytes 393224 | tf_op jit(solution)/shard_map/ppermute | solution.py:291
